TPU v7x, 32 devices: a whole 2x2x4 slice. The times are simulated.
32 devices in a mesh: row: 16 (over z, y, x), col: 2 (over core).
Axes of the slice: x: 2, y: 2, z: 4, core: 2. Of those that a mesh axis runs over, the one named last changes fastest.
Arguments:
- tokens: bfloat16 [2, 2048, 2048], P(None, 'row'), may hold values from -6 to 6
- cotangent: bfloat16 [2, 2048, 2048], P(None, 'row'), may hold values from -6 to 6
- deal_order: int32 [2, 2048], P(None, 'row'), may hold values from 0 to 2047, as said below
- seq_lengths: int32 [2, 16, 3], P(None, 'row'), may hold values from 1 to 96, 128 in all within a row
- mixer_norm_gain: float32 [2048], replicated, may hold values from 0.5 to 1.5
- mamba_gate_weight: bfloat16 [2048, 3072], P('row', 'col'), may hold values from -0.125 to 0.125
- mamba_input_weight: bfloat16 [2048, 3072], P('row', 'col'), may hold values from -0.125 to 0.125
- state_weight: bfloat16 [2048, 512], P('row'), may hold values from -0.125 to 0.125
- step_weight: bfloat16 [2048, 48], P('row', 'col'), may hold values from -0.0625 to 0.0625
- conv_input: float32 [4, 3072], P(None, 'col'), may hold values from -3 to 3
- conv_input_bias: float32 [3072], P('col'), may hold values from -2 to 2
- conv_state: float32 [4, 512], replicated, may hold values from -3 to 3
- conv_state_bias: float32 [512], replicated, may hold values from -2 to 2
- step_bias: float32 [48], P('col'), may hold values from -4.5 to -2
- decay_log: float32 [48], P('col'), may hold values from -3 to 1
- skip_scale: float32 [48], P('col'), may hold values from 0.5 to 1.5
- mamba_out_weight: bfloat16 [3072, 2048], P('col', 'row'), may hold values from -0.109375 to 0.109375
- query_weight: bfloat16 [2048, 1024], P('row', 'col'), may hold values from -0.125 to 0.125
- key_weight: bfloat16 [2048, 256], P('row', 'col'), may hold values from -0.125 to 0.125
- value_weight: bfloat16 [2048, 256], P('row', 'col'), may hold values from -0.125 to 0.125
- attn_out_weight: bfloat16 [1024, 2048], P('col', 'row'), may hold values from -0.5 to 0.5
- ff_norm_gain: float32 [2048], replicated, may hold values from 0.5 to 1.5
- gate_weight: bfloat16 [2048, 4096], P('row', 'col'), may hold values from -0.125 to 0.125
- up_weight: bfloat16 [2048, 4096], P('row', 'col'), may hold values from -0.125 to 0.125
- down_weight: bfloat16 [4096, 2048], P('col', 'row'), may hold values from -0.09375 to 0.09375
Outputs:
- output: bfloat16 [2, 2048, 2048], P(None, 'row')
- grad_tokens: bfloat16 [2, 2048, 2048], P(None, 'row')
- grad_mixer_norm_gain: float32 [2048], replicated
- grad_mamba_gate_weight: float32 [2048, 3072], P('row', 'col')
- grad_mamba_input_weight: float32 [2048, 3072], P('row', 'col')
- grad_state_weight: float32 [2048, 512], P('row')
- grad_step_weight: float32 [2048, 48], P('row', 'col')
- grad_conv_input: float32 [4, 3072], P(None, 'col')
- grad_conv_input_bias: float32 [3072], P('col')
- grad_conv_state: float32 [4, 512], replicated
- grad_conv_state_bias: float32 [512], replicated
- grad_step_bias: float32 [48], P('col')
- grad_decay_log: float32 [48], P('col')
- grad_skip_scale: float32 [48], P('col')
- grad_mamba_out_weight: float32 [3072, 2048], P('col', 'row')
- grad_query_weight: float32 [2048, 1024], P('row', 'col')
- grad_key_weight: float32 [2048, 256], P('row', 'col')
- grad_value_weight: float32 [2048, 256], P('row', 'col')
- grad_attn_out_weight: float32 [1024, 2048], P('col', 'row')
- grad_ff_norm_gain: float32 [2048], replicated
- grad_gate_weight: float32 [2048, 4096], P('row', 'col')
- grad_up_weight: float32 [2048, 4096], P('row', 'col')
- grad_down_weight: float32 [4096, 2048], P('col', 'row')
Inputs may be any that keep to these rules, and one draw needn't show every extreme that they name: For each micro-batch, deal_order names every token of it once; the slots of each device take exactly 8 tokens from the rows of each device. `seq_lengths`: the 3 lengths of one device and micro-batch sum to 128.
All inputs are finite; a program needn't handle non-finite values.
Results may differ from a plain program's by a relative error of at most 0.018.
Values may be sent and summed in bfloat16 or wider, within the bound.
A program may use at most 320 MiB of HBM per device.

v0:
```python
from functools import partial

import jax
import jax.numpy as jnp
from jax import lax
from jax.sharding import PartitionSpec as P

HD = 128


EPS = 1e-05
NEG_LARGE = -1e30
ROPE_BASE = 100000000000.0


def matmul(first_op, second_op):
    return jnp.dot(first_op, second_op, preferred_element_type=jnp.float32)


def matmul_trans(first_op, second_op):
    return lax.dot_general(
        first_op, second_op, (((1,), (1,)), ((), ())), preferred_element_type=jnp.float32
    )


def matmul_left(first_op, second_op):
    return lax.dot_general(
        first_op, second_op, (((0,), (0,)), ((), ())), preferred_element_type=jnp.float32
    )


def rms_scale(values, gain_vec):
    return values * lax.rsqrt(jnp.mean(values * values, axis=-1, keepdims=True) + EPS) * gain_vec


def layout(lengths, slot_count):
    seg_ends = jnp.cumsum(lengths)
    starts = seg_ends - lengths
    places = jnp.arange(slot_count, dtype=jnp.int32)
    segment = jnp.sum((places[:, None] >= seg_ends[None, :]).astype(jnp.int32), axis=1)
    member = segment[:, None] == jnp.arange(lengths.shape[0], dtype=jnp.int32)[None, :]
    within = places - jnp.sum(jnp.where(member, starts[None, :], 0), axis=1)
    allowed = (segment[:, None] == segment[None, :]) & (places[:, None] >= places[None, :])
    return (segment, within, allowed)


def causal_conv(values_in, kernel, bias_vec, segment):
    slot_count, channels = values_in.shape
    kernel_len = kernel.shape[0]
    summed = bias_vec[None, :] + kernel[kernel_len - 1][None, :] * values_in
    for shift_by in range(1, kernel_len):
        shifted = jnp.concatenate(
            [jnp.zeros((shift_by, channels), values_in.dtype), values_in[: slot_count - shift_by]],
            axis=0,
        )
        earlier = jnp.concatenate(
            [jnp.full((shift_by,), -1, jnp.int32), segment[: slot_count - shift_by]], axis=0
        )
        shifted = jnp.where((earlier == segment)[:, None], shifted, 0.0)
        summed = summed + kernel[kernel_len - 1 - shift_by][None, :] * shifted
    return jax.nn.silu(summed)


def decay_mix(intersection, step_raw, step_bias, decay_log, allowed):
    step_size = jax.nn.softplus(step_raw + step_bias[None, :])
    rates = -jnp.exp(decay_log)
    levels = jnp.cumsum(step_size * rates[None, :], axis=0).T
    spread = levels[:, :, None] - levels[:, None, :]
    decays = jnp.where(allowed[None], jnp.exp(jnp.where(allowed[None], spread, 0.0)), 0.0)
    return intersection[None] * decays * step_size.T[:, None, :]


def gate_mix(scanned, conv_out, mamba_gate, skip_scale):
    slot_count, channels = conv_out.shape
    per_head = channels // skip_scale.shape[0]
    mixed_out = (
        scanned.reshape(slot_count, channels) + conv_out * jnp.repeat(skip_scale, per_head)[None, :]
    )
    return mixed_out * jax.nn.silu(mamba_gate)


def rotary(vectors, within, heads):
    slot_count = vectors.shape[0]
    head_dim = vectors.shape[1] // heads
    half_dim = head_dim // 2
    inverse = ROPE_BASE ** (-2.0 * jnp.arange(half_dim, dtype=jnp.float32) / head_dim)
    angles = within.astype(jnp.float32)[:, None] * inverse[None, :]
    cosine = jnp.concatenate([jnp.cos(angles), jnp.cos(angles)], axis=1)[:, None, :]
    sine = jnp.concatenate([jnp.sin(angles), jnp.sin(angles)], axis=1)[:, None, :]
    shaped = vectors.reshape(slot_count, heads, head_dim)
    turned = jnp.concatenate([-shaped[..., half_dim:], shaped[..., :half_dim]], axis=-1)
    return (shaped * cosine + turned * sine).reshape(slot_count, heads * head_dim)


def swiglu(ff_gate, ff_up):
    return jax.nn.silu(ff_gate) * ff_up


def score_block(query_rot, key_rot, allowed):
    raw_scores = jnp.einsum(
        "ikrd,jkd->krij", query_rot, key_rot, preferred_element_type=jnp.float32
    )
    return jnp.where(allowed[None, None], raw_scores * HD ** (-0.5), NEG_LARGE)


def forward_pass(block_tokens, lengths, weights, smalls):
    (
        mamba_gate_weight,
        mamba_input_weight,
        state_weight,
        step_weight,
        query_weight,
        key_weight,
        value_weight,
        gate_weight,
        up_weight,
        mamba_out_weight,
        attn_out_weight,
        down_weight,
    ) = weights
    (
        mixer_norm_gain,
        conv_input,
        conv_input_bias,
        conv_state,
        conv_state_bias,
        step_bias,
        decay_log,
        skip_scale,
        ff_norm_gain,
    ) = smalls
    slot_count = block_tokens.shape[0]
    segment, within, allowed = layout(lengths, slot_count)
    normed_one = rms_scale(block_tokens, mixer_norm_gain).astype(jnp.bfloat16)
    mamba_gate = matmul(normed_one, mamba_gate_weight)
    conv_in = matmul(normed_one, mamba_input_weight)
    state_raw = matmul(normed_one, state_weight)
    step_raw = matmul(normed_one, step_weight)
    conv_out = causal_conv(conv_in, conv_input, conv_input_bias, segment)
    state_act = causal_conv(state_raw, conv_state, conv_state_bias, segment)
    state_dim = state_act.shape[1] // 2
    state_in_low = state_act[:, :state_dim].astype(jnp.bfloat16)
    state_out_low = state_act[:, state_dim:].astype(jnp.bfloat16)
    intersection = matmul_trans(state_out_low, state_in_low)
    mixing = decay_mix(intersection, step_raw, step_bias, decay_log, allowed)
    heads = step_raw.shape[1]
    mixing_low = mixing.astype(jnp.bfloat16)
    conv_low = conv_out.astype(jnp.bfloat16).reshape(slot_count, heads, -1)
    scanned = jnp.einsum("hij,jhp->ihp", mixing_low, conv_low, preferred_element_type=jnp.float32)
    gated = gate_mix(scanned, conv_out, mamba_gate, skip_scale)
    gated_low = gated.astype(jnp.bfloat16)
    branch_sum = matmul(gated_low, mamba_out_weight)
    queries = matmul(normed_one, query_weight)
    keys_raw = matmul(normed_one, key_weight)
    values_raw = matmul(normed_one, value_weight)
    q_heads = queries.shape[1] // HD
    kv_heads = keys_raw.shape[1] // HD
    group_size = q_heads // kv_heads
    query_rot = (
        rotary(queries, within, q_heads)
        .astype(jnp.bfloat16)
        .reshape(slot_count, kv_heads, group_size, HD)
    )
    key_rot = (
        rotary(keys_raw, within, kv_heads).astype(jnp.bfloat16).reshape(slot_count, kv_heads, HD)
    )
    value_low = values_raw.astype(jnp.bfloat16).reshape(slot_count, kv_heads, HD)
    scores = score_block(query_rot, key_rot, allowed)
    peaks = jnp.max(scores, axis=-1, keepdims=True)
    exp_terms = jnp.exp(scores - peaks)
    row_totals = jnp.sum(exp_terms, axis=-1, keepdims=True)
    log_total = peaks + jnp.log(row_totals)
    attn_probs = exp_terms / row_totals
    attended_low = (
        jnp.einsum(
            "krij,jkd->ikrd",
            attn_probs.astype(jnp.bfloat16),
            value_low,
            preferred_element_type=jnp.float32,
        )
        .reshape(slot_count, -1)
        .astype(jnp.bfloat16)
    )
    branch_sum = branch_sum + matmul(attended_low, attn_out_weight)
    mixer_total = lax.psum(branch_sum.astype(jnp.bfloat16), "col").astype(jnp.float32)
    hidden_mid = block_tokens + mixer_total
    normed_two = rms_scale(hidden_mid, ff_norm_gain).astype(jnp.bfloat16)
    ff_gate = matmul(normed_two, gate_weight)
    ff_up = matmul(normed_two, up_weight)
    ff_hidden = swiglu(ff_gate, ff_up).astype(jnp.bfloat16)
    ff_total = lax.psum(matmul(ff_hidden, down_weight).astype(jnp.bfloat16), "col").astype(
        jnp.float32
    )
    result = hidden_mid + ff_total
    kept = (
        block_tokens,
        segment,
        within,
        allowed,
        normed_one,
        mamba_gate,
        conv_in,
        state_raw,
        step_raw,
        conv_out,
        state_in_low,
        state_out_low,
        intersection,
        mixing_low,
        conv_low,
        scanned,
        gated_low,
        queries,
        keys_raw,
        query_rot,
        key_rot,
        value_low,
        log_total,
        attended_low,
        hidden_mid,
        normed_two,
        ff_gate,
        ff_up,
        ff_hidden,
    )
    return (result, kept)


def backward_pass(grad_out, kept, weights, smalls):
    (
        mamba_gate_weight,
        mamba_input_weight,
        state_weight,
        step_weight,
        query_weight,
        key_weight,
        value_weight,
        gate_weight,
        up_weight,
        mamba_out_weight,
        attn_out_weight,
        down_weight,
    ) = weights
    (
        mixer_norm_gain,
        conv_input,
        conv_input_bias,
        conv_state,
        conv_state_bias,
        step_bias,
        decay_log,
        skip_scale,
        ff_norm_gain,
    ) = smalls
    (
        block_tokens,
        segment,
        within,
        allowed,
        normed_one,
        mamba_gate,
        conv_in,
        state_raw,
        step_raw,
        conv_out,
        state_in_low,
        state_out_low,
        intersection,
        mixing_low,
        conv_low,
        scanned,
        gated_low,
        queries,
        keys_raw,
        query_rot,
        key_rot,
        value_low,
        log_total,
        attended_low,
        hidden_mid,
        normed_two,
        ff_gate,
        ff_up,
        ff_hidden,
    ) = kept
    slot_count = block_tokens.shape[0]
    q_heads = queries.shape[1] // HD
    kv_heads = keys_raw.shape[1] // HD
    group_size = q_heads // kv_heads
    grad_low = grad_out.astype(jnp.bfloat16)
    grad_hidden = matmul_trans(grad_low, down_weight)
    delta_down = matmul_left(ff_hidden, grad_low)
    unused_value, pullback = jax.vjp(swiglu, ff_gate, ff_up)
    grad_gate, grad_up = pullback(grad_hidden)
    grad_gate = grad_gate.astype(jnp.bfloat16)
    grad_up = grad_up.astype(jnp.bfloat16)
    delta_gate = matmul_left(normed_two, grad_gate)
    delta_up = matmul_left(normed_two, grad_up)
    grad_normed_two = lax.psum(
        (matmul_trans(grad_gate, gate_weight) + matmul_trans(grad_up, up_weight)).astype(
            jnp.bfloat16
        ),
        "col",
    ).astype(jnp.float32)
    unused_value, pullback = jax.vjp(rms_scale, hidden_mid, ff_norm_gain)
    grad_mid_norm, delta_ff_gain = pullback(grad_normed_two)
    grad_mid = grad_out + grad_mid_norm
    grad_mixer = grad_mid.astype(jnp.bfloat16)
    grad_gated = matmul_trans(grad_mixer, mamba_out_weight)
    delta_mamba_out = matmul_left(gated_low, grad_mixer)
    unused_value, pullback = jax.vjp(gate_mix, scanned, conv_out, mamba_gate, skip_scale)
    grad_scanned, grad_conv_skip, grad_mamba_gate, delta_skip = pullback(grad_gated)
    grad_scanned = grad_scanned.astype(jnp.bfloat16)
    grad_mamba_gate = grad_mamba_gate.astype(jnp.bfloat16)
    grad_mixing = jnp.einsum(
        "ihp,jhp->hij", grad_scanned, conv_low, preferred_element_type=jnp.float32
    )
    grad_conv_out = grad_conv_skip + jnp.einsum(
        "hij,ihp->jhp", mixing_low, grad_scanned, preferred_element_type=jnp.float32
    ).reshape(slot_count, -1)
    unused_value, pullback = jax.vjp(
        partial(decay_mix, allowed=allowed), intersection, step_raw, step_bias, decay_log
    )
    grad_intersection, grad_step, delta_step_bias, delta_decay = pullback(grad_mixing)
    grad_intersection = grad_intersection.astype(jnp.bfloat16)
    grad_step = grad_step.astype(jnp.bfloat16)
    grad_state = jnp.concatenate(
        [matmul_left(grad_intersection, state_out_low), matmul(grad_intersection, state_in_low)],
        axis=1,
    )
    grad_state = lax.psum(grad_state.astype(jnp.bfloat16), "col").astype(jnp.float32)
    unused_value, pullback = jax.vjp(
        partial(causal_conv, segment=segment), conv_in, conv_input, conv_input_bias
    )
    grad_conv_in, delta_conv_input, delta_conv_input_bias = pullback(grad_conv_out)
    unused_value, pullback = jax.vjp(
        partial(causal_conv, segment=segment), state_raw, conv_state, conv_state_bias
    )
    grad_state_raw, delta_conv_state, delta_conv_state_bias = pullback(grad_state)
    grad_conv_in = grad_conv_in.astype(jnp.bfloat16)
    grad_state_raw = grad_state_raw.astype(jnp.bfloat16)
    delta_mamba_gate = matmul_left(normed_one, grad_mamba_gate)
    delta_mamba_input = matmul_left(normed_one, grad_conv_in)
    delta_state = matmul_left(normed_one, grad_state_raw)
    delta_step = matmul_left(normed_one, grad_step)
    grad_normed_one = (
        matmul_trans(grad_mamba_gate, mamba_gate_weight)
        + matmul_trans(grad_conv_in, mamba_input_weight)
        + matmul_trans(grad_step, step_weight)
    )
    half_rows = state_weight.shape[0] // lax.axis_size("col")
    start_row = lax.axis_index("col") * half_rows
    state_rows = lax.dynamic_slice_in_dim(state_weight, start_row, half_rows, 0)
    own_cols = lax.dynamic_slice_in_dim(grad_normed_one, start_row, half_rows, 1) + matmul_trans(
        grad_state_raw, state_rows
    )
    grad_normed_one = lax.dynamic_update_slice_in_dim(grad_normed_one, own_cols, start_row, 1)
    grad_attended = (
        matmul_trans(grad_mixer, attn_out_weight)
        .astype(jnp.bfloat16)
        .reshape(slot_count, kv_heads, group_size, HD)
    )
    delta_attn_out = matmul_left(attended_low, grad_mixer)
    attn_probs = jnp.exp(score_block(query_rot, key_rot, allowed) - log_total)
    grad_probs = jnp.einsum(
        "ikrd,jkd->krij", grad_attended, value_low, preferred_element_type=jnp.float32
    )
    grad_values = (
        jnp.einsum(
            "krij,ikrd->jkd",
            attn_probs.astype(jnp.bfloat16),
            grad_attended,
            preferred_element_type=jnp.float32,
        )
        .reshape(slot_count, -1)
        .astype(jnp.bfloat16)
    )
    grad_scores = attn_probs * (
        grad_probs - jnp.sum(grad_probs * attn_probs, axis=-1, keepdims=True)
    )
    grad_raw = (grad_scores * HD ** (-0.5)).astype(jnp.bfloat16)
    grad_query_rot = jnp.einsum(
        "krij,jkd->ikrd", grad_raw, key_rot, preferred_element_type=jnp.float32
    ).reshape(slot_count, -1)
    grad_key_rot = jnp.einsum(
        "krij,ikrd->jkd", grad_raw, query_rot, preferred_element_type=jnp.float32
    ).reshape(slot_count, -1)
    unused_value, pullback = jax.vjp(partial(rotary, within=within, heads=q_heads), queries)
    (grad_queries,) = pullback(grad_query_rot)
    unused_value, pullback = jax.vjp(partial(rotary, within=within, heads=kv_heads), keys_raw)
    (grad_keys,) = pullback(grad_key_rot)
    grad_queries = grad_queries.astype(jnp.bfloat16)
    grad_keys = grad_keys.astype(jnp.bfloat16)
    delta_query = matmul_left(normed_one, grad_queries)
    delta_key = matmul_left(normed_one, grad_keys)
    delta_value = matmul_left(normed_one, grad_values)
    grad_normed_one = (
        grad_normed_one
        + matmul_trans(grad_queries, query_weight)
        + matmul_trans(grad_keys, key_weight)
        + matmul_trans(grad_values, value_weight)
    )
    grad_normed_one = lax.psum(grad_normed_one.astype(jnp.bfloat16), "col").astype(jnp.float32)
    unused_value, pullback = jax.vjp(rms_scale, block_tokens, mixer_norm_gain)
    grad_in_norm, delta_mixer_gain = pullback(grad_normed_one)
    grad_tokens = (grad_mid + grad_in_norm).astype(jnp.bfloat16)
    deltas = (
        delta_mamba_gate,
        delta_mamba_input,
        delta_state,
        delta_step,
        delta_query,
        delta_key,
        delta_value,
        delta_gate,
        delta_up,
        delta_mamba_out,
        delta_attn_out,
        delta_down,
    )
    small_deltas = (
        delta_mixer_gain,
        delta_conv_input,
        delta_conv_input_bias,
        delta_conv_state,
        delta_conv_state_bias,
        delta_step_bias,
        delta_decay,
        delta_skip,
        delta_ff_gain,
    )
    return (grad_tokens, deltas, small_deltas)


def local(
    tokens,
    cotangent,
    deal_order,
    seq_lengths,
    mixer_norm_gain,
    mamba_gate_weight,
    mamba_input_weight,
    state_weight,
    step_weight,
    conv_input,
    conv_input_bias,
    conv_state,
    conv_state_bias,
    step_bias,
    decay_log,
    skip_scale,
    mamba_out_weight,
    query_weight,
    key_weight,
    value_weight,
    attn_out_weight,
    ff_norm_gain,
    gate_weight,
    up_weight,
    down_weight,
):
    row_count = lax.axis_size("row")
    micro_count = tokens.shape[0]
    slot_count = tokens.shape[1]
    per_peer = slot_count // row_count
    source_dev = deal_order // slot_count
    local_row = deal_order % slot_count
    sort_order = jnp.argsort(source_dev, axis=1)
    wanted = jnp.take_along_axis(local_row, sort_order, axis=1).reshape(
        micro_count, row_count, per_peer
    )
    asked = lax.all_to_all(wanted, "row", split_axis=1, concat_axis=1, tiled=True).reshape(
        micro_count, slot_count
    )
    slot_rank = jnp.argsort(sort_order, axis=1)
    home_rank = jnp.argsort(asked, axis=1)
    smalls = (
        mixer_norm_gain,
        conv_input,
        conv_input_bias,
        conv_state,
        conv_state_bias,
        step_bias,
        decay_log,
        skip_scale,
        ff_norm_gain,
    )
    shards = (
        mamba_gate_weight,
        mamba_input_weight,
        state_weight,
        step_weight,
        query_weight,
        key_weight,
        value_weight,
        gate_weight,
        up_weight,
        mamba_out_weight,
        attn_out_weight,
        down_weight,
    )
    totals = [
        jnp.zeros((shard.shape[0] * row_count, shard.shape[1]), jnp.float32) for shard in shards[:9]
    ]
    totals = totals + [
        jnp.zeros((shard.shape[0], shard.shape[1] * row_count), jnp.float32) for shard in shards[9:]
    ]
    small_totals = [jnp.zeros(small_arr.shape, jnp.float32) for small_arr in smalls]
    output_rows = []
    gradient_rows = []
    for micro in range(micro_count):
        forward_weights = (
            lax.all_gather(mamba_gate_weight, "row", axis=0, tiled=True),
            lax.all_gather(mamba_input_weight, "row", axis=0, tiled=True),
            lax.all_gather(state_weight, "row", axis=0, tiled=True),
            lax.all_gather(step_weight, "row", axis=0, tiled=True),
            lax.all_gather(query_weight, "row", axis=0, tiled=True),
            lax.all_gather(key_weight, "row", axis=0, tiled=True),
            lax.all_gather(value_weight, "row", axis=0, tiled=True),
            lax.all_gather(gate_weight, "row", axis=0, tiled=True),
            lax.all_gather(up_weight, "row", axis=0, tiled=True),
            lax.all_gather(mamba_out_weight, "row", axis=1, tiled=True),
            lax.all_gather(attn_out_weight, "row", axis=1, tiled=True),
            lax.all_gather(down_weight, "row", axis=1, tiled=True),
        )
        send_tokens = tokens[micro][asked[micro]].reshape(row_count, per_peer, -1)
        send_cotangent = cotangent[micro][asked[micro]].reshape(row_count, per_peer, -1)
        got_tokens, got_cotangent = (
            lax.all_to_all(send_tokens, "row", split_axis=0, concat_axis=0, tiled=True),
            lax.all_to_all(send_cotangent, "row", split_axis=0, concat_axis=0, tiled=True),
        )
        block_tokens = got_tokens.reshape(slot_count, -1)[slot_rank[micro]].astype(jnp.float32)
        grad_out = got_cotangent.reshape(slot_count, -1)[slot_rank[micro]].astype(jnp.float32)
        result, kept = forward_pass(block_tokens, seq_lengths[micro, 0], forward_weights, smalls)
        backward_weights = (
            lax.all_gather(mamba_gate_weight, "row", axis=0, tiled=True),
            lax.all_gather(mamba_input_weight, "row", axis=0, tiled=True),
            lax.all_gather(state_weight, "row", axis=0, tiled=True),
            lax.all_gather(step_weight, "row", axis=0, tiled=True),
            lax.all_gather(query_weight, "row", axis=0, tiled=True),
            lax.all_gather(key_weight, "row", axis=0, tiled=True),
            lax.all_gather(value_weight, "row", axis=0, tiled=True),
            lax.all_gather(gate_weight, "row", axis=0, tiled=True),
            lax.all_gather(up_weight, "row", axis=0, tiled=True),
            lax.all_gather(mamba_out_weight, "row", axis=1, tiled=True),
            lax.all_gather(attn_out_weight, "row", axis=1, tiled=True),
            lax.all_gather(down_weight, "row", axis=1, tiled=True),
        )
        grad_tokens, deltas, small_deltas = backward_pass(grad_out, kept, backward_weights, smalls)
        totals = [running + current for running, current in zip(totals, deltas)]
        small_totals = [running + current for running, current in zip(small_totals, small_deltas)]
        send_result = result.astype(jnp.bfloat16)[sort_order[micro]].reshape(
            row_count, per_peer, -1
        )
        send_grads = grad_tokens[sort_order[micro]].reshape(row_count, per_peer, -1)
        back_result, back_grads = (
            lax.all_to_all(send_result, "row", split_axis=0, concat_axis=0, tiled=True),
            lax.all_to_all(send_grads, "row", split_axis=0, concat_axis=0, tiled=True),
        )
        output_rows.append(back_result.reshape(slot_count, -1)[home_rank[micro]])
        gradient_rows.append(back_grads.reshape(slot_count, -1)[home_rank[micro]])
    reduced = (
        lax.psum_scatter(totals[0], "row", scatter_dimension=0, tiled=True),
        lax.psum_scatter(totals[1], "row", scatter_dimension=0, tiled=True),
        lax.psum_scatter(totals[2], "row", scatter_dimension=0, tiled=True),
        lax.psum_scatter(totals[3], "row", scatter_dimension=0, tiled=True),
        lax.psum_scatter(totals[4], "row", scatter_dimension=0, tiled=True),
        lax.psum_scatter(totals[5], "row", scatter_dimension=0, tiled=True),
        lax.psum_scatter(totals[6], "row", scatter_dimension=0, tiled=True),
        lax.psum_scatter(totals[7], "row", scatter_dimension=0, tiled=True),
        lax.psum_scatter(totals[8], "row", scatter_dimension=0, tiled=True),
        lax.psum_scatter(totals[9], "row", scatter_dimension=1, tiled=True),
        lax.psum_scatter(totals[10], "row", scatter_dimension=1, tiled=True),
        lax.psum_scatter(totals[11], "row", scatter_dimension=1, tiled=True),
    )
    small_sums = lax.psum(
        (
            small_totals[0],
            small_totals[1],
            small_totals[2],
            small_totals[3],
            small_totals[4],
            small_totals[5],
            small_totals[6],
            small_totals[7],
            small_totals[8],
        ),
        "row",
    )
    return (
        jnp.stack(output_rows),
        jnp.stack(gradient_rows),
        small_sums[0],
        reduced[0],
        reduced[1],
        reduced[2],
        reduced[3],
        small_sums[1],
        small_sums[2],
        small_sums[3],
        small_sums[4],
        small_sums[5],
        small_sums[6],
        small_sums[7],
        reduced[9],
        reduced[4],
        reduced[5],
        reduced[6],
        reduced[10],
        small_sums[8],
        reduced[7],
        reduced[8],
        reduced[11],
    )


def solution(mesh):
    in_specs = (
        P(None, "row", None),
        P(None, "row", None),
        P(None, "row"),
        P(None, "row", None),
        P(),
        P("row", "col"),
        P("row", "col"),
        P("row", None),
        P("row", "col"),
        P(None, "col"),
        P("col"),
        P(),
        P(),
        P("col"),
        P("col"),
        P("col"),
        P("col", "row"),
        P("row", "col"),
        P("row", "col"),
        P("row", "col"),
        P("col", "row"),
        P(),
        P("row", "col"),
        P("row", "col"),
        P("col", "row"),
    )
    out_specs = (
        P(None, "row", None),
        P(None, "row", None),
        P(),
        P("row", "col"),
        P("row", "col"),
        P("row", None),
        P("row", "col"),
        P(None, "col"),
        P("col"),
        P(),
        P(),
        P("col"),
        P("col"),
        P("col"),
        P("col", "row"),
        P("row", "col"),
        P("row", "col"),
        P("row", "col"),
        P("col", "row"),
        P(),
        P("row", "col"),
        P("row", "col"),
        P("col", "row"),
    )
    return jax.shard_map(local, mesh=mesh, in_specs=in_specs, out_specs=out_specs, check_vma=False)
```

profile of v0, /device:TPU:9, one launch (start us, length us, event | category | flops | bytes accessed | tf_op | source)
XLA Modules:
  0.0 3316.3 jit_solution(6219811331656511978)
XLA Ops:
  28.6 6.7 all-to-all-start
  48.1 41.6 %all_gather.30 = bf16[2048,128]{1,0:T(8,128)(2,1)S(1)} all-gather(bf16[128,128]{1,0:T(8,128)(2,1)S(1)} %copy-done.149), channel_id=1, replica_groups=mesh['row'=16,'col'=2] {'row'}, dimensions={0}, use_global_device_ids=true | all-gather | bytes 557056 | tf_op jit(solution)/shard_map/all_gather | solution.py:518
  91.6 6.5 all-to-all-start.3
  98.2 29.9 all_gather.26
  128.8 34.3 %all_gather.29 = bf16[2048,128]{1,0:T(8,128)(2,1)S(1)} all-gather(bf16[128,128]{1,0:T(8,128)(2,1)S(1)} %copy-done.150), channel_id=1, replica_groups=mesh['row'=16,'col'=2] {'row'}, dimensions={0}, use_global_device_ids=true | all-gather | bytes 557056 | tf_op jit(solution)/shard_map/all_gather | solution.py:519
  198.3 48.9 %all-gather.10.cloned.1.call-done = bf16[2048,1536]{1,0:T(8,128)(2,1)} async-done(((bf16[128,1536]{1,0:T(8,128)(2,1)}), bf16[2048,1536]{1,0:T(8,128)(2,1)}) %all-gather.10.cloned.1.call-update) | async-done | bytes 6291472 | tf_op jit(solution)/shard_map/all_gather | solution.py:514
  264.2 77.9 %all-gather.14.cloned.1.call-done = bf16[2048,1536]{1,0:T(8,128)(2,1)} async-done(((bf16[128,1536]{1,0:T(8,128)(2,1)}), bf16[2048,1536]{1,0:T(8,128)(2,1)}) %all-gather.14.cloned.1.call-update) | async-done | bytes 6291472 | tf_op jit(solution)/shard_map/all_gather | solution.py:513
  351.7 106.4 %all-gather.16.cloned.1.call-done = bf16[1536,2048]{1,0:T(8,128)(2,1)} async-done(((bf16[1536,128]{1,0:T(8,128)(2,1)}), bf16[1536,2048]{1,0:T(8,128)(2,1)}) %all-gather.16.cloned.1.call-update) | async-done | bytes 6291472 | tf_op jit(solution)/shard_map/all_gather | solution.py:522
  465.0 57.3 %all-gather.20.cloned.1.call-done = bf16[512,2048]{1,0:T(8,128)(2,1)} async-done(((bf16[512,128]{1,0:T(8,128)(2,1)}), bf16[512,2048]{1,0:T(8,128)(2,1)}) %all-gather.20.cloned.1.call-update) | async-done | bytes 2097168 | tf_op jit(solution)/shard_map/all_gather | solution.py:523
  531.7 6.2 all-to-all-start.5
  539.8 17.2 all-to-all-done.5
  557.0 7.7 all-to-all-start.7
  566.6 15.9 all-to-all-done.7
  588.8 66.8 %all-gather.22.cloned.1.call-done = bf16[2048,2048]{1,0:T(8,128)(2,1)} async-done(((bf16[128,2048]{1,0:T(8,128)(2,1)}), bf16[2048,2048]{1,0:T(8,128)(2,1)}) %all-gather.22.cloned.1.call-update) | async-done | bytes 8388624 | tf_op jit(solution)/shard_map/all_gather | solution.py:520
  655.6 5.6 fusion.256
  661.2 108.4 %all-gather.24.cloned.1.call-done = bf16[2048,2048]{1,0:T(8,128)(2,1)} async-done(((bf16[128,2048]{1,0:T(8,128)(2,1)}), bf16[2048,2048]{1,0:T(8,128)(2,1)}) %all-gather.24.cloned.1.call-update) | async-done | bytes 8388624 | tf_op jit(solution)/shard_map/all_gather | solution.py:521
  769.6 5.8 fusion.257
  780.9 131.7 %all-gather.26.cloned.1.call-done = bf16[2048,2048]{1,0:T(8,128)(2,1)} async-done(((bf16[2048,128]{1,0:T(8,128)(2,1)}), bf16[2048,2048]{1,0:T(8,128)(2,1)}) %all-gather.26.cloned.1.call-update) | async-done | bytes 8388624 | tf_op jit(solution)/shard_map/all_gather | solution.py:524
  912.7 8.1 multiply_convert_fusion.3
  921.5 6.4 fusion.261
  928.0 7.6 multiply_convert_fusion.2
  946.2 20.9 all-reduce.66.cloned.1.call-done
  973.5 6.9 multiply_reduce_fusion.7
  990.3 10.1 multiply_reduce_fusion.6
  1020.0 5.5 convolution_convert_fusion.1
  1025.5 5.6 convolution_convert_fusion
  1117.1 6.4 convolution_add_fusion
  1126.4 6.5 convolution_add_fusion.1
  1135.8 6.5 convolution_add_fusion.2
  1145.8 8.2 convolution_add_fusion.5
  1157.4 8.2 convolution_add_fusion.4
  1169.2 8.2 convolution_add_fusion.3
  1187.5 6.4 all-to-all-start.8
  1195.6 13.7 all-to-all-done.8
  1209.3 4.9 all-to-all-start.6
  1216.2 14.0 all-to-all-done.6
  1236.1 12.4 all-to-all-done.4
  1248.5 5.9 all-to-all-start.2
  1255.3 59.8 %all-reduce.52 = (f32[2048]{0:T(1024)}, f32[4,1536]{1,0:T(4,128)}, f32[1536]{0:T(1024)}, f32[4,512]{1,0:T(4,128)}, f32[512]{0:T(512)}, /*index=5*/f32[24]{0:T(128)}, f32[24]{0:T(128)}, f32[24]{0:T(128)}, f32[2048]{0:T(1024)}) all-reduce(f32[2048]{0:T(1024)S(1)} %add.761, ...), channel_id=1, replica_groups=mesh['row'=16,'col'=2] {'row'}, use_global_device_ids=true, to_apply=%region_49.51 | all-reduce | flops 14408 | bytes 115264 | tf_op jit(solution)/shard_map/psum | solution.py:576
  1321.0 106.3 %reduce-scatter.23.cloned.1.call-done = f32[128,512]{1,0:T(8,128)} async-done(((f32[2048,512]{1,0:T(8,128)}), f32[128,512]{1,0:T(8,128)}) %reduce-scatter.23.cloned.1.call-update) | async-done | bytes 262160 | tf_op jit(solution)/shard_map/reduce_scatter | solution.py:567
  1427.3 97.7 %reduce-scatter.29.cloned.1.call-done = f32[512,128]{1,0:T(8,128)} async-done(((f32[512,2048]{1,0:T(8,128)}), f32[512,128]{1,0:T(8,128)}) %reduce-scatter.29.cloned.1.call-update) | async-done | bytes 262160 | tf_op jit(solution)/shard_map/reduce_scatter | solution.py:573
  1525.0 97.6 %reduce-scatter.17.cloned.1.call-done = f32[128,512]{1,0:T(8,128)} async-done(((f32[2048,512]{1,0:T(8,128)}), f32[128,512]{1,0:T(8,128)}) %reduce-scatter.17.cloned.1.call-update) | async-done | bytes 262160 | tf_op jit(solution)/shard_map/reduce_scatter | solution.py:565
  1622.6 211.0 %reduce-scatter.21.cloned.1.call-done = f32[1536,128]{1,0:T(8,128)} async-done(((f32[1536,2048]{1,0:T(8,128)}), f32[1536,128]{1,0:T(8,128)}) %reduce-scatter.21.cloned.1.call-update) | async-done | bytes 786448 | tf_op jit(solution)/shard_map/reduce_scatter | solution.py:572
  1833.7 207.8 %reduce-scatter.15.cloned.1.call-done = f32[128,1536]{1,0:T(8,128)} async-done(((f32[2048,1536]{1,0:T(8,128)}), f32[128,1536]{1,0:T(8,128)}) %reduce-scatter.15.cloned.1.call-update) | async-done | bytes 786448 | tf_op jit(solution)/shard_map/reduce_scatter | solution.py:564
  2041.5 208.8 %reduce-scatter.13.cloned.1.call-done = f32[128,1536]{1,0:T(8,128)} async-done(((f32[2048,1536]{1,0:T(8,128)}), f32[128,1536]{1,0:T(8,128)}) %reduce-scatter.13.cloned.1.call-update) | async-done | bytes 786448 | tf_op jit(solution)/shard_map/reduce_scatter | solution.py:563
  2250.3 348.9 %reduce-scatter.31.cloned.1.call-done = f32[128,2048]{1,0:T(8,128)} async-done(((f32[2048,2048]{1,0:T(8,128)}), f32[128,2048]{1,0:T(8,128)}) %reduce-scatter.31.cloned.1.call-update) | async-done | bytes 1048592 | tf_op jit(solution)/shard_map/reduce_scatter | solution.py:570
  2599.1 354.8 %reduce-scatter.33.cloned.1.call-done = f32[128,2048]{1,0:T(8,128)} async-done(((f32[2048,2048]{1,0:T(8,128)}), f32[128,2048]{1,0:T(8,128)}) %reduce-scatter.33.cloned.1.call-update) | async-done | bytes 1048592 | tf_op jit(solution)/shard_map/reduce_scatter | solution.py:571
  2953.9 354.7 %reduce-scatter.35.cloned.1.call-done = f32[2048,128]{1,0:T(8,128)} async-done(((f32[2048,2048]{1,0:T(8,128)}), f32[2048,128]{1,0:T(8,128)}) %reduce-scatter.35.cloned.1.call-update) | async-done | bytes 1048592 | tf_op jit(solution)/shard_map/reduce_scatter | solution.py:574
  (842 shorter events, 302.5 us)
Async XLA Ops:
  15.2 162.0 %all-gather.18.cloned.1.call-start = ((), (), s32[]{:S(2)}) async-start(), calls=%async_computation.25 | async-start | bytes 2228224 | tf_op jit(solution)/shard_map/all_gather | solution.py:517
  15.7 164.1 %all-gather.12.cloned.1.call-start = ((), (), s32[]{:S(2)}) async-start(), calls=%async_computation.22 | async-start | bytes 2228224 | tf_op jit(solution)/shard_map/all_gather | solution.py:515
  16.3 230.9 %all-gather.10.cloned.1.call-start = ((), (), s32[]{:S(2)}) async-start(), calls=%async_computation.21 | async-start | bytes 6684672 | tf_op jit(solution)/shard_map/all_gather | solution.py:514
  16.9 325.3 %all-gather.14.cloned.1.call-start = ((), (), s32[]{:S(2)}) async-start(), calls=%async_computation.23 | async-start | bytes 6684672 | tf_op jit(solution)/shard_map/all_gather | solution.py:513
  17.6 440.4 %all-gather.16.cloned.1.call-start = ((), (), s32[]{:S(2)}) async-start(), calls=%async_computation.24 | async-start | bytes 6684672 | tf_op jit(solution)/shard_map/all_gather | solution.py:522
  18.4 503.9 %all-gather.20.cloned.1.call-start = ((), (), s32[]{:S(2)}) async-start(), calls=%async_computation.26 | async-start | bytes 2228224 | tf_op jit(solution)/shard_map/all_gather | solution.py:523
  28.6 11.8 all-to-all-start
  43.1 48.6 %all-to-all-start.1 = ((bf16[16,8,2048]{2,1,0:T(8,128)(2,1)}), bf16[16,8,2048]{2,1,0:T(8,128)(2,1)S(1)}, u32[]{:S(2)}, u32[]{:S(2)}) async-start(bf16[16,8,2048]{2,1,0:T(8,128)(2,1)} %bitcast.5), calls=%async_computation.1 | async-start | bytes 1048576 | tf_op jit(solution)/shard_map/all_to_all | solution.py:529
  47.7 126.3 %copy-start.212 = (f32[24]{0:T(128)}, f32[24]{0:T(128)S(1)}, u32[]{:S(2)}) copy-start(f32[24]{0:T(128)S(1)} %exponential_negate_fusion) | copy-start | bytes 292
  48.1 123.0 %copy-start.106 = (f32[128,64]{0,1:T(8,128)}, f32[128,64]{0,1:T(8,128)S(1)}, u32[]{:S(2)}) copy-start(f32[128,64]{0,1:T(8,128)S(1)} %get-tuple-element.206) | copy-start | bytes 98308
  48.1 123.0 %copy-start.110 = (f32[128,64]{0,1:T(8,128)}, f32[128,64]{0,1:T(8,128)S(1)}, u32[]{:S(2)}) copy-start(f32[128,64]{0,1:T(8,128)S(1)} %get-tuple-element.207) | copy-start | bytes 98308
  48.1 127.5 %copy-start.104 = (f32[128,64]{0,1:T(8,128)}, f32[128,64]{0,1:T(8,128)S(1)}, u32[]{:S(2)}) copy-start(f32[128,64]{0,1:T(8,128)S(1)} %get-tuple-element.222) | copy-start | bytes 98308
  48.1 127.5 %copy-start.108 = (f32[128,64]{0,1:T(8,128)}, f32[128,64]{0,1:T(8,128)S(1)}, u32[]{:S(2)}) copy-start(f32[128,64]{0,1:T(8,128)S(1)} %get-tuple-element.221) | copy-start | bytes 98308
  91.6 72.6 %all-to-all-start.3 = ((bf16[16,8,2048]{2,1,0:T(8,128)(2,1)}), bf16[16,8,2048]{2,1,0:T(8,128)(2,1)S(1)}, u32[]{:S(2)}, u32[]{:S(2)}) async-start(bf16[16,8,2048]{2,1,0:T(8,128)(2,1)} %bitcast.43), calls=%async_computation.3 | async-start | bytes 1048576 | tf_op jit(solution)/shard_map/all_to_all | solution.py:529
  98.1 486.3 %all-reduce.68.cloned.1.call-start = ((), (), s32[]{:S(2)}) async-start(), calls=%async_computation.45 | async-start | bytes 2097152 | tf_op jit(solution)/shard_map/psum | solution.py:185
  198.3 327.2 %copy-start.90 = (bf16[128,4,128]{2,0,1:T(8,128)(2,1)}, bf16[128,4,128]{2,0,1:T(8,128)(2,1)S(1)}, u32[]{:S(2)}) copy-start(bf16[128,4,128]{2,0,1:T(8,128)(2,1)S(1)} %convolution_convert_fusion.4) | copy-start | bytes 393220
  351.7 111.3 %copy-start.50 = (bf16[128,1536]{1,0:T(8,128)(2,1)}, bf16[128,1536]{1,0:T(8,128)(2,1)S(1)}, u32[]{:S(2)}) copy-start(bf16[128,1536]{1,0:T(8,128)(2,1)S(1)} %get-tuple-element.188) | copy-start | bytes 1179652
  351.7 111.3 %copy-start.39 = (bf16[128,1536]{1,0:T(8,128)(2,1)}, bf16[128,1536]{1,0:T(8,128)(2,1)S(1)}, u32[]{:S(2)}) copy-start(bf16[128,1536]{1,0:T(8,128)(2,1)S(1)} %get-tuple-element.189) | copy-start | bytes 1179652
  526.8 128.7 %all-gather.22.cloned.1.call-start = ((), (), s32[]{:S(2)}) async-start(), calls=%async_computation.27 | async-start | bytes 8912896 | tf_op jit(solution)/shard_map/all_gather | solution.py:520
  527.4 242.1 %all-gather.24.cloned.1.call-start = ((), (), s32[]{:S(2)}) async-start(), calls=%async_computation.28 | async-start | bytes 8912896 | tf_op jit(solution)/shard_map/all_gather | solution.py:521
  528.0 384.6 %all-gather.26.cloned.1.call-start = ((), (), s32[]{:S(2)}) async-start(), calls=%async_computation.29 | async-start | bytes 8912896 | tf_op jit(solution)/shard_map/all_gather | solution.py:524
  531.7 25.3 all-to-all-start.5
  557.0 25.5 all-to-all-start.7
  564.7 402.4 %all-reduce.66.cloned.1.call-start = ((), (), s32[]{:S(2)}) async-start(), calls=%async_computation.44 | async-start | bytes 2097152 | tf_op jit(solution)/shard_map/psum | solution.py:299
  587.0 383.1 %copy-start.203 = (f32[128]{0:T(128)}, f32[128]{0:T(128)S(1)}, u32[]{:S(2)}) copy-start(f32[128]{0:T(128)S(1)} %fusion.181) | copy-start | bytes 1540
  587.0 383.1 %copy-start.205 = (f32[128]{0:T(128)}, f32[128]{0:T(128)S(1)}, u32[]{:S(2)}) copy-start(f32[128]{0:T(128)S(1)} %fusion.179) | copy-start | bytes 1540
  588.7 180.8 %copy-start.10 = (bf16[128,2048]{1,0:T(8,128)(2,1)}, bf16[128,2048]{1,0:T(8,128)(2,1)S(1)}, u32[]{:S(2)}) copy-start(bf16[128,2048]{1,0:T(8,128)(2,1)S(1)} %get-tuple-element.186) | copy-start | bytes 1572868
  588.8 188.9 %copy-start.8 = (bf16[128,2048]{1,0:T(8,128)(2,1)}, bf16[128,2048]{1,0:T(8,128)(2,1)S(1)}, u32[]{:S(2)}) copy-start(bf16[128,2048]{1,0:T(8,128)(2,1)S(1)} %get-tuple-element.187) | copy-start | bytes 1572868
  778.6 134.0 %copy-start.28 = (bf16[128,2048]{1,0:T(8,128)(2,1)S(1)}, bf16[128,2048]{1,0:T(8,128)(2,1)}, u32[]{:S(2)}) copy-start(bf16[128,2048]{1,0:T(8,128)(2,1)} %gather_fusion.9) | copy-start | bytes 1572868
  945.9 138.9 %all-reduce.64.cloned.1.call-start = ((), (), s32[]{:S(2)}) async-start(), calls=%async_computation.43 | async-start | bytes 524288 | tf_op jit(solution)/shard_map/psum | solution.py:331
  1007.3 170.3 %sort.45.cloned.1.call-start = ((), (), s32[]{:S(2)}) async-start(), calls=%async_computation.48 | async-start | bytes 6176 | tf_op jit(solution)/shard_map/jit(argsort)/sort | solution.py:476
  1017.0 161.8 %all-reduce.62.cloned.1.call-start = ((), (), s32[]{:S(2)}) async-start(), calls=%async_computation.42 | async-start | bytes 4194304 | tf_op jit(solution)/shard_map/psum | solution.py:191
  1096.9 224.1 %reduce-scatter.19.cloned.1.call-start = ((), (), s32[]{:S(2)}) async-start(), calls=%async_computation.33 | async-start | bytes 208896 | tf_op jit(solution)/shard_map/reduce_scatter | solution.py:566
  1098.2 222.7 %reduce-scatter.27.cloned.1.call-start = ((), (), s32[]{:S(2)}) async-start(), calls=%async_computation.37 | async-start | bytes 1114112 | tf_op jit(solution)/shard_map/reduce_scatter | solution.py:569
  1100.1 220.9 %reduce-scatter.25.cloned.1.call-start = ((), (), s32[]{:S(2)}) async-start(), calls=%async_computation.36 | async-start | bytes 1114112 | tf_op jit(solution)/shard_map/reduce_scatter | solution.py:568
  1102.0 325.3 %reduce-scatter.23.cloned.1.call-start = ((), (), s32[]{:S(2)}) async-start(), calls=%async_computation.35 | async-start | bytes 4456448 | tf_op jit(solution)/shard_map/reduce_scatter | solution.py:567
  1105.7 419.2 %reduce-scatter.29.cloned.1.call-start = ((), (), s32[]{:S(2)}) async-start(), calls=%async_computation.38 | async-start | bytes 4456448 | tf_op jit(solution)/shard_map/reduce_scatter | solution.py:573
  1110.2 512.4 %reduce-scatter.17.cloned.1.call-start = ((), (), s32[]{:S(2)}) async-start(), calls=%async_computation.32 | async-start | bytes 4456448 | tf_op jit(solution)/shard_map/reduce_scatter | solution.py:565
  1114.3 719.4 %reduce-scatter.21.cloned.1.call-start = ((), (), s32[]{:S(2)}) async-start(), calls=%async_computation.34 | async-start | bytes 13369344 | tf_op jit(solution)/shard_map/reduce_scatter | solution.py:572
  1123.5 918.0 %reduce-scatter.15.cloned.1.call-start = ((), (), s32[]{:S(2)}) async-start(), calls=%async_computation.31 | async-start | bytes 13369344 | tf_op jit(solution)/shard_map/reduce_scatter | solution.py:564
  1132.9 1117.4 %reduce-scatter.13.cloned.1.call-start = ((), (), s32[]{:S(2)}) async-start(), calls=%async_computation.30 | async-start | bytes 13369344 | tf_op jit(solution)/shard_map/reduce_scatter | solution.py:563
  1142.3 1456.8 %reduce-scatter.31.cloned.1.call-start = ((), (), s32[]{:S(2)}) async-start(), calls=%async_computation.39 | async-start | bytes 17825792 | tf_op jit(solution)/shard_map/reduce_scatter | solution.py:570
  1154.1 1799.9 %reduce-scatter.33.cloned.1.call-start = ((), (), s32[]{:S(2)}) async-start(), calls=%async_computation.40 | async-start | bytes 17825792 | tf_op jit(solution)/shard_map/reduce_scatter | solution.py:571
  1165.6 2143.0 %reduce-scatter.35.cloned.1.call-start = ((), (), s32[]{:S(2)}) async-start(), calls=%async_computation.41 | async-start | bytes 17825792 | tf_op jit(solution)/shard_map/reduce_scatter | solution.py:574
  1187.5 21.8 all-to-all-start.8
  1209.3 20.9 all-to-all-start.6
  1230.2 18.3 all-to-all-start.4
  1248.5 69.4 %all-to-all-start.2 = ((bf16[16,8,2048]{2,1,0:T(8,128)(2,1)}), bf16[16,8,2048]{2,1,0:T(8,128)(2,1)S(1)}, u32[]{:S(2)}, u32[]{:S(2)}) async-start(bf16[16,8,2048]{2,1,0:T(8,128)(2,1)} %bitcast.36), calls=%async_computation.2 | async-start | bytes 1048576 | tf_op jit(solution)/shard_map/all_to_all | solution.py:557
  (236 other events, 3264.3 us)
Sparse Core Ops, SparseCore 0:
  12.3 2.0 sort.47.cloned.1.call-done
  18.0 2.4 sort.49.cloned.1.call-done
  527.0 20.9 all-reduce.67
  946.1 20.9 all-reduce.65
  1007.4 19.4 all-reduce.63
  1029.1 2.3 sort.51.cloned.1.call-done
  1097.0 22.5 all-reduce.61
  (3 shorter events, 0.0 us)
Sparse Core Ops, SparseCore 1:
  18.4 66.3 all-gather.17
  87.4 64.2 all-gather.11
  154.3 92.8 all-gather.9
  250.0 92.1 all-gather.13
  344.9 113.1 all-gather.15
  460.8 61.4 all-gather.19
  530.5 125.0 all-gather.21
  658.6 110.9 all-gather.23
  772.5 140.1 all-gather.25
  1100.5 58.7 reduce-scatter.18
  1162.0 76.5 reduce-scatter.26
  1241.5 74.9 reduce-scatter.24
  1319.3 108.0 reduce-scatter.22
  1430.3 94.6 reduce-scatter.28
  1528.0 94.6 reduce-scatter.16
  1629.8 203.8 reduce-scatter.20
  1839.9 201.5 reduce-scatter.14
  2048.7 201.5 reduce-scatter.12
  2253.0 346.1 reduce-scatter.30
  2602.0 351.9 reduce-scatter.32
  2956.7 351.9 reduce-scatter.34
where the time goes:
time: 3330 us; the launch traced here: 3320 us
  waiting for transfers between devices  2690 us (81%)
  matrix products  241 us (7%)
  blocking collectives  166 us (5%)
  local copies, waits for them, and re-layouts  84.8 us (3%)
  other arithmetic  62.7 us (2%)
  starting transfers between devices  55.6 us (2%)
    reduce_scatter x1, waiting for transfers between devices, local(): lax.psum_scatter(totals[8], 'row', scatter_dimension=0, tiled=True)  355 us
    reduce_scatter x1, waiting for transfers between devices, local(): lax.psum_scatter(totals[11], 'row', scatter_dimension=1, tiled=True)  355 us
    reduce_scatter x1, waiting for transfers between devices, local(): lax.psum_scatter(totals[7], 'row', scatter_dimension=0, tiled=True)  349 us
    reduce_scatter x1, waiting for transfers between devices, local(): lax.psum_scatter(totals[9], 'row', scatter_dimension=1, tiled=True)  211 us
    reduce_scatter x1, waiting for transfers between devices, local(): lax.psum_scatter(totals[0], 'row', scatter_dimension=0, tiled=True)  209 us
    reduce_scatter x1, waiting for transfers between devices, local(): lax.psum_scatter(totals[1], 'row', scatter_dimension=0, tiled=True)  208 us
    all_gather x1, waiting for transfers between devices, local(): lax.all_gather(down_weight, 'row', axis=1, tiled=True)  132 us
    all_gather x1, waiting for transfers between devices, local(): lax.all_gather(up_weight, 'row', axis=0, tiled=True)  108 us
  transfers between devices with their start and end apart: 34, of which 23 were waited for; matrix products, arithmetic and copies ran while one was open for 8% of the time, Pallas kernels for 0%

commit v1 on v0

v1 whole, which is shorter than its diff:
```python
from functools import partial

import jax
import jax.numpy as jnp
from jax import lax
from jax.experimental import pallas as pl
from jax.experimental.pallas import tpu as pltpu
from jax.sharding import PartitionSpec as P

HD = 128
TP = 4
GROUP = 2 * TP
CHUNK = 16
EPS = 1e-05
NEG_LARGE = -1e30
ROPE_BASE = 100000000000.0
MESH = pl.DeviceIdType.MESH
HIGH = lax.Precision.HIGHEST
VMEM = pltpu.VMEM
ANY = pl.ANY


def matmul(first_op, second_op):
    return jnp.dot(first_op, second_op, preferred_element_type=jnp.float32)


def matmul_trans(first_op, second_op):
    return lax.dot_general(
        first_op, second_op, (((1,), (1,)), ((), ())), preferred_element_type=jnp.float32
    )


def matmul_left(first_op, second_op):
    return lax.dot_general(
        first_op, second_op, (((0,), (0,)), ((), ())), preferred_element_type=jnp.float32
    )


def place():
    r = lax.axis_index("row")
    c = lax.axis_index("col")
    t = lax.rem(r, TP)
    return r, c, r - t, t


def partner(t, m):
    if m == 0:
        return t
    if m == 1:
        return t + 1 - 2 * lax.rem(t, 2)
    if m == 2:
        return lax.rem(t + 2, TP)
    return TP - 1 - t


def remote(src, dst, send, recv, row, col):
    return pltpu.make_async_remote_copy(
        src_ref=src, dst_ref=dst, send_sem=send, recv_sem=recv, device_id=(row, col), device_id_type=MESH
    )


def greet_group(cross=False):
    r, c, base, t = place()
    barrier = pltpu.get_barrier_semaphore()
    pl.semaphore_signal(barrier, inc=1, device_id=(r, 1 - c), device_id_type=MESH)
    count = 1
    for m in (1, 2, 3):
        pl.semaphore_signal(barrier, inc=1, device_id=(base + partner(t, m), c), device_id_type=MESH)
        count += 1
        if cross:
            pl.semaphore_signal(
                barrier, inc=1, device_id=(base + partner(t, m), 1 - c), device_id_type=MESH
            )
            count += 1
    pl.semaphore_wait(barrier, count)


def gather_start(src, out, send, recv, here):
    r, c, base, t = place()
    mine = out.at[t * 2 + c]
    local = pltpu.make_async_copy(src, mine, here)
    peers = [
        remote(src, mine, send.at[m], recv.at[m], base + partner(t, m), c) for m in (1, 2, 3)
    ]
    sibling = remote(src, mine, send.at[0], recv.at[0], r, 1 - c)
    for copy in (peers[2], peers[0], peers[1], sibling, local):
        copy.start()
    return peers, sibling, local


def gather_finish(started, out, send, recv):
    r, c, base, t = place()
    peers, sibling, local = started
    forwards = []
    for m in (1, 2, 3):
        peers[m - 1].wait_recv()
        block = out.at[partner(t, m) * 2 + c]
        forward = remote(block, block, send.at[3 + m], recv.at[3 + m], r, 1 - c)
        forward.start()
        forwards.append(forward)
    local.wait()
    sibling.wait()
    for copy in peers:
        copy.wait_send()
    for copy in forwards:
        copy.wait()


ROWS = 16


def by_rows(count, body):
    def step(i, carry):
        body(pl.ds(pl.multiple_of(i * ROWS, ROWS), ROWS))
        return carry

    lax.fori_loop(0, count // ROWS, step, 0)


def scatter_sum(parts, near, out2, far, s1, r1, s2, r2, total):
    r, c, base, t = place()
    order = (3, 1, 2, 0)
    first = {}
    for m in order:
        first[m] = remote(
            parts.at[partner(t, m) * 2 + 1 - c], near.at[m], s1.at[m], r1.at[m], r, 1 - c
        )
        first[m].start()
    second = {}
    for m in order[:3]:
        first[m].wait_recv()
        block = partner(t, m) * 2 + c

        def add(rows, m=m, block=block):
            out2[m - 1, rows, :] = (
                parts[block, rows, :].astype(jnp.float32) + near[m, rows, :].astype(jnp.float32)
            ).astype(jnp.bfloat16)

        by_rows(total.shape[0], add)
        second[m] = remote(
            out2.at[m - 1], far.at[m - 1], s2.at[m - 1], r2.at[m - 1], base + partner(t, m), c
        )
        second[m].start()
    first[0].wait_recv()
    own = t * 2 + c
    for m in (1, 2, 3):
        second[m].wait_recv()

    def fold(rows):
        total[rows, :] = (
            parts[own, rows, :].astype(jnp.float32)
            + near[0, rows, :].astype(jnp.float32)
            + far[0, rows, :].astype(jnp.float32)
            + far[1, rows, :].astype(jnp.float32)
            + far[2, rows, :].astype(jnp.float32)
        )

    by_rows(total.shape[0], fold)
    for m in order:
        first[m].wait_send()
    for m in (1, 2, 3):
        second[m].wait_send()


def scatter_scratch(slots, width):
    return [
        VMEM((TP, slots, width), jnp.bfloat16),
        VMEM((TP - 1, slots, width), jnp.bfloat16),
        VMEM((TP - 1, slots, width), jnp.bfloat16),
        pltpu.SemaphoreType.DMA((TP,)),
        pltpu.SemaphoreType.DMA((TP,)),
        pltpu.SemaphoreType.DMA((TP - 1,)),
        pltpu.SemaphoreType.DMA((TP - 1,)),
    ]


def gather_scratch():
    return [
        pltpu.SemaphoreType.DMA((7,)),
        pltpu.SemaphoreType.DMA((7,)),
        pltpu.SemaphoreType.DMA,
    ]


def exchange_rows(buf, land, send, recv):
    r, c, base, t = place()
    n_row = lax.axis_size("row")

    def copy(other):
        return remote(
            buf.at[other], land.at[r], send.at[other], recv.at[r], other, c
        )

    def start(off, carry):
        copy(lax.rem(r + off, n_row)).start()
        return carry

    lax.fori_loop(1, n_row, start, 0)


def finish_rows(buf, land, send, recv):
    r, c, base, t = place()
    n_row = lax.axis_size("row")

    def finish(off, carry):
        other = lax.rem(r + off, n_row)
        copy = remote(buf.at[other], land.at[other], send.at[other], recv.at[other], other, c)
        copy.wait_send()
        copy.wait_recv()
        return carry

    lax.fori_loop(1, n_row, finish, 0)


def greet_rows():
    r, c, base, t = place()
    n_row = lax.axis_size("row")
    barrier = pltpu.get_barrier_semaphore()

    def greet(off, carry):
        pl.semaphore_signal(
            barrier, inc=1, device_id=(lax.rem(r + off, n_row), c), device_id_type=MESH
        )
        return carry

    lax.fori_loop(1, n_row, greet, 0)
    pl.semaphore_signal(barrier, inc=1, device_id=(r, 1 - c), device_id_type=MESH)
    pl.semaphore_wait(barrier, n_row)


COLS = 512


def permute_out(choice, buf, first, second, slots):
    n_row = buf.shape[0]

    def column(i, carry):
        cols = pl.ds(pl.multiple_of(i * COLS, COLS), COLS)
        picked = matmul(choice[:, :slots], first[:, cols]) + matmul(choice[:, slots:], second[:, cols])
        buf[:, :, cols] = picked.astype(jnp.bfloat16).reshape(n_row, CHUNK, COLS)
        return carry

    lax.fori_loop(0, buf.shape[2] // COLS, column, 0)


def permute_in(choice, land, first, second, slots):
    n_row = land.shape[0]

    def column(i, carry):
        cols = pl.ds(pl.multiple_of(i * COLS, COLS), COLS)
        got = land[:, :, cols].reshape(n_row * CHUNK, COLS)
        first[:, cols] = matmul_left(choice[:, :slots], got).astype(jnp.bfloat16)
        second[:, cols] = matmul_left(choice[:, slots:], got).astype(jnp.bfloat16)
        return carry

    lax.fori_loop(0, land.shape[2] // COLS, column, 0)


def deal_kernel(
    meta, tokens, cotangent, gain,
    meta_all, give, take, x_out, gy_out, normed_all, gy_all,
    x_mine, g_mine, buf, land, normed,
    load, msend, mrecv, csend, crecv, nsend, nrecv, nhere, gsend, grecv, ghere,
):
    r, c, base, t = place()
    n_row = lax.axis_size("row")
    slots = x_mine.shape[0]
    per_peer = slots // n_row
    loads = [
        pltpu.make_async_copy(tokens.at[c], x_mine, load.at[0]),
        pltpu.make_async_copy(cotangent.at[c], g_mine, load.at[1]),
    ]
    for copy in loads:
        copy.start()
    greet_rows()

    def meta_copy(other, slot):
        return remote(meta, meta_all.at[slot], msend.at[other], mrecv.at[slot], other, c)

    def start(off, carry):
        meta_copy(lax.rem(r + off, n_row), r).start()
        return carry

    lax.fori_loop(1, n_row, start, 0)
    meta_all[r] = meta[...]

    def finish(off, carry):
        other = lax.rem(r + off, n_row)
        copy = meta_copy(other, other)
        copy.wait_send()
        copy.wait_recv()
        return carry

    lax.fori_loop(1, n_row, finish, 0)

    shift = slots.bit_length() - 1
    row_no = lax.broadcasted_iota(jnp.int32, (CHUNK, slots), 0)
    wanted = jnp.where(row_no < per_peer, row_no, row_no - per_peer).astype(jnp.float32)
    early = row_no < per_peer
    late = (row_no >= per_peer) & (row_no < 2 * per_peer)
    tri = (
        lax.broadcasted_iota(jnp.int32, (slots, slots), 0)
        < lax.broadcasted_iota(jnp.int32, (slots, slots), 1)
    ).astype(jnp.float32).astype(jnp.bfloat16)
    places = lax.broadcasted_iota(jnp.int32, (slots, slots), 0)

    def order_of(block):
        picked = jnp.where(c == 0, block[0:1, :], block[1:2, :])
        return lax.shift_right_logical(picked, shift), picked - lax.shift_left(
            lax.shift_right_logical(picked, shift), shift
        )

    own_source, own_local = order_of(meta[...])

    def select(mask):
        wide = jnp.broadcast_to(mask.astype(jnp.float32), (CHUNK, slots)).astype(jnp.bfloat16)
        rank = matmul(wide, tri)
        return jnp.where(
            (rank == wanted) & (wide.astype(jnp.float32) > 0.5), 1.0, 0.0
        )

    def build(d, carry):
        rows = pl.ds(pl.multiple_of(d * CHUNK, CHUNK), CHUNK)
        source, local = order_of(meta_all[d])
        chosen = select(source == r).astype(jnp.bfloat16)
        at_home = (places == local).astype(jnp.float32).astype(jnp.bfloat16)
        picks = matmul_trans(chosen, at_home)
        give[rows, :slots] = jnp.where(early, picks, 0.0).astype(jnp.bfloat16)
        give[rows, slots:] = jnp.where(late, picks, 0.0).astype(jnp.bfloat16)
        kept = select(own_source == d)
        take[rows, :slots] = jnp.where(early, kept, 0.0).astype(jnp.bfloat16)
        take[rows, slots:] = jnp.where(late, kept, 0.0).astype(jnp.bfloat16)
        return carry

    lax.fori_loop(0, n_row, build, 0)
    for copy in loads:
        copy.wait()
    permute_out(give, buf, x_mine, g_mine, slots)
    exchange_rows(buf, land, csend, crecv)
    land[r] = buf[r]
    finish_rows(buf, land, csend, crecv)
    permute_in(take, land, x_out, gy_out, slots)

    def norm(rows):
        values = x_out[rows, :].astype(jnp.float32)
        scale = lax.rsqrt(jnp.mean(values * values, axis=-1, keepdims=True) + EPS)
        normed[rows, :] = (values * scale * gain[...]).astype(jnp.bfloat16)

    by_rows(slots, norm)
    first = gather_start(normed, normed_all, nsend, nrecv, nhere)
    second = gather_start(gy_out, gy_all, gsend, grecv, ghere)
    gather_finish(first, normed_all, nsend, nrecv)
    gather_finish(second, gy_all, gsend, grecv)


def deal(meta, tokens, cotangent, gain, n_row):
    slots, width = tokens.shape[1:]
    bf = jnp.bfloat16
    return pl.pallas_call(
        deal_kernel,
        name="deal",
        out_shape=(
            jax.ShapeDtypeStruct((n_row, 8, 128), jnp.int32),
            jax.ShapeDtypeStruct((n_row * CHUNK, 2 * slots), bf),
            jax.ShapeDtypeStruct((n_row * CHUNK, 2 * slots), bf),
            jax.ShapeDtypeStruct((slots, width), bf),
            jax.ShapeDtypeStruct((slots, width), bf),
            jax.ShapeDtypeStruct((GROUP, slots, width), bf),
            jax.ShapeDtypeStruct((GROUP, slots, width), bf),
        ),
        in_specs=[
            pl.BlockSpec(memory_space=VMEM),
            pl.BlockSpec(memory_space=ANY),
            pl.BlockSpec(memory_space=ANY),
            pl.BlockSpec(memory_space=VMEM),
        ],
        out_specs=(pl.BlockSpec(memory_space=VMEM),) * 5 + (pl.BlockSpec(memory_space=ANY),) * 2,
        scratch_shapes=[
            VMEM((slots, width), bf),
            VMEM((slots, width), bf),
            VMEM((n_row, CHUNK, width), bf),
            VMEM((n_row, CHUNK, width), bf),
            VMEM((slots, width), bf),
            pltpu.SemaphoreType.DMA((2,)),
            pltpu.SemaphoreType.DMA((n_row,)),
            pltpu.SemaphoreType.DMA((n_row,)),
            pltpu.SemaphoreType.DMA((n_row,)),
            pltpu.SemaphoreType.DMA((n_row,)),
        ]
        + gather_scratch()
        + gather_scratch(),
        compiler_params=pltpu.CompilerParams(
            collective_id=0, has_side_effects=True, vmem_limit_bytes=40 << 20
        ),
    )(meta, tokens, cotangent, gain)


def middle_kernel(parts, x, gain, mid, normed_all, near, out2, far, s1, r1, s2, r2, normed, nsend, nrecv, nhere):
    greet_group()
    scatter_sum(parts, near, out2, far, s1, r1, s2, r2, mid)

    def norm(rows):
        values = x[rows, :].astype(jnp.float32) + mid[rows, :]
        mid[rows, :] = values
        scale = lax.rsqrt(jnp.mean(values * values, axis=-1, keepdims=True) + EPS)
        normed[rows, :] = (values * scale * gain[...]).astype(jnp.bfloat16)

    by_rows(mid.shape[0], norm)
    started = gather_start(normed, normed_all, nsend, nrecv, nhere)
    gather_finish(started, normed_all, nsend, nrecv)


def middle(parts, x, gain):
    slots, width = x.shape
    return pl.pallas_call(
        middle_kernel,
        name="middle",
        out_shape=(
            jax.ShapeDtypeStruct((slots, width), jnp.float32),
            jax.ShapeDtypeStruct((GROUP, slots, width), jnp.bfloat16),
        ),
        in_specs=[pl.BlockSpec(memory_space=VMEM)] * 3,
        out_specs=(pl.BlockSpec(memory_space=VMEM), pl.BlockSpec(memory_space=ANY)),
        scratch_shapes=scatter_scratch(slots, width)
        + [VMEM((slots, width), jnp.bfloat16)]
        + gather_scratch(),
        compiler_params=pltpu.CompilerParams(
            collective_id=1, has_side_effects=True, vmem_limit_bytes=40 << 20
        ),
    )(parts, x, gain)


def norm_back(values, gain, grad):
    inverse = lax.rsqrt(jnp.mean(values * values, axis=-1, keepdims=True) + EPS)
    scaled = grad * gain
    back = inverse * scaled - values * (
        inverse * inverse * inverse * jnp.mean(values * scaled, axis=-1, keepdims=True)
    )
    return back, jnp.sum(grad * values * inverse, axis=0, keepdims=True)


def turn_kernel(
    parts, ff_parts, mid, gy, gain, d_mid, result, d_gain, branch_all,
    near, out2, far, s1, r1, s2, r2, near_b, out2_b, far_b, s1b, r1b, s2b, r2b, branch, nsend, nrecv, nhere,
):
    greet_group()
    scatter_sum(parts, near, out2, far, s1, r1, s2, r2, d_mid)
    d_gain[...] = jnp.zeros_like(d_gain)

    def back(rows):
        values = mid[rows, :]
        grad, gain_part = norm_back(values, gain[...], d_mid[rows, :])
        grad = gy[rows, :].astype(jnp.float32) + grad
        d_mid[rows, :] = grad
        branch[rows, :] = grad.astype(jnp.bfloat16)
        d_gain[...] += gain_part

    by_rows(mid.shape[0], back)
    started = gather_start(branch, branch_all, nsend, nrecv, nhere)
    scatter_sum(ff_parts, near_b, out2_b, far_b, s1b, r1b, s2b, r2b, result)

    def add(rows):
        result[rows, :] += mid[rows, :]

    by_rows(mid.shape[0], add)
    gather_finish(started, branch_all, nsend, nrecv)


def turn(parts, ff_parts, mid, gy, gain):
    slots, width = mid.shape
    return pl.pallas_call(
        turn_kernel,
        name="turn",
        out_shape=(
            jax.ShapeDtypeStruct((slots, width), jnp.float32),
            jax.ShapeDtypeStruct((slots, width), jnp.float32),
            jax.ShapeDtypeStruct((1, width), jnp.float32),
            jax.ShapeDtypeStruct((GROUP, slots, width), jnp.bfloat16),
        ),
        in_specs=[pl.BlockSpec(memory_space=VMEM)] * 5,
        out_specs=(pl.BlockSpec(memory_space=VMEM),) * 3 + (pl.BlockSpec(memory_space=ANY),),
        scratch_shapes=scatter_scratch(slots, width)
        + scatter_scratch(slots, width)
        + [VMEM((slots, width), jnp.bfloat16)]
        + gather_scratch(),
        compiler_params=pltpu.CompilerParams(
            collective_id=2, has_side_effects=True, vmem_limit_bytes=48 << 20
        ),
    )(parts, ff_parts, mid, gy, gain)


def home_kernel(
    parts, x, d_mid, result, gain, give, take, output, gradient, d_gain,
    near, out2, far, s1, r1, s2, r2, total, first, second, buf, land, csend, crecv, here, osend, orecv,
):
    r, c, base, t = place()
    slots = x.shape[0]
    greet_rows()
    scatter_sum(parts, near, out2, far, s1, r1, s2, r2, total)
    d_gain[...] = jnp.zeros_like(d_gain)

    def back(rows):
        values = x[rows, :].astype(jnp.float32)
        grad, gain_part = norm_back(values, gain[...], total[rows, :])
        second[rows, :] = (d_mid[rows, :] + grad).astype(jnp.bfloat16)
        first[rows, :] = result[rows, :].astype(jnp.bfloat16)
        d_gain[...] += gain_part

    by_rows(slots, back)
    permute_out(take, buf, first, second, slots)
    exchange_rows(buf, land, csend, crecv)
    land[r] = buf[r]
    finish_rows(buf, land, csend, crecv)
    permute_in(give, land, first, second, slots)
    copies = []
    for i, (mine, out) in enumerate(((first, output), (second, gradient))):
        copies.append(pltpu.make_async_copy(mine, out.at[c], here.at[i]))
        copies.append(remote(mine, out.at[c], osend.at[i], orecv.at[i], r, 1 - c))
    for copy in copies:
        copy.start()
    for copy in copies:
        copy.wait()


def send_home(parts, x, d_mid, result, gain, give, take, n_row):
    slots, width = x.shape
    bf = jnp.bfloat16
    return pl.pallas_call(
        home_kernel,
        name="home",
        out_shape=(
            jax.ShapeDtypeStruct((2, slots, width), bf),
            jax.ShapeDtypeStruct((2, slots, width), bf),
            jax.ShapeDtypeStruct((1, width), jnp.float32),
        ),
        in_specs=[pl.BlockSpec(memory_space=VMEM)] * 7,
        out_specs=(pl.BlockSpec(memory_space=ANY),) * 2 + (pl.BlockSpec(memory_space=VMEM),),
        scratch_shapes=scatter_scratch(slots, width)
        + [
            VMEM((slots, width), jnp.float32),
            VMEM((slots, width), bf),
            VMEM((slots, width), bf),
            VMEM((n_row, CHUNK, width), bf),
            VMEM((n_row, CHUNK, width), bf),
            pltpu.SemaphoreType.DMA((n_row,)),
            pltpu.SemaphoreType.DMA((n_row,)),
            pltpu.SemaphoreType.DMA((2,)),
            pltpu.SemaphoreType.DMA((2,)),
            pltpu.SemaphoreType.DMA((2,)),
        ],
        compiler_params=pltpu.CompilerParams(
            collective_id=3, has_side_effects=True, vmem_limit_bytes=48 << 20
        ),
    )(parts, x, d_mid, result, gain, give, take)


def blocks_kernel(parts, total, low, land, mine, s1, r1, s2, r2, here):
    r, c, base, t = place()
    greet_group(cross=True)
    low[...] = parts[...].astype(jnp.bfloat16)
    others = [(m, f) for m in (3, 1, 2) for f in (0, 1)] + [(0, 1)]

    def where(m, f):
        row, col = partner(t, m), (1 - c if f else c)
        return row, col, row * 2 + col

    first = []
    for m, f in others:
        row, col, block = where(m, f)
        k = m * 2 + f
        first.append(remote(low.at[block], land.at[k], s1.at[k], r1.at[k], base + row, col))
        first[-1].start()
    own = t * 2 + c
    for copy in first:
        copy.wait_recv()
    summed = parts[own]
    for m, f in others:
        summed = summed + land[m * 2 + f].astype(jnp.float32)
    mine[...] = summed.astype(jnp.bfloat16)
    local = pltpu.make_async_copy(mine, total.at[own], here)
    local.start()
    second = []
    for m, f in others:
        row, col, block = where(m, f)
        k = m * 2 + f
        second.append(remote(mine, total.at[own], s2.at[k], r2.at[k], base + row, col))
        second[-1].start()
    local.wait()
    for copy in first:
        copy.wait_send()
    for copy in second:
        copy.wait()


def sum_blocks(parts, number):
    slots = parts.shape[1]
    return pl.pallas_call(
        blocks_kernel,
        name=f"blocks{number}",
        out_shape=jax.ShapeDtypeStruct(parts.shape, jnp.bfloat16),
        in_specs=[pl.BlockSpec(memory_space=VMEM)],
        out_specs=pl.BlockSpec(memory_space=VMEM),
        scratch_shapes=[
            VMEM(parts.shape, jnp.bfloat16),
            VMEM(parts.shape, jnp.bfloat16),
            VMEM(parts.shape[1:], jnp.bfloat16),
            pltpu.SemaphoreType.DMA((GROUP,)),
            pltpu.SemaphoreType.DMA((GROUP,)),
            pltpu.SemaphoreType.DMA((GROUP,)),
            pltpu.SemaphoreType.DMA((GROUP,)),
            pltpu.SemaphoreType.DMA,
        ],
        compiler_params=pltpu.CompilerParams(
            collective_id=number, has_side_effects=True, vmem_limit_bytes=16 << 20
        ),
    )(parts)


def layout(lengths, slot_count):
    count = lengths.shape[0]
    ends = [lengths[0]]
    for i in range(1, count):
        ends.append(ends[-1] + lengths[i])
    places = jnp.arange(slot_count, dtype=jnp.int32)
    segment = sum((places >= end).astype(jnp.int32) for end in ends)
    within = places
    for i in range(1, count):
        within = jnp.where(places >= ends[i - 1], places - ends[i - 1], within)
    allowed = (segment[:, None] == segment[None, :]) & (places[:, None] >= places[None, :])
    return (segment, within, allowed)


def causal_conv(values_in, kernel, bias_vec, segment):
    slot_count, channels = values_in.shape
    kernel_len = kernel.shape[0]
    summed = bias_vec[None, :] + kernel[kernel_len - 1][None, :] * values_in
    for shift_by in range(1, kernel_len):
        shifted = jnp.concatenate(
            [jnp.zeros((shift_by, channels), values_in.dtype), values_in[: slot_count - shift_by]],
            axis=0,
        )
        earlier = jnp.concatenate(
            [jnp.full((shift_by,), -1, jnp.int32), segment[: slot_count - shift_by]], axis=0
        )
        shifted = jnp.where((earlier == segment)[:, None], shifted, 0.0)
        summed = summed + kernel[kernel_len - 1 - shift_by][None, :] * shifted
    return jax.nn.silu(summed)


def decay_mix(intersection, step_raw, step_bias, decay_log, allowed):
    slot_count = step_raw.shape[0]
    step_size = jax.nn.softplus(step_raw + step_bias[None, :])
    rates = -jnp.exp(decay_log)
    places = jnp.arange(slot_count)
    tri = (places[:, None] >= places[None, :]).astype(jnp.float32)
    levels = jnp.dot(tri, step_size * rates[None, :], precision=HIGH).T
    spread = levels[:, :, None] - levels[:, None, :]
    decays = jnp.where(allowed[None], jnp.exp(jnp.where(allowed[None], spread, 0.0)), 0.0)
    return intersection[None] * decays * step_size.T[:, None, :]


def gate_mix(scanned, conv_out, mamba_gate, skip_scale):
    slot_count, channels = conv_out.shape
    per_head = channels // skip_scale.shape[0]
    mixed_out = (
        scanned.reshape(slot_count, channels) + conv_out * jnp.repeat(skip_scale, per_head)[None, :]
    )
    return mixed_out * jax.nn.silu(mamba_gate)


def rotary(vectors, cosine, sine):
    half_dim = vectors.shape[1] // 2
    turned = jnp.concatenate([-vectors[:, half_dim:], vectors[:, :half_dim]], axis=-1)
    return vectors * cosine + turned * sine


def rotary_back(vectors, cosine, sine):
    half_dim = vectors.shape[1] // 2
    scaled = vectors * sine
    turned = jnp.concatenate([scaled[:, half_dim:], -scaled[:, :half_dim]], axis=-1)
    return vectors * cosine + turned


def swiglu(ff_gate, ff_up):
    return jax.nn.silu(ff_gate) * ff_up


def cut(array, parts, axis=1):
    rows, cols = array.shape
    return array.reshape(rows, parts, cols // parts).transpose(1, 0, 2)


def local(
    tokens,
    cotangent,
    deal_order,
    seq_lengths,
    mixer_norm_gain,
    mamba_gate_weight,
    mamba_input_weight,
    state_weight,
    step_weight,
    conv_input,
    conv_input_bias,
    conv_state,
    conv_state_bias,
    step_bias,
    decay_log,
    skip_scale,
    mamba_out_weight,
    query_weight,
    key_weight,
    value_weight,
    attn_out_weight,
    ff_norm_gain,
    gate_weight,
    up_weight,
    down_weight,
):
    n_row = lax.axis_size("row")
    r = lax.axis_index("row")
    c = lax.axis_index("col")
    t = lax.rem(r, TP)
    data = n_row // TP
    slots, width = tokens.shape[1:]
    bf = jnp.bfloat16
    plane = [[i * TP + j for j in range(TP)] for i in range(data)]
    along = [[i * TP + j for i in range(data)] for j in range(TP)]

    rows = mamba_gate_weight.shape[0]
    mh = mamba_gate_weight.shape[1] // TP
    qh = query_weight.shape[1] // TP
    kvh = key_weight.shape[1]
    sh = state_weight.shape[1] // (2 * GROUP)
    ph = step_weight.shape[1] // TP
    fh = gate_weight.shape[1] // TP
    used = 2 * mh + qh + 2 * kvh + 2 * sh + ph
    spare = -used % 256

    def wide(array):
        return jnp.broadcast_to(array[None], (TP,) + array.shape)

    half = state_weight.shape[1] // 2
    state_in_part = lax.dynamic_slice_in_dim(state_weight[:, :half], c * (half // 2), half // 2, 1)
    state_out_part = lax.dynamic_slice_in_dim(state_weight[:, half:], c * (half // 2), half // 2, 1)
    packed_in = jnp.concatenate(
        [
            cut(mamba_gate_weight, TP),
            cut(mamba_input_weight, TP),
            cut(query_weight, TP),
            wide(key_weight),
            wide(value_weight),
            cut(state_in_part, TP),
            cut(state_out_part, TP),
            cut(step_weight, TP),
            jnp.zeros((TP, rows, spare), bf),
        ],
        axis=2,
    )
    packed_out = jnp.concatenate([cut(mamba_out_weight.T, TP), cut(attn_out_weight.T, TP)], axis=2)
    packed_ff = jnp.concatenate(
        [cut(gate_weight, TP), cut(up_weight, TP), cut(down_weight.T, TP)], axis=2
    )

    def assemble(packed):
        cols = packed.shape[2]
        mine = lax.all_to_all(
            packed, "row", split_axis=0, concat_axis=0, axis_index_groups=plane, tiled=True
        )
        return lax.all_gather(
            mine.reshape(TP * rows, cols), "row", axis=0, axis_index_groups=along, tiled=True
        )

    def disperse(grad):
        cols = grad.shape[1]
        mine = lax.psum_scatter(
            grad.astype(bf), "row", scatter_dimension=0, axis_index_groups=along, tiled=True
        )
        return lax.all_to_all(
            mine.reshape(TP, rows, cols),
            "row",
            split_axis=0,
            concat_axis=0,
            axis_index_groups=plane,
            tiled=True,
        )

    w_in = assemble(packed_in)
    w_out = assemble(packed_out)
    w_ff = assemble(packed_ff)

    meta = jnp.concatenate(
        [
            deal_order,
            jnp.pad(seq_lengths[:, 0, :], ((0, 0), (0, 128 - seq_lengths.shape[2]))),
            jnp.zeros((4, 128), jnp.int32),
        ],
        axis=0,
    )
    meta_all, give, take, x_home, gy_home, normed_one, gy_all = deal(
        meta, tokens, cotangent, mixer_norm_gain[None, :], n_row
    )
    normed_one = normed_one.reshape(GROUP * slots, width)
    gy_all = gy_all.reshape(GROUP * slots, width)
    group_meta = lax.dynamic_slice_in_dim(meta_all, r - t, TP, 0)
    lengths = group_meta[:, 2:4, : seq_lengths.shape[2]].reshape(GROUP, seq_lengths.shape[2])
    segment, within, allowed = jax.vmap(lambda own: layout(own, slots))(lengths)
    segment = (segment + 8 * jnp.arange(GROUP, dtype=jnp.int32)[:, None]).reshape(-1)
    half_dim = HD // 2
    inverse = ROPE_BASE ** (-2.0 * jnp.arange(half_dim, dtype=jnp.float32) / HD)
    angles = within.reshape(-1).astype(jnp.float32)[:, None] * inverse[None, :]
    cosine = jnp.concatenate([jnp.cos(angles), jnp.cos(angles)], axis=1)
    sine = jnp.concatenate([jnp.sin(angles), jnp.sin(angles)], axis=1)

    def piece(array, size, start):
        return lax.dynamic_slice_in_dim(array, start, size, array.ndim - 1)

    eighth = c * TP + t
    conv_k = piece(conv_input, mh, t * mh)
    conv_b = piece(conv_input_bias, mh, t * mh)
    state_k = jnp.concatenate(
        [piece(conv_state, sh, eighth * sh), piece(conv_state, sh, half + eighth * sh)], axis=1
    )
    state_b = jnp.concatenate(
        [piece(conv_state_bias, sh, eighth * sh), piece(conv_state_bias, sh, half + eighth * sh)]
    )
    bias_h = piece(step_bias, ph, t * ph)
    decay_h = piece(decay_log, ph, t * ph)
    skip_h = piece(skip_scale, ph, t * ph)

    projected = matmul(normed_one, w_in)
    edges = [0, mh, 2 * mh, 2 * mh + qh, 2 * mh + qh + kvh, 2 * mh + qh + 2 * kvh]
    edges = edges + [edges[-1] + 2 * sh, edges[-1] + 2 * sh + ph]
    mamba_gate, conv_in, queries, keys_raw, values_raw, state_raw, step_raw = (
        projected[:, low:high] for low, high in zip(edges[:-1], edges[1:])
    )
    conv_out = causal_conv(conv_in, conv_k, conv_b, segment)
    state_act = causal_conv(state_raw, state_k, state_b, segment)
    state_in_low = state_act[:, :sh].astype(bf).reshape(GROUP, slots, sh)
    state_out_low = state_act[:, sh:].astype(bf).reshape(GROUP, slots, sh)
    cross_part = jnp.einsum(
        "bin,bjn->bij", state_out_low, state_in_low, preferred_element_type=jnp.float32
    )
    intersection = sum_blocks(cross_part, 4).astype(jnp.float32)
    step_blocks = step_raw.reshape(GROUP, slots, ph)

    def mix_all(crossed, step_values, bias_values, decay_values):
        return jax.vmap(
            lambda one, two, three: decay_mix(one, two, bias_values, decay_values, three)
        )(crossed, step_values, allowed)

    mixing, mix_back = jax.vjp(mix_all, intersection, step_blocks, bias_h, decay_h)
    mixing_low = mixing.astype(bf)
    conv_low = conv_out.astype(bf).reshape(GROUP, slots, ph, -1)
    scanned = jnp.einsum(
        "bhij,bjhp->bihp", mixing_low, conv_low, preferred_element_type=jnp.float32
    ).reshape(GROUP * slots, mh)
    gated_low = gate_mix(scanned, conv_out, mamba_gate, skip_h).astype(bf)

    query_rot = rotary(queries, cosine, sine).astype(bf).reshape(GROUP, slots, HD)
    key_rot = rotary(keys_raw, cosine, sine).astype(bf).reshape(GROUP, slots, HD)
    value_low = values_raw.astype(bf).reshape(GROUP, slots, HD)
    raw = jnp.einsum("bid,bjd->bij", query_rot, key_rot, preferred_element_type=jnp.float32)
    scores = jnp.where(allowed, raw * HD ** (-0.5), NEG_LARGE)
    exp_terms = jnp.exp(scores - jnp.max(scores, axis=-1, keepdims=True))
    probs = exp_terms / jnp.sum(exp_terms, axis=-1, keepdims=True)
    attended_low = (
        jnp.einsum("bij,bjd->bid", probs.astype(bf), value_low, preferred_element_type=jnp.float32)
        .astype(bf)
        .reshape(GROUP * slots, HD)
    )
    branch_in = jnp.concatenate([gated_low, attended_low], axis=1)
    branch_part = matmul_trans(branch_in, w_out).astype(bf).reshape(GROUP, slots, width)
    mid, normed_two = middle(branch_part, x_home, ff_norm_gain[None, :])
    normed_two = normed_two.reshape(GROUP * slots, width)

    ff_gate_up = matmul(normed_two, w_ff[:, : 2 * fh])
    ff_gate, ff_up = ff_gate_up[:, :fh], ff_gate_up[:, fh:]
    w_down = w_ff[:, 2 * fh :]
    ff_hidden = swiglu(ff_gate, ff_up).astype(bf)
    ff_part = matmul_trans(ff_hidden, w_down).astype(bf).reshape(GROUP, slots, width)
    grad_hidden = matmul(gy_all, w_down)
    unused_value, pullback = jax.vjp(swiglu, ff_gate, ff_up)
    grad_gate, grad_up = pullback(grad_hidden)
    grad_gate_up = jnp.concatenate([grad_gate.astype(bf), grad_up.astype(bf)], axis=1)
    normed_two_part = (
        matmul_trans(grad_gate_up, w_ff[:, : 2 * fh]).astype(bf).reshape(GROUP, slots, width)
    )
    d_mid, result, delta_ff_gain, branch_all = turn(
        normed_two_part, ff_part, mid, gy_home, ff_norm_gain[None, :]
    )
    branch_all = branch_all.reshape(GROUP * slots, width)
    delta_gate_up = disperse(matmul_left(normed_two, grad_gate_up))
    delta_down = disperse(matmul_left(gy_all, ff_hidden))

    delta_out = disperse(matmul_left(branch_all, branch_in))
    grad_branch_in = matmul(branch_all, w_out)
    grad_gated = grad_branch_in[:, :mh]
    unused_value, pullback = jax.vjp(gate_mix, scanned, conv_out, mamba_gate, skip_h)
    grad_scanned, grad_conv_skip, grad_mamba_gate, delta_skip = pullback(grad_gated)
    grad_scanned = grad_scanned.astype(bf).reshape(GROUP, slots, ph, -1)
    grad_mixing = jnp.einsum(
        "bihp,bjhp->bhij", grad_scanned, conv_low, preferred_element_type=jnp.float32
    )
    grad_conv_out = grad_conv_skip + jnp.einsum(
        "bhij,bihp->bjhp", mixing_low, grad_scanned, preferred_element_type=jnp.float32
    ).reshape(GROUP * slots, mh)
    grad_cross, grad_step, delta_step_bias, delta_decay = mix_back(grad_mixing)
    grad_cross = sum_blocks(grad_cross, 5)
    grad_step = grad_step.reshape(GROUP * slots, ph).astype(bf)

    grad_attended = grad_branch_in[:, mh:].astype(bf).reshape(GROUP, slots, HD)
    grad_probs = jnp.einsum(
        "bid,bjd->bij", grad_attended, value_low, preferred_element_type=jnp.float32
    )
    grad_values = jnp.einsum(
        "bij,bid->bjd", probs.astype(bf), grad_attended, preferred_element_type=jnp.float32
    ).reshape(GROUP * slots, HD)
    grad_raw = probs * (grad_probs - jnp.sum(grad_probs * probs, axis=-1, keepdims=True))
    grad_raw = (grad_raw * HD ** (-0.5)).astype(bf)
    grad_query_rot = jnp.einsum(
        "bij,bjd->bid", grad_raw, key_rot, preferred_element_type=jnp.float32
    ).reshape(GROUP * slots, HD)
    grad_key_rot = jnp.einsum(
        "bij,bid->bjd", grad_raw, query_rot, preferred_element_type=jnp.float32
    ).reshape(GROUP * slots, HD)
    grad_queries = rotary_back(grad_query_rot, cosine, sine)
    grad_keys = rotary_back(grad_key_rot, cosine, sine)

    unused_value, pullback = jax.vjp(partial(causal_conv, segment=segment), conv_in, conv_k, conv_b)
    grad_conv_in, delta_conv_k, delta_conv_b = pullback(grad_conv_out)
    grad_state = jnp.concatenate(
        [
            jnp.einsum("bij,bin->bjn", grad_cross, state_out_low, preferred_element_type=jnp.float32),
            jnp.einsum("bij,bjn->bin", grad_cross, state_in_low, preferred_element_type=jnp.float32),
        ],
        axis=2,
    ).reshape(GROUP * slots, 2 * sh)
    unused_value, pullback = jax.vjp(
        partial(causal_conv, segment=segment), state_raw, state_k, state_b
    )
    grad_state_raw, delta_state_k, delta_state_b = pullback(grad_state)
    grad_projected = jnp.concatenate(
        [
            grad_mamba_gate.astype(bf),
            grad_conv_in.astype(bf),
            grad_queries.astype(bf),
            grad_keys.astype(bf),
            grad_values.astype(bf),
            grad_state_raw.astype(bf),
            grad_step,
            jnp.zeros((GROUP * slots, spare), bf),
        ],
        axis=1,
    )
    normed_one_part = matmul_trans(grad_projected, w_in).astype(bf).reshape(GROUP, slots, width)
    output, grad_tokens, delta_mixer_gain = send_home(
        normed_one_part, x_home, d_mid, result, mixer_norm_gain[None, :], give, take, n_row
    )
    delta_in = disperse(matmul_left(normed_one, grad_projected))

    def join(stacked):
        return stacked.transpose(1, 0, 2).reshape(stacked.shape[1], -1).astype(jnp.float32)

    pieces = [delta_in[:, :, low:high] for low, high in zip(edges[:-1], edges[1:])]
    state_mine = pieces[5]
    state_other = lax.ppermute(state_mine, "col", [(0, 1), (1, 0)])
    state_first = jnp.where(c == 0, state_mine, state_other)
    state_second = jnp.where(c == 0, state_other, state_mine)
    delta_state = jnp.concatenate(
        [
            join(state_first[:, :, :sh]),
            join(state_second[:, :, :sh]),
            join(state_first[:, :, sh:]),
            join(state_second[:, :, sh:]),
        ],
        axis=1,
    )
    delta_key = jnp.sum(pieces[3].astype(jnp.float32), axis=0)
    delta_value = jnp.sum(pieces[4].astype(jnp.float32), axis=0)

    def spread(array, whole, start):
        return lax.dynamic_update_slice_in_dim(
            jnp.zeros(array.shape[:-1] + (whole,), jnp.float32), array, start, array.ndim - 1
        )

    by_col = [
        spread(delta_conv_k, conv_input.shape[1], t * mh),
        spread(delta_conv_b, conv_input_bias.shape[0], t * mh),
        spread(delta_step_bias, step_bias.shape[0], t * ph),
        spread(delta_decay, decay_log.shape[0], t * ph),
        spread(delta_skip, skip_scale.shape[0], t * ph),
    ]
    by_all = [
        spread(delta_state_k[:, :sh], 2 * half, eighth * sh)
        + spread(delta_state_k[:, sh:], 2 * half, half + eighth * sh),
        spread(delta_state_b[:sh], 2 * half, eighth * sh)
        + spread(delta_state_b[sh:], 2 * half, half + eighth * sh),
        delta_mixer_gain[0],
        delta_ff_gain[0],
    ]
    by_col = lax.psum(by_col, "row")
    by_all = lax.psum(by_all, ("row", "col"))

    return (
        output,
        grad_tokens,
        by_all[2],
        join(pieces[0]),
        join(pieces[1]),
        delta_state,
        join(pieces[6]),
        by_col[0],
        by_col[1],
        by_all[0],
        by_all[1],
        by_col[2],
        by_col[3],
        by_col[4],
        join(delta_out[:, :, :mh]).T,
        join(pieces[2]),
        delta_key,
        delta_value,
        join(delta_out[:, :, mh:]).T,
        by_all[3],
        join(delta_gate_up[:, :, :fh]),
        join(delta_gate_up[:, :, fh:]),
        join(delta_down).T,
    )


def solution(mesh):
    both = P("row", "col")
    turned = P("col", "row")
    in_specs = (
        P(None, "row", None),
        P(None, "row", None),
        P(None, "row"),
        P(None, "row", None),
        P(),
        both,
        both,
        P("row", None),
        both,
        P(None, "col"),
        P("col"),
        P(),
        P(),
        P("col"),
        P("col"),
        P("col"),
        turned,
        both,
        both,
        both,
        turned,
        P(),
        both,
        both,
        turned,
    )
    out_specs = (
        P(None, "row", None),
        P(None, "row", None),
        P(),
        both,
        both,
        P("row", None),
        both,
        P(None, "col"),
        P("col"),
        P(),
        P(),
        P("col"),
        P("col"),
        P("col"),
        turned,
        both,
        both,
        both,
        turned,
        P(),
        both,
        both,
        turned,
    )
    return jax.shard_map(local, mesh=mesh, in_specs=in_specs, out_specs=out_specs, check_vma=False)
```

time: 3330 us -> 854 us (0.26)
  the two profiles are of different devices: /device:TPU:9 before, /device:TPU:1 now
where the time goes in v1:
time: 854 us; the launch traced here: 843 us
  Pallas kernels  349 us (41%)
  blocking collectives  174 us (20%)
  matrix products  109 us (13%)
  local copies, waits for them, and re-layouts  92.8 us (11%)
  other arithmetic  49.6 us (6%)
  starting transfers between devices  32.7 us (4%)
  waiting for transfers between devices  19.5 us (2%)
  between operations  16.1 us (2%)
    pallas_call x1, Pallas kernels, deal(): pl.pallas_call(deal_kernel, name='deal', out_shape=(jax.ShapeDtypeStruct(...  102 us
    pallas_call x1, Pallas kernels, turn(): pl.pallas_call(turn_kernel, name='turn', out_shape=(jax.ShapeDtypeStruct(...  85.7 us
    pallas_call x1, Pallas kernels, send_home(): pl.pallas_call(home_kernel, name='home', out_shape=(jax.ShapeDtypeStruct(...  78.5 us
    psum x1, blocking collectives, local(): by_all = lax.psum(by_all, ('row', 'col'))  65 us
    psum x1, blocking collectives, local(): by_col = lax.psum(by_col, 'row')  61.3 us
    pallas_call x1, Pallas kernels, middle(): pl.pallas_call(middle_kernel, name='middle', out_shape=(jax.ShapeDtypeStr...  58 us
    all_to_all x3, blocking collectives, assemble(): lax.all_to_all(packed, 'row', split_axis=0, concat_axis=0, axis_index_gro...  47.5 us
    unnamed x235, local copies, waits for them, and re-layouts  38 us
  transfers between devices with their start and end apart: 12, of which 2 were waited for; matrix products, arithmetic and copies ran while one was open for 24% of the time, Pallas kernels for 41%

profile of v1, /device:TPU:1, one launch (start us, length us, event | category | flops | bytes accessed | tf_op | source)
XLA Modules:
  0.0 843.3 jit_solution(15117475378507485569)
XLA Ops:
  15.1 19.8 %all_to_all.35 = bf16[4,128,1280]{1,2,0:T(8,128)(2,1)S(1)} all-to-all(bf16[4,128,1280]{1,2,0:T(8,128)(2,1)S(1)} %concatenate.101), channel_id=1, replica_groups={{0,2,4,6},{8,10,12,14},{16,18,20,22},{24,26,28,30},{1,3,5,7},{9,11,13,1..., dimensions={0} | all-to-all | bytes 2621440 | tf_op jit(solution)/shard_map/all_to_all | solution.py:767
  36.5 8.6 %all_to_all.36 = bf16[4,128,512]{1,2,0:T(8,128)(2,1)S(1)} all-to-all(bf16[4,128,512]{1,2,0:T(8,128)(2,1)S(1)} %pad_maximum_fusion.9), channel_id=1, replica_groups={{0,2,4,6},{8,10,12,14},{16,18,20,22},{24,26,28,30},{1,3,5,7},{9,11,13,1..., dimensions={0} | all-to-all | bytes 1048576 | tf_op jit(solution)/shard_map/all_to_all | solution.py:767
  46.8 19.2 %all_to_all.37 = bf16[4,128,1536]{1,2,0:T(8,128)(2,1)} all-to-all(bf16[4,128,1536]{1,2,0:T(8,128)(2,1)S(1)} %pad_maximum_fusion.1), channel_id=1, replica_groups={{0,2,4,6},{8,10,12,14},{16,18,20,22},{24,26,28,30},{1,3,5,7},{9,11,13,1..., dimensions={0} | all-to-all | bytes 3145728 | tf_op jit(solution)/shard_map/all_to_all | solution.py:767
  66.1 2.8 copy.241
  69.6 102.0 %deal.1 = (s32[16,8,128]{2,1,0:T(8,128)S(1)}, bf16[256,256]{1,0:T(8,128)(2,1)S(1)}, bf16[256,256]{1,0:T(8,128)(2,1)S(1)}, bf16[128,2048]{1,0:T(8,128)(2,1)S(1)},...) custom-call(s32[8,128]{1,0:T(8,128)S(1)} %fusion.74.meta, ...), custom_call_target="tpu_custom_call" | custom-call | tf_op jit(solution)/shard_map/deal/pallas_call | solution.py:359
  179.4 3.1 multiply_cosine_fusion
  182.5 8.9 %fusion.105 = f32[1024,1280]{1,0:T(8,128)S(1)} fusion(bf16[1024,2048]{1,0:T(8,128)(2,1)} %bitcast.320, bf16[2048,1280]{1,0:T(8,128)(2,1)} %all-gather.4.cloned.1.call-done), kind=kOutput, calls=%fused_computation.252 | convolution fusion | flops 5368709120 | bytes 14680064 | tf_op jit(solution)/shard_map/dot_general | solution.py:24
  199.2 4.5 fusion.90
  203.7 2.8 copy.227
  207.9 3.8 multiply_convert_fusion.6
  212.9 14.2 %blocks4.1 = bf16[8,128,128]{2,1,0:T(8,128)(2,1)S(1)} custom-call(f32[8,128,128]{2,1,0:T(8,128)S(1)} %fusion.106.parts), custom_call_target="tpu_custom_call" | custom-call | tf_op jit(solution)/shard_map/blocks4/pallas_call | solution.py:597
  231.8 3.0 copy.238
  234.9 3.1 fusion.50
  242.4 3.6 multiply_convert_fusion.3
  246.0 4.3 convolution_convert_fusion.3
  250.4 58.0 %middle.1 = (f32[128,2048]{1,0:T(8,128)S(1)}, bf16[8,128,2048]{2,1,0:T(8,128)(2,1)S(1)}) custom-call(bf16[8,128,2048]{2,1,0:T(8,128)(2,1)S(1)} %bitcast.313, bf16[128,2048]{1,0:T(8,128)(2,1)S(1)} %get-tuple-element.42.x, f32[1,2048]{1,0:T(1,128)S(1)} %bitcast.314), custom_call_target="tpu_custom_call" | custom-call | tf_op jit(solution)/shard_map/middle/pallas_call | solution.py:415
  310.4 11.3 %all-gather.6.cloned.1.call-done = bf16[2048,1536]{1,0:T(8,128)(2,1)} async-done(((bf16[512,1536]{1,0:T(8,128)(2,1)}), bf16[2048,1536]{1,0:T(8,128)(2,1)}) %all-gather.6.cloned.1.call-update) | async-done | bytes 6291472 | tf_op jit(solution)/shard_map/all_gather | solution.py:770
  321.8 7.8 fusion.3
  329.6 6.3 fusion.9
  336.9 3.7 convolution_convert_fusion.6
  340.7 6.4 convolution_convert_fusion.2
  347.1 8.4 convolution_convert_fusion.5
  355.5 85.7 %turn.1 = (f32[128,2048]{1,0:T(8,128)S(1)}, f32[128,2048]{1,0:T(8,128)S(1)}, f32[1,2048]{1,0:T(1,128)S(1)}, bf16[8,128,2048]{2,1,0:T(8,128)(2,1)}) custom-call(bf16[8,128,2048]{2,1,0:T(8,128)(2,1)} %bitcast.334, bf16[8,128,2048]{2,1,0:T(8,128)(2,1)} %bitcast.333, f32[128,2048]{1,0:T(8,128)S(1)} %get-tuple-element.44.mid, ...), custom_call_target="tpu_custom_call" | custom-call | tf_op jit(solution)/shard_map/turn/pallas_call | solution.py:471
  443.2 5.9 convolution_convert_fusion.7
  451.0 9.5 %convolution_convert_fusion.4 = bf16[2048,1024]{1,0:T(8,128)(2,1)} fusion(bf16[1024,2048]{1,0:T(8,128)(2,1)} %bitcast.325, bf16[1024,512]{0,1:T(8,128)(2,1)S(1)} %copy-done.106, bf16[1024,512]{0,1:T(8,128)(2,1)S(1)} %copy-done.104), kind=kOutput, calls=%fused_computation.6 | convolution fusion | flops 4301258752 | bytes 10485760 | tf_op jit(solution)/shard_map/dot_general | solution.py:34
  460.6 5.3 fusion.107
  465.9 4.3 multiply_reduce_fusion.2
  472.4 2.4 copy.244
  476.2 3.1 convolution_bitcast_fusion
  481.7 3.1 copy.247
  484.8 5.3 fusion.15
  490.1 10.9 %blocks5.1 = bf16[8,128,128]{2,1,0:T(8,128)(2,1)S(1)} custom-call(f32[8,128,128]{2,1,0:T(8,128)S(1)} %get-tuple-element.150.parts), custom_call_target="tpu_custom_call" | custom-call | tf_op jit(solution)/shard_map/blocks5/pallas_call | solution.py:597
  515.6 2.7 fusion.33
  523.4 3.7 fusion.91
  530.8 5.5 concatenate.124
  536.2 10.1 %convolution_convert_fusion = bf16[2048,1280]{1,0:T(8,128)(2,1)} fusion(bf16[1024,2048]{1,0:T(8,128)(2,1)} %bitcast.321, bf16[1024,1280]{1,0:T(8,128)(2,1)} %concatenate.124), kind=kOutput, calls=%fused_computation.2 | convolution fusion | flops 5371330560 | bytes 12058624 | tf_op jit(solution)/shard_map/dot_general | solution.py:34
  546.4 4.3 all-to-all-start.6
  550.7 8.0 all-to-all-done.6
  558.8 4.2 all-to-all-start.4
  563.0 9.7 %convolution_convert_fusion.1 = bf16[1024,2048]{1,0:T(8,128)(2,1)} fusion(bf16[1024,1280]{1,0:T(8,128)(2,1)S(1)} %copy-done.26, bf16[2048,1280]{1,0:T(8,128)(2,1)} %all-gather.4.cloned.1.call-done), kind=kOutput, calls=%fused_computation.3 | convolution fusion | flops 5370806272 | bytes 12058624 | tf_op jit(solution)/shard_map/dot_general | solution.py:28
  575.6 78.5 %home.1 = (bf16[2,128,2048]{2,1,0:T(8,128)(2,1)S(1)}, bf16[2,128,2048]{2,1,0:T(8,128)(2,1)S(1)}, f32[1,2048]{1,0:T(1,128)S(1)}) custom-call(bf16[8,128,2048]{2,1,0:T(8,128)(2,1)} %bitcast.332, bf16[128,2048]{1,0:T(8,128)(2,1)S(1)} %get-tuple-element.42.x, f32[128,2048]{1,0:T(8,128)S(1)} %copy-done.3, f32[128,2048]{1,0:T(8,128)S(1)} %copy-done.5, ...), custom_call_target="tpu_custom_call" | custom-call | tf_op jit(solution)/shard_map/home/pallas_call | solution.py:528
  654.9 4.3 all-to-all-start.5
  659.5 65.0 %all-reduce.23 = (f32[2048]{0:T(1024)}, f32[4,512]{1,0:T(4,128)}, f32[512]{0:T(512)}, f32[2048]{0:T(1024)}) all-reduce(f32[2048]{0:T(1024)S(1)} %bitcast.319, f32[4,512]{1,0:T(4,128)S(1)} %add.326, f32[512]{0:T(512)S(1)} %add_dynamic-update-slice_fusion.1, f32[2048]{0:T(1024)S(1)} %bitcast.318), channel_id=1, replica_groups=mesh['row'=16,'col'=2] {'row','col'}, use_global_device_ids=true, to_apply=%region_7.8 | all-reduce | flops 6656 | bytes 53248 | tf_op jit(solution)/shard_map/psum | solution.py:1003
  724.7 61.3 %all-reduce.24 = (f32[4,1536]{1,0:T(4,128)}, f32[1536]{0:T(1024)}, f32[24]{0:T(128)}, f32[24]{0:T(128)}, f32[24]{0:T(128)}) all-reduce(f32[4,1536]{1,0:T(4,128)S(1)} %add_dynamic-update-slice_fusion, f32[1536]{0:T(1024)S(1)} %dynamic_update_slice.32, f32[24]{0:T(128)S(1)} %dynamic_update_slice.39, ...), channel_id=1, replica_groups=mesh['row'=16,'col'=2] {'row'}, use_global_device_ids=true, to_apply=%region_13.14 | all-reduce | flops 7752 | bytes 62016 | tf_op jit(solution)/shard_map/psum | solution.py:1002
  786.0 2.4 copy.257
  788.4 4.3 all-to-all-start.3
  794.9 2.5 copy.262
  807.1 15.4 %collective-permute-start = (bf16[4,128,64]{1,2,0:T(8,128)(2,1)S(1)}, bf16[4,128,64]{1,2,0:T(8,128)(2,1)S(1)}, u32[]{:S(2)}, u32[]{:S(2)}) collective-permute-start(bf16[4,128,64]{1,2,0:T(8,128)(2,1)S(1)} %slice.340), channel_id=1, source_target_pairs={{0,1},{1,0},{2,3},{3,2},{4,5},{5,4},{6,7},{7,6},{8,9},{9,8},{10,11... | collective-permute-start | bytes 196616 | tf_op jit(solution)/shard_map/ppermute | solution.py:967
  (388 shorter events, 104.4 us)
Async XLA Ops:
  7.2 175.3 %all-gather.4.cloned.1.call-start = ((), (), s32[]{:S(2)}) async-start(), calls=%async_computation.11 | async-start | bytes 6553600 | tf_op jit(solution)/shard_map/all_gather | solution.py:770
  36.4 9.8 %copy-start.43 = (bf16[128,2048]{1,0:T(8,128)(2,1)S(1)}, bf16[128,2048]{1,0:T(8,128)(2,1)}, u32[]{:S(2)}) copy-start(bf16[128,2048]{1,0:T(8,128)(2,1)} %param.47) | copy-start | bytes 1572868
  36.4 209.6 %all-gather.8.cloned.1.call-start = ((), (), s32[]{:S(2)}) async-start(), calls=%async_computation.13 | async-start | bytes 2621440 | tf_op jit(solution)/shard_map/all_gather | solution.py:770
  36.5 9.9 %copy-start.44 = (bf16[128,2048]{1,0:T(8,128)(2,1)S(1)}, bf16[128,2048]{1,0:T(8,128)(2,1)}, u32[]{:S(2)}) copy-start(bf16[128,2048]{1,0:T(8,128)(2,1)} %param.48) | copy-start | bytes 1572868
  46.1 275.7 %all-gather.6.cloned.1.call-start = ((), (), s32[]{:S(2)}) async-start(), calls=%async_computation.12 | async-start | bytes 7864320 | tf_op jit(solution)/shard_map/all_gather | solution.py:770
  68.8 109.9 %copy-start.97 = (f32[24]{0:T(128)S(1)}, f32[24]{0:T(128)}, u32[]{:S(2)}) copy-start(f32[24]{0:T(128)} %param.39) | copy-start | bytes 292
  68.8 110.0 %copy-start.96 = (f32[512]{0:T(512)S(1)}, f32[512]{0:T(512)}, u32[]{:S(2)}) copy-start(f32[512]{0:T(512)} %param.37) | copy-start | bytes 6148
  68.8 110.2 %copy-start.89 = (f32[4,512]{1,0:T(4,128)S(1)}, f32[4,512]{1,0:T(4,128)}, u32[]{:S(2)}) copy-start(f32[4,512]{1,0:T(4,128)} %param.36) | copy-start | bytes 24580
  68.9 477.5 %reduce-scatter.11.cloned.1.call-start = ((), (), s32[]{:S(2)}) async-start(), calls=%async_computation.17 | async-start | bytes 2621440 | tf_op jit(solution)/shard_map/reduce_scatter | solution.py:776
  69.0 129.5 %copy-start.92 = (f32[6]{0:T(128)}, f32[6]{0:T(128)S(1)}, u32[]{:S(2)}) copy-start(f32[6]{0:T(128)S(1)} %dynamic_slice.45) | copy-start | bytes 76
  69.3 396.6 %copy-start.65 = (f32[384]{0:T(512)}, f32[384]{0:T(512)S(1)}, u32[]{:S(2)}) copy-start(f32[384]{0:T(512)S(1)} %mul.495) | copy-start | bytes 4612
  178.7 20.5 %copy-start.67 = (f32[384]{0:T(512)}, f32[384]{0:T(512)S(1)}, u32[]{:S(2)}) copy-start(f32[384]{0:T(512)S(1)} %get-tuple-element.165) | copy-start | bytes 4612
  178.7 20.5 %copy-start.69 = (f32[384]{0:T(512)}, f32[384]{0:T(512)S(1)}, u32[]{:S(2)}) copy-start(f32[384]{0:T(512)S(1)} %get-tuple-element.164) | copy-start | bytes 4612
  178.7 20.5 %copy-start.71 = (f32[384]{0:T(512)}, f32[384]{0:T(512)S(1)}, u32[]{:S(2)}) copy-start(f32[384]{0:T(512)S(1)} %get-tuple-element.166) | copy-start | bytes 4612
  178.7 20.5 %copy-start.73 = (f32[384]{0:T(512)}, f32[384]{0:T(512)S(1)}, u32[]{:S(2)}) copy-start(f32[384]{0:T(512)S(1)} %get-tuple-element.163) | copy-start | bytes 4612
  178.9 19.7 %copy-start.94 = (f32[6]{0:T(128)}, f32[6]{0:T(128)S(1)}, u32[]{:S(2)}) copy-start(f32[6]{0:T(128)S(1)} %fusion.82) | copy-start | bytes 76
  179.2 28.6 %copy-start.79 = (f32[64]{0:T(128)}, f32[64]{0:T(128)S(1)}, u32[]{:S(2)}) copy-start(f32[64]{0:T(128)S(1)} %get-tuple-element.230) | copy-start | bytes 772
  179.2 28.6 %copy-start.81 = (f32[64]{0:T(128)}, f32[64]{0:T(128)S(1)}, u32[]{:S(2)}) copy-start(f32[64]{0:T(128)S(1)} %get-tuple-element.231) | copy-start | bytes 772
  179.2 28.7 %copy-start.83 = (f32[64]{0:T(128)}, f32[64]{0:T(128)S(1)}, u32[]{:S(2)}) copy-start(f32[64]{0:T(128)S(1)} %get-tuple-element.232) | copy-start | bytes 772
  179.2 28.6 %copy-start.85 = (f32[64]{0:T(128)}, f32[64]{0:T(128)S(1)}, u32[]{:S(2)}) copy-start(f32[64]{0:T(128)S(1)} %get-tuple-element.233) | copy-start | bytes 772
  179.4 269.8 %copy-start.55 = (pred[1024]{0:T(1024)(128)(4,1)}, pred[1024]{0:T(1024)(128)(4,1)S(1)}, u32[]{:S(2)}) copy-start(pred[1024]{0:T(1024)(128)(4,1)S(1)} %get-tuple-element.234) | copy-start | bytes 3076
  179.4 270.4 %copy-start.57 = (pred[1024]{0:T(1024)(128)(4,1)}, pred[1024]{0:T(1024)(128)(4,1)S(1)}, u32[]{:S(2)}) copy-start(pred[1024]{0:T(1024)(128)(4,1)S(1)} %get-tuple-element.235) | copy-start | bytes 3076
  179.4 271.0 %copy-start.59 = (pred[1024]{0:T(1024)(128)(4,1)}, pred[1024]{0:T(1024)(128)(4,1)S(1)}, u32[]{:S(2)}) copy-start(pred[1024]{0:T(1024)(128)(4,1)S(1)} %get-tuple-element.236) | copy-start | bytes 3076
  198.7 28.7 %copy-start.63 = (f32[8,6,128]{2,1,0:T(8,128)}, f32[8,6,128]{2,1,0:T(8,128)S(1)}, u32[]{:S(2)}) copy-start(f32[8,6,128]{2,1,0:T(8,128)S(1)} %copy.235) | copy-start | bytes 73732
  203.7 38.7 %copy-start.13 = (f32[1024,384]{1,0:T(8,128)}, f32[1024,384]{1,0:T(8,128)S(1)}, u32[]{:S(2)}) copy-start(f32[1024,384]{1,0:T(8,128)S(1)} %get-tuple-element.186) | copy-start | bytes 4718596
  207.8 19.6 %copy-start.39 = (bf16[48,8,8,128]{3,2,1,0:T(8,128)(2,1)}, bf16[48,8,8,128]{3,2,1,0:T(8,128)(2,1)S(1)}, u32[]{:S(2)}) copy-start(bf16[48,8,8,128]{3,2,1,0:T(8,128)(2,1)S(1)} %copy.283) | copy-start | bytes 2359300
  211.6 15.7 %copy-start.50 = (pred[8,128,128]{2,1,0:T(8,128)(4,1)S(1)}, pred[8,128,128]{2,1,0:T(8,128)(4,1)}, u32[]{:S(2)}) copy-start(pred[8,128,128]{2,1,0:T(8,128)(4,1)} %copy.231) | copy-start | bytes 393220
  340.6 210.1 %reduce-scatter.7.cloned.1.call-start = ((), (), s32[]{:S(2)}) async-start(), calls=%async_computation.15 | async-start | bytes 2621440 | tf_op jit(solution)/shard_map/reduce_scatter | solution.py:776
  355.5 87.7 %copy-start.38 = (bf16[1024,384]{1,0:T(8,128)(2,1)S(1)}, bf16[1024,384]{1,0:T(8,128)(2,1)}, u32[]{:S(2)}) copy-start(bf16[1024,384]{1,0:T(8,128)(2,1)} %multiply_convert_fusion.3) | copy-start | bytes 2359300
  355.5 87.7 %copy-start.101 = (bf16[8,128,128]{2,1,0:T(8,128)(2,1)S(1)}, bf16[8,128,128]{2,1,0:T(8,128)(2,1)}, u32[]{:S(2)}) copy-start(bf16[8,128,128]{2,1,0:T(8,128)(2,1)} %convolution_convert_fusion.9) | copy-start | bytes 786436
  449.1 205.9 %reduce-scatter.9.cloned.1.call-start = ((), (), s32[]{:S(2)}) async-start(), calls=%async_computation.16 | async-start | bytes 5242880 | tf_op jit(solution)/shard_map/reduce_scatter | solution.py:776
  460.5 325.5 %reduce-scatter.5.cloned.1.call-start = ((), (), s32[]{:S(2)}) async-start(), calls=%async_computation.14 | async-start | bytes 6553600 | tf_op jit(solution)/shard_map/reduce_scatter | solution.py:776
  484.8 16.2 %copy-start.30 = (bf16[1024,32]{1,0:T(8,128)(2,1)S(1)}, bf16[1024,32]{1,0:T(8,128)(2,1)}, u32[]{:S(2)}) copy-start(bf16[1024,32]{1,0:T(8,128)(2,1)} %copy-done.29) | copy-start | bytes 196612
  484.8 16.5 %copy-start.28 = (bf16[1024,32]{1,0:T(8,128)(2,1)S(1)}, bf16[1024,32]{1,0:T(8,128)(2,1)}, u32[]{:S(2)}) copy-start(bf16[1024,32]{1,0:T(8,128)(2,1)} %copy-done.27) | copy-start | bytes 196612
  490.1 14.2 %copy-start.61 = (f32[8,6,128]{2,1,0:T(8,128)S(1)}, f32[8,6,128]{2,1,0:T(8,128)}, u32[]{:S(2)}) copy-start(f32[8,6,128]{2,1,0:T(8,128)} %get-tuple-element.147) | copy-start | bytes 73732
  490.1 14.2 %copy-start.62 = (f32[8,6,128]{2,1,0:T(8,128)S(1)}, f32[8,6,128]{2,1,0:T(8,128)}, u32[]{:S(2)}) copy-start(f32[8,6,128]{2,1,0:T(8,128)} %get-tuple-element.148) | copy-start | bytes 73732
  490.1 14.2 %copy-start.54 = (f32[8,128,6]{1,0,2:T(8,128)S(1)}, f32[8,128,6]{1,0,2:T(8,128)}, u32[]{:S(2)}) copy-start(f32[8,128,6]{1,0,2:T(8,128)} %copy-done.53) | copy-start | bytes 73732
  490.1 14.2 %copy-start.93 = (f32[6]{0:T(128)S(1)}, f32[6]{0:T(128)}, u32[]{:S(2)}) copy-start(f32[6]{0:T(128)} %copy-done.92) | copy-start | bytes 76
  490.1 14.2 %copy-start.95 = (f32[6]{0:T(128)S(1)}, f32[6]{0:T(128)}, u32[]{:S(2)}) copy-start(f32[6]{0:T(128)} %copy-done.94) | copy-start | bytes 76
  490.1 16.1 %copy-start.88 = (f32[8,128]{1,0:T(8,128)S(1)}, f32[8,128]{1,0:T(8,128)}, u32[]{:S(2)}) copy-start(f32[8,128]{1,0:T(8,128)} %copy-done.87) | copy-start | bytes 12292
  546.3 16.6 %copy-start.26 = (bf16[1024,1280]{1,0:T(8,128)(2,1)S(1)}, bf16[1024,1280]{1,0:T(8,128)(2,1)}, u32[]{:S(2)}) copy-start(bf16[1024,1280]{1,0:T(8,128)(2,1)} %concatenate.124) | copy-start | bytes 7864324
  546.4 12.4 %all-to-all-start.6 = ((bf16[4,128,512]{2,1,0:T(8,128)(2,1)}), bf16[4,128,512]{2,1,0:T(8,128)(2,1)}, u32[]{:S(2)}, u32[]{:S(2)}) async-start(bf16[4,128,512]{2,1,0:T(8,128)(2,1)} %bitcast.367), calls=%async_computation.10 | async-start | bytes 1048576 | tf_op jit(solution)/shard_map/all_to_all | solution.py:779
  558.8 96.2 %all-to-all-start.4 = ((bf16[4,128,512]{2,1,0:T(8,128)(2,1)}), bf16[4,128,512]{2,1,0:T(8,128)(2,1)}, u32[]{:S(2)}, u32[]{:S(2)}) async-start(bf16[4,128,512]{2,1,0:T(8,128)(2,1)} %bitcast.366), calls=%async_computation.6 | async-start | bytes 1048576 | tf_op jit(solution)/shard_map/all_to_all | solution.py:779
  562.9 9.7 %copy-start.78 = (f32[384]{0:T(512)S(1)}, f32[384]{0:T(512)}, u32[]{:S(2)}) copy-start(f32[384]{0:T(512)} %get-tuple-element.179) | copy-start | bytes 4612
  654.1 70.4 %copy-start.98 = (f32[24]{0:T(128)S(1)}, f32[24]{0:T(128)}, u32[]{:S(2)}) copy-start(f32[24]{0:T(128)} %param.39) | copy-start | bytes 292
  654.9 133.5 %all-to-all-start.5 = ((bf16[4,128,1024]{2,1,0:T(8,128)(2,1)}), bf16[4,128,1024]{2,1,0:T(8,128)(2,1)}, u32[]{:S(2)}, u32[]{:S(2)}) async-start(bf16[4,128,1024]{2,1,0:T(8,128)(2,1)} %bitcast.351), calls=%async_computation.8 | async-start | bytes 2097152 | tf_op jit(solution)/shard_map/all_to_all | solution.py:779
  788.4 16.6 %all-to-all-start.3 = ((bf16[4,128,1280]{1,2,0:T(8,128)(2,1)}), bf16[4,128,1280]{1,2,0:T(8,128)(2,1)}, u32[]{:S(2)}, u32[]{:S(2)}) async-start(bf16[4,128,1280]{1,2,0:T(8,128)(2,1)} %copy.257), calls=%async_computation.4 | async-start | bytes 2621440 | tf_op jit(solution)/shard_map/all_to_all | solution.py:779
  807.1 25.2 %collective-permute-start = (bf16[4,128,64]{1,2,0:T(8,128)(2,1)S(1)}, bf16[4,128,64]{1,2,0:T(8,128)(2,1)S(1)}, u32[]{:S(2)}, u32[]{:S(2)}) collective-permute-start(bf16[4,128,64]{1,2,0:T(8,128)(2,1)S(1)} %slice.340), channel_id=1, source_target_pairs={{0,1},{1,0},{2,3},{3,2},{4,5},{5,4},{6,7},{7,6},{8,9},{9,8},{10,11... | collective-permute-start | bytes 196616 | tf_op jit(solution)/shard_map/ppermute | solution.py:967
  (71 other events, 196.0 us)
Sparse Core Ops, SparseCore 0:
  36.5 123.0 all-gather.3
  161.7 44.1 all-gather.7
  207.5 114.2 all-gather.5
  340.8 47.4 reduce-scatter.10
  449.2 46.0 reduce-scatter.6
  497.5 76.2 reduce-scatter.8
  576.2 111.1 reduce-scatter.4

commit v2 on v1

v2 whole, which is shorter than its diff:
```python
from functools import partial

import jax
import jax.numpy as jnp
from jax import lax
from jax.experimental import pallas as pl
from jax.experimental.pallas import tpu as pltpu
from jax.sharding import PartitionSpec as P

HD = 128
TP = 4
GROUP = 2 * TP
CHUNK = 16
EPS = 1e-05
NEG_LARGE = -1e30
ROPE_BASE = 100000000000.0
MESH = pl.DeviceIdType.MESH
HIGH = lax.Precision.HIGHEST
VMEM = pltpu.VMEM
ANY = pl.ANY


def matmul(first_op, second_op):
    return jnp.dot(first_op, second_op, preferred_element_type=jnp.float32)


def matmul_trans(first_op, second_op):
    return lax.dot_general(
        first_op, second_op, (((1,), (1,)), ((), ())), preferred_element_type=jnp.float32
    )


def matmul_left(first_op, second_op):
    return lax.dot_general(
        first_op, second_op, (((0,), (0,)), ((), ())), preferred_element_type=jnp.float32
    )


TP_BITS = (0, 1)


def data_bits(n_row):
    return [b for b in reversed(range(n_row.bit_length() - 1)) if b not in TP_BITS]


def bit(row, b):
    return lax.rem(lax.div(row, 1 << b), 2)


def flip(row, b):
    return row + (1 << b) * (1 - 2 * bit(row, b))


def member(row):
    return bit(row, TP_BITS[0]) + 2 * bit(row, TP_BITS[1])


def partner(row, m):
    if m & 1:
        row = flip(row, TP_BITS[0])
    if m & 2:
        row = flip(row, TP_BITS[1])
    return row


def turned_row(row, mask):
    for b in range(mask.bit_length()):
        row = flip(row, b) if mask >> b & 1 else row
    return row


def group_of(row, n_row):
    index = 0
    for b in data_bits(n_row):
        index = index * 2 + bit(row, b)
    return index


def spot(row, n_row):
    return group_of(row, n_row) * TP + member(row)


def flips(n_row, mask):
    return [(row, row ^ mask) for row in range(n_row)]


def mask_of(m):
    return (m & 1) * (1 << TP_BITS[0]) + (m // 2) * (1 << TP_BITS[1])


def place():
    r = lax.axis_index("row")
    c = lax.axis_index("col")
    return r, c, member(r)


def block_of(m):
    return member(partner(lax.axis_index("row"), m)) * 2


def params(number, megabytes):
    return pltpu.CompilerParams(
        collective_id=number, has_side_effects=True, vmem_limit_bytes=megabytes << 20
    )


def cost(microseconds):
    return pl.CostEstimate(flops=0, transcendentals=0, bytes_accessed=microseconds * 3_400_000)


def remote(src, dst, send, recv, row, col):
    return pltpu.make_async_remote_copy(
        src_ref=src, dst_ref=dst, send_sem=send, recv_sem=recv, device_id=(row, col), device_id_type=MESH
    )


def greet_group(cross=False):
    r, c, t = place()
    barrier = pltpu.get_barrier_semaphore()
    pl.semaphore_signal(barrier, inc=1, device_id=(r, 1 - c), device_id_type=MESH)
    count = 1
    for m in (1, 2, 3):
        pl.semaphore_signal(barrier, inc=1, device_id=(partner(r, m), c), device_id_type=MESH)
        count += 1
        if cross:
            pl.semaphore_signal(
                barrier, inc=1, device_id=(partner(r, m), 1 - c), device_id_type=MESH
            )
            count += 1
    pl.semaphore_wait(barrier, count)


def gather_start(src, out, send, recv, here):
    r, c, t = place()
    mine = out.at[t * 2 + c]
    local = pltpu.make_async_copy(src, mine, here)
    peers = [
        remote(src, mine, send.at[m], recv.at[m], partner(r, m), c) for m in (1, 2, 3)
    ]
    sibling = remote(src, mine, send.at[0], recv.at[0], r, 1 - c)
    for copy in (peers[2], peers[0], peers[1], sibling, local):
        copy.start()
    return peers, sibling, local


def gather_finish(started, out, send, recv):
    r, c, t = place()
    peers, sibling, local = started
    forwards = []
    for m in (1, 2, 3):
        peers[m - 1].wait_recv()
        block = out.at[block_of(m) + c]
        forward = remote(block, block, send.at[3 + m], recv.at[3 + m], r, 1 - c)
        forward.start()
        forwards.append(forward)
    local.wait()
    sibling.wait()
    for copy in peers:
        copy.wait_send()
    for copy in forwards:
        copy.wait()


ROWS = 16


def by_rows(count, body):
    def step(i, carry):
        body(pl.ds(pl.multiple_of(i * ROWS, ROWS), ROWS))
        return carry

    lax.fori_loop(0, count // ROWS, step, 0)


def scatter_sum(parts, near, out2, far, s1, r1, s2, r2, total):
    r, c, t = place()
    order = (3, 1, 2, 0)
    first = {}
    for m in order:
        first[m] = remote(
            parts.at[block_of(m) + 1 - c], near.at[m], s1.at[m], r1.at[m], r, 1 - c
        )
        first[m].start()
    second = {}
    for m in order[:3]:
        first[m].wait_recv()
        block = block_of(m) + c

        def add(rows, m=m, block=block):
            out2[m - 1, rows, :] = (
                parts[block, rows, :].astype(jnp.float32) + near[m, rows, :].astype(jnp.float32)
            ).astype(jnp.bfloat16)

        by_rows(total.shape[0], add)
        second[m] = remote(
            out2.at[m - 1], far.at[m - 1], s2.at[m - 1], r2.at[m - 1], partner(r, m), c
        )
        second[m].start()
    first[0].wait_recv()
    own = t * 2 + c
    for m in (1, 2, 3):
        second[m].wait_recv()

    def fold(rows):
        total[rows, :] = (
            parts[own, rows, :].astype(jnp.float32)
            + near[0, rows, :].astype(jnp.float32)
            + far[0, rows, :].astype(jnp.float32)
            + far[1, rows, :].astype(jnp.float32)
            + far[2, rows, :].astype(jnp.float32)
        )

    by_rows(total.shape[0], fold)
    for m in order:
        first[m].wait_send()
    for m in (1, 2, 3):
        second[m].wait_send()


def scatter_scratch(slots, width):
    return [
        VMEM((TP, slots, width), jnp.bfloat16),
        VMEM((TP - 1, slots, width), jnp.bfloat16),
        VMEM((TP - 1, slots, width), jnp.bfloat16),
        pltpu.SemaphoreType.DMA((TP,)),
        pltpu.SemaphoreType.DMA((TP,)),
        pltpu.SemaphoreType.DMA((TP - 1,)),
        pltpu.SemaphoreType.DMA((TP - 1,)),
    ]


def gather_scratch():
    return [
        pltpu.SemaphoreType.DMA((7,)),
        pltpu.SemaphoreType.DMA((7,)),
        pltpu.SemaphoreType.DMA,
    ]


def strips(refs, shared, size):
    found, at = [], 0
    for ref, whole in zip(refs, shared):
        count = ref.shape[1] if whole else ref.shape[1] // TP
        found.append((ref, whole, count, at))
        at += count
    return found


def strip_views(refs, shared, owner, piece):
    for ref, whole, count, at in strips(refs, shared, piece.shape[1]):
        cols = slice(None) if whole else pl.ds(pl.multiple_of(owner * count, 128), count)
        yield ref.at[:, cols], piece.at[:, at : at + count]


def cut_start(refs, shared, place_of, send, recv, here):
    r, c, t = place()
    for source, target in strip_views(refs, shared, t, place_of()):
        pltpu.make_async_copy(source, target, here).start()
    for m in (3, 1, 2):
        other = partner(r, m)
        for source, target in strip_views(refs, shared, member(other), place_of()):
            remote(source, target, send.at[m], recv.at[m], other, c).start()


def piece_done(piece, sem):
    pltpu.make_async_copy(piece, piece, sem).wait()


def cut_finish(place_of, send, recv, here):
    piece_done(place_of(), here)
    for m in (3, 1, 2):
        piece_done(place_of(), send.at[m])
        piece_done(place_of(), recv.at[m])


def weight_copy(whole, mask, b, send, recv):
    r, c, t = place()
    n_row = lax.axis_size("row")
    at = whole.at[spot(turned_row(r, mask), n_row)]
    lands = mask | 1 << b
    return remote(at, at, send.at[lands], recv.at[lands], flip(r, b), c)


def weight_forward(masks, whole, send, recv):
    r, c, t = place()
    n_row = lax.axis_size("row")
    bits = data_bits(n_row)
    copies = []
    for mask in masks:
        at = whole.at[spot(turned_row(r, mask), n_row)]
        if mask:
            piece_done(at, recv.at[mask])
        last = max([-1] + [i for i, b in enumerate(bits) if mask >> b & 1])
        for b in bits[last + 1 :]:
            copies.append(weight_copy(whole, mask, b, send, recv))
            copies[-1].start()
    return copies


def weight_masks(n_row):
    held = [mask_of(m) for m in range(TP)]
    rounds = [held[1:]]
    for b in data_bits(n_row):
        rounds.append([mask | 1 << b for mask in held])
        held = held + rounds[-1]
    return rounds


def place_kernel(masks, n_row, *refs):
    slabs, whole, sems = refs[: len(masks)], refs[-2], refs[-1]
    r, c, t = place()
    copies = []
    for i, mask in enumerate(masks):
        at = whole.at[group_of(turned_row(r, mask), n_row)]
        copies.append(pltpu.make_async_copy(slabs[i], at, sems.at[i]))
        copies[-1].start()
    for copy in copies:
        copy.wait()


def place_slabs(masks, slabs, n_row):
    return pl.pallas_call(
        partial(place_kernel, masks, n_row),
        name="place",
        out_shape=jax.ShapeDtypeStruct((len(masks),) + slabs[0].shape, slabs[0].dtype),
        in_specs=[pl.BlockSpec(memory_space=ANY)] * len(masks),
        out_specs=pl.BlockSpec(memory_space=ANY),
        scratch_shapes=[pltpu.SemaphoreType.DMA((len(masks),))],
        compiler_params=pltpu.CompilerParams(vmem_limit_bytes=4 << 20),
        cost_estimate=cost(4),
    )(*slabs)


def exchange_rows(buf, land, send, recv):
    r, c, t = place()
    n_row = lax.axis_size("row")

    def copy(other):
        return remote(
            buf.at[other], land.at[r], send.at[other], recv.at[r], other, c
        )

    def start(off, carry):
        copy(lax.rem(r + off, n_row)).start()
        return carry

    lax.fori_loop(1, n_row, start, 0)


def finish_rows(buf, land, send, recv):
    r, c, t = place()
    n_row = lax.axis_size("row")

    def finish(off, carry):
        other = lax.rem(r + off, n_row)
        copy = remote(buf.at[other], land.at[other], send.at[other], recv.at[other], other, c)
        copy.wait_send()
        copy.wait_recv()
        return carry

    lax.fori_loop(1, n_row, finish, 0)


def greet_rows():
    r, c, t = place()
    n_row = lax.axis_size("row")
    barrier = pltpu.get_barrier_semaphore()

    def greet(off, carry):
        pl.semaphore_signal(
            barrier, inc=1, device_id=(lax.rem(r + off, n_row), c), device_id_type=MESH
        )
        return carry

    lax.fori_loop(1, n_row, greet, 0)
    pl.semaphore_signal(barrier, inc=1, device_id=(r, 1 - c), device_id_type=MESH)
    pl.semaphore_wait(barrier, n_row)


COLS = 512


def permute_out(choice, buf, first, second, slots):
    n_row = buf.shape[0]

    def column(i, carry):
        cols = pl.ds(pl.multiple_of(i * COLS, COLS), COLS)
        picked = matmul(choice[:, :slots], first[:, cols]) + matmul(choice[:, slots:], second[:, cols])
        buf[:, :, cols] = picked.astype(jnp.bfloat16).reshape(n_row, CHUNK, COLS)
        return carry

    lax.fori_loop(0, buf.shape[2] // COLS, column, 0)


def permute_in(choice, land, first, second, slots):
    n_row = land.shape[0]

    def column(i, carry):
        cols = pl.ds(pl.multiple_of(i * COLS, COLS), COLS)
        got = land[:, :, cols].reshape(n_row * CHUNK, COLS)
        first[:, cols] = matmul_left(choice[:, :slots], got).astype(jnp.bfloat16)
        second[:, cols] = matmul_left(choice[:, slots:], got).astype(jnp.bfloat16)
        return carry

    lax.fori_loop(0, land.shape[2] // COLS, column, 0)


def deal_kernel(
    meta, tokens, cotangent, gain, *refs
):
    in_refs, ff_refs, refs = refs[:8], refs[8:11], refs[11:]
    meta_all, give, take, x_out, gy_out, normed_all, gy_all, whole, slab_ff = refs[:9]
    x_mine, g_mine, buf, land, normed = refs[9:14]
    load, msend, mrecv, csend, crecv, nsend, nrecv, nhere, gsend, grecv, ghere = refs[14:25]
    wsend, wrecv, wcut, whole_here, fsend, frecv, fhere = refs[25:]
    r, c, t = place()
    n_row = lax.axis_size("row")
    slots = x_mine.shape[0]
    per_peer = slots // n_row
    loads = [
        pltpu.make_async_copy(tokens.at[c], x_mine, load.at[0]),
        pltpu.make_async_copy(cotangent.at[c], g_mine, load.at[1]),
    ]
    for copy in loads:
        copy.start()
    greet_rows()
    rounds = weight_masks(n_row)
    in_shared = [False, False, False, True, True, False, False, False]

    def in_place():
        return whole.at[spot(r, n_row)]

    def meta_copy(other, slot):
        return remote(meta, meta_all.at[slot], msend.at[other], mrecv.at[slot], other, c)

    def start(off, carry):
        meta_copy(lax.rem(r + off, n_row), r).start()
        return carry

    lax.fori_loop(1, n_row, start, 0)
    meta_all[r] = meta[...]

    def finish(off, carry):
        other = lax.rem(r + off, n_row)
        copy = meta_copy(other, other)
        copy.wait_send()
        copy.wait_recv()
        return carry

    lax.fori_loop(1, n_row, finish, 0)
    for source, target in strip_views(in_refs, in_shared, t, in_place()):
        pltpu.make_async_copy(source, target, whole_here).start()
    for m in (3, 1, 2):
        other = partner(r, m)
        for source, target in strip_views(in_refs, in_shared, member(other), in_place()):
            remote(source, target, wcut.at[m], wrecv.at[mask_of(m)], other, c).start()
    piece_done(in_place(), whole_here)
    forwards = weight_forward([0], whole, wsend, wrecv)

    shift = slots.bit_length() - 1
    row_no = lax.broadcasted_iota(jnp.int32, (CHUNK, slots), 0)
    wanted = jnp.where(row_no < per_peer, row_no, row_no - per_peer).astype(jnp.float32)
    early = row_no < per_peer
    late = (row_no >= per_peer) & (row_no < 2 * per_peer)
    tri = (
        lax.broadcasted_iota(jnp.int32, (slots, slots), 0)
        < lax.broadcasted_iota(jnp.int32, (slots, slots), 1)
    ).astype(jnp.float32).astype(jnp.bfloat16)
    places = lax.broadcasted_iota(jnp.int32, (slots, slots), 0)

    def order_of(block):
        picked = jnp.where(c == 0, block[0:1, :], block[1:2, :])
        return lax.shift_right_logical(picked, shift), picked - lax.shift_left(
            lax.shift_right_logical(picked, shift), shift
        )

    own_source, own_local = order_of(meta[...])

    def select(mask):
        wide = jnp.broadcast_to(mask.astype(jnp.float32), (CHUNK, slots)).astype(jnp.bfloat16)
        rank = matmul(wide, tri)
        return jnp.where(
            (rank == wanted) & (wide.astype(jnp.float32) > 0.5), 1.0, 0.0
        )

    def build(d, carry):
        rows = pl.ds(pl.multiple_of(d * CHUNK, CHUNK), CHUNK)
        source, local = order_of(meta_all[d])
        chosen = select(source == r).astype(jnp.bfloat16)
        at_home = (places == local).astype(jnp.float32).astype(jnp.bfloat16)
        picks = matmul_trans(chosen, at_home)
        give[rows, :slots] = jnp.where(early, picks, 0.0).astype(jnp.bfloat16)
        give[rows, slots:] = jnp.where(late, picks, 0.0).astype(jnp.bfloat16)
        kept = select(own_source == d)
        take[rows, :slots] = jnp.where(early, kept, 0.0).astype(jnp.bfloat16)
        take[rows, slots:] = jnp.where(late, kept, 0.0).astype(jnp.bfloat16)
        return carry

    lax.fori_loop(0, n_row, build, 0)
    for copy in loads:
        copy.wait()
    permute_out(give, buf, x_mine, g_mine, slots)
    exchange_rows(buf, land, csend, crecv)
    land[r] = buf[r]
    forwards = forwards + weight_forward(rounds[0], whole, wsend, wrecv)
    finish_rows(buf, land, csend, crecv)
    permute_in(take, land, x_out, gy_out, slots)

    def norm(rows):
        values = x_out[rows, :].astype(jnp.float32)
        scale = lax.rsqrt(jnp.mean(values * values, axis=-1, keepdims=True) + EPS)
        normed[rows, :] = (values * scale * gain[...]).astype(jnp.bfloat16)

    by_rows(slots, norm)
    first = gather_start(normed, normed_all, nsend, nrecv, nhere)
    cut_start(ff_refs, [False] * 3, lambda: slab_ff.at[t], fsend, frecv, fhere)
    second = gather_start(gy_out, gy_all, gsend, grecv, ghere)
    for masks in rounds[1:]:
        forwards = forwards + weight_forward(masks, whole, wsend, wrecv)
    gather_finish(first, normed_all, nsend, nrecv)
    gather_finish(second, gy_all, gsend, grecv)
    for copy in forwards:
        copy.wait_send()
    for m in (1, 2, 3):
        piece_done(in_place(), wcut.at[m])
    cut_finish(lambda: slab_ff.at[t], fsend, frecv, fhere)


def deal(meta, tokens, cotangent, gain, in_weights, ff_weights, n_row):
    slots, width = tokens.shape[1:]
    bf = jnp.bfloat16
    rows = in_weights[0].shape[0]
    in_cols = sum(
        array.shape[1] // (1 if i in (3, 4) else TP) for i, array in enumerate(in_weights)
    )
    ff_cols = sum(array.shape[1] for array in ff_weights) // TP
    vm, hb = pl.BlockSpec(memory_space=VMEM), pl.BlockSpec(memory_space=ANY)
    dma = pltpu.SemaphoreType.DMA
    return pl.pallas_call(
        deal_kernel,
        name="deal",
        out_shape=(
            jax.ShapeDtypeStruct((n_row, 8, 128), jnp.int32),
            jax.ShapeDtypeStruct((n_row * CHUNK, 2 * slots), bf),
            jax.ShapeDtypeStruct((n_row * CHUNK, 2 * slots), bf),
            jax.ShapeDtypeStruct((slots, width), bf),
            jax.ShapeDtypeStruct((slots, width), bf),
            jax.ShapeDtypeStruct((GROUP, slots, width), bf),
            jax.ShapeDtypeStruct((GROUP, slots, width), bf),
            jax.ShapeDtypeStruct((n_row, rows, in_cols), bf),
            jax.ShapeDtypeStruct((TP, rows, ff_cols), bf),
        ),
        in_specs=[vm, hb, hb, vm] + [hb] * 11,
        out_specs=(vm,) * 5 + (hb,) * 4,
        scratch_shapes=[
            VMEM((slots, width), bf),
            VMEM((slots, width), bf),
            VMEM((n_row, CHUNK, width), bf),
            VMEM((n_row, CHUNK, width), bf),
            VMEM((slots, width), bf),
            dma((2,)),
            dma((n_row,)),
            dma((n_row,)),
            dma((n_row,)),
            dma((n_row,)),
        ]
        + gather_scratch()
        + gather_scratch()
        + [dma((n_row,)), dma((n_row,)), dma((TP,)), dma]
        + [dma((TP,)), dma((TP,)), dma],
        compiler_params=params(0, 40),
        cost_estimate=cost(100),
    )(meta, tokens, cotangent, gain, *in_weights, *ff_weights)


def middle_kernel(parts, x, gain, mid, normed_all, near, out2, far, s1, r1, s2, r2, normed, nsend, nrecv, nhere):
    greet_group()
    scatter_sum(parts, near, out2, far, s1, r1, s2, r2, mid)

    def norm(rows):
        values = x[rows, :].astype(jnp.float32) + mid[rows, :]
        mid[rows, :] = values
        scale = lax.rsqrt(jnp.mean(values * values, axis=-1, keepdims=True) + EPS)
        normed[rows, :] = (values * scale * gain[...]).astype(jnp.bfloat16)

    by_rows(mid.shape[0], norm)
    started = gather_start(normed, normed_all, nsend, nrecv, nhere)
    gather_finish(started, normed_all, nsend, nrecv)


def middle(parts, x, gain):
    slots, width = x.shape
    return pl.pallas_call(
        middle_kernel,
        name="middle",
        out_shape=(
            jax.ShapeDtypeStruct((slots, width), jnp.float32),
            jax.ShapeDtypeStruct((GROUP, slots, width), jnp.bfloat16),
        ),
        in_specs=[pl.BlockSpec(memory_space=VMEM)] * 3,
        out_specs=(pl.BlockSpec(memory_space=VMEM), pl.BlockSpec(memory_space=ANY)),
        scratch_shapes=scatter_scratch(slots, width)
        + [VMEM((slots, width), jnp.bfloat16)]
        + gather_scratch(),
        compiler_params=params(1, 40),
        cost_estimate=cost(60),
    )(parts, x, gain)


def norm_back(values, gain, grad):
    inverse = lax.rsqrt(jnp.mean(values * values, axis=-1, keepdims=True) + EPS)
    scaled = grad * gain
    back = inverse * scaled - values * (
        inverse * inverse * inverse * jnp.mean(values * scaled, axis=-1, keepdims=True)
    )
    return back, jnp.sum(grad * values * inverse, axis=0, keepdims=True)


def turn_kernel(
    parts, mid, gy, gain, d_mid, d_gain, branch_all,
    near, out2, far, s1, r1, s2, r2, branch, nsend, nrecv, nhere,
):
    greet_group()
    scatter_sum(parts, near, out2, far, s1, r1, s2, r2, d_mid)
    d_gain[...] = jnp.zeros_like(d_gain)

    def back(rows):
        values = mid[rows, :]
        grad, gain_part = norm_back(values, gain[...], d_mid[rows, :])
        grad = gy[rows, :].astype(jnp.float32) + grad
        d_mid[rows, :] = grad
        branch[rows, :] = grad.astype(jnp.bfloat16)
        d_gain[...] += gain_part

    by_rows(mid.shape[0], back)
    started = gather_start(branch, branch_all, nsend, nrecv, nhere)
    gather_finish(started, branch_all, nsend, nrecv)


def turn(parts, mid, gy, gain):
    slots, width = mid.shape
    return pl.pallas_call(
        turn_kernel,
        name="turn",
        out_shape=(
            jax.ShapeDtypeStruct((slots, width), jnp.float32),
            jax.ShapeDtypeStruct((1, width), jnp.float32),
            jax.ShapeDtypeStruct((GROUP, slots, width), jnp.bfloat16),
        ),
        in_specs=[pl.BlockSpec(memory_space=VMEM)] * 4,
        out_specs=(pl.BlockSpec(memory_space=VMEM),) * 2 + (pl.BlockSpec(memory_space=ANY),),
        scratch_shapes=scatter_scratch(slots, width)
        + [VMEM((slots, width), jnp.bfloat16)]
        + gather_scratch(),
        compiler_params=params(2, 48),
        cost_estimate=cost(60),
    )(parts, mid, gy, gain)


def home_kernel(
    parts, x, d_mid, result, gain, give, take, small, output, gradient, small_all,
    near, out2, far, s1, r1, s2, r2, total, first, second, buf, land, csend, crecv, here, osend, orecv,
    d_gain, stages, stage_land, tsend, trecv, gsend, grecv, ghere,
):
    r, c, t = place()
    slots, width = x.shape
    bits = data_bits(lax.axis_size("row"))
    greet_rows()
    scatter_sum(parts, near, out2, far, s1, r1, s2, r2, total)
    d_gain[...] = jnp.zeros_like(d_gain)

    def back(rows):
        values = x[rows, :].astype(jnp.float32)
        grad, gain_part = norm_back(values, gain[...], total[rows, :])
        second[rows, :] = (d_mid[rows, :] + grad).astype(jnp.bfloat16)
        first[rows, :] = result[rows, :].astype(jnp.bfloat16)
        d_gain[...] += gain_part

    by_rows(slots, back)
    head = small.shape[0]
    stages[0, :head, :] = small[...]
    for k in range(width // 128):
        stages[0, head + k : head + k + 1, :] = d_gain[:, k * 128 : (k + 1) * 128]

    def stage_copy(i):
        return remote(
            stages.at[i], stage_land.at[i], tsend.at[i], trecv.at[i], flip(r, bits[i]), c
        )

    stage_copy(0).start()
    permute_out(take, buf, first, second, slots)
    exchange_rows(buf, land, csend, crecv)
    land[r] = buf[r]
    for i in range(len(bits)):
        stage_copy(i).wait()
        stages[i + 1] = stages[i] + stage_land[i]
        if i + 1 < len(bits):
            stage_copy(i + 1).start()
    started = gather_start(stages.at[len(bits)], small_all, gsend, grecv, ghere)
    finish_rows(buf, land, csend, crecv)
    permute_in(give, land, first, second, slots)
    copies = []
    for i, (mine, out) in enumerate(((first, output), (second, gradient))):
        copies.append(pltpu.make_async_copy(mine, out.at[c], here.at[i]))
        copies.append(remote(mine, out.at[c], osend.at[i], orecv.at[i], r, 1 - c))
    for copy in copies:
        copy.start()
    gather_finish(started, small_all, gsend, grecv)
    for copy in copies:
        copy.wait()


def send_home(parts, x, d_mid, result, gain, give, take, small, n_row):
    slots, width = x.shape
    bf = jnp.bfloat16
    size = small.shape[0] + width // 128
    phases = len(data_bits(n_row))
    return pl.pallas_call(
        home_kernel,
        name="home",
        out_shape=(
            jax.ShapeDtypeStruct((2, slots, width), bf),
            jax.ShapeDtypeStruct((2, slots, width), bf),
            jax.ShapeDtypeStruct((GROUP, size, 128), jnp.float32),
        ),
        in_specs=[pl.BlockSpec(memory_space=VMEM)] * 8,
        out_specs=(pl.BlockSpec(memory_space=ANY),) * 3,
        scratch_shapes=scatter_scratch(slots, width)
        + [
            VMEM((slots, width), jnp.float32),
            VMEM((slots, width), bf),
            VMEM((slots, width), bf),
            VMEM((n_row, CHUNK, width), bf),
            VMEM((n_row, CHUNK, width), bf),
            pltpu.SemaphoreType.DMA((n_row,)),
            pltpu.SemaphoreType.DMA((n_row,)),
            pltpu.SemaphoreType.DMA((2,)),
            pltpu.SemaphoreType.DMA((2,)),
            pltpu.SemaphoreType.DMA((2,)),
            VMEM((1, width), jnp.float32),
            VMEM((phases + 1, size, 128), jnp.float32),
            VMEM((phases, size, 128), jnp.float32),
            pltpu.SemaphoreType.DMA((phases,)),
            pltpu.SemaphoreType.DMA((phases,)),
        ]
        + gather_scratch(),
        compiler_params=params(3, 48),
        cost_estimate=cost(75),
    )(parts, x, d_mid, result, gain, give, take, small)


def blocks_start(low, land, s1, r1):
    r, c, t = place()
    copies = []
    for m, f in CROSSED:
        col = 1 - c if f else c
        k = m * 2 + f
        copies.append(
            remote(low.at[block_of(m) + col], land.at[k], s1.at[k], r1.at[k], partner(r, m), col)
        )
        copies[-1].start()
    return copies


def blocks_turn(first, low, land, mine, total, s2, r2, here):
    r, c, t = place()
    own = t * 2 + c
    for copy in first:
        copy.wait_recv()
    summed = low[own].astype(jnp.float32)
    for m, f in CROSSED:
        summed = summed + land[m * 2 + f].astype(jnp.float32)
    mine[...] = summed.astype(jnp.bfloat16)
    copies = [pltpu.make_async_copy(mine, total.at[own], here)]
    for m, f in CROSSED:
        k = m * 2 + f
        copies.append(
            remote(mine, total.at[own], s2.at[k], r2.at[k], partner(r, m), 1 - c if f else c)
        )
    for copy in copies:
        copy.start()
    return copies


def blocks_finish(first, second):
    for copy in first:
        copy.wait_send()
    for copy in second:
        copy.wait()


CROSSED = [(m, f) for m in (3, 1, 2) for f in (0, 1)] + [(0, 1)]


def blocks_scratch(slots):
    dma = pltpu.SemaphoreType.DMA
    return [
        VMEM((GROUP, slots, slots), jnp.bfloat16),
        VMEM((GROUP, slots, slots), jnp.bfloat16),
        VMEM((slots, slots), jnp.bfloat16),
        dma((GROUP,)),
        dma((GROUP,)),
        dma((GROUP,)),
        dma((GROUP,)),
        dma,
    ]


def dot(first_op, second_op, first_dim, second_dim, precision=None):
    return lax.dot_general(
        first_op,
        second_op,
        (((first_dim,), (second_dim,)), ((), ())),
        precision=precision,
        preferred_element_type=jnp.float32,
    )


def block_rows(b, slots):
    return pl.ds(pl.multiple_of(b * slots, slots), slots)


def marks(lens, b, slots):
    row = lax.broadcasted_iota(jnp.int32, (slots, slots), 0)
    col = lax.broadcasted_iota(jnp.int32, (slots, slots), 1)
    row_segment, col_segment, within = jnp.zeros_like(row), jnp.zeros_like(row), row
    end = 0
    for k in range(lens.shape[1] - 1):
        end = end + lens[b, k]
        row_segment = row_segment + (row >= end).astype(jnp.int32)
        col_segment = col_segment + (col >= end).astype(jnp.int32)
        within = jnp.where(row >= end, row - end, within)
    return (row_segment == col_segment) & (row >= col), within


def conv_pre(values, within, weights):
    width = values.shape[1]
    shifted = [values]
    for k in range(1, 4):
        valid = within[:, :1] >= k
        shifted.append(jnp.where(valid, pltpu.roll(values, k, 0), 0.0))
    pre = weights[4:5, :]
    for k in range(4):
        pre = pre + weights[3 - k : 4 - k, :] * shifted[k]
    return pre, shifted


def conv_back(grad, pre, shifted, within, weights):
    slots = grad.shape[0]
    gate = jax.nn.sigmoid(pre)
    e = grad * gate * (1.0 + pre * (1.0 - gate))
    sums = [jnp.sum(e * shifted[3 - i], axis=0, keepdims=True) for i in range(4)]
    sums.append(jnp.sum(e, axis=0, keepdims=True))
    back = weights[3:4, :] * e
    for k in range(1, 4):
        valid = within[:, :1] >= k
        back = back + weights[3 - k : 4 - k, :] * pltpu.roll(jnp.where(valid, e, 0.0), slots - k, 0)
    return back, sums


def softplus(values):
    return jnp.maximum(values, 0.0) + jnp.log1p(jnp.exp(-jnp.abs(values)))


def steps_and_levels(mixed, side, low, count):
    slots, width = mixed.shape
    lane = lax.broadcasted_iota(jnp.int32, (slots, width), 1)
    inside = (lane >= low) & (lane < low + count)
    step = jnp.where(inside, softplus(mixed + side[5:6, :]), 0.0)
    rate = jnp.where(inside, -jnp.exp(side[6:7, :]), 0.0)
    row = lax.broadcasted_iota(jnp.int32, (slots, slots), 0)
    col = lax.broadcasted_iota(jnp.int32, (slots, slots), 1)
    tri = (row >= col).astype(jnp.float32)
    level = dot(tri, step * rate, 1, 0, HIGH)
    return step, rate, level, tri, inside


def halves(first, second):
    lane = lax.broadcasted_iota(jnp.int32, first.shape, 1)
    return jnp.where(lane < first.shape[1] // 2, first, second)


def state_parts(mixed, within, side, sh):
    pre, shifted = conv_pre(mixed, within, side)
    act = pre * jax.nn.sigmoid(pre)
    lane = lax.broadcasted_iota(jnp.int32, act.shape, 1)
    first = jnp.where(lane < sh, act, 0.0).astype(jnp.bfloat16)
    second = jnp.where(lane < sh, pltpu.roll(act, act.shape[1] - sh, 1), 0.0).astype(jnp.bfloat16)
    return first, second, pre, shifted


def turned_pair(values, waves):
    half = values.shape[1] // 2
    return values * waves[:, : 2 * half] + pltpu.roll(values, half, 1) * waves[:, 2 * half :]


def turned_back(values, waves):
    half = values.shape[1] // 2
    return values * waves[:, : 2 * half] - pltpu.roll(values, half, 1) * waves[:, 2 * half :]


def wave_rows(within, table):
    slots = within.shape[0]
    picks = (within == lax.broadcasted_iota(jnp.int32, (slots, slots), 1)).astype(jnp.float32)
    return dot(picks, table[...], 1, 0, HIGH)


def attend(projected, rows, at, lens, table, b, slots):
    allowed, within = marks(lens, b, slots)
    waves = wave_rows(within, table)
    query = turned_pair(projected[rows, at : at + HD], waves).astype(jnp.bfloat16)
    key = turned_pair(projected[rows, at + HD : at + 2 * HD], waves).astype(jnp.bfloat16)
    value = projected[rows, at + 2 * HD : at + 3 * HD].astype(jnp.bfloat16)
    scores = jnp.where(allowed, dot(query, key, 1, 1) * HD ** (-0.5), NEG_LARGE)
    exps = jnp.exp(scores - jnp.max(scores, axis=-1, keepdims=True))
    probs = exps / jnp.sum(exps, axis=-1, keepdims=True)
    return query, key, value, probs, waves


def each_block(first, last, body):
    def step(b, carry):
        body(b)
        return carry

    lax.fori_loop(first, last, step, 0)


def mixer_kernel(
    sh, ph, lens, projected, chan, side, table, branch, scanned, crossed,
    low, land, mine, s1, r1, s2, r2, here, conv,
):
    slots = crossed.shape[1]
    mh = chan.shape[1]
    heads_at = 2 * sh
    greet_group(cross=True)

    def before(b):
        rows = block_rows(b, slots)
        allowed, within = marks(lens, b, slots)
        pre, unused = conv_pre(projected[rows, mh : 2 * mh], within, chan)
        conv[rows, :] = pre * jax.nn.sigmoid(pre)
        mixed = projected[rows, 2 * mh + 3 * HD :]
        first, second, unused, unused = state_parts(mixed, within, side, sh)
        low[b] = dot(second, first, 1, 1).astype(jnp.bfloat16)

    def attention(b):
        rows = block_rows(b, slots)
        query, key, value, probs, waves = attend(projected, rows, 2 * mh, lens, table, b, slots)
        branch[rows, mh:] = dot(probs.astype(jnp.bfloat16), value, 1, 0).astype(jnp.bfloat16)

    def after(b):
        rows = block_rows(b, slots)
        allowed, within = marks(lens, b, slots)
        mixed = projected[rows, 2 * mh + 3 * HD :]
        step, rate, level, tri, inside = steps_and_levels(mixed, side, heads_at, ph)
        step_t, level_t = step.T, level.T
        cross = crossed[b].astype(jnp.float32)
        for pair in range(ph // 2):
            cols = slice(pair * 128, (pair + 1) * 128)
            convs = conv[rows, cols]
            conv_low = convs.astype(jnp.bfloat16)
            outs = []
            for h in (2 * pair, 2 * pair + 1):
                at = heads_at + h
                spread = level[:, at : at + 1] - level_t[at : at + 1, :]
                decay = jnp.exp(jnp.where(allowed, spread, NEG_LARGE))
                mixing = cross * decay * step_t[at : at + 1, :]
                outs.append(dot(mixing.astype(jnp.bfloat16), conv_low, 1, 0))
            total = halves(outs[0], outs[1])
            scanned[rows, cols] = total
            gate = projected[rows, cols]
            gated = (total + chan[5:6, cols] * convs) * (gate * jax.nn.sigmoid(gate))
            branch[rows, cols] = gated.astype(jnp.bfloat16)

    each_block(0, GROUP, before)
    first = blocks_start(low, land, s1, r1)
    each_block(0, GROUP // 2, attention)
    second = blocks_turn(first, low, land, mine, crossed, s2, r2, here)
    each_block(GROUP // 2, GROUP, attention)
    blocks_finish(first, second)
    each_block(0, GROUP, after)


def mixer(lens, projected, chan, side, table, sh, ph):
    tokens = projected.shape[0]
    slots = tokens // GROUP
    mh = chan.shape[1]
    vm = pl.BlockSpec(memory_space=VMEM)
    return pl.pallas_call(
        partial(mixer_kernel, sh, ph),
        name="mixer",
        out_shape=(
            jax.ShapeDtypeStruct((tokens, mh + HD), jnp.bfloat16),
            jax.ShapeDtypeStruct((tokens, mh), jnp.float32),
            jax.ShapeDtypeStruct((GROUP, slots, slots), jnp.bfloat16),
        ),
        in_specs=[pl.BlockSpec(memory_space=pltpu.SMEM)] + [vm] * 4,
        out_specs=(vm,) * 3,
        scratch_shapes=blocks_scratch(slots) + [VMEM((tokens, mh), jnp.float32)],
        compiler_params=params(4, 40),
        cost_estimate=cost(30),
    )(lens, projected, chan, side, table)


def mixer_back_kernel(
    sh, ph, lens, projected, chan, side, table, scanned, crossed, grads, out, chan_sums, side_sums,
    low, land, mine, s1, r1, s2, r2, here, summed, misc,
):
    slots = crossed.shape[1]
    mh = chan.shape[1]
    heads_at = 2 * sh
    bf = jnp.bfloat16
    greet_group(cross=True)
    chan_sums[...] = jnp.zeros_like(chan_sums)
    side_sums[...] = jnp.zeros_like(side_sums)

    def scan(b):
        rows = block_rows(b, slots)
        allowed, within = marks(lens, b, slots)
        mixed = projected[rows, 2 * mh + 3 * HD :]
        step, rate, level, tri, inside = steps_and_levels(mixed, side, heads_at, ph)
        step_t, level_t = step.T, level.T
        cross = crossed[b].astype(jnp.float32)
        lane = lax.broadcasted_iota(jnp.int32, (slots, 128), 1)
        place_row = lax.broadcasted_iota(jnp.int32, (slots, slots), 0)
        grad_cross = jnp.zeros((slots, slots), jnp.float32)
        row_sums = jnp.zeros((slots, slots), jnp.float32)
        col_sums = jnp.zeros((slots, slots), jnp.float32)
        for pair in range(ph // 2):
            cols = slice(pair * 128, (pair + 1) * 128)
            weights = chan[:, cols]
            pre, shifted = conv_pre(
                projected[rows, mh + pair * 128 : mh + (pair + 1) * 128], within, weights
            )
            convs = pre * jax.nn.sigmoid(pre)
            conv_low = convs.astype(bf)
            gate = projected[rows, cols]
            sig = jax.nn.sigmoid(gate)
            grad = grads[rows, cols]
            skip = weights[5:6, :]
            grad_mix = grad * (gate * sig)
            out[rows, cols] = (
                grad * (scanned[rows, cols] + skip * convs) * (sig * (1.0 + gate * (1.0 - sig)))
            ).astype(bf)
            skip_sum = jnp.sum(grad_mix * convs, axis=0, keepdims=True)
            grad_low = grad_mix.astype(bf)
            backs = []
            for f in (0, 1):
                at = heads_at + 2 * pair + f
                mask = lane < 64 if f == 0 else lane >= 64
                spread = level[:, at : at + 1] - level_t[at : at + 1, :]
                decay = jnp.exp(jnp.where(allowed, spread, NEG_LARGE))
                step_row = step_t[at : at + 1, :]
                mixing = cross * decay * step_row
                backs.append(dot(mixing.astype(bf), grad_low, 0, 0))
                grad_mixing = dot(jnp.where(mask, grad_mix, 0.0).astype(bf), conv_low, 1, 1)
                weighted = grad_mixing * decay
                grad_cross = grad_cross + weighted * step_row
                weighted = weighted * cross
                col = jnp.sum(weighted, axis=0, keepdims=True)
                row = jnp.sum(weighted * step_row, axis=1, keepdims=True)
                row_sums = jnp.where(lane == at, row, row_sums)
                col_sums = jnp.where(place_row == at, col, col_sums)
            grad_conv = grad_mix * skip + halves(backs[0], backs[1])
            back, sums = conv_back(grad_conv, pre, shifted, within, weights)
            out[rows, mh + pair * 128 : mh + (pair + 1) * 128] = back.astype(bf)
            for i, part in enumerate(sums + [skip_sum]):
                chan_sums[i : i + 1, cols] += part
        low[b] = grad_cross.astype(bf)
        col_sums = col_sums.T
        grad_level = row_sums - step * col_sums
        grad_rate_step = dot(tri, grad_level, 0, 0, HIGH)
        grad_step = (col_sums + grad_rate_step * rate) * jax.nn.sigmoid(mixed + side[5:6, :])
        grad_step = jnp.where(inside, grad_step, 0.0)
        misc[rows, :] = grad_step
        side_sums[5:6, :] += jnp.sum(grad_step, axis=0, keepdims=True)
        side_sums[6:7, :] += jnp.sum(grad_rate_step * step, axis=0, keepdims=True) * rate[:1, :]

    def attention(b):
        rows = block_rows(b, slots)
        at = 2 * mh
        query, key, value, probs, waves = attend(projected, rows, at, lens, table, b, slots)
        grad = grads[rows, mh:].astype(bf)
        grad_probs = dot(grad, value, 1, 1)
        out[rows, at + 2 * HD : at + 3 * HD] = dot(probs.astype(bf), grad, 0, 0).astype(bf)
        grad_raw = probs * (grad_probs - jnp.sum(grad_probs * probs, axis=-1, keepdims=True))
        grad_raw = (grad_raw * HD ** (-0.5)).astype(bf)
        out[rows, at : at + HD] = turned_back(dot(grad_raw, key, 1, 0), waves).astype(bf)
        out[rows, at + HD : at + 2 * HD] = turned_back(dot(grad_raw, query, 0, 0), waves).astype(bf)

    def state(b):
        rows = block_rows(b, slots)
        allowed, within = marks(lens, b, slots)
        mixed = projected[rows, 2 * mh + 3 * HD :]
        first, second, pre, shifted = state_parts(mixed, within, side, sh)
        lane = lax.broadcasted_iota(jnp.int32, pre.shape, 1)
        grad_first = dot(summed[b], second, 0, 0)
        grad_second = pltpu.roll(dot(summed[b], first, 1, 0), sh, 1)
        grad = jnp.where(lane < sh, grad_first, jnp.where(lane < 2 * sh, grad_second, 0.0))
        back, sums = conv_back(grad, pre, shifted, within, side)
        out[rows, 2 * mh + 3 * HD :] = jnp.where(lane < 2 * sh, back, misc[rows, :]).astype(bf)
        for i, part in enumerate(sums):
            side_sums[i : i + 1, :] += part

    each_block(0, GROUP, scan)
    begun = blocks_start(low, land, s1, r1)
    each_block(0, GROUP // 2, attention)
    done = blocks_turn(begun, low, land, mine, summed, s2, r2, here)
    each_block(GROUP // 2, GROUP, attention)
    blocks_finish(begun, done)
    each_block(0, GROUP, state)


def mixer_back(lens, projected, chan, side, table, scanned, crossed, grads, sh, ph):
    tokens = projected.shape[0]
    slots = tokens // GROUP
    mh = chan.shape[1]
    vm = pl.BlockSpec(memory_space=VMEM)
    return pl.pallas_call(
        partial(mixer_back_kernel, sh, ph),
        name="mixer_back",
        out_shape=(
            jax.ShapeDtypeStruct(projected.shape, jnp.bfloat16),
            jax.ShapeDtypeStruct(chan.shape, jnp.float32),
            jax.ShapeDtypeStruct(side.shape, jnp.float32),
        ),
        in_specs=[pl.BlockSpec(memory_space=pltpu.SMEM)] + [vm] * 7,
        out_specs=(vm,) * 3,
        scratch_shapes=blocks_scratch(slots)
        + [
            VMEM((GROUP, slots, slots), jnp.bfloat16),
            VMEM((tokens, 128), jnp.float32),
        ],
        compiler_params=params(5, 48),
        cost_estimate=cost(50),
    )(lens, projected, chan, side, table, scanned, crossed, grads)


def swiglu(ff_gate, ff_up):
    return jax.nn.silu(ff_gate) * ff_up


def cut(array, parts, axis=1):
    rows, cols = array.shape
    return array.reshape(rows, parts, cols // parts).transpose(1, 0, 2)


def local(
    tokens,
    cotangent,
    deal_order,
    seq_lengths,
    mixer_norm_gain,
    mamba_gate_weight,
    mamba_input_weight,
    state_weight,
    step_weight,
    conv_input,
    conv_input_bias,
    conv_state,
    conv_state_bias,
    step_bias,
    decay_log,
    skip_scale,
    mamba_out_weight,
    query_weight,
    key_weight,
    value_weight,
    attn_out_weight,
    ff_norm_gain,
    gate_weight,
    up_weight,
    down_weight,
):
    n_row = lax.axis_size("row")
    r = lax.axis_index("row")
    c = lax.axis_index("col")
    t = member(r)
    bits = data_bits(n_row)
    n_bits = n_row.bit_length() - 1
    slots, width = tokens.shape[1:]
    bf = jnp.bfloat16
    rows = mamba_gate_weight.shape[0]
    mh = mamba_gate_weight.shape[1] // TP
    qh = query_weight.shape[1] // TP
    kvh = key_weight.shape[1]
    sh = state_weight.shape[1] // (2 * GROUP)
    ph = step_weight.shape[1] // TP
    fh = gate_weight.shape[1] // TP
    used = 2 * mh + qh + 2 * kvh + 2 * sh + ph
    spare = -used % 256

    half = state_weight.shape[1] // 2
    state_in_part = lax.dynamic_slice_in_dim(state_weight[:, :half], c * (half // 2), half // 2, 1)
    state_out_part = lax.dynamic_slice_in_dim(state_weight[:, half:], c * (half // 2), half // 2, 1)
    mixed = jnp.concatenate(
        [
            state_in_part.reshape(rows, TP, sh),
            state_out_part.reshape(rows, TP, sh),
            step_weight.reshape(rows, TP, ph),
            jnp.zeros((rows, TP, spare), bf),
        ],
        axis=2,
    ).reshape(rows, TP * (2 * sh + ph + spare))
    in_weights = (
        mamba_gate_weight, mamba_input_weight, query_weight, key_weight, value_weight, mixed,
        mamba_out_weight.T, attn_out_weight.T,
    )
    ff_weights = (gate_weight, up_weight, down_weight.T)

    def assemble(slab):
        held = [(0, slab)]
        for b in bits:
            held = held + [
                (mask | 1 << b, lax.ppermute(part, "row", flips(n_row, 1 << b))) for mask, part in held
            ]
        return place_slabs(
            [mask for mask, part in held], [part for mask, part in held], n_row
        ).reshape(n_row * rows, slab.shape[2])

    def pick(array, index, axis=0):
        return lax.dynamic_index_in_dim(array, index, axis, keepdims=False)

    by_group = sorted(range(n_row), key=lambda row: [row >> b & 1 for b in bits])
    alike = [
        [row for row in by_group if [row >> b & 1 for b in TP_BITS] == [m & 1, m >> 1]]
        for m in range(TP)
    ]

    def sum_groups(grad, after=None):
        grad = grad.astype(bf)
        if after is not None:
            grad, after = lax.optimization_barrier((grad, after))
        part = lax.psum_scatter(
            grad, "row", scatter_dimension=0, axis_index_groups=alike, tiled=True
        ).reshape(TP, rows, grad.shape[1])
        return part, after

    def disperse(part):
        near = [pick(part, t)] + [
            lax.ppermute(pick(part, member(partner(r, m))), "row", flips(n_row, mask_of(m)))
            for m in (1, 2, 3)
        ]
        low, high = bit(r, TP_BITS[0]), bit(r, TP_BITS[1])

        def of(owner):
            inner = [
                jnp.where(low == owner % 2, near[2 * k], near[2 * k + 1]) for k in range(2)
            ]
            return jnp.where(high == owner // 2, inner[0], inner[1])

        return jnp.stack([of(owner) for owner in range(TP)])

    order = [n_bits - 1 - b for b in bits] + [n_bits - 1 - b for b in reversed(TP_BITS)]

    def regroup(array):
        lead = array.shape[:-1]
        cutup = array.reshape(lead + (2,) * n_bits + (rows,))
        dims = list(range(len(lead))) + [len(lead) + i for i in order] + [len(lead) + n_bits]
        return cutup.transpose(dims).reshape(array.shape)

    def ungroup(array):
        lead = array.shape[:-1]
        cutup = array.reshape(lead + (2,) * n_bits + (rows,))
        back = [order.index(i) for i in range(n_bits)]
        dims = list(range(len(lead))) + [len(lead) + i for i in back] + [len(lead) + n_bits]
        return cutup.transpose(dims).reshape(array.shape)

    mixer_gain = regroup(mixer_norm_gain)[None, :]
    ff_gain = regroup(ff_norm_gain)[None, :]

    meta = jnp.concatenate(
        [
            deal_order,
            jnp.pad(seq_lengths[:, 0, :], ((0, 0), (0, 128 - seq_lengths.shape[2]))),
            jnp.zeros((4, 128), jnp.int32),
        ],
        axis=0,
    )
    meta_all, give, take, x_home, gy_home, normed_one, gy_all, w_mixer, slab_ff = deal(
        meta, regroup(tokens), regroup(cotangent), mixer_gain, in_weights, ff_weights, n_row
    )
    normed_one = normed_one.reshape(GROUP * slots, width)
    gy_all = gy_all.reshape(GROUP * slots, width)
    w_mixer = w_mixer.reshape(width, -1)
    w_in, w_out = w_mixer[:, : used + spare], w_mixer[:, used + spare :]
    w_ff = assemble(slab_ff)
    w_gate_up = w_ff[:, : 2 * fh]
    w_down = w_ff[:, 2 * fh :]

    def across(array):
        return lax.ppermute(array, "col", [(0, 1), (1, 0)])

    base = r - bit(r, TP_BITS[0]) * (1 << TP_BITS[0]) - bit(r, TP_BITS[1]) * (1 << TP_BITS[1])
    group_meta = jnp.stack([pick(meta_all, base + mask_of(m)) for m in range(TP)])
    lengths = group_meta[:, 2:4, : seq_lengths.shape[2]].reshape(GROUP, seq_lengths.shape[2])
    half_dim = HD // 2
    inverse = ROPE_BASE ** (-2.0 * jnp.arange(half_dim, dtype=jnp.float32) / HD)
    angles = jnp.arange(slots, dtype=jnp.float32)[:, None] * inverse[None, :]
    cosine, sine = jnp.cos(angles), jnp.sin(angles)
    table = jnp.concatenate([cosine, cosine, -sine, sine], axis=1)

    def piece(array, size, start):
        return lax.dynamic_slice_in_dim(array, start, size, array.ndim - 1)

    eighth = c * TP + t
    chan = jnp.concatenate(
        [
            piece(conv_input, mh, t * mh),
            piece(conv_input_bias[None], mh, t * mh),
            jnp.repeat(piece(skip_scale[None], ph, t * ph), mh // ph, axis=1),
            jnp.zeros((2, mh), jnp.float32),
        ],
        axis=0,
    )
    states = jnp.concatenate([conv_state, conv_state_bias[None]], axis=0)
    states = jnp.concatenate(
        [piece(states, sh, eighth * sh), piece(states, sh, half + eighth * sh)], axis=1
    )
    heads = jnp.concatenate(
        [piece(step_bias[None], ph, t * ph), piece(decay_log[None], ph, t * ph)], axis=0
    )
    after = 128 - 2 * sh - ph
    side = jnp.concatenate(
        [
            jnp.pad(states, ((0, 0), (0, 128 - 2 * sh))),
            jnp.pad(heads, ((0, 0), (2 * sh, after))),
            jnp.zeros((1, 128), jnp.float32),
        ],
        axis=0,
    )

    projected = matmul(normed_one, w_in)
    edges = [0, mh, 2 * mh, 2 * mh + qh, 2 * mh + qh + kvh, 2 * mh + qh + 2 * kvh]
    edges = edges + [edges[-1] + 2 * sh, edges[-1] + 2 * sh + ph]
    branch_in, scanned, crossed = mixer(lengths, projected, chan, side, table, sh, ph)
    branch_part = matmul_trans(branch_in, w_out).astype(bf).reshape(GROUP, slots, width)
    mid, normed_two = middle(branch_part, x_home, ff_gain)
    normed_two = normed_two.reshape(GROUP * slots, width)

    ff_gate_up = matmul(normed_two, w_gate_up)
    ff_gate, ff_up = ff_gate_up[:, :fh], ff_gate_up[:, fh:]
    ff_hidden = swiglu(ff_gate, ff_up).astype(bf)
    ff_part = matmul_trans(ff_hidden, w_down).astype(bf).reshape(GROUP, slots, width)
    grad_hidden = matmul(gy_all, w_down)
    unused_value, pullback = jax.vjp(swiglu, ff_gate, ff_up)
    grad_gate, grad_up = pullback(grad_hidden)
    grad_gate_up = jnp.concatenate([grad_gate.astype(bf), grad_up.astype(bf)], axis=1)
    normed_two_part = (
        matmul_trans(grad_gate_up, w_gate_up).astype(bf).reshape(GROUP, slots, width)
    )
    grad_ff = jnp.concatenate(
        [matmul_left(normed_two, grad_gate_up).astype(bf), matmul_left(gy_all, ff_hidden).astype(bf)],
        axis=1,
    )
    normed_two_part, grad_ff = lax.optimization_barrier((normed_two_part, grad_ff))
    ff_sums, unused_value = sum_groups(grad_ff)
    d_mid, delta_ff_gain, branch_all = turn(
        normed_two_part, mid, gy_home, ff_gain
    )
    ff_pairs = ff_part.reshape(TP, 2, slots, width)
    ff_sum = (
        pick(ff_pairs, c, 1).astype(jnp.float32)
        + across(pick(ff_pairs, 1 - c, 1)).astype(jnp.float32)
    ).astype(bf)
    result = mid + pick(ff_sum, t).astype(jnp.float32)
    for m in (1, 2, 3):
        result = result + lax.ppermute(
            pick(ff_sum, member(partner(r, m))), "row", flips(n_row, mask_of(m))
        ).astype(jnp.float32)
    result = result.astype(bf)
    branch_all = branch_all.reshape(GROUP * slots, width)

    out_sums, ff_sums = sum_groups(matmul_left(branch_all, branch_in), ff_sums)
    grad_branch_in = matmul(branch_all, w_out)
    grad_projected, chan_sums, side_sums = mixer_back(
        lengths, projected, chan, side, table, scanned, crossed, grad_branch_in, sh, ph
    )
    early = jnp.concatenate([grad_projected[:, :mh], grad_projected[:, 2 * mh : edges[5]]], axis=1)
    early_sums, out_sums = sum_groups(matmul_left(normed_one, early), out_sums)
    grad_late = matmul_left(
        normed_one, jnp.concatenate([grad_projected[:, mh : 2 * mh], grad_projected[:, edges[5] :]], axis=1)
    ).astype(bf)
    grad_projected, grad_late = lax.optimization_barrier((grad_projected, grad_late))
    late_sums, early_sums = sum_groups(grad_late, early_sums)
    normed_one_part = matmul_trans(grad_projected, w_in).astype(bf).reshape(GROUP, slots, width)

    def lanes(array):
        array = array.reshape((-1, array.shape[-1]))
        array = jnp.pad(array, ((0, 0), (0, -array.shape[1] % 128)))
        return array.reshape(-1, 128)

    small_parts = [
        lanes(part)
        for part in (
            chan_sums[:4],
            chan_sums[4:5],
            side_sums[5:6, 2 * sh : 2 * sh + ph],
            side_sums[6:7, 2 * sh : 2 * sh + ph],
            jnp.sum(chan_sums[5].reshape(ph, -1), axis=1)[None],
            side_sums[:4, : 2 * sh],
            side_sums[4:5, : 2 * sh],
            delta_ff_gain,
        )
    ]
    counts = [part.shape[0] for part in small_parts] + [width // 128]
    small_parts.append(jnp.zeros((-sum(counts) % 8, 128), jnp.float32))
    starts = [sum(counts[:i]) for i in range(len(counts))]
    starts[-1] += small_parts[-1].shape[0]
    output, grad_tokens, small_all = send_home(
        normed_one_part, x_home, d_mid, result, mixer_gain, give, take,
        jnp.concatenate(small_parts, axis=0), n_row,
    )
    delta_ff, delta_out, delta_early, delta_late = (
        disperse(part) for part in (ff_sums, out_sums, early_sums, late_sums)
    )
    delta_in = jnp.concatenate(
        [delta_early[:, :, :mh], delta_late[:, :, :mh], delta_early[:, :, mh:], delta_late[:, :, mh:]], axis=2
    )

    def join(stacked):
        return stacked.transpose(1, 0, 2).reshape(stacked.shape[1], -1).astype(jnp.float32)

    pieces = [delta_in[:, :, low:high] for low, high in zip(edges[:-1], edges[1:])]
    state_mine = pieces[5]
    state_other = across(state_mine)
    state_first = jnp.where(c == 0, state_mine, state_other)
    state_second = jnp.where(c == 0, state_other, state_mine)
    delta_state = jnp.concatenate(
        [
            join(state_first[:, :, :sh]),
            join(state_second[:, :, :sh]),
            join(state_first[:, :, sh:]),
            join(state_second[:, :, sh:]),
        ],
        axis=1,
    )
    delta_key = jnp.sum(pieces[3].astype(jnp.float32), axis=0)
    delta_value = jnp.sum(pieces[4].astype(jnp.float32), axis=0)

    small_all = small_all.reshape(TP, 2, -1, 128)
    small_col = pick(small_all, c, 1)

    def taken(array, i):
        return lax.slice_in_dim(array, starts[i], starts[i] + counts[i], axis=array.ndim - 2)

    def along(array, i, size):
        got = taken(array, i).reshape(TP, -1, size + -size % 128)[:, :, :size]
        return got.transpose(1, 0, 2).reshape(got.shape[1], TP * size)

    def state_along(i):
        got = taken(small_all, i)[..., : 2 * sh].reshape(TP, 2, -1, 2, sh)
        return got.transpose(2, 3, 1, 0, 4).reshape(got.shape[2], 2 * half)

    def over_all(i):
        return ungroup(jnp.sum(taken(small_all, i), axis=(0, 1)).reshape(width))

    by_col = [
        along(small_col, 0, mh),
        along(small_col, 1, mh)[0],
        along(small_col, 2, ph)[0],
        along(small_col, 3, ph)[0],
        along(small_col, 4, ph)[0],
    ]
    by_all = [state_along(5), state_along(6)[0], over_all(8), over_all(7)]

    return (
        ungroup(output),
        ungroup(grad_tokens),
        by_all[2],
        join(pieces[0]),
        join(pieces[1]),
        delta_state,
        join(pieces[6]),
        by_col[0],
        by_col[1],
        by_all[0],
        by_all[1],
        by_col[2],
        by_col[3],
        by_col[4],
        join(delta_out[:, :, :mh]).T,
        join(pieces[2]),
        delta_key,
        delta_value,
        join(delta_out[:, :, mh:]).T,
        by_all[3],
        join(delta_ff[:, :, :fh]),
        join(delta_ff[:, :, fh : 2 * fh]),
        join(delta_ff[:, :, 2 * fh :]).T,
    )


def solution(mesh):
    both = P("row", "col")
    turned = P("col", "row")
    in_specs = (
        P(None, "row", None),
        P(None, "row", None),
        P(None, "row"),
        P(None, "row", None),
        P(),
        both,
        both,
        P("row", None),
        both,
        P(None, "col"),
        P("col"),
        P(),
        P(),
        P("col"),
        P("col"),
        P("col"),
        turned,
        both,
        both,
        both,
        turned,
        P(),
        both,
        both,
        turned,
    )
    out_specs = (
        P(None, "row", None),
        P(None, "row", None),
        P(),
        both,
        both,
        P("row", None),
        both,
        P(None, "col"),
        P("col"),
        P(),
        P(),
        P("col"),
        P("col"),
        P("col"),
        turned,
        both,
        both,
        both,
        turned,
        P(),
        both,
        both,
        turned,
    )
    return jax.shard_map(local, mesh=mesh, in_specs=in_specs, out_specs=out_specs, check_vma=False)
```

time: 854 us -> 777 us (0.910)
  the two profiles are of different devices: /device:TPU:1 before, /device:TPU:9 now
where the time goes in v2:
time: 777 us; the launch traced here: 768 us
  Pallas kernels  395 us (51%)
  waiting for transfers between devices  155 us (20%)
  local copies, waits for them, and re-layouts  79.7 us (10%)
  matrix products  74.2 us (10%)
  starting transfers between devices  25.2 us (3%)
  other arithmetic  24.4 us (3%)
  between operations  15.1 us (2%)
    pallas_call x1, Pallas kernels, deal(): pl.pallas_call(deal_kernel, name='deal', out_shape=(jax.ShapeDtypeStruct(...  153 us
    reduce_scatter x4, waiting for transfers between devices, sum_groups(): lax.psum_scatter(grad, 'row', scatter_dimension=0, axis_index_groups=alik...  68.7 us
    pallas_call x1, Pallas kernels, send_home(): pl.pallas_call(home_kernel, name='home', out_shape=(jax.ShapeDtypeStruct(...  67.3 us
    ppermute x3, waiting for transfers between devices, assemble(): lax.ppermute(part, 'row', flips(n_row, 1 << b))  66 us
    pallas_call x1, Pallas kernels, turn(): pl.pallas_call(turn_kernel, name='turn', out_shape=(jax.ShapeDtypeStruct(...  60.9 us
    pallas_call x1, Pallas kernels, middle(): pl.pallas_call(middle_kernel, name='middle', out_shape=(jax.ShapeDtypeStr...  57.1 us
    unnamed x107, local copies, waits for them, and re-layouts  36.6 us
    pallas_call x1, Pallas kernels, mixer_back(): pl.pallas_call(partial(mixer_back_kernel, sh, ph), name='mixer_back', out...  32.8 us
  transfers between devices with their start and end apart: 24, of which 10 were waited for; matrix products, arithmetic and copies ran while one was open for 15% of the time, Pallas kernels for 31%

profile of v2, /device:TPU:9, one launch (start us, length us, event | category | flops | bytes accessed | tf_op | source)
XLA Modules:
  0.0 768.2 jit_solution(10589179447760471248)
XLA Ops:
  24.0 152.7 %deal.1 = (s32[16,8,128]{2,1,0:T(8,128)S(1)}, bf16[256,256]{1,0:T(8,128)(2,1)S(1)}, bf16[256,256]{1,0:T(8,128)(2,1)S(1)}, bf16[128,2048]{1,0:T(8,128)(2,1)S(1)},...) custom-call(s32[8,128]{1,0:T(8,128)S(1)} %fusion.36.meta, ...), custom_call_target="tpu_custom_call" | custom-call | bytes 340000000 | tf_op jit(solution)/shard_map/deal/pallas_call | solution.py:539
  178.2 2.1 copy-done.26
  181.0 2.7 collective-permute-start
  185.7 66.0 %collective-permute-done.refs_1_ = bf16[4,128,1536]{2,1,0:T(8,128)(2,1)} collective-permute-done((bf16[4,128,1536]{2,1,0:T(8,128)(2,1)S(1)}, bf16[4,128,1536]{2,1,0:T(8,128)(2,1)}, u32[]{:S(2)}, u32[]{:S(2)}) %collective-permute-start) | collective-permute-done | bytes 1572896 | tf_op jit(solution)/shard_map/ppermute | solution.py:1215
  251.6 8.9 %fusion.2.projected = f32[1024,1280]{1,0:T(8,128)S(1)} fusion(bf16[1024,2048]{1,0:T(8,128)(2,1)} %bitcast.258, bf16[2048,1792]{1,0:T(8,128)(2,1)} %bitcast.302), kind=kOutput, calls=%fused_computation.3 | convolution fusion | flops 5368709120 | bytes 14680064 | tf_op jit(solution)/shard_map/dot_general | solution.py:24
  260.5 22.1 %mixer.1 = (bf16[1024,512]{1,0:T(8,128)(2,1)S(1)}, f32[1024,384]{1,0:T(8,128)S(1)}, bf16[8,128,128]{2,1,0:T(8,128)(2,1)S(1)}) custom-call(s32[8,3]{1,0:T(8,128)S(1)} %bitcast.251, f32[1024,1280]{1,0:T(8,128)S(1)} %fusion.2.projected, f32[8,384]{1,0:T(8,128)S(1)} %maximum_maximum_fusion.1.chan, f32[8,128]{1,0:T(8,128)S(1)} %pad_maximum_fusion.10.side, ...), custom_call_target="tpu_custom_call" | custom-call | bytes 102000000 | tf_op jit(solution)/shard_map/mixer/pallas_call | solution.py:989
  282.7 5.0 convolution_convert_fusion.1
  287.8 57.1 %middle.1 = (f32[128,2048]{1,0:T(8,128)S(1)}, bf16[8,128,2048]{2,1,0:T(8,128)(2,1)S(1)}) custom-call(bf16[8,128,2048]{2,1,0:T(8,128)(2,1)S(1)} %bitcast.242, bf16[128,2048]{1,0:T(8,128)(2,1)S(1)} %get-tuple-element.64.x, f32[1,2048]{1,0:T(1,128)S(1)} %bitcast.253), custom_call_target="tpu_custom_call" | custom-call | bytes 204000000 | tf_op jit(solution)/shard_map/middle/pallas_call | solution.py:593
  344.9 2.1 place.1
  347.0 4.7 fusion.9
  351.7 3.3 fusion.13
  355.0 7.0 convolution_convert_fusion.2
  362.0 6.3 convolution_convert_fusion.3
  368.3 2.4 convolution_convert_fusion.5
  370.7 3.4 pad_maximum_fusion
  375.1 60.9 %turn.1 = (f32[128,2048]{1,0:T(8,128)S(1)}, f32[1,2048]{1,0:T(1,128)S(1)}, bf16[8,128,2048]{2,1,0:T(8,128)(2,1)}) custom-call(bf16[8,128,2048]{2,1,0:T(8,128)(2,1)} %bitcast.266, f32[128,2048]{1,0:T(8,128)S(1)} %get-tuple-element.67.mid, bf16[128,2048]{1,0:T(8,128)(2,1)S(1)} %copy-done.13, f32[1,2048]{1,0:T(1,128)S(1)} %bitcast.254), custom_call_target="tpu_custom_call" | custom-call | bytes 204000000 | tf_op jit(solution)/shard_map/turn/pallas_call | solution.py:642
  436.1 6.3 convolution_convert_fusion.6
  442.3 43.1 %reduce-scatter.5.cloned.1.call-done = bf16[512,1536]{0,1:T(8,128)(2,1)} async-done(((bf16[2048,1536]{0,1:T(8,128)(2,1)}), bf16[512,1536]{0,1:T(8,128)(2,1)}) %reduce-scatter.5.cloned.1.call-update) | async-done | bytes 1572880 | tf_op jit(solution)/shard_map/reduce_scatter | solution.py:1234
  485.4 3.5 reshape.201
  489.0 5.3 fusion.15.grads
  494.3 32.8 %mixer_back.1 = (bf16[1024,1280]{1,0:T(8,128)(2,1)}, f32[8,384]{1,0:T(8,128)S(1)}, f32[8,128]{1,0:T(8,128)S(1)}) custom-call(s32[8,3]{1,0:T(8,128)S(1)} %bitcast.252, f32[1024,1280]{1,0:T(8,128)} %copy-done.2, f32[8,384]{1,0:T(8,128)S(1)} %maximum_maximum_fusion.1.chan, f32[8,128]{1,0:T(8,128)S(1)} %pad_maximum_fusion.10.side, ...), custom_call_target="tpu_custom_call" | custom-call | bytes 170000000 | tf_op jit(solution)/shard_map/mixer_back/pallas_call | solution.py:1119
  527.1 2.1 fusion.41
  530.1 5.0 convolution_convert_fusion.4
  535.1 4.3 convolution_convert_fusion
  539.5 2.0 copy-done.31
  544.0 5.9 convolution_convert_fusion.7
  549.9 4.6 fusion.4
  554.5 2.3 dynamic-slice_bitcast_fusion.3
  559.5 10.0 %fusion.5 = bf16[1024,2048]{1,0:T(8,128)(2,1)} fusion(bf16[1024,1280]{1,0:T(8,128)(2,1)S(1)} %copy-done.36, bf16[2048,1792]{1,0:T(8,128)(2,1)} %bitcast.305), kind=kOutput, calls=%fused_computation.7 | convolution fusion | flops 5370806272 | bytes 12058624 | tf_op jit(solution)/shard_map/dot_general | solution.py:28
  569.4 25.6 %reduce-scatter.9.cloned.1.call-done = bf16[512,768]{1,0:T(8,128)(2,1)} async-done(((bf16[2048,768]{1,0:T(8,128)(2,1)}), bf16[512,768]{1,0:T(8,128)(2,1)}) %reduce-scatter.9.cloned.1.call-update) | async-done | bytes 786448 | tf_op jit(solution)/shard_map/reduce_scatter | solution.py:1234
  595.6 1.9 fusion.30.result
  598.8 67.3 %home.1 = (bf16[2,128,2048]{2,1,0:T(8,128)(2,1)S(1)}, bf16[2,128,2048]{2,1,0:T(8,128)(2,1)S(1)}, f32[8,56,128]{2,1,0:T(8,128)S(1)}) custom-call(bf16[8,128,2048]{2,1,0:T(8,128)(2,1)} %bitcast.265, bf16[128,2048]{1,0:T(8,128)(2,1)S(1)} %get-tuple-element.64.x, f32[128,2048]{1,0:T(8,128)S(1)} %copy-done.9, bf16[128,2048]{1,0:T(8,128)(2,1)S(1)} %fusion.30.result, ...), custom_call_target="tpu_custom_call" | custom-call | bytes 255000000 | tf_op jit(solution)/shard_map/home/pallas_call | solution.py:718
  666.1 3.8 copy.110
  669.9 2.3 dynamic-slice_bitcast_fusion.6
  672.1 2.5 collective-permute-start.17
  674.7 2.8 collective-permute-start.19
  684.3 11.2 %collective-permute-done.19 = bf16[128,1536]{1,0:T(8,128)(2,1)} collective-permute-done((bf16[128,1536]{1,0:T(8,128)(2,1)}, bf16[128,1536]{1,0:T(8,128)(2,1)}, u32[]{:S(2)}, u32[]{:S(2)}) %collective-permute-start.19) | collective-permute-done | bytes 393248 | tf_op jit(solution)/shard_map/ppermute | solution.py:1241
  700.9 1.8 convert_bitcast_fusion
  702.7 2.5 copy.116
  705.2 2.5 copy.115
  707.8 2.5 copy.122
  710.3 2.5 copy.114
  712.8 2.5 copy.121
  717.3 1.9 dynamic-slice_bitcast_fusion.9
  724.0 3.7 collective-permute-done.9
  731.6 2.3 copy.117
  745.6 5.3 collective-permute-start.13
  754.5 2.3 copy.118
  (244 shorter events, 72.2 us)
Async XLA Ops:
  7.2 178.0 %copy-start = (f32[4,1536]{1,0:T(4,128)S(1)}, f32[4,1536]{1,0:T(4,128)}, u32[]{:S(2)}) copy-start(f32[4,1536]{1,0:T(4,128)} %param.34) | copy-start | bytes 73732
  7.2 478.2 %reduce-scatter.5.cloned.1.call-start = ((), (), s32[]{:S(2)}) async-start(), calls=%async_computation.4 | async-start | bytes 7864320 | tf_op jit(solution)/shard_map/reduce_scatter | solution.py:1234
  10.4 174.0 %copy-start.44 = (f32[24]{0:T(128)S(1)}, f32[24]{0:T(128)}, u32[]{:S(2)}) copy-start(f32[24]{0:T(128)} %param.40) | copy-start | bytes 292
  10.4 174.4 %copy-start.41 = (f32[24]{0:T(128)S(1)}, f32[24]{0:T(128)}, u32[]{:S(2)}) copy-start(f32[24]{0:T(128)} %param.39) | copy-start | bytes 292
  10.4 174.3 %copy-start.42 = (f32[24]{0:T(128)S(1)}, f32[24]{0:T(128)}, u32[]{:S(2)}) copy-start(f32[24]{0:T(128)} %param.38) | copy-start | bytes 292
  10.4 174.5 %copy-start.39 = (f32[4,512]{1,0:T(4,128)S(1)}, f32[4,512]{1,0:T(4,128)}, u32[]{:S(2)}) copy-start(f32[4,512]{1,0:T(4,128)} %param.36) | copy-start | bytes 24580
  10.5 174.5 %copy-start.40 = (f32[512]{0:T(512)S(1)}, f32[512]{0:T(512)}, u32[]{:S(2)}) copy-start(f32[512]{0:T(512)} %param.37) | copy-start | bytes 6148
  180.3 164.6 %collective-permute-start.1 = (bf16[4,128,1536]{2,1,0:T(8,128)(2,1)S(1)}, bf16[4,128,1536]{2,1,0:T(8,128)(2,1)}, u32[]{:S(2)}, u32[]{:S(2)}) collective-permute-start(bf16[4,128,1536]{2,1,0:T(8,128)(2,1)S(1)} %get-tuple-element.62.refs_0_), channel_id=1, source_target_pairs={{0,8},{2,10},{4,12},{6,14},{8,0},{10,2},{12,4},{14,6},{16,24},{18,... | collective-permute-start | bytes 4718600 | tf_op jit(solution)/shard_map/ppermute | solution.py:1215
  181.0 70.6 %collective-permute-start = (bf16[4,128,1536]{2,1,0:T(8,128)(2,1)S(1)}, bf16[4,128,1536]{2,1,0:T(8,128)(2,1)}, u32[]{:S(2)}, u32[]{:S(2)}) collective-permute-start(bf16[4,128,1536]{2,1,0:T(8,128)(2,1)S(1)} %get-tuple-element.62.refs_0_), channel_id=1, source_target_pairs={{0,16},{2,18},{4,20},{6,22},{8,24},{10,26},{12,28},{14,30},{16,0},... | collective-permute-start | bytes 4718600 | tf_op jit(solution)/shard_map/ppermute | solution.py:1215
  251.6 93.3 %collective-permute-start.2 = (bf16[4,128,1536]{2,1,0:T(8,128)(2,1)}, bf16[4,128,1536]{2,1,0:T(8,128)(2,1)S(1)}, u32[]{:S(2)}, u32[]{:S(2)}) collective-permute-start(bf16[4,128,1536]{2,1,0:T(8,128)(2,1)} %collective-permute-done.refs_1_), channel_id=1, source_target_pairs={{0,8},{2,10},{4,12},{6,14},{8,0},{10,2},{12,4},{14,6},{16,24},{18,... | collective-permute-start | bytes 4718600 | tf_op jit(solution)/shard_map/ppermute | solution.py:1215
  260.5 27.2 %copy-start.2 = (f32[1024,1280]{1,0:T(8,128)}, f32[1024,1280]{1,0:T(8,128)S(1)}, u32[]{:S(2)}) copy-start(f32[1024,1280]{1,0:T(8,128)S(1)} %fusion.2.projected) | copy-start | bytes 15728644
  282.7 5.1 copy-start.4
  282.7 5.1 copy-start.16
  282.7 5.1 copy-start.28
  347.0 15.0 %copy-start.3 = (bf16[4,4,128,1536]{3,2,1,0:T(8,128)(2,1)}, bf16[4,4,128,1536]{3,2,1,0:T(8,128)(2,1)S(1)}, u32[]{:S(2)}) copy-start(bf16[4,4,128,1536]{3,2,1,0:T(8,128)(2,1)S(1)} %place.1) | copy-start | bytes 18874372
  355.0 13.3 %copy-start.45 = (bf16[1024,512]{0,1:T(8,128)(2,1)}, bf16[1024,512]{0,1:T(8,128)(2,1)S(1)}, u32[]{:S(2)}) copy-start(bf16[1024,512]{0,1:T(8,128)(2,1)S(1)} %get-tuple-element.143) | copy-start | bytes 3145732
  374.1 160.9 %reduce-scatter.7.cloned.1.call-start = ((), (), s32[]{:S(2)}) async-start(), calls=%async_computation.5 | async-start | bytes 2621440 | tf_op jit(solution)/shard_map/reduce_scatter | solution.py:1234
  374.2 61.9 %copy-start.29 = (bf16[1024,512]{1,0:T(8,128)(2,1)S(1)}, bf16[1024,512]{1,0:T(8,128)(2,1)}, u32[]{:S(2)}) copy-start(bf16[1024,512]{1,0:T(8,128)(2,1)} %copy-done.28) | copy-start | bytes 3145732
  436.1 6.3 copy-start.8
  488.9 5.4 copy-start.5
  489.0 106.0 %reduce-scatter.9.cloned.1.call-start = ((), (), s32[]{:S(2)}) async-start(), calls=%async_computation.6 | async-start | bytes 3932160 | tf_op jit(solution)/shard_map/reduce_scatter | solution.py:1234
  489.0 5.3 copy-start.17
  535.1 198.9 %reduce-scatter.11.cloned.1.call-start = ((), (), s32[]{:S(2)}) async-start(), calls=%async_computation.7 | async-start | bytes 2621440 | tf_op jit(solution)/shard_map/reduce_scatter | solution.py:1234
  542.9 7.0 collective-permute-start.3
  549.9 9.5 %copy-start.36 = (bf16[1024,1280]{1,0:T(8,128)(2,1)S(1)}, bf16[1024,1280]{1,0:T(8,128)(2,1)}, u32[]{:S(2)}) copy-start(bf16[1024,1280]{1,0:T(8,128)(2,1)} %get-tuple-element.71) | copy-start | bytes 7864324
  556.8 38.8 %collective-permute-start.4 = (bf16[128,2048]{1,0:T(8,128)(2,1)}, bf16[128,2048]{1,0:T(8,128)(2,1)}, u32[]{:S(2)}, u32[]{:S(2)}) collective-permute-start(bf16[128,2048]{1,0:T(8,128)(2,1)} %get-tuple-element.151), channel_id=1, source_target_pairs={{0,2},{2,0},{4,6},{6,4},{8,10},{10,8},{12,14},{14,12},{16,18},{18,... | collective-permute-start | bytes 1572872 | tf_op jit(solution)/shard_map/ppermute | solution.py:1368
  557.1 38.5 %collective-permute-start.6 = (bf16[128,2048]{1,0:T(8,128)(2,1)S(1)}, bf16[128,2048]{1,0:T(8,128)(2,1)}, u32[]{:S(2)}, u32[]{:S(2)}) collective-permute-start(bf16[128,2048]{1,0:T(8,128)(2,1)S(1)} %get-tuple-element.152), channel_id=1, source_target_pairs={{0,6},{2,4},{4,2},{6,0},{8,14},{10,12},{12,10},{14,8},{16,22},{18,... | collective-permute-start | bytes 1572872 | tf_op jit(solution)/shard_map/ppermute | solution.py:1368
  558.4 37.2 %collective-permute-start.5 = (bf16[128,2048]{1,0:T(8,128)(2,1)S(1)}, bf16[128,2048]{1,0:T(8,128)(2,1)}, u32[]{:S(2)}, u32[]{:S(2)}) collective-permute-start(bf16[128,2048]{1,0:T(8,128)(2,1)S(1)} %get-tuple-element.153), channel_id=1, source_target_pairs={{0,4},{2,6},{4,0},{6,2},{8,12},{10,14},{12,8},{14,10},{16,20},{18,... | collective-permute-start | bytes 1572872 | tf_op jit(solution)/shard_map/ppermute | solution.py:1368
  569.4 28.1 %copy-start.20 = (bf16[256,256]{1,0:T(8,128)(2,1)S(1)}, bf16[256,256]{1,0:T(8,128)(2,1)}, u32[]{:S(2)}) copy-start(bf16[256,256]{1,0:T(8,128)(2,1)} %copy-done.19) | copy-start | bytes 393220
  569.4 28.1 %copy-start.25 = (f32[2048]{0:T(1024)S(1)}, f32[2048]{0:T(1024)}, u32[]{:S(2)}) copy-start(f32[2048]{0:T(1024)} %param.29) | copy-start | bytes 24580
  672.1 26.0 %copy-start.37 = (bf16[512,512]{1,0:T(8,128)(2,1)S(1)}, bf16[512,512]{1,0:T(8,128)(2,1)}, u32[]{:S(2)}) copy-start(bf16[512,512]{1,0:T(8,128)(2,1)} %reduce-scatter.7.cloned.1.call-done) | copy-start | bytes 1572868
  672.1 12.2 %collective-permute-start.17 = (bf16[128,1536]{1,0:T(8,128)(2,1)}, bf16[128,1536]{1,0:T(8,128)(2,1)S(1)}, u32[]{:S(2)}, u32[]{:S(2)}) collective-permute-start(bf16[128,1536]{1,0:T(8,128)(2,1)} %get-tuple-element.157), channel_id=1, source_target_pairs={{0,2},{2,0},{4,6},{6,4},{8,10},{10,8},{12,14},{14,12},{16,18},{18,... | collective-permute-start | bytes 1179656 | tf_op jit(solution)/shard_map/ppermute | solution.py:1241
  674.7 20.9 %collective-permute-start.19 = (bf16[128,1536]{1,0:T(8,128)(2,1)}, bf16[128,1536]{1,0:T(8,128)(2,1)}, u32[]{:S(2)}, u32[]{:S(2)}) collective-permute-start(bf16[128,1536]{1,0:T(8,128)(2,1)} %get-tuple-element.158), channel_id=1, source_target_pairs={{0,6},{2,4},{4,2},{6,0},{8,14},{10,12},{12,10},{14,8},{16,22},{18,... | collective-permute-start | bytes 1179656 | tf_op jit(solution)/shard_map/ppermute | solution.py:1241
  677.4 19.0 %collective-permute-start.18 = (bf16[128,1536]{1,0:T(8,128)(2,1)}, bf16[128,1536]{1,0:T(8,128)(2,1)}, u32[]{:S(2)}, u32[]{:S(2)}) collective-permute-start(bf16[128,1536]{1,0:T(8,128)(2,1)} %get-tuple-element.159), channel_id=1, source_target_pairs={{0,4},{2,6},{4,0},{6,2},{8,12},{10,14},{12,8},{14,10},{16,20},{18,... | collective-permute-start | bytes 1179656 | tf_op jit(solution)/shard_map/ppermute | solution.py:1241
  684.3 11.2 %copy-start.38 = (bf16[128,1536]{1,0:T(8,128)(2,1)}, bf16[128,1536]{1,0:T(8,128)(2,1)S(1)}, u32[]{:S(2)}) copy-start(bf16[128,1536]{1,0:T(8,128)(2,1)S(1)} %collective-permute-done.17) | copy-start | bytes 1179652
  698.2 17.2 %collective-permute-start.14 = (bf16[128,512]{1,0:T(8,128)(2,1)S(1)}, bf16[128,512]{1,0:T(8,128)(2,1)S(1)}, u32[]{:S(2)}, u32[]{:S(2)}) collective-permute-start(bf16[128,512]{1,0:T(8,128)(2,1)S(1)} %get-tuple-element.175), channel_id=1, source_target_pairs={{0,2},{2,0},{4,6},{6,4},{8,10},{10,8},{12,14},{14,12},{16,18},{18,... | collective-permute-start | bytes 393224 | tf_op jit(solution)/shard_map/ppermute | solution.py:1241
  699.4 16.0 %collective-permute-start.16 = (bf16[128,512]{1,0:T(8,128)(2,1)S(1)}, bf16[128,512]{1,0:T(8,128)(2,1)S(1)}, u32[]{:S(2)}, u32[]{:S(2)}) collective-permute-start(bf16[128,512]{1,0:T(8,128)(2,1)S(1)} %get-tuple-element.176), channel_id=1, source_target_pairs={{0,6},{2,4},{4,2},{6,0},{8,14},{10,12},{12,10},{14,8},{16,22},{18,... | collective-permute-start | bytes 393224 | tf_op jit(solution)/shard_map/ppermute | solution.py:1241
  699.7 15.6 %collective-permute-start.15 = (bf16[128,512]{1,0:T(8,128)(2,1)S(1)}, bf16[128,512]{1,0:T(8,128)(2,1)S(1)}, u32[]{:S(2)}, u32[]{:S(2)}) collective-permute-start(bf16[128,512]{1,0:T(8,128)(2,1)S(1)} %get-tuple-element.177), channel_id=1, source_target_pairs={{0,4},{2,6},{4,0},{6,2},{8,12},{10,14},{12,8},{14,10},{16,20},{18,... | collective-permute-start | bytes 393224 | tf_op jit(solution)/shard_map/ppermute | solution.py:1241
  719.2 4.8 collective-permute-start.7
  720.4 7.4 collective-permute-start.9
  720.7 7.7 collective-permute-start.8
  731.6 10.1 %copy-start.33 = (bf16[1,128,768]{2,1,0:T(8,128)(2,1)S(1)}, bf16[1,128,768]{2,1,0:T(8,128)(2,1)}, u32[]{:S(2)}) copy-start(bf16[1,128,768]{2,1,0:T(8,128)(2,1)} %copy-done.32) | copy-start | bytes 589828
  731.6 10.1 %copy-start.35 = (bf16[1,128,768]{2,1,0:T(8,128)(2,1)S(1)}, bf16[1,128,768]{2,1,0:T(8,128)(2,1)}, u32[]{:S(2)}) copy-start(bf16[1,128,768]{2,1,0:T(8,128)(2,1)} %copy-done.34) | copy-start | bytes 589828
  735.7 6.8 collective-permute-start.10
  736.9 5.6 collective-permute-start.12
  738.0 5.6 collective-permute-start.11
  745.6 11.2 %collective-permute-start.13 = (bf16[4,128,64]{2,1,0:T(8,128)(2,1)}, bf16[4,128,64]{2,1,0:T(8,128)(2,1)}, u32[]{:S(2)}, u32[]{:S(2)}) collective-permute-start(bf16[4,128,64]{2,1,0:T(8,128)(2,1)} %pad_maximum_fusion.8), channel_id=1, source_target_pairs={{0,1},{1,0},{2,3},{3,2},{4,5},{5,4},{6,7},{7,6},{8,9},{9,8},{10,11... | collective-permute-start | bytes 196616 | tf_op jit(solution)/shard_map/ppermute | solution.py:1292
  754.5 6.7 copy-start.1
  (22 other events, 34.0 us)
Sparse Core Ops, SparseCore 0:
  374.2 111.1 reduce-scatter.4
  489.1 41.9 reduce-scatter.6
  535.2 59.7 reduce-scatter.8
  597.3 57.2 reduce-scatter.10

commit v3 on v2

--- a/solution.py
+++ b/solution.py
@@ -36,11 +36,11 @@
     )
 
 
-TP_BITS = (0, 1)
-
-
-def data_bits(n_row):
-    return [b for b in reversed(range(n_row.bit_length() - 1)) if b not in TP_BITS]
+MIX, FFN = (0, 1), (0, 1)
+
+
+def data_bits(n_row, axes):
+    return [b for b in reversed(range(n_row.bit_length() - 1)) if b not in axes]
 
 
 def bit(row, b):
@@ -51,15 +51,15 @@
     return row + (1 << b) * (1 - 2 * bit(row, b))
 
 
-def member(row):
-    return bit(row, TP_BITS[0]) + 2 * bit(row, TP_BITS[1])
-
-
-def partner(row, m):
+def member(row, axes):
+    return bit(row, axes[0]) + 2 * bit(row, axes[1])
+
+
+def partner(row, m, axes):
     if m & 1:
-        row = flip(row, TP_BITS[0])
+        row = flip(row, axes[0])
     if m & 2:
-        row = flip(row, TP_BITS[1])
+        row = flip(row, axes[1])
     return row
 
 
@@ -69,33 +69,33 @@
     return row
 
 
-def group_of(row, n_row):
+def group_of(row, n_row, axes):
     index = 0
-    for b in data_bits(n_row):
+    for b in data_bits(n_row, axes):
         index = index * 2 + bit(row, b)
     return index
 
 
-def spot(row, n_row):
-    return group_of(row, n_row) * TP + member(row)
-
-
 def flips(n_row, mask):
     return [(row, row ^ mask) for row in range(n_row)]
 
 
-def mask_of(m):
-    return (m & 1) * (1 << TP_BITS[0]) + (m // 2) * (1 << TP_BITS[1])
+def mask_of(m, axes):
+    return (m & 1) * (1 << axes[0]) + (m // 2) * (1 << axes[1])
 
 
 def place():
-    r = lax.axis_index("row")
-    c = lax.axis_index("col")
-    return r, c, member(r)
-
-
-def block_of(m):
-    return member(partner(lax.axis_index("row"), m)) * 2
+    return lax.axis_index("row"), lax.axis_index("col")
+
+
+def block_of(m, axes):
+    return member(partner(lax.axis_index("row"), m, axes), axes) * 2
+
+
+def plan_of(axes, slots):
+    if axes != (0, 1) or slots % 32:
+        return [(0, slots, 2, 1)]
+    return [(0, slots // 2, 1, 2), (slots // 2, slots, 2, 1)]
 
 
 def params(number, megabytes):
@@ -114,107 +114,148 @@
     )
 
 
-def greet_group(cross=False):
-    r, c, t = place()
+def greet(*groups, cross=False):
+    r, c = place()
     barrier = pltpu.get_barrier_semaphore()
-    pl.semaphore_signal(barrier, inc=1, device_id=(r, 1 - c), device_id_type=MESH)
-    count = 1
-    for m in (1, 2, 3):
-        pl.semaphore_signal(barrier, inc=1, device_id=(partner(r, m), c), device_id_type=MESH)
-        count += 1
-        if cross:
-            pl.semaphore_signal(
-                barrier, inc=1, device_id=(partner(r, m), 1 - c), device_id_type=MESH
+    others = [(r, 1 - c)]
+    for axes in groups:
+        for m in (1, 2, 3) if cross else (1, 2):
+            others.append((partner(r, m, axes), c))
+            if cross:
+                others.append((partner(r, m, axes), 1 - c))
+    for other in others:
+        pl.semaphore_signal(barrier, inc=1, device_id=other, device_id_type=MESH)
+    pl.semaphore_wait(barrier, len(others))
+
+
+def gather_start(src, out, send, recv, here, axes):
+    r, c = place()
+    own = member(r, axes) * 2 + c
+    copies = [
+        pltpu.make_async_copy(src, out.at[own], here),
+        remote(src, out.at[own], send.at[0], recv.at[0], r, 1 - c),
+    ]
+    for p, (low, high, near, far) in enumerate(plan_of(axes, src.shape[0])):
+        for k, m in ((1, near), (2, far)):
+            copies.append(
+                remote(
+                    src.at[low:high], out.at[own, low:high], send.at[6 * p + k], recv.at[6 * p + k],
+                    partner(r, m, axes), c,
+                )
             )
-            count += 1
-    pl.semaphore_wait(barrier, count)
-
-
-def gather_start(src, out, send, recv, here):
-    r, c, t = place()
-    mine = out.at[t * 2 + c]
-    local = pltpu.make_async_copy(src, mine, here)
-    peers = [
-        remote(src, mine, send.at[m], recv.at[m], partner(r, m), c) for m in (1, 2, 3)
-    ]
-    sibling = remote(src, mine, send.at[0], recv.at[0], r, 1 - c)
-    for copy in (peers[2], peers[0], peers[1], sibling, local):
+    for copy in copies[2:] + copies[:2]:
         copy.start()
-    return peers, sibling, local
-
-
-def gather_finish(started, out, send, recv):
-    r, c, t = place()
-    peers, sibling, local = started
-    forwards = []
-    for m in (1, 2, 3):
-        peers[m - 1].wait_recv()
-        block = out.at[block_of(m) + c]
-        forward = remote(block, block, send.at[3 + m], recv.at[3 + m], r, 1 - c)
-        forward.start()
-        forwards.append(forward)
-    local.wait()
-    sibling.wait()
-    for copy in peers:
+    return copies
+
+
+def gather_finish(copies, out, send, recv, axes):
+    r, c = place()
+    plan = plan_of(axes, out.shape[1])
+    steps = []
+
+    def pass_on(p, k, m, row, col):
+        low, high, near, far = plan[p]
+        part = out.at[block_of(m, axes) + c, low:high]
+        steps.append(remote(part, part, send.at[6 * p + k], recv.at[6 * p + k], row, col))
+        steps[-1].start()
+
+    for p, (low, high, near, far) in enumerate(plan):
+        copies[2 + 2 * p].wait_recv()
+        pass_on(p, 3, near, partner(r, far, axes), c)
+        pass_on(p, 4, near, r, 1 - c)
+    for p, (low, high, near, far) in enumerate(plan):
+        copies[3 + 2 * p].wait_recv()
+        pass_on(p, 5, far, r, 1 - c)
+    for p, (low, high, near, far) in enumerate(plan):
+        steps[2 * p].wait_recv()
+        pass_on(p, 6, 3, r, 1 - c)
+    copies[0].wait()
+    copies[1].wait()
+    for copy in copies[2:] + steps[: 2 * len(plan) : 2]:
         copy.wait_send()
-    for copy in forwards:
-        copy.wait()
+    for i, copy in enumerate(steps):
+        if i >= 2 * len(plan) or i % 2:
+            copy.wait()
 
 
 ROWS = 16
 
 
-def by_rows(count, body):
+def by_rows(count, body, first=0):
     def step(i, carry):
         body(pl.ds(pl.multiple_of(i * ROWS, ROWS), ROWS))
         return carry
 
-    lax.fori_loop(0, count // ROWS, step, 0)
-
-
-def scatter_sum(parts, near, out2, far, s1, r1, s2, r2, total):
-    r, c, t = place()
-    order = (3, 1, 2, 0)
-    first = {}
-    for m in order:
-        first[m] = remote(
-            parts.at[block_of(m) + 1 - c], near.at[m], s1.at[m], r1.at[m], r, 1 - c
+    lax.fori_loop(first // ROWS, count // ROWS, step, 0)
+
+
+def scatter_sum(parts, near, held, far, s1, r1, s2, r2, total, axes):
+    r, c = place()
+    slots = total.shape[0]
+    plan = plan_of(axes, slots)
+    pairs = {}
+    for m in (3, 1, 2, 0):
+        pairs[m] = remote(
+            parts.at[block_of(m, axes) + 1 - c], near.at[m], s1.at[m], r1.at[m], r, 1 - c
         )
-        first[m].start()
-    second = {}
-    for m in order[:3]:
-        first[m].wait_recv()
-        block = block_of(m) + c
-
-        def add(rows, m=m, block=block):
-            out2[m - 1, rows, :] = (
+        pairs[m].start()
+    sent = {}
+
+    def pair_sum(m, i, low, high):
+        block = block_of(m, axes) + c
+
+        def add(rows):
+            held[i, rows, :] = (
                 parts[block, rows, :].astype(jnp.float32) + near[m, rows, :].astype(jnp.float32)
             ).astype(jnp.bfloat16)
 
-        by_rows(total.shape[0], add)
-        second[m] = remote(
-            out2.at[m - 1], far.at[m - 1], s2.at[m - 1], r2.at[m - 1], partner(r, m), c
+        by_rows(high, add, low)
+
+    def send(i, p, m):
+        low, high = plan[p][:2]
+        k = 3 * p + i
+        sent[i, p] = remote(
+            held.at[i, low:high], far.at[i, low:high], s2.at[k], r2.at[k], partner(r, m, axes), c
         )
-        second[m].start()
-    first[0].wait_recv()
-    own = t * 2 + c
-    for m in (1, 2, 3):
-        second[m].wait_recv()
+        sent[i, p].start()
+
+    pairs[3].wait_recv()
+    for p, (low, high, first, then) in enumerate(plan):
+        pair_sum(3, 1, low, high)
+        send(1, p, then)
+    for m in (1, 2):
+        pairs[m].wait_recv()
+        for p, (low, high, first, then) in enumerate(plan):
+            pair_sum(m, 0 if m == then else 2, low, high)
+            if m == then:
+                send(0, p, then)
+    for p, (low, high, first, then) in enumerate(plan):
+        sent[1, p].wait_recv()
+
+        def add(rows):
+            held[2, rows, :] = (
+                held[2, rows, :].astype(jnp.float32) + far[1, rows, :].astype(jnp.float32)
+            ).astype(jnp.bfloat16)
+
+        by_rows(high, add, low)
+        send(2, p, first)
+    pairs[0].wait_recv()
+    for p in range(len(plan)):
+        sent[0, p].wait_recv()
+        sent[2, p].wait_recv()
+    own = member(r, axes) * 2 + c
 
     def fold(rows):
         total[rows, :] = (
             parts[own, rows, :].astype(jnp.float32)
             + near[0, rows, :].astype(jnp.float32)
             + far[0, rows, :].astype(jnp.float32)
-            + far[1, rows, :].astype(jnp.float32)
             + far[2, rows, :].astype(jnp.float32)
         )
 
-    by_rows(total.shape[0], fold)
-    for m in order:
-        first[m].wait_send()
-    for m in (1, 2, 3):
-        second[m].wait_send()
+    by_rows(slots, fold)
+    for copy in list(pairs.values()) + list(sent.values()):
+        copy.wait_send()
 
 
 def scatter_scratch(slots, width):
@@ -224,15 +265,15 @@
         VMEM((TP - 1, slots, width), jnp.bfloat16),
         pltpu.SemaphoreType.DMA((TP,)),
         pltpu.SemaphoreType.DMA((TP,)),
-        pltpu.SemaphoreType.DMA((TP - 1,)),
-        pltpu.SemaphoreType.DMA((TP - 1,)),
+        pltpu.SemaphoreType.DMA((6,)),
+        pltpu.SemaphoreType.DMA((6,)),
     ]
 
 
 def gather_scratch():
     return [
-        pltpu.SemaphoreType.DMA((7,)),
-        pltpu.SemaphoreType.DMA((7,)),
+        pltpu.SemaphoreType.DMA((13,)),
+        pltpu.SemaphoreType.DMA((13,)),
         pltpu.SemaphoreType.DMA,
     ]
 
@@ -252,13 +293,13 @@
         yield ref.at[:, cols], piece.at[:, at : at + count]
 
 
-def cut_start(refs, shared, place_of, send, recv, here):
-    r, c, t = place()
-    for source, target in strip_views(refs, shared, t, place_of()):
+def cut_start(refs, shared, place_of, send, recv, here, axes):
+    r, c = place()
+    for source, target in strip_views(refs, shared, member(r, axes), place_of()):
         pltpu.make_async_copy(source, target, here).start()
     for m in (3, 1, 2):
-        other = partner(r, m)
-        for source, target in strip_views(refs, shared, member(other), place_of()):
+        other = partner(r, m, axes)
+        for source, target in strip_views(refs, shared, member(other, axes), place_of()):
             remote(source, target, send.at[m], recv.at[m], other, c).start()
 
 
@@ -266,41 +307,33 @@
     pltpu.make_async_copy(piece, piece, sem).wait()
 
 
-def cut_finish(place_of, send, recv, here):
-    piece_done(place_of(), here)
-    for m in (3, 1, 2):
-        piece_done(place_of(), send.at[m])
-        piece_done(place_of(), recv.at[m])
-
-
-def weight_copy(whole, mask, b, send, recv):
-    r, c, t = place()
+def weight_orders(n_row, cols):
+    bits = data_bits(n_row, MIX)
+    half = cols // 256 * 128
+    return [(slice(0, half), bits), (slice(half, cols), bits)]
+
+
+def weight_forward(masks, i, whole, send, recv):
+    r, c = place()
     n_row = lax.axis_size("row")
-    at = whole.at[spot(turned_row(r, mask), n_row)]
-    lands = mask | 1 << b
-    return remote(at, at, send.at[lands], recv.at[lands], flip(r, b), c)
-
-
-def weight_forward(masks, whole, send, recv):
-    r, c, t = place()
-    n_row = lax.axis_size("row")
-    bits = data_bits(n_row)
+    cols, bits = weight_orders(n_row, whole.shape[2])[i]
     copies = []
     for mask in masks:
-        at = whole.at[spot(turned_row(r, mask), n_row)]
-        if mask:
-            piece_done(at, recv.at[mask])
-        last = max([-1] + [i for i, b in enumerate(bits) if mask >> b & 1])
-        for b in bits[last + 1 :]:
-            copies.append(weight_copy(whole, mask, b, send, recv))
+        at = whole.at[turned_row(r, mask), :, cols]
+        crossed = [k for k, b in enumerate(bits) if mask >> b & 1]
+        if crossed:
+            piece_done(at, recv.at[i, mask])
+        for b in bits[max([-1] + crossed) + 1 :]:
+            lands = mask | 1 << b
+            copies.append(remote(at, at, send.at[i, lands], recv.at[i, lands], flip(r, b), c))
             copies[-1].start()
     return copies
 
 
-def weight_masks(n_row):
-    held = [mask_of(m) for m in range(TP)]
-    rounds = [held[1:]]
-    for b in data_bits(n_row):
+def weight_rounds(n_row, i, cols):
+    held = [mask_of(m, MIX) for m in range(TP)]
+    rounds = [held]
+    for b in weight_orders(n_row, cols)[i][1]:
         rounds.append([mask | 1 << b for mask in held])
         held = held + rounds[-1]
     return rounds
@@ -308,10 +341,10 @@
 
 def place_kernel(masks, n_row, *refs):
     slabs, whole, sems = refs[: len(masks)], refs[-2], refs[-1]
-    r, c, t = place()
+    r, c = place()
     copies = []
     for i, mask in enumerate(masks):
-        at = whole.at[group_of(turned_row(r, mask), n_row)]
+        at = whole.at[group_of(turned_row(r, mask), n_row, FFN)]
         copies.append(pltpu.make_async_copy(slabs[i], at, sems.at[i]))
         copies[-1].start()
     for copy in copies:
@@ -332,7 +365,7 @@
 
 
 def exchange_rows(buf, land, send, recv):
-    r, c, t = place()
+    r, c = place()
     n_row = lax.axis_size("row")
 
     def copy(other):
@@ -348,7 +381,7 @@
 
 
 def finish_rows(buf, land, send, recv):
-    r, c, t = place()
+    r, c = place()
     n_row = lax.axis_size("row")
 
     def finish(off, carry):
@@ -362,7 +395,7 @@
 
 
 def greet_rows():
-    r, c, t = place()
+    r, c = place()
     n_row = lax.axis_size("row")
     barrier = pltpu.get_barrier_semaphore()
 
@@ -408,13 +441,14 @@
 def deal_kernel(
     meta, tokens, cotangent, gain, *refs
 ):
-    in_refs, ff_refs, refs = refs[:8], refs[8:11], refs[11:]
-    meta_all, give, take, x_out, gy_out, normed_all, gy_all, whole, slab_ff = refs[:9]
-    x_mine, g_mine, buf, land, normed = refs[9:14]
-    load, msend, mrecv, csend, crecv, nsend, nrecv, nhere, gsend, grecv, ghere = refs[14:25]
-    wsend, wrecv, wcut, whole_here, fsend, frecv, fhere = refs[25:]
-    r, c, t = place()
+    in_refs, up_refs, down_refs, refs = refs[:8], refs[8:10], refs[10:11], refs[11:]
+    meta_all, give, take, x_out, gy_out, normed_all, gy_all, whole, slab_up, slab_down = refs[:10]
+    x_mine, g_mine, buf, land, normed = refs[10:15]
+    load, msend, mrecv, csend, crecv, nsend, nrecv, nhere, gsend, grecv, ghere = refs[15:26]
+    wsend, wrecv, wcut, wcut_recv, whole_here, usend, urecv, uhere, dsend, drecv, dhere = refs[26:]
+    r, c = place()
     n_row = lax.axis_size("row")
+    f = member(r, FFN)
     slots = x_mine.shape[0]
     per_peer = slots // n_row
     loads = [
@@ -424,11 +458,11 @@
     for copy in loads:
         copy.start()
     greet_rows()
-    rounds = weight_masks(n_row)
+    rounds = [weight_rounds(n_row, i, whole.shape[2]) for i in (0, 1)]
     in_shared = [False, False, False, True, True, False, False, False]
 
     def in_place():
-        return whole.at[spot(r, n_row)]
+        return whole.at[r]
 
     def meta_copy(other, slot):
         return remote(meta, meta_all.at[slot], msend.at[other], mrecv.at[slot], other, c)
@@ -448,14 +482,11 @@
         return carry
 
     lax.fori_loop(1, n_row, finish, 0)
-    for source, target in strip_views(in_refs, in_shared, t, in_place()):
-        pltpu.make_async_copy(source, target, whole_here).start()
-    for m in (3, 1, 2):
-        other = partner(r, m)
-        for source, target in strip_views(in_refs, in_shared, member(other), in_place()):
-            remote(source, target, wcut.at[m], wrecv.at[mask_of(m)], other, c).start()
+    cut_start(in_refs, in_shared, in_place, wcut, wcut_recv, whole_here, MIX)
     piece_done(in_place(), whole_here)
-    forwards = weight_forward([0], whole, wsend, wrecv)
+    forwards = []
+    for i in (0, 1):
+        forwards = forwards + weight_forward([0], i, whole, wsend, wrecv)
 
     shift = slots.bit_length() - 1
     row_no = lax.broadcasted_iota(jnp.int32, (CHUNK, slots), 0)
@@ -502,7 +533,10 @@
     permute_out(give, buf, x_mine, g_mine, slots)
     exchange_rows(buf, land, csend, crecv)
     land[r] = buf[r]
-    forwards = forwards + weight_forward(rounds[0], whole, wsend, wrecv)
+    for m in (1, 2, 3):
+        piece_done(in_place(), wcut_recv.at[m])
+        for i in (0, 1):
+            forwards = forwards + weight_forward([mask_of(m, MIX)], i, whole, wsend, wrecv)
     finish_rows(buf, land, csend, crecv)
     permute_in(take, land, x_out, gy_out, slots)
 
@@ -512,18 +546,24 @@
         normed[rows, :] = (values * scale * gain[...]).astype(jnp.bfloat16)
 
     by_rows(slots, norm)
-    first = gather_start(normed, normed_all, nsend, nrecv, nhere)
-    cut_start(ff_refs, [False] * 3, lambda: slab_ff.at[t], fsend, frecv, fhere)
-    second = gather_start(gy_out, gy_all, gsend, grecv, ghere)
-    for masks in rounds[1:]:
-        forwards = forwards + weight_forward(masks, whole, wsend, wrecv)
-    gather_finish(first, normed_all, nsend, nrecv)
-    gather_finish(second, gy_all, gsend, grecv)
+    first = gather_start(normed, normed_all, nsend, nrecv, nhere, MIX)
+    cut_start(up_refs, [False] * 2, lambda: slab_up.at[f], usend, urecv, uhere, FFN)
+    cut_start(down_refs, [False], lambda: slab_down.at[f], dsend, drecv, dhere, FFN)
+    second = gather_start(gy_out, gy_all, gsend, grecv, ghere, FFN)
+    for k in range(1, len(rounds[0])):
+        for i in (0, 1):
+            forwards = forwards + weight_forward(rounds[i][k], i, whole, wsend, wrecv)
+    gather_finish(first, normed_all, nsend, nrecv, MIX)
+    gather_finish(second, gy_all, gsend, grecv, FFN)
     for copy in forwards:
         copy.wait_send()
     for m in (1, 2, 3):
         piece_done(in_place(), wcut.at[m])
-    cut_finish(lambda: slab_ff.at[t], fsend, frecv, fhere)
+    for slab, send, recv, here in ((slab_up, usend, urecv, uhere), (slab_down, dsend, drecv, dhere)):
+        piece_done(slab.at[f], here)
+        for m in (1, 2, 3):
+            piece_done(slab.at[f], send.at[m])
+            piece_done(slab.at[f], recv.at[m])
 
 
 def deal(meta, tokens, cotangent, gain, in_weights, ff_weights, n_row):
@@ -533,7 +573,7 @@
     in_cols = sum(
         array.shape[1] // (1 if i in (3, 4) else TP) for i, array in enumerate(in_weights)
     )
-    ff_cols = sum(array.shape[1] for array in ff_weights) // TP
+    up_cols, down_cols = 2 * ff_weights[0].shape[1] // TP, ff_weights[2].shape[1] // TP
     vm, hb = pl.BlockSpec(memory_space=VMEM), pl.BlockSpec(memory_space=ANY)
     dma = pltpu.SemaphoreType.DMA
     return pl.pallas_call(
@@ -548,10 +588,11 @@
             jax.ShapeDtypeStruct((GROUP, slots, width), bf),
             jax.ShapeDtypeStruct((GROUP, slots, width), bf),
             jax.ShapeDtypeStruct((n_row, rows, in_cols), bf),
-            jax.ShapeDtypeStruct((TP, rows, ff_cols), bf),
+            jax.ShapeDtypeStruct((TP, rows, up_cols), bf),
+            jax.ShapeDtypeStruct((TP, rows, down_cols), bf),
         ),
         in_specs=[vm, hb, hb, vm] + [hb] * 11,
-        out_specs=(vm,) * 5 + (hb,) * 4,
+        out_specs=(vm,) * 5 + (hb,) * 5,
         scratch_shapes=[
             VMEM((slots, width), bf),
             VMEM((slots, width), bf),
@@ -566,16 +607,16 @@
         ]
         + gather_scratch()
         + gather_scratch()
-        + [dma((n_row,)), dma((n_row,)), dma((TP,)), dma]
-        + [dma((TP,)), dma((TP,)), dma],
+        + [dma((2, n_row)), dma((2, n_row))]
+        + [dma((TP,)), dma((TP,)), dma] * 3,
         compiler_params=params(0, 40),
         cost_estimate=cost(100),
     )(meta, tokens, cotangent, gain, *in_weights, *ff_weights)
 
 
 def middle_kernel(parts, x, gain, mid, normed_all, near, out2, far, s1, r1, s2, r2, normed, nsend, nrecv, nhere):
-    greet_group()
-    scatter_sum(parts, near, out2, far, s1, r1, s2, r2, mid)
+    greet(*{MIX, FFN})
+    scatter_sum(parts, near, out2, far, s1, r1, s2, r2, mid, MIX)
 
     def norm(rows):
         values = x[rows, :].astype(jnp.float32) + mid[rows, :]
@@ -584,8 +625,8 @@
         normed[rows, :] = (values * scale * gain[...]).astype(jnp.bfloat16)
 
     by_rows(mid.shape[0], norm)
-    started = gather_start(normed, normed_all, nsend, nrecv, nhere)
-    gather_finish(started, normed_all, nsend, nrecv)
+    started = gather_start(normed, normed_all, nsend, nrecv, nhere, FFN)
+    gather_finish(started, normed_all, nsend, nrecv, FFN)
 
 
 def middle(parts, x, gain):
@@ -620,8 +661,8 @@
     parts, mid, gy, gain, d_mid, d_gain, branch_all,
     near, out2, far, s1, r1, s2, r2, branch, nsend, nrecv, nhere,
 ):
-    greet_group()
-    scatter_sum(parts, near, out2, far, s1, r1, s2, r2, d_mid)
+    greet(*{MIX, FFN})
+    scatter_sum(parts, near, out2, far, s1, r1, s2, r2, d_mid, FFN)
     d_gain[...] = jnp.zeros_like(d_gain)
 
     def back(rows):
@@ -633,8 +674,8 @@
         d_gain[...] += gain_part
 
     by_rows(mid.shape[0], back)
-    started = gather_start(branch, branch_all, nsend, nrecv, nhere)
-    gather_finish(started, branch_all, nsend, nrecv)
+    started = gather_start(branch, branch_all, nsend, nrecv, nhere, MIX)
+    gather_finish(started, branch_all, nsend, nrecv, MIX)
 
 
 def turn(parts, mid, gy, gain):
@@ -658,15 +699,17 @@
 
 
 def home_kernel(
-    parts, x, d_mid, result, gain, give, take, small, output, gradient, small_all,
+    parts, x, d_mid, result, gain, give, take, small, ff_sums,
+    output, gradient, small_all, ff_land,
     near, out2, far, s1, r1, s2, r2, total, first, second, buf, land, csend, crecv, here, osend, orecv,
-    d_gain, stages, stage_land, tsend, trecv, gsend, grecv, ghere,
+    d_gain, stages, stage_land, tsend, trecv, gsend, grecv, ghere, *more
 ):
-    r, c, t = place()
+    r, c = place()
     slots, width = x.shape
-    bits = data_bits(lax.axis_size("row"))
+    bits = data_bits(lax.axis_size("row"), MIX)
     greet_rows()
-    scatter_sum(parts, near, out2, far, s1, r1, s2, r2, total)
+    delivered = deliver(ff_sums, ff_land, *more, FFN)
+    scatter_sum(parts, near, out2, far, s1, r1, s2, r2, total, MIX)
     d_gain[...] = jnp.zeros_like(d_gain)
 
     def back(rows):
@@ -696,7 +739,7 @@
         stages[i + 1] = stages[i] + stage_land[i]
         if i + 1 < len(bits):
             stage_copy(i + 1).start()
-    started = gather_start(stages.at[len(bits)], small_all, gsend, grecv, ghere)
+    started = gather_start(stages.at[len(bits)], small_all, gsend, grecv, ghere, MIX)
     finish_rows(buf, land, csend, crecv)
     permute_in(give, land, first, second, slots)
     copies = []
@@ -705,16 +748,109 @@
         copies.append(remote(mine, out.at[c], osend.at[i], orecv.at[i], r, 1 - c))
     for copy in copies:
         copy.start()
-    gather_finish(started, small_all, gsend, grecv)
+    gather_finish(started, small_all, gsend, grecv, MIX)
+    for copy in copies + delivered:
+        copy.wait()
+
+
+def deliver(sums, land, send, recv, here, axes):
+    r, c = place()
+    own = member(r, axes)
+    copies = [pltpu.make_async_copy(sums.at[own], land.at[own], here)]
+    for m in (3, 1, 2):
+        other = partner(r, m, axes)
+        copies.append(
+            remote(sums.at[member(other, axes)], land.at[own], send.at[m], recv.at[m], other, c)
+        )
     for copy in copies:
+        copy.start()
+    return copies
+
+
+def deliver_scratch():
+    dma = pltpu.SemaphoreType.DMA
+    return [dma((TP,)), dma((TP,)), dma]
+
+
+def last_kernel(at, sums, land, other, s1, r1, here, send, recv):
+    r, c = place()
+    barrier = pltpu.get_barrier_semaphore()
+    for m in (1, 2, 3):
+        pl.semaphore_signal(barrier, inc=1, device_id=(partner(r, m, MIX), c), device_id_type=MESH)
+    pl.semaphore_signal(barrier, inc=1, device_id=(r, 1 - c), device_id_type=MESH)
+    pl.semaphore_wait(barrier, 4)
+    for copy in deliver(sums, land, s1, r1, here, MIX):
         copy.wait()
-
-
-def send_home(parts, x, d_mid, result, gain, give, take, small, n_row):
+    across = remote(land.at[:, :, at : at + 128], other, send, recv, r, 1 - c)
+    across.start()
+    across.wait()
+
+
+def last(sums, at):
+    hb = pl.BlockSpec(memory_space=ANY)
+    dma = pltpu.SemaphoreType.DMA
+    return pl.pallas_call(
+        partial(last_kernel, at),
+        name="last",
+        out_shape=(
+            jax.ShapeDtypeStruct(sums.shape, sums.dtype),
+            jax.ShapeDtypeStruct(sums.shape[:2] + (128,), sums.dtype),
+        ),
+        in_specs=[hb],
+        out_specs=(hb,) * 2,
+        scratch_shapes=deliver_scratch() + [dma, dma],
+        compiler_params=params(6, 4),
+        cost_estimate=cost(25),
+    )(sums)
+
+
+def unpack_kernel(
+    ff, mixer, gate, up, down, mamba_gate, mamba_input, query, key, value, mamba_out, attn_out
+):
+    f32 = jnp.float32
+    mh = mamba_gate.shape[1] // TP
+    fh = gate.shape[1] // TP
+    qh = query.shape[1] // TP
+    kv = key.shape[1]
+    at = 2 * mh + qh
+    out = mixer.shape[2] - mh - qh
+    for m in range(TP):
+        def cols(size):
+            return slice(m * size, (m + 1) * size)
+
+        gate[:, cols(fh)] = ff[m, :, :fh].astype(f32)
+        up[:, cols(fh)] = ff[m, :, fh : 2 * fh].astype(f32)
+        down[cols(fh), :] = ff[m, :, 2 * fh :].astype(f32).T
+        mamba_gate[:, cols(mh)] = mixer[m, :, :mh].astype(f32)
+        mamba_input[:, cols(mh)] = mixer[m, :, mh : 2 * mh].astype(f32)
+        query[:, cols(qh)] = mixer[m, :, 2 * mh : at].astype(f32)
+        mamba_out[cols(mh), :] = mixer[m, :, out : out + mh].astype(f32).T
+        attn_out[cols(qh), :] = mixer[m, :, out + mh :].astype(f32).T
+    key[...] = sum(mixer[m, :, at : at + kv].astype(f32) for m in range(TP))
+    value[...] = sum(mixer[m, :, at + kv : at + 2 * kv].astype(f32) for m in range(TP))
+
+
+def unpack(ff, mixer, mh, qh, kv, fh):
+    rows = ff.shape[1]
+    vm = pl.BlockSpec(memory_space=VMEM)
+    shapes = [(rows, TP * fh)] * 2 + [(TP * fh, rows)] + [(rows, TP * mh)] * 2
+    shapes += [(rows, TP * qh), (rows, kv), (rows, kv), (TP * mh, rows), (TP * qh, rows)]
+    return pl.pallas_call(
+        unpack_kernel,
+        name="unpack",
+        out_shape=tuple(jax.ShapeDtypeStruct(shape, jnp.float32) for shape in shapes),
+        in_specs=[vm] * 2,
+        out_specs=(vm,) * len(shapes),
+        compiler_params=pltpu.CompilerParams(vmem_limit_bytes=40 << 20),
+        cost_estimate=cost(8),
+    )(ff, mixer)
+
+
+def send_home(parts, x, d_mid, result, gain, give, take, small, ff_sums, n_row):
     slots, width = x.shape
     bf = jnp.bfloat16
     size = small.shape[0] + width // 128
-    phases = len(data_bits(n_row))
+    phases = len(data_bits(n_row, MIX))
     return pl.pallas_call(
         home_kernel,
         name="home",
@@ -722,9 +858,10 @@
             jax.ShapeDtypeStruct((2, slots, width), bf),
             jax.ShapeDtypeStruct((2, slots, width), bf),
             jax.ShapeDtypeStruct((GROUP, size, 128), jnp.float32),
+            jax.ShapeDtypeStruct(ff_sums.shape, bf),
         ),
-        in_specs=[pl.BlockSpec(memory_space=VMEM)] * 8,
-        out_specs=(pl.BlockSpec(memory_space=ANY),) * 3,
+        in_specs=[pl.BlockSpec(memory_space=VMEM)] * 8 + [pl.BlockSpec(memory_space=ANY)],
+        out_specs=(pl.BlockSpec(memory_space=ANY),) * 4,
         scratch_shapes=scatter_scratch(slots, width)
         + [
             VMEM((slots, width), jnp.float32),
@@ -743,28 +880,29 @@
             pltpu.SemaphoreType.DMA((phases,)),
             pltpu.SemaphoreType.DMA((phases,)),
         ]
-        + gather_scratch(),
+        + gather_scratch()
+        + deliver_scratch(),
         compiler_params=params(3, 48),
         cost_estimate=cost(75),
-    )(parts, x, d_mid, result, gain, give, take, small)
+    )(parts, x, d_mid, result, gain, give, take, small, ff_sums)
 
 
 def blocks_start(low, land, s1, r1):
-    r, c, t = place()
+    r, c = place()
     copies = []
     for m, f in CROSSED:
         col = 1 - c if f else c
         k = m * 2 + f
         copies.append(
-            remote(low.at[block_of(m) + col], land.at[k], s1.at[k], r1.at[k], partner(r, m), col)
+            remote(low.at[block_of(m, MIX) + col], land.at[k], s1.at[k], r1.at[k], partner(r, m, MIX), col)
         )
         copies[-1].start()
     return copies
 
 
 def blocks_turn(first, low, land, mine, total, s2, r2, here):
-    r, c, t = place()
-    own = t * 2 + c
+    r, c = place()
+    own = member(r, MIX) * 2 + c
     for copy in first:
         copy.wait_recv()
     summed = low[own].astype(jnp.float32)
@@ -775,7 +913,7 @@
     for m, f in CROSSED:
         k = m * 2 + f
         copies.append(
-            remote(mine, total.at[own], s2.at[k], r2.at[k], partner(r, m), 1 - c if f else c)
+            remote(mine, total.at[own], s2.at[k], r2.at[k], partner(r, m, MIX), 1 - c if f else c)
         )
     for copy in copies:
         copy.start()
@@ -932,7 +1070,7 @@
     slots = crossed.shape[1]
     mh = chan.shape[1]
     heads_at = 2 * sh
-    greet_group(cross=True)
+    greet(MIX, cross=True)
 
     def before(b):
         rows = block_rows(b, slots)
@@ -1010,7 +1148,7 @@
     mh = chan.shape[1]
     heads_at = 2 * sh
     bf = jnp.bfloat16
-    greet_group(cross=True)
+    greet(MIX, cross=True)
     chan_sums[...] = jnp.zeros_like(chan_sums)
     side_sums[...] = jnp.zeros_like(side_sums)
 
@@ -1175,8 +1313,7 @@
     n_row = lax.axis_size("row")
     r = lax.axis_index("row")
     c = lax.axis_index("col")
-    t = member(r)
-    bits = data_bits(n_row)
+    t = member(r, MIX)
     n_bits = n_row.bit_length() - 1
     slots, width = tokens.shape[1:]
     bf = jnp.bfloat16
@@ -1208,12 +1345,15 @@
     )
     ff_weights = (gate_weight, up_weight, down_weight.T)
 
-    def assemble(slab):
+    def assemble(slab, after):
         held = [(0, slab)]
-        for b in bits:
-            held = held + [
-                (mask | 1 << b, lax.ppermute(part, "row", flips(n_row, 1 << b))) for mask, part in held
-            ]
+        for b in data_bits(n_row, FFN):
+            next_held = []
+            for mask, part in held:
+                if mask:
+                    part, unused_value = lax.optimization_barrier((part, after))
+                next_held.append((mask | 1 << b, lax.ppermute(part, "row", flips(n_row, 1 << b))))
+            held = held + next_held
         return place_slabs(
             [mask for mask, part in held], [part for mask, part in held], n_row
         ).reshape(n_row * rows, slab.shape[2])
@@ -1221,53 +1361,24 @@
     def pick(array, index, axis=0):
         return lax.dynamic_index_in_dim(array, index, axis, keepdims=False)
 
-    by_group = sorted(range(n_row), key=lambda row: [row >> b & 1 for b in bits])
-    alike = [
-        [row for row in by_group if [row >> b & 1 for b in TP_BITS] == [m & 1, m >> 1]]
-        for m in range(TP)
-    ]
-
-    def sum_groups(grad, after=None):
+    def sum_groups(grad, axes, after=None):
         grad = grad.astype(bf)
+        bits = data_bits(n_row, axes)
+        order = [n_bits - 1 - b for b in bits + [axes[1], axes[0]]]
+        if order != sorted(order):
+            cutup = grad.reshape((2,) * n_bits + (rows, grad.shape[1]))
+            grad = cutup.transpose(order + [n_bits, n_bits + 1]).reshape(grad.shape)
         if after is not None:
             grad, after = lax.optimization_barrier((grad, after))
+        by_group = sorted(range(n_row), key=lambda row: [row >> b & 1 for b in bits])
+        alike = [
+            [row for row in by_group if [row >> b & 1 for b in axes] == [m & 1, m >> 1]]
+            for m in range(TP)
+        ]
         part = lax.psum_scatter(
             grad, "row", scatter_dimension=0, axis_index_groups=alike, tiled=True
         ).reshape(TP, rows, grad.shape[1])
         return part, after
-
-    def disperse(part):
-        near = [pick(part, t)] + [
-            lax.ppermute(pick(part, member(partner(r, m))), "row", flips(n_row, mask_of(m)))
-            for m in (1, 2, 3)
-        ]
-        low, high = bit(r, TP_BITS[0]), bit(r, TP_BITS[1])
-
-        def of(owner):
-            inner = [
-                jnp.where(low == owner % 2, near[2 * k], near[2 * k + 1]) for k in range(2)
-            ]
-            return jnp.where(high == owner // 2, inner[0], inner[1])
-
-        return jnp.stack([of(owner) for owner in range(TP)])
-
-    order = [n_bits - 1 - b for b in bits] + [n_bits - 1 - b for b in reversed(TP_BITS)]
-
-    def regroup(array):
-        lead = array.shape[:-1]
-        cutup = array.reshape(lead + (2,) * n_bits + (rows,))
-        dims = list(range(len(lead))) + [len(lead) + i for i in order] + [len(lead) + n_bits]
-        return cutup.transpose(dims).reshape(array.shape)
-
-    def ungroup(array):
-        lead = array.shape[:-1]
-        cutup = array.reshape(lead + (2,) * n_bits + (rows,))
-        back = [order.index(i) for i in range(n_bits)]
-        dims = list(range(len(lead))) + [len(lead) + i for i in back] + [len(lead) + n_bits]
-        return cutup.transpose(dims).reshape(array.shape)
-
-    mixer_gain = regroup(mixer_norm_gain)[None, :]
-    ff_gain = regroup(ff_norm_gain)[None, :]
 
     meta = jnp.concatenate(
         [
@@ -1277,22 +1388,19 @@
         ],
         axis=0,
     )
-    meta_all, give, take, x_home, gy_home, normed_one, gy_all, w_mixer, slab_ff = deal(
-        meta, regroup(tokens), regroup(cotangent), mixer_gain, in_weights, ff_weights, n_row
+    meta_all, give, take, x_home, gy_home, normed_one, gy_all, w_mixer, slab_up, slab_down = deal(
+        meta, tokens, cotangent, mixer_norm_gain[None, :], in_weights, ff_weights, n_row
     )
     normed_one = normed_one.reshape(GROUP * slots, width)
     gy_all = gy_all.reshape(GROUP * slots, width)
     w_mixer = w_mixer.reshape(width, -1)
     w_in, w_out = w_mixer[:, : used + spare], w_mixer[:, used + spare :]
-    w_ff = assemble(slab_ff)
-    w_gate_up = w_ff[:, : 2 * fh]
-    w_down = w_ff[:, 2 * fh :]
 
     def across(array):
         return lax.ppermute(array, "col", [(0, 1), (1, 0)])
 
-    base = r - bit(r, TP_BITS[0]) * (1 << TP_BITS[0]) - bit(r, TP_BITS[1]) * (1 << TP_BITS[1])
-    group_meta = jnp.stack([pick(meta_all, base + mask_of(m)) for m in range(TP)])
+    base = r - sum(bit(r, b) * (1 << b) for b in MIX)
+    group_meta = jnp.stack([pick(meta_all, base + mask_of(m, MIX)) for m in range(TP)])
     lengths = group_meta[:, 2:4, : seq_lengths.shape[2]].reshape(GROUP, seq_lengths.shape[2])
     half_dim = HD // 2
     inverse = ROPE_BASE ** (-2.0 * jnp.arange(half_dim, dtype=jnp.float32) / HD)
@@ -1335,8 +1443,11 @@
     edges = edges + [edges[-1] + 2 * sh, edges[-1] + 2 * sh + ph]
     branch_in, scanned, crossed = mixer(lengths, projected, chan, side, table, sh, ph)
     branch_part = matmul_trans(branch_in, w_out).astype(bf).reshape(GROUP, slots, width)
+    ff_gain = ff_norm_gain[None, :]
     mid, normed_two = middle(branch_part, x_home, ff_gain)
     normed_two = normed_two.reshape(GROUP * slots, width)
+    w_gate_up = assemble(slab_up, branch_part)
+    w_down = assemble(slab_down, normed_two)
 
     ff_gate_up = matmul(normed_two, w_gate_up)
     ff_gate, ff_up = ff_gate_up[:, :fh], ff_gate_up[:, fh:]
@@ -1354,7 +1465,7 @@
         axis=1,
     )
     normed_two_part, grad_ff = lax.optimization_barrier((normed_two_part, grad_ff))
-    ff_sums, unused_value = sum_groups(grad_ff)
+    ff_sums, unused_value = sum_groups(grad_ff, FFN)
     d_mid, delta_ff_gain, branch_all = turn(
         normed_two_part, mid, gy_home, ff_gain
     )
@@ -1363,26 +1474,27 @@
         pick(ff_pairs, c, 1).astype(jnp.float32)
         + across(pick(ff_pairs, 1 - c, 1)).astype(jnp.float32)
     ).astype(bf)
-    result = mid + pick(ff_sum, t).astype(jnp.float32)
+    result = mid + pick(ff_sum, member(r, FFN)).astype(jnp.float32)
     for m in (1, 2, 3):
         result = result + lax.ppermute(
-            pick(ff_sum, member(partner(r, m))), "row", flips(n_row, mask_of(m))
+            pick(ff_sum, member(partner(r, m, FFN), FFN)), "row", flips(n_row, mask_of(m, FFN))
         ).astype(jnp.float32)
     result = result.astype(bf)
     branch_all = branch_all.reshape(GROUP * slots, width)
 
-    out_sums, ff_sums = sum_groups(matmul_left(branch_all, branch_in), ff_sums)
     grad_branch_in = matmul(branch_all, w_out)
     grad_projected, chan_sums, side_sums = mixer_back(
         lengths, projected, chan, side, table, scanned, crossed, grad_branch_in, sh, ph
     )
-    early = jnp.concatenate([grad_projected[:, :mh], grad_projected[:, 2 * mh : edges[5]]], axis=1)
-    early_sums, out_sums = sum_groups(matmul_left(normed_one, early), out_sums)
-    grad_late = matmul_left(
-        normed_one, jnp.concatenate([grad_projected[:, mh : 2 * mh], grad_projected[:, edges[5] :]], axis=1)
-    ).astype(bf)
-    grad_projected, grad_late = lax.optimization_barrier((grad_projected, grad_late))
-    late_sums, early_sums = sum_groups(grad_late, early_sums)
+    grad_mixer = jnp.concatenate(
+        [
+            matmul_left(normed_one, grad_projected).astype(bf),
+            matmul_left(branch_all, branch_in).astype(bf),
+        ],
+        axis=1,
+    )
+    grad_projected, grad_mixer = lax.optimization_barrier((grad_projected, grad_mixer))
+    mixer_sums, ff_sums = sum_groups(grad_mixer, MIX, ff_sums)
     normed_one_part = matmul_trans(grad_projected, w_in).astype(bf).reshape(GROUP, slots, width)
 
     def lanes(array):
@@ -1407,36 +1519,32 @@
     small_parts.append(jnp.zeros((-sum(counts) % 8, 128), jnp.float32))
     starts = [sum(counts[:i]) for i in range(len(counts))]
     starts[-1] += small_parts[-1].shape[0]
-    output, grad_tokens, small_all = send_home(
-        normed_one_part, x_home, d_mid, result, mixer_gain, give, take,
-        jnp.concatenate(small_parts, axis=0), n_row,
-    )
-    delta_ff, delta_out, delta_early, delta_late = (
-        disperse(part) for part in (ff_sums, out_sums, early_sums, late_sums)
-    )
-    delta_in = jnp.concatenate(
-        [delta_early[:, :, :mh], delta_late[:, :, :mh], delta_early[:, :, mh:], delta_late[:, :, mh:]], axis=2
-    )
+    output, grad_tokens, small_all, ff_land = send_home(
+        normed_one_part, x_home, d_mid, result, mixer_norm_gain[None, :], give, take,
+        jnp.concatenate(small_parts, axis=0), ff_sums, n_row,
+    )
+    mixer_land, other_land = last(mixer_sums, edges[5])
+    (
+        delta_gate, delta_up, delta_down, delta_mamba_gate, delta_mamba_input,
+        delta_query, delta_key, delta_value, delta_mamba_out, delta_attn_out,
+    ) = unpack(ff_land, mixer_land, mh, qh, kvh, fh)
 
     def join(stacked):
         return stacked.transpose(1, 0, 2).reshape(stacked.shape[1], -1).astype(jnp.float32)
 
-    pieces = [delta_in[:, :, low:high] for low, high in zip(edges[:-1], edges[1:])]
-    state_mine = pieces[5]
-    state_other = across(state_mine)
-    state_first = jnp.where(c == 0, state_mine, state_other)
-    state_second = jnp.where(c == 0, state_other, state_mine)
+    mine = mixer_land[:, :, edges[5] : edges[5] + 128]
+    state_first = jnp.where(c == 0, mine, other_land)
+    state_second = jnp.where(c == 0, other_land, mine)
     delta_state = jnp.concatenate(
         [
             join(state_first[:, :, :sh]),
             join(state_second[:, :, :sh]),
-            join(state_first[:, :, sh:]),
-            join(state_second[:, :, sh:]),
+            join(state_first[:, :, sh : 2 * sh]),
+            join(state_second[:, :, sh : 2 * sh]),
         ],
         axis=1,
     )
-    delta_key = jnp.sum(pieces[3].astype(jnp.float32), axis=0)
-    delta_value = jnp.sum(pieces[4].astype(jnp.float32), axis=0)
+    delta_step = join(mine[:, :, 2 * sh : 2 * sh + ph])
 
     small_all = small_all.reshape(TP, 2, -1, 128)
     small_col = pick(small_all, c, 1)
@@ -1453,7 +1561,7 @@
         return got.transpose(2, 3, 1, 0, 4).reshape(got.shape[2], 2 * half)
 
     def over_all(i):
-        return ungroup(jnp.sum(taken(small_all, i), axis=(0, 1)).reshape(width))
+        return jnp.sum(taken(small_all, i), axis=(0, 1)).reshape(width)
 
     by_col = [
         along(small_col, 0, mh),
@@ -1465,13 +1573,13 @@
     by_all = [state_along(5), state_along(6)[0], over_all(8), over_all(7)]
 
     return (
-        ungroup(output),
-        ungroup(grad_tokens),
+        output,
+        grad_tokens,
         by_all[2],
-        join(pieces[0]),
-        join(pieces[1]),
+        delta_mamba_gate,
+        delta_mamba_input,
         delta_state,
-        join(pieces[6]),
+        delta_step,
         by_col[0],
         by_col[1],
         by_all[0],
@@ -1479,15 +1587,15 @@
         by_col[2],
         by_col[3],
         by_col[4],
-        join(delta_out[:, :, :mh]).T,
-        join(pieces[2]),
+        delta_mamba_out,
+        delta_query,
         delta_key,
         delta_value,
-        join(delta_out[:, :, mh:]).T,
+        delta_attn_out,
         by_all[3],
-        join(delta_ff[:, :, :fh]),
-        join(delta_ff[:, :, fh : 2 * fh]),
-        join(delta_ff[:, :, 2 * fh :]).T,
+        delta_gate,
+        delta_up,
+        delta_down,
     )
 
 

time: 777 us -> 657 us (0.85)
  waiting for transfers between devices: 155 us -> 32 us
  Pallas kernels: 395 us -> 458 us
  local copies, waits for them, and re-layouts: 79.7 us -> 47 us
  starting transfers between devices: 25.2 us -> 10.2 us
    reduce_scatter x4 -> x2, waiting for transfers between devices: 68.7 us -> 0.01 us  [sum_groups(): lax.psum_scatter(grad, 'row', scatter_dimension=0, axis_index_groups=alik...]
    ppermute x3 -> x6, waiting for transfers between devices: 66 us -> 14.5 us  [assemble(): lax.ppermute(part, 'row', flips(n_row, 1 << b))]
    pallas_call x1, Pallas kernels: 67.3 us -> 105 us  [send_home(): pl.pallas_call(home_kernel, name='home', out_shape=(jax.ShapeDtypeStruct(...]
    pallas_call x0 -> x2, Pallas kernels: none -> 28.2 us  [the longest x1 25.2 us: last(): pl.pallas_call(partial(last_kernel, at), name='last', out_shape=(jax.Shap...]
    ppermute x15 -> x3, starting transfers between devices: 16.2 us -> 2.65 us  [local(): lax.ppermute(pick(ff_sum, member(partner(r, m, FFN), FFN)), 'row', flips(...]
    pallas_call x1, Pallas kernels: 153 us -> 165 us  [deal(): pl.pallas_call(deal_kernel, name='deal', out_shape=(jax.ShapeDtypeStruct(...]
    pallas_call x1, Pallas kernels: 57.1 us -> 45.7 us  [middle(): pl.pallas_call(middle_kernel, name='middle', out_shape=(jax.ShapeDtypeStr...]
    convert_element_type x13 -> x8, local copies, waits for them, and re-layouts: 10.7 us -> 1.33 us  [join(): stacked.transpose(1, 0, 2).reshape(stacked.shape[1], -1).astype(jnp.float32)]
  transfers between devices with their start and end apart: 24 -> 12, of which waited for: 10 -> 5; matrix products, arithmetic and copies ran while one was open for 15% -> 11% of each run, Pallas kernels for 31% -> 40%
where the time goes in v3:
time: 657 us; the launch traced here: 648 us
  Pallas kernels  458 us (70%)
  matrix products  67.6 us (10%)
  local copies, waits for them, and re-layouts  47 us (7%)
  waiting for transfers between devices  32 us (5%)
  other arithmetic  18.6 us (3%)
  between operations  15.1 us (2%)
  starting transfers between devices  10.2 us (2%)
    pallas_call x1, Pallas kernels, deal(): pl.pallas_call(deal_kernel, name='deal', out_shape=(jax.ShapeDtypeStruct(...  165 us
    pallas_call x1, Pallas kernels, send_home(): pl.pallas_call(home_kernel, name='home', out_shape=(jax.ShapeDtypeStruct(...  105 us
    pallas_call x1, Pallas kernels, turn(): pl.pallas_call(turn_kernel, name='turn', out_shape=(jax.ShapeDtypeStruct(...  57 us
    pallas_call x1, Pallas kernels, middle(): pl.pallas_call(middle_kernel, name='middle', out_shape=(jax.ShapeDtypeStr...  45.7 us
    pallas_call x1, Pallas kernels, mixer_back(): pl.pallas_call(partial(mixer_back_kernel, sh, ph), name='mixer_back', out...  31.1 us
    unnamed x100, local copies, waits for them, and re-layouts  29.5 us
    pallas_call x1, Pallas kernels, last(): pl.pallas_call(partial(last_kernel, at), name='last', out_shape=(jax.Shap...  25.2 us
    dot_general x4, matrix products, matmul_trans(): lax.dot_general(first_op, second_op, (((1,), (1,)), ((), ())), preferred_...  24.3 us
  transfers between devices with their start and end apart: 12, of which 5 were waited for; matrix products, arithmetic and copies ran while one was open for 11% of the time, Pallas kernels for 40%

profile of v3, /device:TPU:9, one launch (start us, length us, event | category | flops | bytes accessed | tf_op | source)
XLA Modules:
  0.0 648.3 jit_solution(1378529192150613119)
XLA Ops:
  10.2 1.2 copy.81
  12.4 1.2 copy.83
  14.5 1.2 copy-done.11
  21.8 165.4 %deal.1 = (s32[16,8,128]{2,1,0:T(8,128)S(1)}, bf16[256,256]{1,0:T(8,128)(2,1)S(1)}, bf16[256,256]{1,0:T(8,128)(2,1)S(1)}, bf16[128,2048]{1,0:T(8,128)(2,1)S(1)},...) custom-call(s32[8,128]{1,0:T(8,128)S(1)} %fusion.24.meta, ...), custom_call_target="tpu_custom_call" | custom-call | bytes 340000000 | tf_op jit(solution)/shard_map/deal/pallas_call | solution.py:579
  188.7 2.0 copy-done.28
  190.7 1.3 collective-permute-start.3
  192.0 1.2 collective-permute-start.4
  194.8 10.5 %fusion.2.projected = f32[1024,1280]{1,0:T(8,128)} fusion(bf16[1024,2048]{1,0:T(8,128)(2,1)} %bitcast.131, bf16[2048,1792]{1,0:T(8,128)(2,1)} %bitcast.161), kind=kOutput, calls=%fused_computation.5 | convolution fusion | flops 5368709120 | bytes 14680064 | tf_op jit(solution)/shard_map/dot_general | solution.py:24
  206.2 2.5 copy-done.2
  208.7 21.7 %mixer.1 = (bf16[1024,512]{1,0:T(8,128)(2,1)S(1)}, f32[1024,384]{1,0:T(8,128)S(1)}, bf16[8,128,128]{2,1,0:T(8,128)(2,1)S(1)}) custom-call(s32[8,3]{1,0:T(8,128)S(1)} %bitcast.124, f32[1024,1280]{1,0:T(8,128)S(1)} %copy-done.2, f32[8,384]{1,0:T(8,128)S(1)} %maximum_maximum_fusion.1.chan, f32[8,128]{1,0:T(8,128)S(1)} %pad_maximum_fusion.6.side, ...), custom_call_target="tpu_custom_call" | custom-call | bytes 102000000 | tf_op jit(solution)/shard_map/mixer/pallas_call | solution.py:1127
  230.4 4.4 convolution_convert_fusion.2
  234.9 2.3 collective-permute-done.3.refs_1_
  237.2 2.6 collective-permute-start.5
  239.8 45.7 %middle.1 = (f32[128,2048]{1,0:T(8,128)S(1)}, bf16[8,128,2048]{2,1,0:T(8,128)(2,1)S(1)}) custom-call(bf16[8,128,2048]{2,1,0:T(8,128)(2,1)S(1)} %bitcast.111, bf16[128,2048]{1,0:T(8,128)(2,1)S(1)} %get-tuple-element.76.x, f32[1,2048]{1,0:T(1,128)S(1)} %bitcast.126), custom_call_target="tpu_custom_call" | custom-call | bytes 204000000 | tf_op jit(solution)/shard_map/middle/pallas_call | solution.py:634
  285.6 1.8 collective-permute-start.2
  287.3 12.2 %collective-permute-done.2.refs_3_ = bf16[4,128,512]{2,1,0:T(8,128)(2,1)S(1)} collective-permute-done((bf16[4,128,512]{2,1,0:T(8,128)(2,1)}, bf16[4,128,512]{2,1,0:T(8,128)(2,1)S(1)}, u32[]{:S(2)}, u32[]{:S(2)}) %collective-permute-start.2) | collective-permute-done | bytes 524320 | tf_op jit(solution)/shard_map/ppermute | solution.py:1355
  299.5 1.2 place.2
  300.8 2.6 place.3
  303.4 4.7 fusion.30
  308.2 3.3 fusion.10
  311.5 6.2 convolution_convert_fusion.4
  317.7 5.7 convolution_convert_fusion.3
  323.4 2.4 convolution_convert_fusion.5
  325.8 3.4 pad_maximum_fusion.1
  330.3 57.0 %turn.1 = (f32[128,2048]{1,0:T(8,128)S(1)}, f32[1,2048]{1,0:T(1,128)S(1)}, bf16[8,128,2048]{2,1,0:T(8,128)(2,1)}) custom-call(bf16[8,128,2048]{2,1,0:T(8,128)(2,1)} %bitcast.139, f32[128,2048]{1,0:T(8,128)S(1)} %get-tuple-element.82.mid, bf16[128,2048]{1,0:T(8,128)(2,1)S(1)} %copy-done.15, f32[1,2048]{1,0:T(1,128)S(1)} %bitcast.127), custom_call_target="tpu_custom_call" | custom-call | bytes 204000000 | tf_op jit(solution)/shard_map/turn/pallas_call | solution.py:683
  388.3 5.2 fusion.12.grads
  393.5 31.1 %mixer_back.1 = (bf16[1024,1280]{1,0:T(8,128)(2,1)}, f32[8,384]{1,0:T(8,128)S(1)}, f32[8,128]{1,0:T(8,128)S(1)}) custom-call(s32[8,3]{1,0:T(8,128)S(1)} %bitcast.125, f32[1024,1280]{1,0:T(8,128)} %fusion.2.projected, f32[8,384]{1,0:T(8,128)S(1)} %maximum_maximum_fusion.1.chan, f32[8,128]{1,0:T(8,128)S(1)} %pad_maximum_fusion.6.side, ...), custom_call_target="tpu_custom_call" | custom-call | bytes 170000000 | tf_op jit(solution)/shard_map/mixer_back/pallas_call | solution.py:1257
  424.6 3.8 convolution_convert_fusion.6
  428.4 7.7 %convolution_convert_fusion = bf16[2048,1280]{0,1:T(8,128)(2,1)} fusion(bf16[1024,2048]{1,0:T(8,128)(2,1)S(1)} %bitcast.132, bf16[1024,1280]{1,0:T(8,128)(2,1)S(1)} %copy-done.40), kind=kOutput, calls=%fused_computation | convolution fusion | flops 5371330560 | bytes 12058624 | tf_op jit(solution)/shard_map/dot_general | solution.py:34
  436.2 7.5 %pad_maximum_fusion = bf16[2048,1792]{0,1:T(8,128)(2,1)} fusion(bf16[2048,512]{0,1:T(8,128)(2,1)} %convolution_convert_fusion.6, bf16[2048,1280]{0,1:T(8,128)(2,1)} %convolution_convert_fusion), kind=kLoop, calls=%fused_computation.1 | loop fusion | flops 14680064 | bytes 14680064 | tf_op jit(solution)/shard_map/concatenate | solution.py:1489
  443.7 2.8 copy.85
  446.5 1.2 copy-done.44
  447.7 4.0 convolution_convert_fusion.1
  451.7 2.5 copy-done.33
  454.2 1.5 dynamic-slice_bitcast_fusion
  455.7 4.5 collective-permute-done.6
  460.2 3.0 fusion.4
  463.2 1.3 dynamic-slice_bitcast_fusion.3
  465.4 1.7 collective-permute-start.7
  467.1 9.7 %fusion.5 = bf16[1024,2048]{1,0:T(8,128)(2,1)} fusion(bf16[1024,1280]{1,0:T(8,128)(2,1)S(1)} %copy-done.41, bf16[2048,1792]{1,0:T(8,128)(2,1)} %bitcast.164), kind=kOutput, calls=%fused_computation.9 | convolution fusion | flops 5370806272 | bytes 12058624 | tf_op jit(solution)/shard_map/dot_general | solution.py:28
  477.3 1.8 collective-permute-done.9
  479.1 11.2 %collective-permute-done.8 = bf16[128,2048]{1,0:T(8,128)(2,1)} collective-permute-done((bf16[128,2048]{1,0:T(8,128)(2,1)}, bf16[128,2048]{1,0:T(8,128)(2,1)}, u32[]{:S(2)}, u32[]{:S(2)}) %collective-permute-start.8) | collective-permute-done | bytes 524320 | tf_op jit(solution)/shard_map/ppermute | solution.py:1479
  490.3 1.9 fusion.18.result
  492.2 105.0 %home.1 = (bf16[2,128,2048]{2,1,0:T(8,128)(2,1)S(1)}, bf16[2,128,2048]{2,1,0:T(8,128)(2,1)S(1)}, f32[8,56,128]{2,1,0:T(8,128)S(1)}, bf16[4,128,1536]{2,1,0:T(8,128)(2,1)}) custom-call(bf16[8,128,2048]{2,1,0:T(8,128)(2,1)} %bitcast.138, bf16[128,2048]{1,0:T(8,128)(2,1)S(1)} %get-tuple-element.76.x, f32[128,2048]{1,0:T(8,128)S(1)} %copy-done.6, ...), custom_call_target="tpu_custom_call" | custom-call | bytes 255000000 | tf_op jit(solution)/shard_map/home/pallas_call | solution.py:854
  604.5 2.8 copy.86
  607.3 25.2 %last.1 = (bf16[4,128,1792]{2,1,0:T(8,128)(2,1)S(1)}, bf16[4,128,128]{2,1,0:T(8,128)(2,1)S(1)}) custom-call(bf16[4,128,1792]{2,1,0:T(8,128)(2,1)S(1)} %bitcast.110), custom_call_target="tpu_custom_call" | custom-call | bytes 85000000 | tf_op jit(solution)/shard_map/last/pallas_call | solution.py:792
  632.7 3.0 unpack.1
  637.9 2.3 copy.114
  (184 shorter events, 28.9 us)
Async XLA Ops:
  7.2 187.6 %copy-start = (f32[4,1536]{1,0:T(4,128)S(1)}, f32[4,1536]{1,0:T(4,128)}, u32[]{:S(2)}) copy-start(f32[4,1536]{1,0:T(4,128)} %param.34) | copy-start | bytes 73732
  7.2 7.2 %copy-start.10 = (bf16[2,128,2048]{2,1,0:T(8,128)(2,1)S(1)}, bf16[2,128,2048]{2,1,0:T(8,128)(2,1)}, u32[]{:S(2)}) copy-start(bf16[2,128,2048]{2,1,0:T(8,128)(2,1)} %tokens.1) | copy-start | bytes 3145732
  7.2 7.2 %copy-start.12 = (bf16[128,2048]{1,0:T(8,128)(2,1)S(1)}, bf16[128,2048]{1,0:T(8,128)(2,1)}, u32[]{:S(2)}) copy-start(bf16[128,2048]{1,0:T(8,128)(2,1)} %refs_8_.1) | copy-start | bytes 1572868
  7.2 436.5 %reduce-scatter.3.cloned.1.call-start = ((), (), s32[]{:S(2)}) async-start(), calls=%async_computation.2 | async-start | bytes 7864320 | tf_op jit(solution)/shard_map/reduce_scatter | solution.py:1378
  9.8 184.0 %copy-start.42 = (f32[24]{0:T(128)S(1)}, f32[24]{0:T(128)}, u32[]{:S(2)}) copy-start(f32[24]{0:T(128)} %param.40) | copy-start | bytes 292
  14.5 1.2 copy-start.11
  15.7 1.0 copy-start.13
  16.7 1.0 copy-start.16
  188.7 2.0 copy-start.28
  190.7 46.5 %collective-permute-start.3 = (bf16[4,128,1024]{2,1,0:T(8,128)(2,1)}, bf16[4,128,1024]{2,1,0:T(8,128)(2,1)}, u32[]{:S(2)}, u32[]{:S(2)}) collective-permute-start(bf16[4,128,1024]{2,1,0:T(8,128)(2,1)} %get-tuple-element.79.refs_0_), channel_id=1, source_target_pairs={{0,16},{2,18},{4,20},{6,22},{8,24},{10,26},{12,28},{14,30},{16,0},... | collective-permute-start | bytes 3145736 | tf_op jit(solution)/shard_map/ppermute | solution.py:1355
  192.0 108.8 %collective-permute-start.4 = (bf16[4,128,1024]{2,1,0:T(8,128)(2,1)}, bf16[4,128,1024]{2,1,0:T(8,128)(2,1)}, u32[]{:S(2)}, u32[]{:S(2)}) collective-permute-start(bf16[4,128,1024]{2,1,0:T(8,128)(2,1)} %get-tuple-element.79.refs_0_), channel_id=1, source_target_pairs={{0,8},{2,10},{4,12},{6,14},{8,0},{10,2},{12,4},{14,6},{16,24},{18,... | collective-permute-start | bytes 3145736 | tf_op jit(solution)/shard_map/ppermute | solution.py:1355
  193.2 92.3 %collective-permute-start = (bf16[4,128,512]{2,1,0:T(8,128)(2,1)}, bf16[4,128,512]{2,1,0:T(8,128)(2,1)}, u32[]{:S(2)}, u32[]{:S(2)}) collective-permute-start(bf16[4,128,512]{2,1,0:T(8,128)(2,1)} %get-tuple-element.74.refs_0_), channel_id=1, source_target_pairs={{0,16},{2,18},{4,20},{6,22},{8,24},{10,26},{12,28},{14,30},{16,0},... | collective-permute-start | bytes 1572872 | tf_op jit(solution)/shard_map/ppermute | solution.py:1355
  194.8 10.6 %copy-start.36 = (f32[24]{0:T(128)S(1)}, f32[24]{0:T(128)}, u32[]{:S(2)}) copy-start(f32[24]{0:T(128)} %param.39) | copy-start | bytes 292
  194.8 10.6 %copy-start.37 = (f32[24]{0:T(128)S(1)}, f32[24]{0:T(128)}, u32[]{:S(2)}) copy-start(f32[24]{0:T(128)} %param.38) | copy-start | bytes 292
  194.8 10.8 %copy-start.34 = (f32[4,512]{1,0:T(4,128)S(1)}, f32[4,512]{1,0:T(4,128)}, u32[]{:S(2)}) copy-start(f32[4,512]{1,0:T(4,128)} %param.36) | copy-start | bytes 24580
  194.8 10.7 %copy-start.35 = (f32[512]{0:T(512)S(1)}, f32[512]{0:T(512)}, u32[]{:S(2)}) copy-start(f32[512]{0:T(512)} %param.37) | copy-start | bytes 6148
  206.2 2.5 copy-start.2
  230.4 4.5 copy-start.18
  230.4 4.5 copy-start.30
  230.4 9.4 %copy-start.25 = (f32[2048]{0:T(1024)S(1)}, f32[2048]{0:T(1024)}, u32[]{:S(2)}) copy-start(f32[2048]{0:T(1024)} %param.46) | copy-start | bytes 24580
  237.2 63.6 %collective-permute-start.5 = (bf16[4,128,1024]{2,1,0:T(8,128)(2,1)}, bf16[4,128,1024]{2,1,0:T(8,128)(2,1)S(1)}, u32[]{:S(2)}, u32[]{:S(2)}) collective-permute-start(bf16[4,128,1024]{2,1,0:T(8,128)(2,1)} %collective-permute-done.3.refs_1_), channel_id=1, source_target_pairs={{0,8},{2,10},{4,12},{6,14},{8,0},{10,2},{12,4},{14,6},{16,24},{18,... | collective-permute-start | bytes 3145736 | tf_op jit(solution)/shard_map/ppermute | solution.py:1355
  239.8 47.6 %collective-permute-start.1 = (bf16[4,128,512]{2,1,0:T(8,128)(2,1)}, bf16[4,128,512]{2,1,0:T(8,128)(2,1)S(1)}, u32[]{:S(2)}, u32[]{:S(2)}) collective-permute-start(bf16[4,128,512]{2,1,0:T(8,128)(2,1)} %get-tuple-element.74.refs_0_), channel_id=1, source_target_pairs={{0,8},{2,10},{4,12},{6,14},{8,0},{10,2},{12,4},{14,6},{16,24},{18,... | collective-permute-start | bytes 1572872 | tf_op jit(solution)/shard_map/ppermute | solution.py:1355
  285.6 14.0 %collective-permute-start.2 = (bf16[4,128,512]{2,1,0:T(8,128)(2,1)}, bf16[4,128,512]{2,1,0:T(8,128)(2,1)S(1)}, u32[]{:S(2)}, u32[]{:S(2)}) collective-permute-start(bf16[4,128,512]{2,1,0:T(8,128)(2,1)} %collective-permute-done.refs_1_), channel_id=1, source_target_pairs={{0,8},{2,10},{4,12},{6,14},{8,0},{10,2},{12,4},{14,6},{16,24},{18,... | collective-permute-start | bytes 1572872 | tf_op jit(solution)/shard_map/ppermute | solution.py:1355
  300.8 7.4 %copy-start.3 = (bf16[4,4,128,512]{3,2,1,0:T(8,128)(2,1)}, bf16[4,4,128,512]{3,2,1,0:T(8,128)(2,1)S(1)}, u32[]{:S(2)}) copy-start(bf16[4,4,128,512]{3,2,1,0:T(8,128)(2,1)S(1)} %place.2) | copy-start | bytes 6291460
  303.4 4.7 copy-start.38
  311.5 12.0 %copy-start.43 = (bf16[1024,512]{0,1:T(8,128)(2,1)}, bf16[1024,512]{0,1:T(8,128)(2,1)S(1)}, u32[]{:S(2)}) copy-start(bf16[1024,512]{0,1:T(8,128)(2,1)S(1)} %get-tuple-element.165) | copy-start | bytes 3145732
  329.2 275.3 %reduce-scatter.5.cloned.1.call-start = ((), (), s32[]{:S(2)}) async-start(), calls=%async_computation.3 | async-start | bytes 9175040 | tf_op jit(solution)/shard_map/reduce_scatter | solution.py:1378
  329.3 1.0 copy-start.15
  388.3 5.2 copy-start.19
  393.5 31.1 %copy-start.31 = (bf16[1024,512]{1,0:T(8,128)(2,1)S(1)}, bf16[1024,512]{1,0:T(8,128)(2,1)}, u32[]{:S(2)}) copy-start(bf16[1024,512]{1,0:T(8,128)(2,1)} %copy-done.30) | copy-start | bytes 3145732
  393.5 31.1 %copy-start.39 = (bf16[8,128,2048]{2,1,0:T(8,128)(2,1)S(1)}, bf16[8,128,2048]{2,1,0:T(8,128)(2,1)}, u32[]{:S(2)}) copy-start(bf16[8,128,2048]{2,1,0:T(8,128)(2,1)} %get-tuple-element.84) | copy-start | bytes 12582916
  424.6 3.8 copy-start.29
  424.6 3.8 copy-start.40
  446.5 1.2 copy-start.44
  451.7 2.5 copy-start.33
  455.7 4.5 collective-permute-start.6
  455.7 11.4 %copy-start.41 = (bf16[1024,1280]{1,0:T(8,128)(2,1)S(1)}, bf16[1024,1280]{1,0:T(8,128)(2,1)}, u32[]{:S(2)}) copy-start(bf16[1024,1280]{1,0:T(8,128)(2,1)} %get-tuple-element.86) | copy-start | bytes 7864324
  463.2 2.2 copy-start.32
  464.5 14.6 %collective-permute-start.9 = (bf16[128,2048]{1,0:T(8,128)(2,1)}, bf16[128,2048]{1,0:T(8,128)(2,1)}, u32[]{:S(2)}, u32[]{:S(2)}) collective-permute-start(bf16[128,2048]{1,0:T(8,128)(2,1)} %get-tuple-element.167), channel_id=1, source_target_pairs={{0,6},{2,4},{4,2},{6,0},{8,14},{10,12},{12,10},{14,8},{16,22},{18,... | collective-permute-start | bytes 1572872 | tf_op jit(solution)/shard_map/ppermute | solution.py:1479
  465.1 25.2 %collective-permute-start.8 = (bf16[128,2048]{1,0:T(8,128)(2,1)}, bf16[128,2048]{1,0:T(8,128)(2,1)}, u32[]{:S(2)}, u32[]{:S(2)}) collective-permute-start(bf16[128,2048]{1,0:T(8,128)(2,1)} %get-tuple-element.168), channel_id=1, source_target_pairs={{0,4},{2,6},{4,0},{6,2},{8,12},{10,14},{12,8},{14,10},{16,20},{18,... | collective-permute-start | bytes 1572872 | tf_op jit(solution)/shard_map/ppermute | solution.py:1479
  465.4 26.8 %copy-start.21 = (bf16[256,256]{1,0:T(8,128)(2,1)S(1)}, bf16[256,256]{1,0:T(8,128)(2,1)}, u32[]{:S(2)}) copy-start(bf16[256,256]{1,0:T(8,128)(2,1)} %copy-done.20) | copy-start | bytes 393220
  465.4 26.8 %copy-start.27 = (f32[2048]{0:T(1024)S(1)}, f32[2048]{0:T(1024)}, u32[]{:S(2)}) copy-start(f32[2048]{0:T(1024)} %param.29) | copy-start | bytes 24580
  465.4 24.9 %collective-permute-start.7 = (bf16[128,2048]{1,0:T(8,128)(2,1)}, bf16[128,2048]{1,0:T(8,128)(2,1)}, u32[]{:S(2)}, u32[]{:S(2)}) collective-permute-start(bf16[128,2048]{1,0:T(8,128)(2,1)} %get-tuple-element.166), channel_id=1, source_target_pairs={{0,2},{2,0},{4,6},{6,4},{8,10},{10,8},{12,14},{14,12},{16,18},{18,... | collective-permute-start | bytes 1572872 | tf_op jit(solution)/shard_map/ppermute | solution.py:1479
  476.8 15.5 %copy-start.6 = (f32[128,2048]{1,0:T(8,128)S(1)}, f32[128,2048]{1,0:T(8,128)}, u32[]{:S(2)}) copy-start(f32[128,2048]{1,0:T(8,128)} %copy-done.5) | copy-start | bytes 3145732
  597.2 1.0 copy-start.7
  599.2 33.4 %copy-start.4 = (bf16[4,128,1536]{2,1,0:T(8,128)(2,1)S(1)}, bf16[4,128,1536]{2,1,0:T(8,128)(2,1)}, u32[]{:S(2)}) copy-start(bf16[4,128,1536]{2,1,0:T(8,128)(2,1)} %get-tuple-element.99.ff) | copy-start | bytes 4718596
  632.7 7.6 %copy-start.8 = (bf16[2,128,2048]{2,1,0:T(8,128)(2,1)S(1)}, bf16[2,128,2048]{2,1,0:T(8,128)(2,1)}, u32[]{:S(2)}) copy-start(bf16[2,128,2048]{2,1,0:T(8,128)(2,1)} %copy-done.7) | copy-start | bytes 3145732
  632.7 8.5 %copy-start.1 = (f32[4,1536]{1,0:T(4,128)S(1)}, f32[4,1536]{1,0:T(4,128)}, u32[]{:S(2)}) copy-start(f32[4,1536]{1,0:T(4,128)} %param.34) | copy-start | bytes 73732
  (9 other events, 7.5 us)
Sparse Core Ops, SparseCore 0:
  329.4 111.0 reduce-scatter.2
  446.6 151.2 reduce-scatter.4

commit v4 on v3

--- a/solution.py
+++ b/solution.py
@@ -17,7 +17,7 @@
 MESH = pl.DeviceIdType.MESH
 HIGH = lax.Precision.HIGHEST
 VMEM = pltpu.VMEM
-ANY = pl.ANY
+ANY = pltpu.HBM
 
 
 def matmul(first_op, second_op):
@@ -148,27 +148,33 @@
     return copies
 
 
-def gather_finish(copies, out, send, recv, axes):
+def gather_pass(steps, p, k, m, row, col, out, send, recv, axes):
+    r, c = place()
+    low, high = plan_of(axes, out.shape[1])[p][:2]
+    part = out.at[block_of(m, axes) + c, low:high]
+    steps.append(remote(part, part, send.at[6 * p + k], recv.at[6 * p + k], row, col))
+    steps[-1].start()
+
+
+def gather_turn(copies, out, send, recv, axes):
+    r, c = place()
+    steps = []
+    for p, (low, high, near, far) in enumerate(plan_of(axes, out.shape[1])):
+        copies[2 + 2 * p].wait_recv()
+        gather_pass(steps, p, 3, near, partner(r, far, axes), c, out, send, recv, axes)
+        gather_pass(steps, p, 4, near, r, 1 - c, out, send, recv, axes)
+    return steps
+
+
+def gather_finish(copies, steps, out, send, recv, axes):
     r, c = place()
     plan = plan_of(axes, out.shape[1])
-    steps = []
-
-    def pass_on(p, k, m, row, col):
-        low, high, near, far = plan[p]
-        part = out.at[block_of(m, axes) + c, low:high]
-        steps.append(remote(part, part, send.at[6 * p + k], recv.at[6 * p + k], row, col))
-        steps[-1].start()
-
-    for p, (low, high, near, far) in enumerate(plan):
-        copies[2 + 2 * p].wait_recv()
-        pass_on(p, 3, near, partner(r, far, axes), c)
-        pass_on(p, 4, near, r, 1 - c)
     for p, (low, high, near, far) in enumerate(plan):
         copies[3 + 2 * p].wait_recv()
-        pass_on(p, 5, far, r, 1 - c)
-    for p, (low, high, near, far) in enumerate(plan):
+        gather_pass(steps, p, 5, far, r, 1 - c, out, send, recv, axes)
+    for p in range(len(plan)):
         steps[2 * p].wait_recv()
-        pass_on(p, 6, 3, r, 1 - c)
+        gather_pass(steps, p, 6, 3, r, 1 - c, out, send, recv, axes)
     copies[0].wait()
     copies[1].wait()
     for copy in copies[2:] + steps[: 2 * len(plan) : 2]:
@@ -178,6 +184,11 @@
             copy.wait()
 
 
+def gather(src, out, send, recv, here, axes):
+    copies = gather_start(src, out, send, recv, here, axes)
+    gather_finish(copies, gather_turn(copies, out, send, recv, axes), out, send, recv, axes)
+
+
 ROWS = 16
 
 
@@ -189,7 +200,7 @@
     lax.fori_loop(first // ROWS, count // ROWS, step, 0)
 
 
-def scatter_sum(parts, near, held, far, s1, r1, s2, r2, total, axes):
+def scatter_steps(parts, near, held, far, s1, r1, s2, r2, total, axes):
     r, c = place()
     slots = total.shape[0]
     plan = plan_of(axes, slots)
@@ -219,6 +230,7 @@
         )
         sent[i, p].start()
 
+    yield
     pairs[3].wait_recv()
     for p, (low, high, first, then) in enumerate(plan):
         pair_sum(3, 1, low, high)
@@ -229,6 +241,7 @@
             pair_sum(m, 0 if m == then else 2, low, high)
             if m == then:
                 send(0, p, then)
+    yield
     for p, (low, high, first, then) in enumerate(plan):
         sent[1, p].wait_recv()
 
@@ -239,6 +252,7 @@
 
         by_rows(high, add, low)
         send(2, p, first)
+    yield
     pairs[0].wait_recv()
     for p in range(len(plan)):
         sent[0, p].wait_recv()
@@ -256,6 +270,12 @@
     by_rows(slots, fold)
     for copy in list(pairs.values()) + list(sent.values()):
         copy.wait_send()
+    yield
+
+
+def scatter_sum(*args):
+    for step in scatter_steps(*args):
+        pass
 
 
 def scatter_scratch(slots, width):
@@ -278,28 +298,21 @@
     ]
 
 
-def strips(refs, shared, size):
-    found, at = [], 0
-    for ref, whole in zip(refs, shared):
-        count = ref.shape[1] if whole else ref.shape[1] // TP
-        found.append((ref, whole, count, at))
+def strip_views(refs, owner, piece):
+    at = 0
+    for ref in refs:
+        count = ref.shape[1] // TP
+        yield ref.at[:, pl.ds(pl.multiple_of(owner * count, 128), count)], piece.at[:, at : at + count]
         at += count
-    return found
-
-
-def strip_views(refs, shared, owner, piece):
-    for ref, whole, count, at in strips(refs, shared, piece.shape[1]):
-        cols = slice(None) if whole else pl.ds(pl.multiple_of(owner * count, 128), count)
-        yield ref.at[:, cols], piece.at[:, at : at + count]
-
-
-def cut_start(refs, shared, place_of, send, recv, here, axes):
-    r, c = place()
-    for source, target in strip_views(refs, shared, member(r, axes), place_of()):
+
+
+def cut_start(refs, piece, send, recv, here, axes):
+    r, c = place()
+    for source, target in strip_views(refs, member(r, axes), piece):
         pltpu.make_async_copy(source, target, here).start()
     for m in (3, 1, 2):
         other = partner(r, m, axes)
-        for source, target in strip_views(refs, shared, member(other, axes), place_of()):
+        for source, target in strip_views(refs, member(other, axes), piece):
             remote(source, target, send.at[m], recv.at[m], other, c).start()
 
 
@@ -307,36 +320,41 @@
     pltpu.make_async_copy(piece, piece, sem).wait()
 
 
-def weight_orders(n_row, cols):
+def weight_forward(masks, whole, cols, send, recv):
+    r, c = place()
+    n_row = lax.axis_size("row")
     bits = data_bits(n_row, MIX)
-    half = cols // 256 * 128
-    return [(slice(0, half), bits), (slice(half, cols), bits)]
-
-
-def weight_forward(masks, i, whole, send, recv):
-    r, c = place()
-    n_row = lax.axis_size("row")
-    cols, bits = weight_orders(n_row, whole.shape[2])[i]
     copies = []
     for mask in masks:
         at = whole.at[turned_row(r, mask), :, cols]
         crossed = [k for k, b in enumerate(bits) if mask >> b & 1]
         if crossed:
-            piece_done(at, recv.at[i, mask])
+            piece_done(at, recv.at[mask])
         for b in bits[max([-1] + crossed) + 1 :]:
             lands = mask | 1 << b
-            copies.append(remote(at, at, send.at[i, lands], recv.at[i, lands], flip(r, b), c))
+            copies.append(remote(at, at, send.at[lands], recv.at[lands], flip(r, b), c))
             copies[-1].start()
     return copies
 
 
-def weight_rounds(n_row, i, cols):
-    held = [mask_of(m, MIX) for m in range(TP)]
-    rounds = [held]
-    for b in weight_orders(n_row, cols)[i][1]:
+def weight_rounds(n_row, held):
+    rounds = []
+    for b in data_bits(n_row, MIX):
         rounds.append([mask | 1 << b for mask in held])
         held = held + rounds[-1]
     return rounds
+
+
+def spread(masks, whole, cols, send, recv):
+    r, c = place()
+    copies = []
+    for mask in masks:
+        at = whole.at[turned_row(r, mask), :, cols]
+        for m in (3, 1, 2):
+            lands = mask | mask_of(m, MIX)
+            copies.append(remote(at, at, send.at[lands], recv.at[lands], partner(r, m, MIX), c))
+            copies[-1].start()
+    return copies
 
 
 def place_kernel(masks, n_row, *refs):
@@ -441,11 +459,12 @@
 def deal_kernel(
     meta, tokens, cotangent, gain, *refs
 ):
-    in_refs, up_refs, down_refs, refs = refs[:8], refs[8:10], refs[10:11], refs[11:]
+    kv_refs, first_refs, second_refs, refs = refs[:2], refs[2:5], refs[5:8], refs[8:]
+    up_refs, down_refs, refs = refs[:2], refs[2:3], refs[3:]
     meta_all, give, take, x_out, gy_out, normed_all, gy_all, whole, slab_up, slab_down = refs[:10]
     x_mine, g_mine, buf, land, normed = refs[10:15]
     load, msend, mrecv, csend, crecv, nsend, nrecv, nhere, gsend, grecv, ghere = refs[15:26]
-    wsend, wrecv, wcut, wcut_recv, whole_here, usend, urecv, uhere, dsend, drecv, dhere = refs[26:]
+    wsend, wrecv, acut, arecv, ahere, bcut, brecv, bhere, usend, urecv, uhere, dsend, drecv, dhere, kv_here = refs[26:]
     r, c = place()
     n_row = lax.axis_size("row")
     f = member(r, FFN)
@@ -458,11 +477,14 @@
     for copy in loads:
         copy.start()
     greet_rows()
-    rounds = [weight_rounds(n_row, i, whole.shape[2]) for i in (0, 1)]
-    in_shared = [False, False, False, True, True, False, False, False]
-
-    def in_place():
-        return whole.at[r]
+    group = [mask_of(m, MIX) for m in range(TP)]
+    first_cols = sum(ref.shape[1] for ref in first_refs) // TP
+    kv_cols = first_cols + sum(ref.shape[1] for ref in kv_refs)
+    cuts = (
+        (slice(0, first_cols), first_refs, acut, arecv, ahere),
+        (slice(kv_cols, whole.shape[2]), second_refs, bcut, brecv, bhere),
+    )
+    kv = slice(first_cols, kv_cols)
 
     def meta_copy(other, slot):
         return remote(meta, meta_all.at[slot], msend.at[other], mrecv.at[slot], other, c)
@@ -473,6 +495,18 @@
 
     lax.fori_loop(1, n_row, start, 0)
     meta_all[r] = meta[...]
+    at = first_cols
+    for ref in kv_refs:
+        pltpu.make_async_copy(ref, whole.at[r, :, at : at + ref.shape[1]], kv_here).start()
+        at += ref.shape[1]
+    for cols, refs_of, send, recv, here in cuts:
+        cut_start(refs_of, whole.at[r, :, cols], send, recv, here, MIX)
+    forwards = []
+    for i, (cols, refs_of, send, recv, here) in enumerate(cuts):
+        piece_done(whole.at[r, :, cols], here)
+        forwards = forwards + weight_forward([0], whole, cols, wsend.at[i], wrecv.at[i])
+    piece_done(whole.at[r, :, kv], kv_here)
+    forwards = forwards + weight_forward([0], whole, kv, wsend.at[2], wrecv.at[2])
 
     def finish(off, carry):
         other = lax.rem(r + off, n_row)
@@ -482,11 +516,6 @@
         return carry
 
     lax.fori_loop(1, n_row, finish, 0)
-    cut_start(in_refs, in_shared, in_place, wcut, wcut_recv, whole_here, MIX)
-    piece_done(in_place(), whole_here)
-    forwards = []
-    for i in (0, 1):
-        forwards = forwards + weight_forward([0], i, whole, wsend, wrecv)
 
     shift = slots.bit_length() - 1
     row_no = lax.broadcasted_iota(jnp.int32, (CHUNK, slots), 0)
@@ -533,10 +562,10 @@
     permute_out(give, buf, x_mine, g_mine, slots)
     exchange_rows(buf, land, csend, crecv)
     land[r] = buf[r]
-    for m in (1, 2, 3):
-        piece_done(in_place(), wcut_recv.at[m])
-        for i in (0, 1):
-            forwards = forwards + weight_forward([mask_of(m, MIX)], i, whole, wsend, wrecv)
+    for i, (cols, refs_of, send, recv, here) in enumerate(cuts):
+        for m in (1, 2, 3):
+            piece_done(whole.at[r, :, cols], recv.at[m])
+            forwards = forwards + weight_forward([group[m]], whole, cols, wsend.at[i], wrecv.at[i])
     finish_rows(buf, land, csend, crecv)
     permute_in(take, land, x_out, gy_out, slots)
 
@@ -547,18 +576,31 @@
 
     by_rows(slots, norm)
     first = gather_start(normed, normed_all, nsend, nrecv, nhere, MIX)
-    cut_start(up_refs, [False] * 2, lambda: slab_up.at[f], usend, urecv, uhere, FFN)
-    cut_start(down_refs, [False], lambda: slab_down.at[f], dsend, drecv, dhere, FFN)
+    cut_start(up_refs, slab_up.at[f], usend, urecv, uhere, FFN)
+    cut_start(down_refs, slab_down.at[f], dsend, drecv, dhere, FFN)
     second = gather_start(gy_out, gy_all, gsend, grecv, ghere, FFN)
-    for k in range(1, len(rounds[0])):
+    kv_rounds = weight_rounds(n_row, [0])
+    steps = []
+    for k, masks in enumerate(weight_rounds(n_row, group)):
+        forwards = forwards + weight_forward(kv_rounds[k], whole, kv, wsend.at[2], wrecv.at[2])
         for i in (0, 1):
-            forwards = forwards + weight_forward(rounds[i][k], i, whole, wsend, wrecv)
-    gather_finish(first, normed_all, nsend, nrecv, MIX)
-    gather_finish(second, gy_all, gsend, grecv, FFN)
+            forwards = forwards + weight_forward(masks, whole, cuts[i][0], wsend.at[i], wrecv.at[i])
+            if k == 0 and i == 0:
+                steps.append(gather_turn(first, normed_all, nsend, nrecv, MIX))
+            if k == 0 and i == 1:
+                steps.append(gather_turn(second, gy_all, gsend, grecv, FFN))
+        if k == len(kv_rounds) - 1:
+            kv_held = [0] + [mask for masks in kv_rounds for mask in masks]
+            spreads = spread(kv_held, whole, kv, wsend.at[2], wrecv.at[2])
+    gather_finish(first, steps[0], normed_all, nsend, nrecv, MIX)
+    gather_finish(second, steps[1], gy_all, gsend, grecv, FFN)
     for copy in forwards:
         copy.wait_send()
-    for m in (1, 2, 3):
-        piece_done(in_place(), wcut.at[m])
+    for cols, refs_of, send, recv, here in cuts:
+        for m in (1, 2, 3):
+            piece_done(whole.at[r, :, cols], send.at[m])
+    for copy in spreads:
+        copy.wait()
     for slab, send, recv, here in ((slab_up, usend, urecv, uhere), (slab_down, dsend, drecv, dhere)):
         piece_done(slab.at[f], here)
         for m in (1, 2, 3):
@@ -571,7 +613,7 @@
     bf = jnp.bfloat16
     rows = in_weights[0].shape[0]
     in_cols = sum(
-        array.shape[1] // (1 if i in (3, 4) else TP) for i, array in enumerate(in_weights)
+        array.shape[1] // (1 if i < 2 else TP) for i, array in enumerate(in_weights)
     )
     up_cols, down_cols = 2 * ff_weights[0].shape[1] // TP, ff_weights[2].shape[1] // TP
     vm, hb = pl.BlockSpec(memory_space=VMEM), pl.BlockSpec(memory_space=ANY)
@@ -607,9 +649,10 @@
         ]
         + gather_scratch()
         + gather_scratch()
-        + [dma((2, n_row)), dma((2, n_row))]
-        + [dma((TP,)), dma((TP,)), dma] * 3,
-        compiler_params=params(0, 40),
+        + [dma((3, n_row)), dma((3, n_row))]
+        + [dma((TP,)), dma((TP,)), dma] * 4
+        + [dma],
+        compiler_params=params(0, 58),
         cost_estimate=cost(100),
     )(meta, tokens, cotangent, gain, *in_weights, *ff_weights)
 
@@ -625,8 +668,7 @@
         normed[rows, :] = (values * scale * gain[...]).astype(jnp.bfloat16)
 
     by_rows(mid.shape[0], norm)
-    started = gather_start(normed, normed_all, nsend, nrecv, nhere, FFN)
-    gather_finish(started, normed_all, nsend, nrecv, FFN)
+    gather(normed, normed_all, nsend, nrecv, nhere, FFN)
 
 
 def middle(parts, x, gain):
@@ -674,8 +716,7 @@
         d_gain[...] += gain_part
 
     by_rows(mid.shape[0], back)
-    started = gather_start(branch, branch_all, nsend, nrecv, nhere, MIX)
-    gather_finish(started, branch_all, nsend, nrecv, MIX)
+    gather(branch, branch_all, nsend, nrecv, nhere, MIX)
 
 
 def turn(parts, mid, gy, gain):
@@ -699,8 +740,8 @@
 
 
 def home_kernel(
-    parts, x, d_mid, result, gain, give, take, small, ff_sums,
-    output, gradient, small_all, ff_land,
+    parts, x, d_mid, result, gain, give, take, small, kv_parts, ff_sums,
+    output, gradient, small_all, kv_sums, ff_land,
     near, out2, far, s1, r1, s2, r2, total, first, second, buf, land, csend, crecv, here, osend, orecv,
     d_gain, stages, stage_land, tsend, trecv, gsend, grecv, ghere, *more
 ):
@@ -708,7 +749,8 @@
     slots, width = x.shape
     bits = data_bits(lax.axis_size("row"), MIX)
     greet_rows()
-    delivered = deliver(ff_sums, ff_land, *more, FFN)
+    kv_near, kv_held, kv_far, kv_s1, kv_r1, kv_s2, kv_r2 = more[3:]
+    delivered = deliver(ff_sums, ff_land, *more[:3], FFN)
     scatter_sum(parts, near, out2, far, s1, r1, s2, r2, total, MIX)
     d_gain[...] = jnp.zeros_like(d_gain)
 
@@ -734,12 +776,44 @@
     permute_out(take, buf, first, second, slots)
     exchange_rows(buf, land, csend, crecv)
     land[r] = buf[r]
+    own = member(r, MIX)
+    groups = kv_parts.shape[0]
+    kv_sent = []
+    for m in (3, 1, 2):
+        other = partner(r, m, MIX)
+        kv_sent.append(
+            remote(kv_parts.at[:, member(other, MIX)], kv_near.at[m], kv_s1.at[m], kv_r1.at[m], other, c)
+        )
+        kv_sent[-1].start()
     for i in range(len(bits)):
         stage_copy(i).wait()
         stages[i + 1] = stages[i] + stage_land[i]
         if i + 1 < len(bits):
             stage_copy(i + 1).start()
     started = gather_start(stages.at[len(bits)], small_all, gsend, grecv, ghere, MIX)
+    for copy in kv_sent:
+        copy.wait()
+    passed = gather_turn(started, small_all, gsend, grecv, MIX)
+
+    def kv_pair(g):
+        kv_held[g] = (
+            kv_parts[g, own].astype(jnp.float32)
+            + kv_near[1, g].astype(jnp.float32)
+            + kv_near[2, g].astype(jnp.float32)
+            + kv_near[3, g].astype(jnp.float32)
+        ).astype(jnp.bfloat16)
+
+    each_block(0, groups, kv_pair)
+    kv_far_sent = []
+    for k in range(1, groups):
+        other = turned_row(r, sum((1 << b) * (k >> i & 1) for i, b in enumerate(bits)))
+        kv_far_sent.append(
+            remote(
+                kv_held.at[group_of(other, lax.axis_size("row"), MIX)],
+                kv_far.at[k], kv_s2.at[k], kv_r2.at[k], other, c,
+            )
+        )
+        kv_far_sent[-1].start()
     finish_rows(buf, land, csend, crecv)
     permute_in(give, land, first, second, slots)
     copies = []
@@ -748,7 +822,13 @@
         copies.append(remote(mine, out.at[c], osend.at[i], orecv.at[i], r, 1 - c))
     for copy in copies:
         copy.start()
-    gather_finish(started, small_all, gsend, grecv, MIX)
+    gather_finish(started, passed, small_all, gsend, grecv, MIX)
+    for copy in kv_far_sent:
+        copy.wait()
+    kv_total = kv_held[group_of(r, lax.axis_size("row"), MIX)].astype(jnp.float32)
+    for k in range(1, groups):
+        kv_total = kv_total + kv_far[k].astype(jnp.float32)
+    kv_sums[...] = kv_total
     for copy in copies + delivered:
         copy.wait()
 
@@ -804,14 +884,43 @@
     )(sums)
 
 
+def products_kernel(parts, *refs):
+    pairs = len(refs) - len(parts)
+    for part, out in zip(parts, refs[pairs:]):
+        at = 0
+        for i, low, high in part:
+            left, right = refs[2 * i], refs[2 * i + 1]
+            out[:, at : at + high - low] = dot(left[...], right[:, low:high], 0, 0).astype(out.dtype)
+            at += high - low
+
+
+def products(pairs, *parts):
+    tokens, width = pairs[0][0].shape
+    tile = 256
+    specs = []
+    for left, right in pairs:
+        specs.append(pl.BlockSpec((tokens, tile), lambda i: (0, i)))
+        specs.append(pl.BlockSpec(right.shape, lambda i: (0, 0)))
+    totals = [sum(high - low for i, low, high in part) for part in parts]
+    return pl.pallas_call(
+        partial(products_kernel, parts),
+        name="products",
+        grid=(width // tile,),
+        out_shape=tuple(jax.ShapeDtypeStruct((width, total), jnp.bfloat16) for total in totals),
+        in_specs=specs,
+        out_specs=tuple(pl.BlockSpec((tile, total), lambda i: (i, 0)) for total in totals),
+        compiler_params=pltpu.CompilerParams(vmem_limit_bytes=40 << 20),
+        cost_estimate=cost(10),
+    )(*[array for pair in pairs for array in pair])
+
+
 def unpack_kernel(
-    ff, mixer, gate, up, down, mamba_gate, mamba_input, query, key, value, mamba_out, attn_out
+    ff, mixer, gate, up, down, mamba_gate, mamba_input, query, mamba_out, attn_out
 ):
     f32 = jnp.float32
     mh = mamba_gate.shape[1] // TP
     fh = gate.shape[1] // TP
     qh = query.shape[1] // TP
-    kv = key.shape[1]
     at = 2 * mh + qh
     out = mixer.shape[2] - mh - qh
     for m in range(TP):
@@ -826,15 +935,13 @@
         query[:, cols(qh)] = mixer[m, :, 2 * mh : at].astype(f32)
         mamba_out[cols(mh), :] = mixer[m, :, out : out + mh].astype(f32).T
         attn_out[cols(qh), :] = mixer[m, :, out + mh :].astype(f32).T
-    key[...] = sum(mixer[m, :, at : at + kv].astype(f32) for m in range(TP))
-    value[...] = sum(mixer[m, :, at + kv : at + 2 * kv].astype(f32) for m in range(TP))
-
-
-def unpack(ff, mixer, mh, qh, kv, fh):
+
+
+def unpack(ff, mixer, mh, qh, fh):
     rows = ff.shape[1]
     vm = pl.BlockSpec(memory_space=VMEM)
     shapes = [(rows, TP * fh)] * 2 + [(TP * fh, rows)] + [(rows, TP * mh)] * 2
-    shapes += [(rows, TP * qh), (rows, kv), (rows, kv), (TP * mh, rows), (TP * qh, rows)]
+    shapes += [(rows, TP * qh), (TP * mh, rows), (TP * qh, rows)]
     return pl.pallas_call(
         unpack_kernel,
         name="unpack",
@@ -846,7 +953,7 @@
     )(ff, mixer)
 
 
-def send_home(parts, x, d_mid, result, gain, give, take, small, ff_sums, n_row):
+def send_home(parts, x, d_mid, result, gain, give, take, small, kv_parts, ff_sums, n_row):
     slots, width = x.shape
     bf = jnp.bfloat16
     size = small.shape[0] + width // 128
@@ -858,10 +965,14 @@
             jax.ShapeDtypeStruct((2, slots, width), bf),
             jax.ShapeDtypeStruct((2, slots, width), bf),
             jax.ShapeDtypeStruct((GROUP, size, 128), jnp.float32),
+            jax.ShapeDtypeStruct(kv_parts.shape[2:], jnp.float32),
             jax.ShapeDtypeStruct(ff_sums.shape, bf),
         ),
-        in_specs=[pl.BlockSpec(memory_space=VMEM)] * 8 + [pl.BlockSpec(memory_space=ANY)],
-        out_specs=(pl.BlockSpec(memory_space=ANY),) * 4,
+        in_specs=[pl.BlockSpec(memory_space=VMEM)] * 9 + [pl.BlockSpec(memory_space=ANY)],
+        out_specs=(
+            (pl.BlockSpec(memory_space=ANY),) * 3
+            + (pl.BlockSpec(memory_space=VMEM), pl.BlockSpec(memory_space=ANY))
+        ),
         scratch_shapes=scatter_scratch(slots, width)
         + [
             VMEM((slots, width), jnp.float32),
@@ -881,10 +992,19 @@
             pltpu.SemaphoreType.DMA((phases,)),
         ]
         + gather_scratch()
-        + deliver_scratch(),
+        + deliver_scratch()
+        + [
+            VMEM((TP, kv_parts.shape[0]) + kv_parts.shape[2:], bf),
+            VMEM((kv_parts.shape[0],) + kv_parts.shape[2:], bf),
+            VMEM((kv_parts.shape[0],) + kv_parts.shape[2:], bf),
+            pltpu.SemaphoreType.DMA((TP,)),
+            pltpu.SemaphoreType.DMA((TP,)),
+            pltpu.SemaphoreType.DMA((kv_parts.shape[0],)),
+            pltpu.SemaphoreType.DMA((kv_parts.shape[0],)),
+        ],
         compiler_params=params(3, 48),
         cost_estimate=cost(75),
-    )(parts, x, d_mid, result, gain, give, take, small, ff_sums)
+    )(parts, x, d_mid, result, gain, give, take, small, kv_parts, ff_sums)
 
 
 def blocks_start(low, land, s1, r1):
@@ -1141,14 +1261,18 @@
 
 
 def mixer_back_kernel(
-    sh, ph, lens, projected, chan, side, table, scanned, crossed, grads, out, chan_sums, side_sums,
-    low, land, mine, s1, r1, s2, r2, here, summed, misc,
+    sh, ph, lens, projected, chan, side, table, scanned, crossed, grads, ff_parts, mid,
+    out, chan_sums, side_sums, result,
+    low, land, mine, s1, r1, s2, r2, here, summed, misc, total, near, held, far, t1, u1, t2, u2,
 ):
     slots = crossed.shape[1]
     mh = chan.shape[1]
     heads_at = 2 * sh
     bf = jnp.bfloat16
     greet(MIX, cross=True)
+    assert MIX == FFN
+    steps = scatter_steps(ff_parts, near, held, far, t1, u1, t2, u2, total, FFN)
+    next(steps)
     chan_sums[...] = jnp.zeros_like(chan_sums)
     side_sums[...] = jnp.zeros_like(side_sums)
 
@@ -1240,16 +1364,25 @@
         for i, part in enumerate(sums):
             side_sums[i : i + 1, :] += part
 
-    each_block(0, GROUP, scan)
+    each_block(0, GROUP // 2, scan)
+    next(steps)
+    each_block(GROUP // 2, GROUP, scan)
     begun = blocks_start(low, land, s1, r1)
+    next(steps)
     each_block(0, GROUP // 2, attention)
     done = blocks_turn(begun, low, land, mine, summed, s2, r2, here)
     each_block(GROUP // 2, GROUP, attention)
     blocks_finish(begun, done)
     each_block(0, GROUP, state)
-
-
-def mixer_back(lens, projected, chan, side, table, scanned, crossed, grads, sh, ph):
+    next(steps)
+
+    def finish(rows):
+        result[rows, :] = (total[rows, :] + mid[rows, :]).astype(bf)
+
+    by_rows(slots, finish)
+
+
+def mixer_back(lens, projected, chan, side, table, scanned, crossed, grads, ff_parts, mid, sh, ph):
     tokens = projected.shape[0]
     slots = tokens // GROUP
     mh = chan.shape[1]
@@ -1261,17 +1394,20 @@
             jax.ShapeDtypeStruct(projected.shape, jnp.bfloat16),
             jax.ShapeDtypeStruct(chan.shape, jnp.float32),
             jax.ShapeDtypeStruct(side.shape, jnp.float32),
+            jax.ShapeDtypeStruct(mid.shape, jnp.bfloat16),
         ),
-        in_specs=[pl.BlockSpec(memory_space=pltpu.SMEM)] + [vm] * 7,
-        out_specs=(vm,) * 3,
+        in_specs=[pl.BlockSpec(memory_space=pltpu.SMEM)] + [vm] * 9,
+        out_specs=(vm,) * 4,
         scratch_shapes=blocks_scratch(slots)
         + [
             VMEM((GROUP, slots, slots), jnp.bfloat16),
             VMEM((tokens, 128), jnp.float32),
-        ],
-        compiler_params=params(5, 48),
+            VMEM(mid.shape, jnp.float32),
+        ]
+        + scatter_scratch(*mid.shape),
+        compiler_params=params(5, 56),
         cost_estimate=cost(50),
-    )(lens, projected, chan, side, table, scanned, crossed, grads)
+    )(lens, projected, chan, side, table, scanned, crossed, grads, ff_parts, mid)
 
 
 def swiglu(ff_gate, ff_up):
@@ -1340,8 +1476,9 @@
         axis=2,
     ).reshape(rows, TP * (2 * sh + ph + spare))
     in_weights = (
-        mamba_gate_weight, mamba_input_weight, query_weight, key_weight, value_weight, mixed,
-        mamba_out_weight.T, attn_out_weight.T,
+        key_weight, value_weight,
+        mamba_gate_weight, mamba_input_weight, query_weight,
+        mixed, mamba_out_weight.T, attn_out_weight.T,
     )
     ff_weights = (gate_weight, up_weight, down_weight.T)
 
@@ -1396,9 +1533,6 @@
     w_mixer = w_mixer.reshape(width, -1)
     w_in, w_out = w_mixer[:, : used + spare], w_mixer[:, used + spare :]
 
-    def across(array):
-        return lax.ppermute(array, "col", [(0, 1), (1, 0)])
-
     base = r - sum(bit(r, b) * (1 << b) for b in MIX)
     group_meta = jnp.stack([pick(meta_all, base + mask_of(m, MIX)) for m in range(TP)])
     lengths = group_meta[:, 2:4, : seq_lengths.shape[2]].reshape(GROUP, seq_lengths.shape[2])
@@ -1457,41 +1591,27 @@
     unused_value, pullback = jax.vjp(swiglu, ff_gate, ff_up)
     grad_gate, grad_up = pullback(grad_hidden)
     grad_gate_up = jnp.concatenate([grad_gate.astype(bf), grad_up.astype(bf)], axis=1)
+    (grad_ff,) = products(
+        [(normed_two, grad_gate_up), (gy_all, ff_hidden)], [(0, 0, 2 * fh), (1, 0, fh)]
+    )
+    grad_gate_up, grad_ff = lax.optimization_barrier((grad_gate_up, grad_ff))
+    ff_sums, unused_value = sum_groups(grad_ff, FFN)
     normed_two_part = (
         matmul_trans(grad_gate_up, w_gate_up).astype(bf).reshape(GROUP, slots, width)
     )
-    grad_ff = jnp.concatenate(
-        [matmul_left(normed_two, grad_gate_up).astype(bf), matmul_left(gy_all, ff_hidden).astype(bf)],
-        axis=1,
-    )
-    normed_two_part, grad_ff = lax.optimization_barrier((normed_two_part, grad_ff))
-    ff_sums, unused_value = sum_groups(grad_ff, FFN)
     d_mid, delta_ff_gain, branch_all = turn(
         normed_two_part, mid, gy_home, ff_gain
     )
-    ff_pairs = ff_part.reshape(TP, 2, slots, width)
-    ff_sum = (
-        pick(ff_pairs, c, 1).astype(jnp.float32)
-        + across(pick(ff_pairs, 1 - c, 1)).astype(jnp.float32)
-    ).astype(bf)
-    result = mid + pick(ff_sum, member(r, FFN)).astype(jnp.float32)
-    for m in (1, 2, 3):
-        result = result + lax.ppermute(
-            pick(ff_sum, member(partner(r, m, FFN), FFN)), "row", flips(n_row, mask_of(m, FFN))
-        ).astype(jnp.float32)
-    result = result.astype(bf)
     branch_all = branch_all.reshape(GROUP * slots, width)
 
     grad_branch_in = matmul(branch_all, w_out)
-    grad_projected, chan_sums, side_sums = mixer_back(
-        lengths, projected, chan, side, table, scanned, crossed, grad_branch_in, sh, ph
-    )
-    grad_mixer = jnp.concatenate(
-        [
-            matmul_left(normed_one, grad_projected).astype(bf),
-            matmul_left(branch_all, branch_in).astype(bf),
-        ],
-        axis=1,
+    grad_projected, chan_sums, side_sums, result = mixer_back(
+        lengths, projected, chan, side, table, scanned, crossed, grad_branch_in, ff_part, mid, sh, ph
+    )
+    grad_mixer, grad_kv = products(
+        [(normed_one, grad_projected), (branch_all, branch_in)],
+        [(0, 0, edges[3]), (0, edges[5], used + spare), (1, 0, mh + qh)],
+        [(0, edges[3], edges[5])],
     )
     grad_projected, grad_mixer = lax.optimization_barrier((grad_projected, grad_mixer))
     mixer_sums, ff_sums = sum_groups(grad_mixer, MIX, ff_sums)
@@ -1519,20 +1639,22 @@
     small_parts.append(jnp.zeros((-sum(counts) % 8, 128), jnp.float32))
     starts = [sum(counts[:i]) for i in range(len(counts))]
     starts[-1] += small_parts[-1].shape[0]
-    output, grad_tokens, small_all, ff_land = send_home(
+    output, grad_tokens, small_all, delta_kv, ff_land = send_home(
         normed_one_part, x_home, d_mid, result, mixer_norm_gain[None, :], give, take,
-        jnp.concatenate(small_parts, axis=0), ff_sums, n_row,
-    )
-    mixer_land, other_land = last(mixer_sums, edges[5])
+        jnp.concatenate(small_parts, axis=0),
+        grad_kv.reshape(n_row // TP, TP, rows, 2 * kvh), ff_sums, n_row,
+    )
+    mixer_land, other_land = last(mixer_sums, edges[3])
     (
         delta_gate, delta_up, delta_down, delta_mamba_gate, delta_mamba_input,
-        delta_query, delta_key, delta_value, delta_mamba_out, delta_attn_out,
-    ) = unpack(ff_land, mixer_land, mh, qh, kvh, fh)
+        delta_query, delta_mamba_out, delta_attn_out,
+    ) = unpack(ff_land, mixer_land, mh, qh, fh)
+    delta_key, delta_value = delta_kv[:, :kvh], delta_kv[:, kvh:]
 
     def join(stacked):
         return stacked.transpose(1, 0, 2).reshape(stacked.shape[1], -1).astype(jnp.float32)
 
-    mine = mixer_land[:, :, edges[5] : edges[5] + 128]
+    mine = mixer_land[:, :, edges[3] : edges[3] + 128]
     state_first = jnp.where(c == 0, mine, other_land)
     state_second = jnp.where(c == 0, other_land, mine)
     delta_state = jnp.concatenate(

time: 657 us -> 620 us (0.944); the launches traced: 648 us -> 619 us
  Pallas kernels: 458 us -> 481 us
  matrix products: 67.6 us -> 50.9 us
  other arithmetic: 18.6 us -> 3.57 us
  local copies, waits for them, and re-layouts: 47 us -> 33.7 us
  waiting for transfers between devices: 32 us -> 24.4 us
    pallas_call x0 -> x2, Pallas kernels: none -> 23 us  [products(): pl.pallas_call(partial(products_kernel, parts), name='products', grid=(wi...]
    dot_general x4 -> x0, matrix products: 19.6 us -> none  [matmul_left(): lax.dot_general(first_op, second_op, (((0,), (0,)), ((), ())), preferred_...]
    ppermute x4 -> x0, waiting for transfers between devices: 17.4 us -> none  [the longest x3 12.9 us: local(): lax.ppermute(pick(ff_sum, member(partner(r, m, FFN), FFN)), 'row', flips(...]
    pallas_call x1, Pallas kernels: 31.1 us -> 43.3 us  [mixer_back(): pl.pallas_call(partial(mixer_back_kernel, sh, ph), name='mixer_back', out...]
    reduce_scatter x2, waiting for transfers between devices: 0.01 us -> 12 us  [sum_groups(): lax.psum_scatter(grad, 'row', scatter_dimension=0, axis_index_groups=alik...]
    pallas_call x1, Pallas kernels: 105 us -> 117 us  [send_home(): pl.pallas_call(home_kernel, name='home', out_shape=(jax.ShapeDtypeStruct(...]
    pallas_call x1, Pallas kernels: 165 us -> 154 us  [deal(): pl.pallas_call(deal_kernel, name='deal', out_shape=(jax.ShapeDtypeStruct(...]
    concatenate x2 -> x1, other arithmetic: 11 us -> 0.31 us  [local(): jnp.concatenate([grad_gate.astype(bf), grad_up.astype(bf)], axis=1)]
  transfers between devices with their start and end apart: 12 -> 8, of which waited for: 5 -> 2; matrix products, arithmetic and copies ran while one was open for 11% -> 8% of each run, Pallas kernels for 40% -> 47%
where the time goes in v4:
time: 620 us; the launch traced here: 619 us
  Pallas kernels  481 us (78%)
  matrix products  50.9 us (8%)
  local copies, waits for them, and re-layouts  33.7 us (5%)
  waiting for transfers between devices  24.4 us (4%)
  between operations  14.8 us (2%)
  starting transfers between devices  10.9 us (2%)
    pallas_call x1, Pallas kernels, deal(): pl.pallas_call(deal_kernel, name='deal', out_shape=(jax.ShapeDtypeStruct(...  154 us
    pallas_call x1, Pallas kernels, send_home(): pl.pallas_call(home_kernel, name='home', out_shape=(jax.ShapeDtypeStruct(...  117 us
    pallas_call x1, Pallas kernels, turn(): pl.pallas_call(turn_kernel, name='turn', out_shape=(jax.ShapeDtypeStruct(...  49 us
    pallas_call x1, Pallas kernels, middle(): pl.pallas_call(middle_kernel, name='middle', out_shape=(jax.ShapeDtypeStr...  46 us
    pallas_call x1, Pallas kernels, mixer_back(): pl.pallas_call(partial(mixer_back_kernel, sh, ph), name='mixer_back', out...  43.3 us
    dot_general x4, matrix products, matmul_trans(): lax.dot_general(first_op, second_op, (((1,), (1,)), ((), ())), preferred_...  27.4 us
    dot_general x4, matrix products, matmul(): return jnp.dot(first_op, second_op, preferred_element_type=jnp.float32)  23.5 us
    unnamed x102, local copies, waits for them, and re-layouts  23.2 us
  transfers between devices with their start and end apart: 8, of which 2 were waited for; matrix products, arithmetic and copies ran while one was open for 8% of the time, Pallas kernels for 47%

profile of v4, /device:TPU:9, one launch (start us, length us, event | category | flops | bytes accessed | tf_op | source)
XLA Modules:
  0.0 619.3 jit_solution(41371235599978960)
XLA Ops:
  7.3 0.7 reshape.166
  8.2 0.9 fusion.21
  10.1 0.7 copy.114
  10.8 1.9 copy.84
  12.7 1.7 copy.85
  14.3 2.0 copy.86
  16.4 1.4 fusion.19.meta
  17.7 154.0 %deal.1 = (s32[16,8,128]{2,1,0:T(8,128)}, bf16[256,256]{1,0:T(8,128)(2,1)}, bf16[256,256]{1,0:T(8,128)(2,1)}, bf16[128,2048]{1,0:T(8,128)(2,1)}, bf16[128,2048]{...) custom-call(s32[8,128]{1,0:T(8,128)} %fusion.19.meta, ...), custom_call_target="tpu_custom_call" | custom-call | bytes 340000000 | tf_op jit(solution)/shard_map/deal/pallas_call | solution.py:621
  172.2 1.5 collective-permute-start.4
  173.7 2.3 collective-permute-start
  176.2 0.8 dynamic-slice.12
  177.0 10.5 %fusion.2.projected = f32[1024,1280]{1,0:T(8,128)} fusion(bf16[1024,2048]{1,0:T(8,128)(2,1)} %bitcast.89, bf16[2048,1792]{1,0:T(8,128)(2,1)} %bitcast.144), kind=kOutput, calls=%fused_computation.2 | convolution fusion | flops 5368709120 | bytes 14680064 | tf_op jit(solution)/shard_map/dot_general | solution.py:24
  187.9 0.7 constant_dynamic-slice_fusion.5
  189.1 2.5 copy-done.2
  191.6 21.9 %mixer.1 = (bf16[1024,512]{1,0:T(8,128)(2,1)S(1)}, f32[1024,384]{1,0:T(8,128)S(1)}, bf16[8,128,128]{2,1,0:T(8,128)(2,1)S(1)}) custom-call(s32[8,3]{1,0:T(8,128)S(1)} %bitcast.108, f32[1024,1280]{1,0:T(8,128)S(1)} %copy-done.2, f32[8,384]{1,0:T(8,128)S(1)} %maximum_maximum_fusion.1.chan, f32[8,128]{1,0:T(8,128)S(1)} %pad_maximum_fusion.2.side, ...), custom_call_target="tpu_custom_call" | custom-call | bytes 102000000 | tf_op jit(solution)/shard_map/mixer/pallas_call | solution.py:1247
  213.5 1.1 copy-done.15
  214.6 4.5 convolution_convert_fusion.1
  219.2 4.8 collective-permute-start.5
  224.1 46.0 %middle.1 = (f32[128,2048]{1,0:T(8,128)S(1)}, bf16[8,128,2048]{2,1,0:T(8,128)(2,1)S(1)}) custom-call(bf16[8,128,2048]{2,1,0:T(8,128)(2,1)S(1)} %bitcast.97, bf16[128,2048]{1,0:T(8,128)(2,1)S(1)} %copy-done.11, f32[1,2048]{1,0:T(1,128)S(1)} %bitcast.110), custom_call_target="tpu_custom_call" | custom-call | bytes 204000000 | tf_op jit(solution)/shard_map/middle/pallas_call | solution.py:676
  270.1 1.8 collective-permute-start.2
  271.9 12.4 %collective-permute-done.2.refs_3_ = bf16[4,128,512]{2,1,0:T(8,128)(2,1)S(1)} collective-permute-done((bf16[4,128,512]{2,1,0:T(8,128)(2,1)}, bf16[4,128,512]{2,1,0:T(8,128)(2,1)S(1)}, u32[]{:S(2)}, u32[]{:S(2)}) %collective-permute-start.2) | collective-permute-done | bytes 524320 | tf_op jit(solution)/shard_map/ppermute | solution.py:1492
  284.3 1.1 place.2
  286.0 4.5 fusion.24
  290.6 3.3 fusion.9
  294.2 0.6 copy-done.25
  294.8 10.3 %products.2 = bf16[2048,1536]{1,0:T(8,128)(2,1)} custom-call(bf16[1024,2048]{1,0:T(8,128)(2,1)S(1)} %bitcast.94, bf16[1024,1024]{1,0:T(8,128)(2,1)S(1)} %pad_maximum_fusion.refs_1_, bf16[1024,2048]{1,0:T(8,128)(2,1)S(1)} %bitcast.92, bf16[1024,512]{1,0:T(8,128)(2,1)S(1)} %get-tuple-element.169.refs_3_), custom_call_target="tpu_custom_call" | custom-call | bytes 34000000 | tf_op jit(solution)/shard_map/products/pallas_call | solution.py:905
  305.2 8.5 %convolution_convert_fusion.2 = bf16[1024,2048]{1,0:T(8,128)(2,1)} fusion(bf16[1024,1024]{1,0:T(8,128)(2,1)S(1)} %pad_maximum_fusion.refs_1_, bf16[2048,1024]{1,0:T(8,128)(2,1)} %bitcast.99), kind=kOutput, calls=%fused_computation.7 | convolution fusion | flops 4297064448 | bytes 10485760 | tf_op jit(solution)/shard_map/dot_general | solution.py:28
  313.7 49.0 %turn.1 = (f32[128,2048]{1,0:T(8,128)S(1)}, f32[1,2048]{1,0:T(1,128)S(1)}, bf16[8,128,2048]{2,1,0:T(8,128)(2,1)}) custom-call(bf16[8,128,2048]{2,1,0:T(8,128)(2,1)} %bitcast.117, f32[128,2048]{1,0:T(8,128)S(1)} %get-tuple-element.84.mid, bf16[128,2048]{1,0:T(8,128)(2,1)S(1)} %copy-done.29, f32[1,2048]{1,0:T(1,128)S(1)} %bitcast.111), custom_call_target="tpu_custom_call" | custom-call | bytes 204000000 | tf_op jit(solution)/shard_map/turn/pallas_call | solution.py:724
  362.8 4.4 convolution_convert_fusion
  367.2 5.2 fusion.11.grads
  372.5 43.3 %mixer_back.1 = (bf16[1024,1280]{1,0:T(8,128)(2,1)}, f32[8,384]{1,0:T(8,128)}, f32[8,128]{1,0:T(8,128)}, bf16[128,2048]{1,0:T(8,128)(2,1)}) custom-call(s32[8,3]{1,0:T(8,128)} %bitcast.109, f32[1024,1280]{1,0:T(8,128)} %fusion.2.projected, f32[8,384]{1,0:T(8,128)} %copy-done.34, f32[8,128]{1,0:T(8,128)} %copy-done.36, f32[128,256]{1,0:T(8,128)} %copy-done.18, ...), custom_call_target="tpu_custom_call" | custom-call | bytes 170000000 | tf_op jit(solution)/shard_map/mixer_back/pallas_call | solution.py:1390
  415.7 2.2 copy-done.6
  417.9 1.7 copy-done.9
  419.7 12.7 %products.3 = (bf16[2048,1536]{1,0:T(8,128)(2,1)}, bf16[2048,256]{1,0:T(8,128)(2,1)S(1)}) custom-call(bf16[1024,2048]{1,0:T(8,128)(2,1)S(1)} %bitcast.90, bf16[1024,1280]{1,0:T(8,128)(2,1)S(1)} %copy-done.9, bf16[1024,2048]{1,0:T(8,128)(2,1)S(1)} %bitcast.96, bf16[1024,512]{1,0:T(8,128)(2,1)S(1)} %copy-done.22), custom_call_target="tpu_custom_call" | custom-call | bytes 34000000 | tf_op jit(solution)/shard_map/products/pallas_call | solution.py:905
  432.4 1.0 copy-done.23
  435.2 10.1 %fusion.4 = bf16[1024,2048]{1,0:T(8,128)(2,1)} fusion(bf16[1024,1280]{1,0:T(8,128)(2,1)S(1)} %copy-done.10, bf16[2048,1792]{1,0:T(8,128)(2,1)} %bitcast.147), kind=kOutput, calls=%fused_computation.4 | convolution fusion | flops 5370806272 | bytes 12058624 | tf_op jit(solution)/shard_map/dot_general | solution.py:28
  445.3 116.8 %home.1 = (bf16[2,128,2048]{2,1,0:T(8,128)(2,1)S(1)}, bf16[2,128,2048]{2,1,0:T(8,128)(2,1)S(1)}, f32[8,56,128]{2,1,0:T(8,128)S(1)}, f32[128,256]{1,0:T(8,128)S(1)}, bf16[4,128,1536]{2,1,0:T(8,128)(2,1)}) custom-call(bf16[8,128,2048]{2,1,0:T(8,128)(2,1)} %bitcast.116, bf16[128,2048]{1,0:T(8,128)(2,1)S(1)} %copy-done.12, f32[128,2048]{1,0:T(8,128)S(1)} %copy-done.20, ...), custom_call_target="tpu_custom_call" | custom-call | bytes 255000000 | tf_op jit(solution)/shard_map/home/pallas_call | solution.py:961
  563.6 0.7 reshape.191
  564.4 0.7 squeeze_reshape.3
  567.4 0.7 fusion.20
  568.1 12.0 %reduce-scatter.5.cloned.1.call-done = bf16[512,1536]{1,0:T(8,128)(2,1)} async-done(((bf16[2048,1536]{1,0:T(8,128)(2,1)}), bf16[512,1536]{1,0:T(8,128)(2,1)}) %reduce-scatter.5.cloned.1.call-update) | async-done | bytes 1572880 | tf_op jit(solution)/shard_map/reduce_scatter | solution.py:1515
  580.1 1.4 copy-done.16
  581.5 22.3 %last.1 = (bf16[4,128,1536]{2,1,0:T(8,128)(2,1)S(1)}, bf16[4,128,128]{2,1,0:T(8,128)(2,1)S(1)}) custom-call(bf16[4,128,1536]{2,1,0:T(8,128)(2,1)S(1)} %bitcast.102), custom_call_target="tpu_custom_call" | custom-call | bytes 85000000 | tf_op jit(solution)/shard_map/last/pallas_call | solution.py:872
  603.9 1.4 copy-done.17
  605.3 2.9 unpack.1
  608.9 0.8 copy.101
  610.5 1.0 copy.119
  611.5 1.0 copy.120
  (170 shorter events, 10.9 us)
Async XLA Ops:
  7.2 169.8 %copy-start = (f32[4,1536]{1,0:T(4,128)S(1)}, f32[4,1536]{1,0:T(4,128)}, u32[]{:S(2)}) copy-start(f32[4,1536]{1,0:T(4,128)} %param.34) | copy-start | bytes 73732
  7.2 426.2 %reduce-scatter.3.cloned.1.call-start = ((), (), s32[]{:S(2)}) async-start(), calls=%async_computation.2 | async-start | bytes 7864320 | tf_op jit(solution)/shard_map/reduce_scatter | solution.py:1515
  9.7 166.3 %copy-start.45 = (f32[24]{0:T(128)S(1)}, f32[24]{0:T(128)}, u32[]{:S(2)}) copy-start(f32[24]{0:T(128)} %param.40) | copy-start | bytes 292
  171.8 47.4 %collective-permute-start.3 = (bf16[4,128,1024]{2,1,0:T(8,128)(2,1)}, bf16[4,128,1024]{2,1,0:T(8,128)(2,1)S(1)}, u32[]{:S(2)}, u32[]{:S(2)}) collective-permute-start(bf16[4,128,1024]{2,1,0:T(8,128)(2,1)} %get-tuple-element.81.refs_0_), channel_id=1, source_target_pairs={{0,16},{2,18},{4,20},{6,22},{8,24},{10,26},{12,28},{14,30},{16,0},... | collective-permute-start | bytes 3145736 | tf_op jit(solution)/shard_map/ppermute | solution.py:1492
  172.2 113.3 %collective-permute-start.4 = (bf16[4,128,1024]{2,1,0:T(8,128)(2,1)}, bf16[4,128,1024]{2,1,0:T(8,128)(2,1)S(1)}, u32[]{:S(2)}, u32[]{:S(2)}) collective-permute-start(bf16[4,128,1024]{2,1,0:T(8,128)(2,1)} %get-tuple-element.81.refs_0_), channel_id=1, source_target_pairs={{0,8},{2,10},{4,12},{6,14},{8,0},{10,2},{12,4},{14,6},{16,24},{18,... | collective-permute-start | bytes 3145736 | tf_op jit(solution)/shard_map/ppermute | solution.py:1492
  173.7 96.4 %collective-permute-start = (bf16[4,128,512]{2,1,0:T(8,128)(2,1)}, bf16[4,128,512]{2,1,0:T(8,128)(2,1)}, u32[]{:S(2)}, u32[]{:S(2)}) collective-permute-start(bf16[4,128,512]{2,1,0:T(8,128)(2,1)} %get-tuple-element.76.refs_0_), channel_id=1, source_target_pairs={{0,16},{2,18},{4,20},{6,22},{8,24},{10,26},{12,28},{14,30},{16,0},... | collective-permute-start | bytes 1572872 | tf_op jit(solution)/shard_map/ppermute | solution.py:1492
  177.0 10.6 %copy-start.43 = (f32[24]{0:T(128)S(1)}, f32[24]{0:T(128)}, u32[]{:S(2)}) copy-start(f32[24]{0:T(128)} %param.39) | copy-start | bytes 292
  177.0 10.6 %copy-start.44 = (f32[24]{0:T(128)S(1)}, f32[24]{0:T(128)}, u32[]{:S(2)}) copy-start(f32[24]{0:T(128)} %param.38) | copy-start | bytes 292
  177.0 10.7 %copy-start.39 = (f32[4,512]{1,0:T(4,128)S(1)}, f32[4,512]{1,0:T(4,128)}, u32[]{:S(2)}) copy-start(f32[4,512]{1,0:T(4,128)} %param.36) | copy-start | bytes 24580
  177.0 10.7 %copy-start.42 = (f32[512]{0:T(512)S(1)}, f32[512]{0:T(512)}, u32[]{:S(2)}) copy-start(f32[512]{0:T(512)} %param.37) | copy-start | bytes 6148
  187.9 31.2 %copy-start.36 = (f32[8,128]{1,0:T(8,128)}, f32[8,128]{1,0:T(8,128)S(1)}, u32[]{:S(2)}) copy-start(f32[8,128]{1,0:T(8,128)S(1)} %pad_maximum_fusion.2.side) | copy-start | bytes 12292
  188.6 30.5 %copy-start.35 = (s32[4,2,3]{2,1,0:T(2,128)}, s32[4,2,3]{2,1,0:T(2,128)S(1)}, u32[]{:S(2)}) copy-start(s32[4,2,3]{2,1,0:T(2,128)S(1)} %pad_add_fusion) | copy-start | bytes 292
  189.0 30.1 %copy-start.18 = (f32[128,256]{1,0:T(8,128)}, f32[128,256]{1,0:T(8,128)S(1)}, u32[]{:S(2)}) copy-start(f32[128,256]{1,0:T(8,128)S(1)} %pad_maximum_fusion.1.table) | copy-start | bytes 393220
  189.1 30.0 %copy-start.34 = (f32[8,384]{1,0:T(8,128)}, f32[8,384]{1,0:T(8,128)S(1)}, u32[]{:S(2)}) copy-start(f32[8,384]{1,0:T(8,128)S(1)} %maximum_maximum_fusion.1.chan) | copy-start | bytes 36868
  189.1 2.5 copy-start.2
  214.6 4.5 copy-start.21
  214.6 4.6 copy-start.31
  214.6 9.4 %copy-start.30 = (bf16[4,128,512]{2,1,0:T(8,128)(2,1)S(1)}, bf16[4,128,512]{2,1,0:T(8,128)(2,1)}, u32[]{:S(2)}) copy-start(bf16[4,128,512]{2,1,0:T(8,128)(2,1)} %get-tuple-element.76.refs_0_) | copy-start | bytes 1572868
  214.6 9.4 %copy-start.11 = (bf16[128,2048]{1,0:T(8,128)(2,1)S(1)}, bf16[128,2048]{1,0:T(8,128)(2,1)}, u32[]{:S(2)}) copy-start(bf16[128,2048]{1,0:T(8,128)(2,1)} %get-tuple-element.78.x) | copy-start | bytes 1572868
  214.6 9.4 %copy-start.37 = (f32[2048]{0:T(1024)S(1)}, f32[2048]{0:T(1024)}, u32[]{:S(2)}) copy-start(f32[2048]{0:T(1024)} %param.46) | copy-start | bytes 24580
  219.2 66.2 %collective-permute-start.5 = (bf16[4,128,1024]{2,1,0:T(8,128)(2,1)S(1)}, bf16[4,128,1024]{2,1,0:T(8,128)(2,1)S(1)}, u32[]{:S(2)}, u32[]{:S(2)}) collective-permute-start(bf16[4,128,1024]{2,1,0:T(8,128)(2,1)S(1)} %collective-permute-done.3.refs_1_), channel_id=1, source_target_pairs={{0,8},{2,10},{4,12},{6,14},{8,0},{10,2},{12,4},{14,6},{16,24},{18,... | collective-permute-start | bytes 3145736 | tf_op jit(solution)/shard_map/ppermute | solution.py:1492
  224.0 47.8 %collective-permute-start.1 = (bf16[4,128,512]{2,1,0:T(8,128)(2,1)S(1)}, bf16[4,128,512]{2,1,0:T(8,128)(2,1)S(1)}, u32[]{:S(2)}, u32[]{:S(2)}) collective-permute-start(bf16[4,128,512]{2,1,0:T(8,128)(2,1)S(1)} %copy-done.30), channel_id=1, source_target_pairs={{0,8},{2,10},{4,12},{6,14},{8,0},{10,2},{12,4},{14,6},{16,24},{18,... | collective-permute-start | bytes 1572872 | tf_op jit(solution)/shard_map/ppermute | solution.py:1492
  224.1 61.4 %copy-start.27 = (bf16[4,128,1024]{2,1,0:T(8,128)(2,1)S(1)}, bf16[4,128,1024]{2,1,0:T(8,128)(2,1)}, u32[]{:S(2)}) copy-start(bf16[4,128,1024]{2,1,0:T(8,128)(2,1)} %get-tuple-element.81.refs_0_) | copy-start | bytes 3145732
  270.1 43.6 %copy-start.8 = (f32[128,2048]{1,0:T(8,128)}, f32[128,2048]{1,0:T(8,128)S(1)}, u32[]{:S(2)}) copy-start(f32[128,2048]{1,0:T(8,128)S(1)} %get-tuple-element.84.mid) | copy-start | bytes 3145732
  270.1 14.2 %collective-permute-start.2 = (bf16[4,128,512]{2,1,0:T(8,128)(2,1)}, bf16[4,128,512]{2,1,0:T(8,128)(2,1)S(1)}, u32[]{:S(2)}, u32[]{:S(2)}) collective-permute-start(bf16[4,128,512]{2,1,0:T(8,128)(2,1)} %collective-permute-done.refs_1_), channel_id=1, source_target_pairs={{0,8},{2,10},{4,12},{6,14},{8,0},{10,2},{12,4},{14,6},{16,24},{18,... | collective-permute-start | bytes 1572872 | tf_op jit(solution)/shard_map/ppermute | solution.py:1492
  285.4 5.1 copy-start.13
  286.0 4.5 copy-start.7
  286.0 4.5 copy-start.4
  305.2 274.9 %reduce-scatter.5.cloned.1.call-start = ((), (), s32[]{:S(2)}) async-start(), calls=%async_computation.3 | async-start | bytes 7864320 | tf_op jit(solution)/shard_map/reduce_scatter | solution.py:1515
  305.2 8.5 %copy-start.29 = (bf16[128,2048]{1,0:T(8,128)(2,1)S(1)}, bf16[128,2048]{1,0:T(8,128)(2,1)}, u32[]{:S(2)}) copy-start(bf16[128,2048]{1,0:T(8,128)(2,1)} %get-tuple-element.85.gy) | copy-start | bytes 1572868
  313.7 49.1 %copy-start.14 = (bf16[4,4,128,512]{3,2,1,0:T(8,128)(2,1)S(1)}, bf16[4,4,128,512]{3,2,1,0:T(8,128)(2,1)}, u32[]{:S(2)}) copy-start(bf16[4,4,128,512]{3,2,1,0:T(8,128)(2,1)} %copy-done.13) | copy-start | bytes 6291460
  313.7 49.1 %copy-start.26 = (bf16[1024,512]{1,0:T(8,128)(2,1)S(1)}, bf16[1024,512]{1,0:T(8,128)(2,1)}, u32[]{:S(2)}) copy-start(bf16[1024,512]{1,0:T(8,128)(2,1)} %copy-done.25) | copy-start | bytes 3145732
  362.8 4.4 copy-start.19
  362.8 4.4 copy-start.5
  372.5 43.3 %copy-start.3 = (bf16[8,128,2048]{2,1,0:T(8,128)(2,1)S(1)}, bf16[8,128,2048]{2,1,0:T(8,128)(2,1)}, u32[]{:S(2)}) copy-start(bf16[8,128,2048]{2,1,0:T(8,128)(2,1)} %get-tuple-element.71) | copy-start | bytes 12582916
  372.5 43.3 %copy-start.22 = (bf16[1024,512]{1,0:T(8,128)(2,1)S(1)}, bf16[1024,512]{1,0:T(8,128)(2,1)}, u32[]{:S(2)}) copy-start(bf16[1024,512]{1,0:T(8,128)(2,1)} %copy-done.21) | copy-start | bytes 3145732
  415.7 2.2 copy-start.6
  417.9 1.7 copy-start.9
  433.4 1.8 copy-start.10
  435.1 10.1 %copy-start.12 = (bf16[128,2048]{1,0:T(8,128)(2,1)S(1)}, bf16[128,2048]{1,0:T(8,128)(2,1)}, u32[]{:S(2)}) copy-start(bf16[128,2048]{1,0:T(8,128)(2,1)} %get-tuple-element.78.x) | copy-start | bytes 1572868
  435.1 10.1 %copy-start.20 = (f32[128,2048]{1,0:T(8,128)S(1)}, f32[128,2048]{1,0:T(8,128)}, u32[]{:S(2)}) copy-start(f32[128,2048]{1,0:T(8,128)} %copy-done.19) | copy-start | bytes 3145732
  435.1 10.1 %copy-start.24 = (bf16[2048,256]{1,0:T(8,128)(2,1)S(1)}, bf16[2048,256]{1,0:T(8,128)(2,1)}, u32[]{:S(2)}) copy-start(bf16[2048,256]{1,0:T(8,128)(2,1)} %copy-done.23) | copy-start | bytes 3145732
  435.1 10.1 %copy-start.28 = (bf16[128,2048]{1,0:T(8,128)(2,1)S(1)}, bf16[128,2048]{1,0:T(8,128)(2,1)}, u32[]{:S(2)}) copy-start(bf16[128,2048]{1,0:T(8,128)(2,1)} %get-tuple-element.91.result) | copy-start | bytes 1572868
  435.1 10.1 %copy-start.32 = (bf16[256,256]{1,0:T(8,128)(2,1)S(1)}, bf16[256,256]{1,0:T(8,128)(2,1)}, u32[]{:S(2)}) copy-start(bf16[256,256]{1,0:T(8,128)(2,1)} %get-tuple-element.92.give) | copy-start | bytes 393220
  435.1 10.1 %copy-start.33 = (bf16[256,256]{1,0:T(8,128)(2,1)S(1)}, bf16[256,256]{1,0:T(8,128)(2,1)}, u32[]{:S(2)}) copy-start(bf16[256,256]{1,0:T(8,128)(2,1)} %get-tuple-element.93.take) | copy-start | bytes 393220
  435.2 10.1 %copy-start.38 = (f32[2048]{0:T(1024)S(1)}, f32[2048]{0:T(1024)}, u32[]{:S(2)}) copy-start(f32[2048]{0:T(1024)} %param.29) | copy-start | bytes 24580
  603.9 1.4 copy-start.17
  605.3 7.1 %copy-start.1 = (f32[4,1536]{1,0:T(4,128)S(1)}, f32[4,1536]{1,0:T(4,128)}, u32[]{:S(2)}) copy-start(f32[4,1536]{1,0:T(4,128)} %param.34) | copy-start | bytes 73732
  (6 other events, 5.9 us)
Sparse Core Ops, SparseCore 0:
  305.3 117.4 reduce-scatter.2
  433.5 146.5 reduce-scatter.4

commit v5 on v4

--- a/solution.py
+++ b/solution.py
@@ -114,7 +114,7 @@
     )
 
 
-def greet(*groups, cross=False):
+def greet(*groups, cross=False, beyond=()):
     r, c = place()
     barrier = pltpu.get_barrier_semaphore()
     others = [(r, 1 - c)]
@@ -123,6 +123,7 @@
             others.append((partner(r, m, axes), c))
             if cross:
                 others.append((partner(r, m, axes), 1 - c))
+    others = others + [(flip(r, b), c) for b in beyond]
     for other in others:
         pl.semaphore_signal(barrier, inc=1, device_id=other, device_id_type=MESH)
     pl.semaphore_wait(barrier, len(others))
@@ -412,7 +413,7 @@
     lax.fori_loop(1, n_row, finish, 0)
 
 
-def greet_rows():
+def greet_rows(meanwhile=None):
     r, c = place()
     n_row = lax.axis_size("row")
     barrier = pltpu.get_barrier_semaphore()
@@ -425,6 +426,8 @@
 
     lax.fori_loop(1, n_row, greet, 0)
     pl.semaphore_signal(barrier, inc=1, device_id=(r, 1 - c), device_id_type=MESH)
+    if meanwhile is not None:
+        meanwhile()
     pl.semaphore_wait(barrier, n_row)
 
 
@@ -457,14 +460,17 @@
 
 
 def deal_kernel(
-    meta, tokens, cotangent, gain, *refs
+    order, lengths, tokens, cotangent, gain, *refs
 ):
-    kv_refs, first_refs, second_refs, refs = refs[:2], refs[2:5], refs[5:8], refs[8:]
-    up_refs, down_refs, refs = refs[:2], refs[2:3], refs[3:]
+    kv_refs, first_refs, refs = refs[:2], refs[2:5], refs[5:]
+    states, steps_in, mamba_out, attn_out, refs = *refs[:4], refs[4:]
+    up_refs, down, refs = refs[:2], refs[2], refs[3:]
     meta_all, give, take, x_out, gy_out, normed_all, gy_all, whole, slab_up, slab_down = refs[:10]
     x_mine, g_mine, buf, land, normed = refs[10:15]
     load, msend, mrecv, csend, crecv, nsend, nrecv, nhere, gsend, grecv, ghere = refs[15:26]
-    wsend, wrecv, acut, arecv, ahere, bcut, brecv, bhere, usend, urecv, uhere, dsend, drecv, dhere, kv_here = refs[26:]
+    wsend, wrecv, acut, arecv, ahere, bcut, brecv, bhere, usend, urecv, uhere, dsend, drecv, dhere, kv_here = refs[26:41]
+    meta, mixed, mamba_turned, attn_turned, down_turned = refs[41:]
+    second_refs, down_refs = (mixed, mamba_turned, attn_turned), (down_turned,)
     r, c = place()
     n_row = lax.axis_size("row")
     f = member(r, FFN)
@@ -476,7 +482,33 @@
     ]
     for copy in loads:
         copy.start()
-    greet_rows()
+    bf = jnp.bfloat16
+
+    def turn_weight(source, target):
+        target[...] = source[...].astype(jnp.float32).T.astype(bf)
+
+    def prepare():
+        count = lengths.shape[2]
+        meta[...] = jnp.zeros_like(meta)
+        meta[0:2, :] = order[...]
+        for i in range(2):
+            meta[2 + i : 3 + i, 0:count] = lengths[i]
+        part = states.shape[1] // 4
+        values = states[...].astype(jnp.float32)
+        first = jnp.where(c == 0, values[:, :part], values[:, part : 2 * part])
+        second = jnp.where(c == 0, values[:, 2 * part : 3 * part], values[:, 3 * part :])
+        step_values = steps_in[...].astype(jnp.float32)
+        sh, ph = part // TP, step_values.shape[1] // TP
+        width = mixed.shape[1] // TP
+        for k in range(TP):
+            cols = slice(k * sh, (k + 1) * sh)
+            strip = [first[:, cols], second[:, cols], step_values[:, k * ph : (k + 1) * ph]]
+            strip.append(jnp.zeros((values.shape[0], width - 2 * sh - ph), jnp.float32))
+            mixed[:, k * width : (k + 1) * width] = jnp.concatenate(strip, axis=1).astype(bf)
+        turn_weight(mamba_out, mamba_turned)
+        turn_weight(attn_out, attn_turned)
+
+    greet_rows(prepare)
     group = [mask_of(m, MIX) for m in range(TP)]
     first_cols = sum(ref.shape[1] for ref in first_refs) // TP
     kv_cols = first_cols + sum(ref.shape[1] for ref in kv_refs)
@@ -566,6 +598,7 @@
         for m in (1, 2, 3):
             piece_done(whole.at[r, :, cols], recv.at[m])
             forwards = forwards + weight_forward([group[m]], whole, cols, wsend.at[i], wrecv.at[i])
+    turn_weight(down, down_turned)
     finish_rows(buf, land, csend, crecv)
     permute_in(take, land, x_out, gy_out, slots)
 
@@ -608,14 +641,14 @@
             piece_done(slab.at[f], recv.at[m])
 
 
-def deal(meta, tokens, cotangent, gain, in_weights, ff_weights, n_row):
+def deal(order, lengths, tokens, cotangent, gain, kv, first, second, ff, strip, n_row):
     slots, width = tokens.shape[1:]
     bf = jnp.bfloat16
-    rows = in_weights[0].shape[0]
-    in_cols = sum(
-        array.shape[1] // (1 if i < 2 else TP) for i, array in enumerate(in_weights)
-    )
-    up_cols, down_cols = 2 * ff_weights[0].shape[1] // TP, ff_weights[2].shape[1] // TP
+    rows = first[0].shape[0]
+    states, steps_in, mamba_out, attn_out = second
+    in_cols = sum(array.shape[1] for array in kv) + sum(array.shape[1] for array in first) // TP
+    in_cols += strip + (mamba_out.shape[0] + attn_out.shape[0]) // TP
+    up_cols, down_cols = 2 * ff[0].shape[1] // TP, ff[2].shape[0] // TP
     vm, hb = pl.BlockSpec(memory_space=VMEM), pl.BlockSpec(memory_space=ANY)
     dma = pltpu.SemaphoreType.DMA
     return pl.pallas_call(
@@ -633,7 +666,7 @@
             jax.ShapeDtypeStruct((TP, rows, up_cols), bf),
             jax.ShapeDtypeStruct((TP, rows, down_cols), bf),
         ),
-        in_specs=[vm, hb, hb, vm] + [hb] * 11,
+        in_specs=[vm, vm, hb, hb, vm] + [hb] * 5 + [vm] * 4 + [hb, hb, vm],
         out_specs=(vm,) * 5 + (hb,) * 5,
         scratch_shapes=[
             VMEM((slots, width), bf),
@@ -651,14 +684,45 @@
         + gather_scratch()
         + [dma((3, n_row)), dma((3, n_row))]
         + [dma((TP,)), dma((TP,)), dma] * 4
-        + [dma],
+        + [dma]
+        + [
+            VMEM((8, 128), jnp.int32),
+            VMEM((rows, TP * strip), bf),
+            VMEM((rows, mamba_out.shape[0]), bf),
+            VMEM((rows, attn_out.shape[0]), bf),
+            VMEM((rows, ff[2].shape[0]), bf),
+        ],
         compiler_params=params(0, 58),
         cost_estimate=cost(100),
-    )(meta, tokens, cotangent, gain, *in_weights, *ff_weights)
-
-
-def middle_kernel(parts, x, gain, mid, normed_all, near, out2, far, s1, r1, s2, r2, normed, nsend, nrecv, nhere):
-    greet(*{MIX, FFN})
+    )(order, lengths, tokens, cotangent, gain, *kv, *first, *second, *ff)
+
+
+def slab_copy(slab, whole, mask, b, send, recv):
+    r, c = place()
+    n_row = lax.axis_size("row")
+    at = whole.at[group_of(turned_row(r, mask), n_row, FFN)]
+    lands = mask | 1 << b
+    k = group_index(lands, n_row)
+    return remote(at if mask else slab, at, send.at[k], recv.at[k], flip(r, b), c)
+
+
+def group_index(mask, n_row):
+    return sum((mask >> b & 1) << i for i, b in enumerate(data_bits(n_row, FFN)))
+
+
+def middle_kernel(
+    parts, x, gain, slab, mid, normed_all, whole,
+    near, out2, far, s1, r1, s2, r2, normed, nsend, nrecv, nhere, wsend, wrecv, where,
+):
+    r, c = place()
+    n_row = lax.axis_size("row")
+    bits = data_bits(n_row, FFN)
+    greet(*{MIX, FFN}, beyond=bits)
+    own = pltpu.make_async_copy(slab, whole.at[group_of(r, n_row, FFN)], where)
+    own.start()
+    copies = {1 << b: slab_copy(slab, whole, 0, b, wsend, wrecv) for b in bits}
+    for copy in copies.values():
+        copy.start()
     scatter_sum(parts, near, out2, far, s1, r1, s2, r2, mid, MIX)
 
     def norm(rows):
@@ -668,26 +732,46 @@
         normed[rows, :] = (values * scale * gain[...]).astype(jnp.bfloat16)
 
     by_rows(mid.shape[0], norm)
-    gather(normed, normed_all, nsend, nrecv, nhere, FFN)
-
-
-def middle(parts, x, gain):
+    started = gather_start(normed, normed_all, nsend, nrecv, nhere, FFN)
+    passed = gather_turn(started, normed_all, nsend, nrecv, FFN)
+    for i, b in enumerate(bits):
+        for mask in [mask for mask in copies if mask >> b & 1]:
+            copies[mask].wait_recv()
+            for later in bits[i + 1 :]:
+                lands = mask | 1 << later
+                copies[lands] = slab_copy(slab, whole, mask, later, wsend, wrecv)
+                copies[lands].start()
+    gather_finish(started, passed, normed_all, nsend, nrecv, FFN)
+    own.wait()
+    for copy in copies.values():
+        copy.wait_send()
+
+
+def middle(parts, x, gain, slab, n_row):
     slots, width = x.shape
+    groups = n_row // TP
+    vm, hb = pl.BlockSpec(memory_space=VMEM), pl.BlockSpec(memory_space=ANY)
     return pl.pallas_call(
         middle_kernel,
         name="middle",
         out_shape=(
             jax.ShapeDtypeStruct((slots, width), jnp.float32),
             jax.ShapeDtypeStruct((GROUP, slots, width), jnp.bfloat16),
+            jax.ShapeDtypeStruct((groups,) + slab.shape, slab.dtype),
         ),
-        in_specs=[pl.BlockSpec(memory_space=VMEM)] * 3,
-        out_specs=(pl.BlockSpec(memory_space=VMEM), pl.BlockSpec(memory_space=ANY)),
+        in_specs=[vm] * 3 + [hb],
+        out_specs=(vm, hb, hb),
         scratch_shapes=scatter_scratch(slots, width)
         + [VMEM((slots, width), jnp.bfloat16)]
-        + gather_scratch(),
+        + gather_scratch()
+        + [
+            pltpu.SemaphoreType.DMA((groups,)),
+            pltpu.SemaphoreType.DMA((groups,)),
+            pltpu.SemaphoreType.DMA,
+        ],
         compiler_params=params(1, 40),
         cost_estimate=cost(60),
-    )(parts, x, gain)
+    )(parts, x, gain, slab)
 
 
 def norm_back(values, gain, grad):
@@ -740,7 +824,7 @@
 
 
 def home_kernel(
-    parts, x, d_mid, result, gain, give, take, small, kv_parts, ff_sums,
+    parts, x, d_mid, ff_parts, mid, gain, give, take, chan_sums, side_sums, ff_gain_sums, kv_parts, ff_sums,
     output, gradient, small_all, kv_sums, ff_land,
     near, out2, far, s1, r1, s2, r2, total, first, second, buf, land, csend, crecv, here, osend, orecv,
     d_gain, stages, stage_land, tsend, trecv, gsend, grecv, ghere, *more
@@ -749,23 +833,29 @@
     slots, width = x.shape
     bits = data_bits(lax.axis_size("row"), MIX)
     greet_rows()
-    kv_near, kv_held, kv_far, kv_s1, kv_r1, kv_s2, kv_r2 = more[3:]
+    kv_near, kv_held, kv_far, kv_s1, kv_r1, kv_s2, kv_r2 = more[3:10]
+    ff_total = more[10]
     delivered = deliver(ff_sums, ff_land, *more[:3], FFN)
-    scatter_sum(parts, near, out2, far, s1, r1, s2, r2, total, MIX)
+    steps = scatter_steps(parts, near, out2, far, s1, r1, s2, r2, total, MIX)
+    ff_steps = scatter_steps(ff_parts, *more[11:], ff_total, FFN)
+    for pair in zip(steps, ff_steps):
+        pass
     d_gain[...] = jnp.zeros_like(d_gain)
 
     def back(rows):
         values = x[rows, :].astype(jnp.float32)
         grad, gain_part = norm_back(values, gain[...], total[rows, :])
         second[rows, :] = (d_mid[rows, :] + grad).astype(jnp.bfloat16)
-        first[rows, :] = result[rows, :].astype(jnp.bfloat16)
+        first[rows, :] = (ff_total[rows, :] + mid[rows, :]).astype(jnp.bfloat16)
         d_gain[...] += gain_part
 
     by_rows(slots, back)
-    head = small.shape[0]
-    stages[0, :head, :] = small[...]
-    for k in range(width // 128):
-        stages[0, head + k : head + k + 1, :] = d_gain[:, k * 128 : (k + 1) * 128]
+    at = 0
+    for sums in (chan_sums, side_sums, ff_gain_sums, d_gain):
+        for i in range(sums.shape[0]):
+            for k in range(sums.shape[1] // 128):
+                stages[0, at : at + 1, :] = sums[i : i + 1, k * 128 : (k + 1) * 128]
+                at += 1
 
     def stage_copy(i):
         return remote(
@@ -896,7 +986,7 @@
 
 def products(pairs, *parts):
     tokens, width = pairs[0][0].shape
-    tile = 256
+    tile = min(512, width)
     specs = []
     for left, right in pairs:
         specs.append(pl.BlockSpec((tokens, tile), lambda i: (0, i)))
@@ -915,12 +1005,22 @@
 
 
 def unpack_kernel(
-    ff, mixer, gate, up, down, mamba_gate, mamba_input, query, mamba_out, attn_out
+    sh, ph, ff, mixer, misc, small, kv, home_out, home_grad,
+    output, gradient, mixer_gain, mamba_gate, mamba_input, state, step, conv_k, conv_b, state_k, state_b,
+    step_bias, decay, skip, mamba_out, query, key, value, attn_out, ff_gain, gate, up, down, sems,
 ):
+    c = lax.axis_index("col")
     f32 = jnp.float32
+    copies = [
+        pltpu.make_async_copy(home_out, output, sems.at[0]),
+        pltpu.make_async_copy(home_grad, gradient, sems.at[1]),
+    ]
+    for copy in copies:
+        copy.start()
     mh = mamba_gate.shape[1] // TP
     fh = gate.shape[1] // TP
     qh = query.shape[1] // TP
+    kvh = key.shape[1]
     at = 2 * mh + qh
     out = mixer.shape[2] - mh - qh
     for m in range(TP):
@@ -935,28 +1035,120 @@
         query[:, cols(qh)] = mixer[m, :, 2 * mh : at].astype(f32)
         mamba_out[cols(mh), :] = mixer[m, :, out : out + mh].astype(f32).T
         attn_out[cols(qh), :] = mixer[m, :, out + mh :].astype(f32).T
-
-
-def unpack(ff, mixer, mh, qh, fh):
-    rows = ff.shape[1]
-    vm = pl.BlockSpec(memory_space=VMEM)
-    shapes = [(rows, TP * fh)] * 2 + [(TP * fh, rows)] + [(rows, TP * mh)] * 2
-    shapes += [(rows, TP * qh), (TP * mh, rows), (TP * qh, rows)]
+    key[...] = kv[:, :kvh]
+    value[...] = kv[:, kvh:]
+
+    mine = [mixer[m, :, at : at + 128].astype(f32) for m in range(TP)]
+    other = [misc[m].astype(f32) for m in range(TP)]
+    by_col = [
+        [jnp.where(c == col, mine[m], other[m]) for m in range(TP)] for col in range(2)
+    ]
+    state[...] = jnp.concatenate(
+        [
+            by_col[col][m][:, part * sh : (part + 1) * sh]
+            for part in range(2)
+            for col in range(2)
+            for m in range(TP)
+        ],
+        axis=1,
+    )
+    step[...] = jnp.concatenate([part[:, 2 * sh : 2 * sh + ph] for part in mine], axis=1)
+
+    lanes = mh // 128
+    channels = [
+        jnp.concatenate(
+            [
+                small[2 * m + c, i * lanes + k : i * lanes + k + 1, :]
+                for m in range(TP)
+                for k in range(lanes)
+            ],
+            axis=1,
+        )
+        for i in range(6)
+    ]
+    for i in range(4):
+        conv_k[i : i + 1, :] = channels[i]
+    conv_b[...] = channels[4]
+    per_head = mh // ph
+    shape = (TP * mh, TP * ph)
+    heads = lax.broadcasted_iota(jnp.int32, shape, 1) * per_head
+    channel = lax.broadcasted_iota(jnp.int32, shape, 0)
+    picks = ((channel >= heads) & (channel < heads + per_head)).astype(f32)
+    skip[...] = dot(jnp.broadcast_to(channels[5], (8, TP * mh)), picks, 1, 0, HIGH)[:1, :]
+    start = 8 * lanes
+    sides = [[small[2 * m + col, start : start + 8, :] for m in range(TP)] for col in range(2)]
+    states = jnp.concatenate(
+        [
+            sides[col][m][:, part * sh : (part + 1) * sh]
+            for part in range(2)
+            for col in range(2)
+            for m in range(TP)
+        ],
+        axis=1,
+    )
+    state_k[...] = states[:4, :]
+    state_b[...] = states[4:5, :]
+    own_heads = jnp.concatenate(
+        [jnp.where(c == 0, sides[0][m], sides[1][m])[:, 2 * sh : 2 * sh + ph] for m in range(TP)], axis=1
+    )
+    step_bias[...] = own_heads[5:6, :]
+    decay[...] = own_heads[6:7, :]
+    start = start + 8
+    for gain in (ff_gain, mixer_gain):
+        count = gain.shape[1] // 128
+        total = sum(small[i, start : start + count, :] for i in range(GROUP))
+        for k in range(count):
+            gain[:, k * 128 : (k + 1) * 128] = total[k : k + 1, :]
+        start = start + count
+    for copy in copies:
+        copy.wait()
+
+
+def unpack(ff, mixer, misc, small, kv, output, gradient, mh, qh, fh, sh, ph):
+    rows, width = ff.shape[1], output.shape[2]
+    kvh = kv.shape[1] // 2
+    vm, hb = pl.BlockSpec(memory_space=VMEM), pl.BlockSpec(memory_space=ANY)
+    f32 = jnp.float32
+    shapes = [
+        (1, width),
+        (rows, TP * mh),
+        (rows, TP * mh),
+        (rows, 2 * GROUP * sh),
+        (rows, TP * ph),
+        (4, TP * mh),
+        (1, TP * mh),
+        (4, 2 * GROUP * sh),
+        (1, 2 * GROUP * sh),
+        (1, TP * ph),
+        (1, TP * ph),
+        (1, TP * ph),
+        (TP * mh, rows),
+        (rows, TP * qh),
+        (rows, kvh),
+        (rows, kvh),
+        (TP * qh, rows),
+        (1, width),
+        (rows, TP * fh),
+        (rows, TP * fh),
+        (TP * fh, rows),
+    ]
     return pl.pallas_call(
-        unpack_kernel,
+        partial(unpack_kernel, sh, ph),
         name="unpack",
-        out_shape=tuple(jax.ShapeDtypeStruct(shape, jnp.float32) for shape in shapes),
-        in_specs=[vm] * 2,
-        out_specs=(vm,) * len(shapes),
+        out_shape=tuple(jax.ShapeDtypeStruct(a.shape, a.dtype) for a in (output, gradient))
+        + tuple(jax.ShapeDtypeStruct(shape, f32) for shape in shapes),
+        in_specs=[vm] * 5 + [hb] * 2,
+        out_specs=(hb,) * 2 + (vm,) * len(shapes),
+        scratch_shapes=[pltpu.SemaphoreType.DMA((2,))],
         compiler_params=pltpu.CompilerParams(vmem_limit_bytes=40 << 20),
         cost_estimate=cost(8),
-    )(ff, mixer)
-
-
-def send_home(parts, x, d_mid, result, gain, give, take, small, kv_parts, ff_sums, n_row):
+    )(ff, mixer, misc, small, kv, output, gradient)
+
+
+def send_home(parts, x, d_mid, ff_parts, mid, gain, give, take, small, kv_parts, ff_sums, n_row):
     slots, width = x.shape
     bf = jnp.bfloat16
-    size = small.shape[0] + width // 128
+    size = sum(part.size for part in small) // 128 + width // 128
     phases = len(data_bits(n_row, MIX))
     return pl.pallas_call(
         home_kernel,
@@ -968,7 +1160,7 @@
             jax.ShapeDtypeStruct(kv_parts.shape[2:], jnp.float32),
             jax.ShapeDtypeStruct(ff_sums.shape, bf),
         ),
-        in_specs=[pl.BlockSpec(memory_space=VMEM)] * 9 + [pl.BlockSpec(memory_space=ANY)],
+        in_specs=[pl.BlockSpec(memory_space=VMEM)] * 12 + [pl.BlockSpec(memory_space=ANY)],
         out_specs=(
             (pl.BlockSpec(memory_space=ANY),) * 3
             + (pl.BlockSpec(memory_space=VMEM), pl.BlockSpec(memory_space=ANY))
@@ -1001,10 +1193,12 @@
             pltpu.SemaphoreType.DMA((TP,)),
             pltpu.SemaphoreType.DMA((kv_parts.shape[0],)),
             pltpu.SemaphoreType.DMA((kv_parts.shape[0],)),
-        ],
-        compiler_params=params(3, 48),
+            VMEM((slots, width), jnp.float32),
+        ]
+        + scatter_scratch(slots, width),
+        compiler_params=params(3, 56),
         cost_estimate=cost(75),
-    )(parts, x, d_mid, result, gain, give, take, small, kv_parts, ff_sums)
+    )(parts, x, d_mid, ff_parts, mid, gain, give, take, *small, kv_parts, ff_sums)
 
 
 def blocks_start(low, land, s1, r1):
@@ -1261,18 +1455,15 @@
 
 
 def mixer_back_kernel(
-    sh, ph, lens, projected, chan, side, table, scanned, crossed, grads, ff_parts, mid,
-    out, chan_sums, side_sums, result,
-    low, land, mine, s1, r1, s2, r2, here, summed, misc, total, near, held, far, t1, u1, t2, u2,
+    sh, ph, lens, projected, chan, side, table, scanned, crossed, grads,
+    out, chan_sums, side_sums,
+    low, land, mine, s1, r1, s2, r2, here, summed, misc,
 ):
     slots = crossed.shape[1]
     mh = chan.shape[1]
     heads_at = 2 * sh
     bf = jnp.bfloat16
     greet(MIX, cross=True)
-    assert MIX == FFN
-    steps = scatter_steps(ff_parts, near, held, far, t1, u1, t2, u2, total, FFN)
-    next(steps)
     chan_sums[...] = jnp.zeros_like(chan_sums)
     side_sums[...] = jnp.zeros_like(side_sums)
 
@@ -1364,25 +1555,16 @@
         for i, part in enumerate(sums):
             side_sums[i : i + 1, :] += part
 
-    each_block(0, GROUP // 2, scan)
-    next(steps)
-    each_block(GROUP // 2, GROUP, scan)
+    each_block(0, GROUP, scan)
     begun = blocks_start(low, land, s1, r1)
-    next(steps)
     each_block(0, GROUP // 2, attention)
     done = blocks_turn(begun, low, land, mine, summed, s2, r2, here)
     each_block(GROUP // 2, GROUP, attention)
     blocks_finish(begun, done)
     each_block(0, GROUP, state)
-    next(steps)
-
-    def finish(rows):
-        result[rows, :] = (total[rows, :] + mid[rows, :]).astype(bf)
-
-    by_rows(slots, finish)
-
-
-def mixer_back(lens, projected, chan, side, table, scanned, crossed, grads, ff_parts, mid, sh, ph):
+
+
+def mixer_back(lens, projected, chan, side, table, scanned, crossed, grads, sh, ph):
     tokens = projected.shape[0]
     slots = tokens // GROUP
     mh = chan.shape[1]
@@ -1394,20 +1576,17 @@
             jax.ShapeDtypeStruct(projected.shape, jnp.bfloat16),
             jax.ShapeDtypeStruct(chan.shape, jnp.float32),
             jax.ShapeDtypeStruct(side.shape, jnp.float32),
-            jax.ShapeDtypeStruct(mid.shape, jnp.bfloat16),
         ),
-        in_specs=[pl.BlockSpec(memory_space=pltpu.SMEM)] + [vm] * 9,
-        out_specs=(vm,) * 4,
+        in_specs=[pl.BlockSpec(memory_space=pltpu.SMEM)] + [vm] * 7,
+        out_specs=(vm,) * 3,
         scratch_shapes=blocks_scratch(slots)
         + [
             VMEM((GROUP, slots, slots), jnp.bfloat16),
             VMEM((tokens, 128), jnp.float32),
-            VMEM(mid.shape, jnp.float32),
-        ]
-        + scatter_scratch(*mid.shape),
-        compiler_params=params(5, 56),
+        ],
+        compiler_params=params(5, 48),
         cost_estimate=cost(50),
-    )(lens, projected, chan, side, table, scanned, crossed, grads, ff_parts, mid)
+    )(lens, projected, chan, side, table, scanned, crossed, grads)
 
 
 def swiglu(ff_gate, ff_up):
@@ -1464,24 +1643,6 @@
     spare = -used % 256
 
     half = state_weight.shape[1] // 2
-    state_in_part = lax.dynamic_slice_in_dim(state_weight[:, :half], c * (half // 2), half // 2, 1)
-    state_out_part = lax.dynamic_slice_in_dim(state_weight[:, half:], c * (half // 2), half // 2, 1)
-    mixed = jnp.concatenate(
-        [
-            state_in_part.reshape(rows, TP, sh),
-            state_out_part.reshape(rows, TP, sh),
-            step_weight.reshape(rows, TP, ph),
-            jnp.zeros((rows, TP, spare), bf),
-        ],
-        axis=2,
-    ).reshape(rows, TP * (2 * sh + ph + spare))
-    in_weights = (
-        key_weight, value_weight,
-        mamba_gate_weight, mamba_input_weight, query_weight,
-        mixed, mamba_out_weight.T, attn_out_weight.T,
-    )
-    ff_weights = (gate_weight, up_weight, down_weight.T)
-
     def assemble(slab, after):
         held = [(0, slab)]
         for b in data_bits(n_row, FFN):
@@ -1517,16 +1678,18 @@
         ).reshape(TP, rows, grad.shape[1])
         return part, after
 
-    meta = jnp.concatenate(
-        [
-            deal_order,
-            jnp.pad(seq_lengths[:, 0, :], ((0, 0), (0, 128 - seq_lengths.shape[2]))),
-            jnp.zeros((4, 128), jnp.int32),
-        ],
-        axis=0,
-    )
     meta_all, give, take, x_home, gy_home, normed_one, gy_all, w_mixer, slab_up, slab_down = deal(
-        meta, tokens, cotangent, mixer_norm_gain[None, :], in_weights, ff_weights, n_row
+        deal_order,
+        seq_lengths,
+        tokens,
+        cotangent,
+        mixer_norm_gain[None, :],
+        (key_weight, value_weight),
+        (mamba_gate_weight, mamba_input_weight, query_weight),
+        (state_weight, step_weight, mamba_out_weight, attn_out_weight),
+        (gate_weight, up_weight, down_weight),
+        2 * sh + ph + spare,
+        n_row,
     )
     normed_one = normed_one.reshape(GROUP * slots, width)
     gy_all = gy_all.reshape(GROUP * slots, width)
@@ -1578,15 +1741,14 @@
     branch_in, scanned, crossed = mixer(lengths, projected, chan, side, table, sh, ph)
     branch_part = matmul_trans(branch_in, w_out).astype(bf).reshape(GROUP, slots, width)
     ff_gain = ff_norm_gain[None, :]
-    mid, normed_two = middle(branch_part, x_home, ff_gain)
+    mid, normed_two, w_down = middle(branch_part, x_home, ff_gain, slab_down, n_row)
     normed_two = normed_two.reshape(GROUP * slots, width)
     w_gate_up = assemble(slab_up, branch_part)
-    w_down = assemble(slab_down, normed_two)
+    w_down = w_down.reshape(n_row * rows, -1)
 
     ff_gate_up = matmul(normed_two, w_gate_up)
     ff_gate, ff_up = ff_gate_up[:, :fh], ff_gate_up[:, fh:]
     ff_hidden = swiglu(ff_gate, ff_up).astype(bf)
-    ff_part = matmul_trans(ff_hidden, w_down).astype(bf).reshape(GROUP, slots, width)
     grad_hidden = matmul(gy_all, w_down)
     unused_value, pullback = jax.vjp(swiglu, ff_gate, ff_up)
     grad_gate, grad_up = pullback(grad_hidden)
@@ -1605,119 +1767,33 @@
     branch_all = branch_all.reshape(GROUP * slots, width)
 
     grad_branch_in = matmul(branch_all, w_out)
-    grad_projected, chan_sums, side_sums, result = mixer_back(
-        lengths, projected, chan, side, table, scanned, crossed, grad_branch_in, ff_part, mid, sh, ph
+    grad_projected, chan_sums, side_sums = mixer_back(
+        lengths, projected, chan, side, table, scanned, crossed, grad_branch_in, sh, ph
     )
     grad_mixer, grad_kv = products(
         [(normed_one, grad_projected), (branch_all, branch_in)],
         [(0, 0, edges[3]), (0, edges[5], used + spare), (1, 0, mh + qh)],
         [(0, edges[3], edges[5])],
     )
-    grad_projected, grad_mixer = lax.optimization_barrier((grad_projected, grad_mixer))
+    grad_projected, grad_mixer, ff_hidden = lax.optimization_barrier(
+        (grad_projected, grad_mixer, ff_hidden)
+    )
+    ff_part = matmul_trans(ff_hidden, w_down).astype(bf).reshape(GROUP, slots, width)
     mixer_sums, ff_sums = sum_groups(grad_mixer, MIX, ff_sums)
     normed_one_part = matmul_trans(grad_projected, w_in).astype(bf).reshape(GROUP, slots, width)
 
-    def lanes(array):
-        array = array.reshape((-1, array.shape[-1]))
-        array = jnp.pad(array, ((0, 0), (0, -array.shape[1] % 128)))
-        return array.reshape(-1, 128)
-
-    small_parts = [
-        lanes(part)
-        for part in (
-            chan_sums[:4],
-            chan_sums[4:5],
-            side_sums[5:6, 2 * sh : 2 * sh + ph],
-            side_sums[6:7, 2 * sh : 2 * sh + ph],
-            jnp.sum(chan_sums[5].reshape(ph, -1), axis=1)[None],
-            side_sums[:4, : 2 * sh],
-            side_sums[4:5, : 2 * sh],
-            delta_ff_gain,
-        )
-    ]
-    counts = [part.shape[0] for part in small_parts] + [width // 128]
-    small_parts.append(jnp.zeros((-sum(counts) % 8, 128), jnp.float32))
-    starts = [sum(counts[:i]) for i in range(len(counts))]
-    starts[-1] += small_parts[-1].shape[0]
     output, grad_tokens, small_all, delta_kv, ff_land = send_home(
-        normed_one_part, x_home, d_mid, result, mixer_norm_gain[None, :], give, take,
-        jnp.concatenate(small_parts, axis=0),
+        normed_one_part, x_home, d_mid, ff_part, mid, mixer_norm_gain[None, :], give, take,
+        (chan_sums, side_sums, delta_ff_gain),
         grad_kv.reshape(n_row // TP, TP, rows, 2 * kvh), ff_sums, n_row,
     )
     mixer_land, other_land = last(mixer_sums, edges[3])
-    (
-        delta_gate, delta_up, delta_down, delta_mamba_gate, delta_mamba_input,
-        delta_query, delta_mamba_out, delta_attn_out,
-    ) = unpack(ff_land, mixer_land, mh, qh, fh)
-    delta_key, delta_value = delta_kv[:, :kvh], delta_kv[:, kvh:]
-
-    def join(stacked):
-        return stacked.transpose(1, 0, 2).reshape(stacked.shape[1], -1).astype(jnp.float32)
-
-    mine = mixer_land[:, :, edges[3] : edges[3] + 128]
-    state_first = jnp.where(c == 0, mine, other_land)
-    state_second = jnp.where(c == 0, other_land, mine)
-    delta_state = jnp.concatenate(
-        [
-            join(state_first[:, :, :sh]),
-            join(state_second[:, :, :sh]),
-            join(state_first[:, :, sh : 2 * sh]),
-            join(state_second[:, :, sh : 2 * sh]),
-        ],
-        axis=1,
-    )
-    delta_step = join(mine[:, :, 2 * sh : 2 * sh + ph])
-
-    small_all = small_all.reshape(TP, 2, -1, 128)
-    small_col = pick(small_all, c, 1)
-
-    def taken(array, i):
-        return lax.slice_in_dim(array, starts[i], starts[i] + counts[i], axis=array.ndim - 2)
-
-    def along(array, i, size):
-        got = taken(array, i).reshape(TP, -1, size + -size % 128)[:, :, :size]
-        return got.transpose(1, 0, 2).reshape(got.shape[1], TP * size)
-
-    def state_along(i):
-        got = taken(small_all, i)[..., : 2 * sh].reshape(TP, 2, -1, 2, sh)
-        return got.transpose(2, 3, 1, 0, 4).reshape(got.shape[2], 2 * half)
-
-    def over_all(i):
-        return jnp.sum(taken(small_all, i), axis=(0, 1)).reshape(width)
-
-    by_col = [
-        along(small_col, 0, mh),
-        along(small_col, 1, mh)[0],
-        along(small_col, 2, ph)[0],
-        along(small_col, 3, ph)[0],
-        along(small_col, 4, ph)[0],
-    ]
-    by_all = [state_along(5), state_along(6)[0], over_all(8), over_all(7)]
-
-    return (
-        output,
-        grad_tokens,
-        by_all[2],
-        delta_mamba_gate,
-        delta_mamba_input,
-        delta_state,
-        delta_step,
-        by_col[0],
-        by_col[1],
-        by_all[0],
-        by_all[1],
-        by_col[2],
-        by_col[3],
-        by_col[4],
-        delta_mamba_out,
-        delta_query,
-        delta_key,
-        delta_value,
-        delta_attn_out,
-        by_all[3],
-        delta_gate,
-        delta_up,
-        delta_down,
+    results = unpack(
+        ff_land, mixer_land, other_land, small_all, delta_kv, output, grad_tokens, mh, qh, fh, sh, ph
+    )
+    flat = (2, 8, 10, 11, 12, 13, 19)
+    return tuple(
+        array.reshape(array.shape[1]) if i in flat else array for i, array in enumerate(results)
     )
 
 

time: 620 us -> 584 us (0.942)
  local copies, waits for them, and re-layouts: 33.7 us -> 15.9 us
  waiting for transfers between devices: 24.4 us -> 7.44 us
  Pallas kernels: 481 us -> 493 us
  starting transfers between devices: 10.9 us -> 1.27 us
    pallas_call x1, Pallas kernels: 46 us -> 62.4 us  [middle(): pl.pallas_call(middle_kernel, name='middle', out_shape=(jax.ShapeDtypeStr...]
    pallas_call x1, Pallas kernels: 43.3 us -> 31.1 us  [mixer_back(): pl.pallas_call(partial(mixer_back_kernel, sh, ph), name='mixer_back', out...]
    pallas_call x1, Pallas kernels: 117 us -> 127 us  [send_home(): pl.pallas_call(home_kernel, name='home', out_shape=(jax.ShapeDtypeStruct(...]
    ppermute x6 -> x3, starting transfers between devices: 10.8 us -> 1.19 us  [assemble(): lax.ppermute(part, 'row', flips(n_row, 1 << b))]
    unnamed x102 -> x84, local copies, waits for them, and re-layouts: 23.2 us -> 13.9 us
    ppermute x6 -> x3, waiting for transfers between devices: 12.4 us -> 3.11 us  [assemble(): lax.ppermute(part, 'row', flips(n_row, 1 << b))]
    reduce_scatter x2, waiting for transfers between devices: 12 us -> 4.3 us  [sum_groups(): lax.psum_scatter(grad, 'row', scatter_dimension=0, axis_index_groups=alik...]
  transfers between devices with their start and end apart: 8 -> 5, of which waited for: 2 -> 3; matrix products, arithmetic and copies ran while one was open for 8% -> 8% of each run, Pallas kernels for 47% -> 52%
where the time goes in v5:
time: 584 us
  Pallas kernels  493 us (84%)
  matrix products  49.2 us (8%)
  local copies, waits for them, and re-layouts  15.9 us (3%)
  between operations  14.6 us (2%)
  waiting for transfers between devices  7.44 us (1%)
    pallas_call x1, Pallas kernels, deal(): pl.pallas_call(deal_kernel, name='deal', out_shape=(jax.ShapeDtypeStruct(...  155 us
    pallas_call x1, Pallas kernels, send_home(): pl.pallas_call(home_kernel, name='home', out_shape=(jax.ShapeDtypeStruct(...  127 us
    pallas_call x1, Pallas kernels, middle(): pl.pallas_call(middle_kernel, name='middle', out_shape=(jax.ShapeDtypeStr...  62.4 us
    pallas_call x1, Pallas kernels, turn(): pl.pallas_call(turn_kernel, name='turn', out_shape=(jax.ShapeDtypeStruct(...  47.9 us
    pallas_call x1, Pallas kernels, mixer_back(): pl.pallas_call(partial(mixer_back_kernel, sh, ph), name='mixer_back', out...  31.1 us
    dot_general x4, matrix products, matmul_trans(): lax.dot_general(first_op, second_op, (((1,), (1,)), ((), ())), preferred_...  26.9 us
    pallas_call x1, Pallas kernels, mixer(): pl.pallas_call(partial(mixer_kernel, sh, ph), name='mixer', out_shape=(ja...  23 us
    dot_general x4, matrix products, matmul(): return jnp.dot(first_op, second_op, preferred_element_type=jnp.float32)  22.3 us
  transfers between devices with their start and end apart: 5, of which 3 were waited for; matrix products, arithmetic and copies ran while one was open for 8% of the time, Pallas kernels for 52%

profile of v5, /device:TPU:9, one launch (start us, length us, event | category | flops | bytes accessed | tf_op | source)
XLA Modules:
  0.0 583.6 jit_solution(10169438463885408889)
XLA Ops:
  7.3 1.4 copy.48.refs_6_
  8.7 154.6 %deal.1 = (s32[16,8,128]{2,1,0:T(8,128)}, bf16[256,256]{1,0:T(8,128)(2,1)}, bf16[256,256]{1,0:T(8,128)(2,1)}, bf16[128,2048]{1,0:T(8,128)(2,1)}, bf16[128,2048]{...) custom-call(s32[2,128]{1,0:T(2,128)} %order.1, ...), custom_call_target="tpu_custom_call" | custom-call | bytes 340000000 | tf_op jit(solution)/shard_map/deal/pallas_call | solution.py:654
  163.4 0.4 collective-permute-start
  163.9 0.1 pad.28.clone
  164.0 0.8 dynamic-slice.12
  164.9 0.1 broadcast_in_dim.29
  165.0 0.3 fusion.15
  165.3 0.1 dynamic-slice_bitcast_fusion
  165.4 0.1 fusion.18
  165.5 0.1 select_maximum_fusion
  165.6 8.9 %fusion.2.projected = f32[1024,1280]{1,0:T(8,128)S(1)} fusion(bf16[1024,2048]{1,0:T(8,128)(2,1)} %bitcast.41, bf16[2048,1792]{1,0:T(8,128)(2,1)} %bitcast.67), kind=kOutput, calls=%fused_computation.2 | convolution fusion | flops 5368709120 | bytes 14680064 | tf_op jit(solution)/shard_map/dot_general | solution.py:24
  174.5 0.1 pad_maximum_fusion.1.table
  174.6 0.7 constant_dynamic-slice_fusion.4
  175.4 0.1 select_maximum_fusion.1
  175.6 23.0 %mixer.1 = (bf16[1024,512]{1,0:T(8,128)(2,1)S(1)}, f32[1024,384]{1,0:T(8,128)S(1)}, bf16[8,128,128]{2,1,0:T(8,128)(2,1)S(1)}) custom-call(s32[8,3]{1,0:T(8,128)S(1)} %bitcast.54, f32[1024,1280]{1,0:T(8,128)S(1)} %fusion.2.projected, f32[8,384]{1,0:T(8,128)S(1)} %maximum_maximum_fusion.chan, f32[8,128]{1,0:T(8,128)S(1)} %maximum_maximum_fusion.1.side, ...), custom_call_target="tpu_custom_call" | custom-call | bytes 102000000 | tf_op jit(solution)/shard_map/mixer/pallas_call | solution.py:1441
  198.6 1.2 copy-done.13
  199.8 4.4 convolution_convert_fusion.1
  204.3 3.1 collective-permute-done.refs_1_
  207.4 0.7 collective-permute-start.2
  208.1 62.4 %middle.1 = (f32[128,2048]{1,0:T(8,128)S(1)}, bf16[8,128,2048]{2,1,0:T(8,128)(2,1)S(1)}, bf16[4,4,128,512]{3,2,1,0:T(8,128)(2,1)S(1)}) custom-call(bf16[8,128,2048]{2,1,0:T(8,128)(2,1)S(1)} %bitcast.49, bf16[128,2048]{1,0:T(8,128)(2,1)S(1)} %copy-done.10, f32[1,2048]{1,0:T(1,128)S(1)} %bitcast.56, bf16[4,128,512]{2,1,0:T(8,128)(2,1)S(1)} %copy-done.24), custom_call_target="tpu_custom_call" | custom-call | bytes 204000000 | tf_op jit(solution)/shard_map/middle/pallas_call | solution.py:754
  270.6 0.6 place.1
  271.2 4.5 fusion.19
  275.7 3.3 fusion.9
  279.0 0.3 pad_maximum_fusion.refs_1_
  279.3 0.6 copy-done.17
  280.0 9.2 %products.2 = bf16[2048,1536]{1,0:T(8,128)(2,1)} custom-call(bf16[1024,2048]{1,0:T(8,128)(2,1)S(1)} %bitcast.46, bf16[1024,1024]{1,0:T(8,128)(2,1)S(1)} %pad_maximum_fusion.refs_1_, bf16[1024,2048]{1,0:T(8,128)(2,1)S(1)} %bitcast.44, bf16[1024,512]{1,0:T(8,128)(2,1)S(1)} %get-tuple-element.106.refs_3_), custom_call_target="tpu_custom_call" | custom-call | bytes 34000000 | tf_op jit(solution)/shard_map/products/pallas_call | solution.py:995
  289.2 8.5 %convolution_convert_fusion.2 = bf16[1024,2048]{1,0:T(8,128)(2,1)} fusion(bf16[1024,1024]{1,0:T(8,128)(2,1)S(1)} %pad_maximum_fusion.refs_1_, bf16[2048,1024]{1,0:T(8,128)(2,1)} %bitcast.51), kind=kOutput, calls=%fused_computation.7 | convolution fusion | flops 4297064448 | bytes 10485760 | tf_op jit(solution)/shard_map/dot_general | solution.py:28
  297.7 47.9 %turn.1 = (f32[128,2048]{1,0:T(8,128)S(1)}, f32[1,2048]{1,0:T(1,128)S(1)}, bf16[8,128,2048]{2,1,0:T(8,128)(2,1)}) custom-call(bf16[8,128,2048]{2,1,0:T(8,128)(2,1)} %bitcast.62, f32[128,2048]{1,0:T(8,128)S(1)} %get-tuple-element.99.mid, bf16[128,2048]{1,0:T(8,128)(2,1)S(1)} %copy-done.25, f32[1,2048]{1,0:T(1,128)S(1)} %bitcast.57), custom_call_target="tpu_custom_call" | custom-call | bytes 204000000 | tf_op jit(solution)/shard_map/turn/pallas_call | solution.py:808
  345.7 5.6 fusion.11.grads
  351.3 31.1 %mixer_back.1 = (bf16[1024,1280]{1,0:T(8,128)(2,1)}, f32[8,384]{1,0:T(8,128)S(1)}, f32[8,128]{1,0:T(8,128)S(1)}) custom-call(s32[8,3]{1,0:T(8,128)S(1)} %bitcast.55, f32[1024,1280]{1,0:T(8,128)} %copy-done.2, f32[8,384]{1,0:T(8,128)S(1)} %maximum_maximum_fusion.chan, f32[8,128]{1,0:T(8,128)S(1)} %maximum_maximum_fusion.1.side, ...), custom_call_target="tpu_custom_call" | custom-call | bytes 170000000 | tf_op jit(solution)/shard_map/mixer_back/pallas_call | solution.py:1572
  382.5 1.7 copy-done.8
  384.2 11.4 %products.3 = (bf16[2048,1536]{1,0:T(8,128)(2,1)}, bf16[2048,256]{1,0:T(8,128)(2,1)S(1)}) custom-call(bf16[1024,2048]{1,0:T(8,128)(2,1)S(1)} %bitcast.42, bf16[1024,1280]{1,0:T(8,128)(2,1)S(1)} %copy-done.8, bf16[1024,2048]{1,0:T(8,128)(2,1)S(1)} %bitcast.48, bf16[1024,512]{1,0:T(8,128)(2,1)S(1)} %copy-done.16), custom_call_target="tpu_custom_call" | custom-call | bytes 34000000 | tf_op jit(solution)/shard_map/products/pallas_call | solution.py:995
  395.6 1.0 copy-done.23
  396.6 2.3 reduce-scatter.3.cloned.1.call-done
  398.9 4.3 convolution_convert_fusion
  403.3 9.7 %fusion.4 = bf16[1024,2048]{1,0:T(8,128)(2,1)} fusion(bf16[1024,1280]{1,0:T(8,128)(2,1)S(1)} %copy-done.9, bf16[2048,1792]{1,0:T(8,128)(2,1)} %bitcast.70), kind=kOutput, calls=%fused_computation.4 | convolution fusion | flops 5370806272 | bytes 12058624 | tf_op jit(solution)/shard_map/dot_general | solution.py:28
  412.9 127.0 %home.1 = (bf16[2,128,2048]{2,1,0:T(8,128)(2,1)}, bf16[2,128,2048]{2,1,0:T(8,128)(2,1)}, f32[8,64,128]{2,1,0:T(8,128)}, f32[128,256]{1,0:T(8,128)}, bf16[4,128,1536]{2,1,0:T(8,128)(2,1)}) custom-call(bf16[8,128,2048]{2,1,0:T(8,128)(2,1)} %bitcast.61, bf16[128,2048]{1,0:T(8,128)(2,1)} %get-tuple-element.92.x, f32[128,2048]{1,0:T(8,128)} %copy-done.22, ...), custom_call_target="tpu_custom_call" | custom-call | bytes 255000000 | tf_op jit(solution)/shard_map/home/pallas_call | solution.py:1153
  540.0 2.0 reduce-scatter.5.cloned.1.call-done
  542.0 1.4 copy-done.11
  543.4 22.1 %last.1 = (bf16[4,128,1536]{2,1,0:T(8,128)(2,1)S(1)}, bf16[4,128,128]{2,1,0:T(8,128)(2,1)S(1)}) custom-call(bf16[4,128,1536]{2,1,0:T(8,128)(2,1)S(1)} %bitcast.52), custom_call_target="tpu_custom_call" | custom-call | bytes 85000000 | tf_op jit(solution)/shard_map/last/pallas_call | solution.py:962
  565.5 1.4 copy-done.12
  566.9 1.2 copy-done.19
  568.1 1.2 copy-done.20
  569.3 0.9 copy-done.28
  570.3 0.9 copy-done.29
  571.2 4.3 unpack.1
  575.5 0.7 copy.53
  576.1 0.6 reduce
  (89 shorter events, 0.7 us)
Async XLA Ops:
  7.2 157.8 %copy-start = (f32[4,1536]{1,0:T(4,128)S(1)}, f32[4,1536]{1,0:T(4,128)}, u32[]{:S(2)}) copy-start(f32[4,1536]{1,0:T(4,128)} %param.34) | copy-start | bytes 73732
  7.2 157.6 %copy-start.40 = (f32[24]{0:T(128)S(1)}, f32[24]{0:T(128)}, u32[]{:S(2)}) copy-start(f32[24]{0:T(128)} %param.40) | copy-start | bytes 292
  7.2 158.1 %copy-start.38 = (f32[24]{0:T(128)S(1)}, f32[24]{0:T(128)}, u32[]{:S(2)}) copy-start(f32[24]{0:T(128)} %param.39) | copy-start | bytes 292
  7.2 158.1 %copy-start.39 = (f32[24]{0:T(128)S(1)}, f32[24]{0:T(128)}, u32[]{:S(2)}) copy-start(f32[24]{0:T(128)} %param.38) | copy-start | bytes 292
  7.2 158.2 %copy-start.37 = (f32[512]{0:T(512)S(1)}, f32[512]{0:T(512)}, u32[]{:S(2)}) copy-start(f32[512]{0:T(512)} %param.37) | copy-start | bytes 6148
  7.3 158.2 %copy-start.36 = (f32[4,512]{1,0:T(4,128)S(1)}, f32[4,512]{1,0:T(4,128)}, u32[]{:S(2)}) copy-start(f32[4,512]{1,0:T(4,128)} %param.36) | copy-start | bytes 24580
  7.3 391.6 %reduce-scatter.3.cloned.1.call-start = ((), (), s32[]{:S(2)}) async-start(), calls=%async_computation.2 | async-start | bytes 7864320 | tf_op jit(solution)/shard_map/reduce_scatter | solution.py:1676
  163.4 107.2 %collective-permute-start.1 = (bf16[4,128,1024]{2,1,0:T(8,128)(2,1)}, bf16[4,128,1024]{2,1,0:T(8,128)(2,1)S(1)}, u32[]{:S(2)}, u32[]{:S(2)}) collective-permute-start(bf16[4,128,1024]{2,1,0:T(8,128)(2,1)} %get-tuple-element.96.refs_0_), channel_id=1, source_target_pairs={{0,8},{2,10},{4,12},{6,14},{8,0},{10,2},{12,4},{14,6},{16,24},{18,... | collective-permute-start | bytes 3145736 | tf_op jit(solution)/shard_map/ppermute | solution.py:1653
  163.4 44.0 %collective-permute-start = (bf16[4,128,1024]{2,1,0:T(8,128)(2,1)}, bf16[4,128,1024]{2,1,0:T(8,128)(2,1)S(1)}, u32[]{:S(2)}, u32[]{:S(2)}) collective-permute-start(bf16[4,128,1024]{2,1,0:T(8,128)(2,1)} %get-tuple-element.96.refs_0_), channel_id=1, source_target_pairs={{0,16},{2,18},{4,20},{6,22},{8,24},{10,26},{12,28},{14,30},{16,0},... | collective-permute-start | bytes 3145736 | tf_op jit(solution)/shard_map/ppermute | solution.py:1653
  174.5 29.8 %copy-start.2 = (f32[1024,1280]{1,0:T(8,128)}, f32[1024,1280]{1,0:T(8,128)S(1)}, u32[]{:S(2)}) copy-start(f32[1024,1280]{1,0:T(8,128)S(1)} %fusion.2.projected) | copy-start | bytes 15728644
  198.6 1.2 copy-start.13
  199.8 4.5 copy-start.15
  199.8 4.5 copy-start.26
  199.8 8.3 %copy-start.10 = (bf16[128,2048]{1,0:T(8,128)(2,1)S(1)}, bf16[128,2048]{1,0:T(8,128)(2,1)}, u32[]{:S(2)}) copy-start(bf16[128,2048]{1,0:T(8,128)(2,1)} %get-tuple-element.92.x) | copy-start | bytes 1572868
  199.8 8.3 %copy-start.24 = (bf16[4,128,512]{2,1,0:T(8,128)(2,1)S(1)}, bf16[4,128,512]{2,1,0:T(8,128)(2,1)}, u32[]{:S(2)}) copy-start(bf16[4,128,512]{2,1,0:T(8,128)(2,1)} %get-tuple-element.93.slab) | copy-start | bytes 1572868
  199.8 8.3 %copy-start.30 = (f32[2048]{0:T(1024)S(1)}, f32[2048]{0:T(1024)}, u32[]{:S(2)}) copy-start(f32[2048]{0:T(1024)} %param.46) | copy-start | bytes 24580
  204.3 66.3 %copy-start.21 = (bf16[4,128,1024]{2,1,0:T(8,128)(2,1)S(1)}, bf16[4,128,1024]{2,1,0:T(8,128)(2,1)}, u32[]{:S(2)}) copy-start(bf16[4,128,1024]{2,1,0:T(8,128)(2,1)} %get-tuple-element.96.refs_0_) | copy-start | bytes 3145732
  207.4 63.1 %collective-permute-start.2 = (bf16[4,128,1024]{2,1,0:T(8,128)(2,1)S(1)}, bf16[4,128,1024]{2,1,0:T(8,128)(2,1)S(1)}, u32[]{:S(2)}, u32[]{:S(2)}) collective-permute-start(bf16[4,128,1024]{2,1,0:T(8,128)(2,1)S(1)} %collective-permute-done.refs_1_), channel_id=1, source_target_pairs={{0,8},{2,10},{4,12},{6,14},{8,0},{10,2},{12,4},{14,6},{16,24},{18,... | collective-permute-start | bytes 3145736 | tf_op jit(solution)/shard_map/ppermute | solution.py:1653
  270.5 5.1 copy-start.34
  270.5 27.2 %copy-start.7 = (f32[128,2048]{1,0:T(8,128)}, f32[128,2048]{1,0:T(8,128)S(1)}, u32[]{:S(2)}) copy-start(f32[128,2048]{1,0:T(8,128)S(1)} %get-tuple-element.99.mid) | copy-start | bytes 3145732
  271.1 4.5 copy-start.6
  271.1 4.5 copy-start.4
  279.0 1.0 copy-start.17
  289.2 252.8 %reduce-scatter.5.cloned.1.call-start = ((), (), s32[]{:S(2)}) async-start(), calls=%async_computation.3 | async-start | bytes 7864320 | tf_op jit(solution)/shard_map/reduce_scatter | solution.py:1676
  289.2 8.5 %copy-start.25 = (bf16[128,2048]{1,0:T(8,128)(2,1)S(1)}, bf16[128,2048]{1,0:T(8,128)(2,1)}, u32[]{:S(2)}) copy-start(bf16[128,2048]{1,0:T(8,128)(2,1)} %get-tuple-element.100.gy) | copy-start | bytes 1572868
  345.6 5.6 copy-start.22
  345.6 5.6 copy-start.32
  345.6 5.6 copy-start.14
  345.7 5.6 copy-start.27
  345.7 36.8 %copy-start.16 = (bf16[1024,512]{1,0:T(8,128)(2,1)S(1)}, bf16[1024,512]{1,0:T(8,128)(2,1)}, u32[]{:S(2)}) copy-start(bf16[1024,512]{1,0:T(8,128)(2,1)} %copy-done.15) | copy-start | bytes 3145732
  351.3 31.2 %copy-start.3 = (bf16[8,128,2048]{2,1,0:T(8,128)(2,1)S(1)}, bf16[8,128,2048]{2,1,0:T(8,128)(2,1)}, u32[]{:S(2)}) copy-start(bf16[8,128,2048]{2,1,0:T(8,128)(2,1)} %get-tuple-element.86) | copy-start | bytes 12582916
  351.3 31.2 %copy-start.5 = (bf16[8,128,2048]{2,1,0:T(8,128)(2,1)S(1)}, bf16[8,128,2048]{2,1,0:T(8,128)(2,1)}, u32[]{:S(2)}) copy-start(bf16[8,128,2048]{2,1,0:T(8,128)(2,1)} %get-tuple-element.101) | copy-start | bytes 12582916
  382.5 13.2 %copy-start.31 = (f32[8,384]{1,0:T(8,128)}, f32[8,384]{1,0:T(8,128)S(1)}, u32[]{:S(2)}) copy-start(f32[8,384]{1,0:T(8,128)S(1)} %get-tuple-element.109.chan_sums) | copy-start | bytes 36868
  382.5 13.2 %copy-start.33 = (f32[8,128]{1,0:T(8,128)}, f32[8,128]{1,0:T(8,128)S(1)}, u32[]{:S(2)}) copy-start(f32[8,128]{1,0:T(8,128)S(1)} %get-tuple-element.110.side_sums) | copy-start | bytes 12292
  382.5 1.7 copy-start.8
  395.6 1.0 copy-start.23
  396.6 2.3 copy-start.18
  396.6 2.3 copy-start.35
  398.9 4.3 copy-start.9
  412.9 163.8 %copy-start.1 = (f32[4,1536]{1,0:T(4,128)S(1)}, f32[4,1536]{1,0:T(4,128)}, u32[]{:S(2)}) copy-start(f32[4,1536]{1,0:T(4,128)} %param.34) | copy-start | bytes 73732
  542.0 1.4 copy-start.11
  565.4 1.4 copy-start.12
  566.9 1.2 copy-start.19
  568.1 1.2 copy-start.20
  569.3 0.9 copy-start.28
  570.3 0.9 copy-start.29
Sparse Core Ops, SparseCore 0:
  289.3 109.5 reduce-scatter.2
  401.2 140.7 reduce-scatter.4

commit v6 on v5

--- a/solution.py
+++ b/solution.py
@@ -666,7 +666,7 @@
             jax.ShapeDtypeStruct((TP, rows, up_cols), bf),
             jax.ShapeDtypeStruct((TP, rows, down_cols), bf),
         ),
-        in_specs=[vm, vm, hb, hb, vm] + [hb] * 5 + [vm] * 4 + [hb, hb, vm],
+        in_specs=[vm, vm, hb, hb, vm] + [vm] * 12,
         out_specs=(vm,) * 5 + (hb,) * 5,
         scratch_shapes=[
             VMEM((slots, width), bf),
@@ -769,7 +769,7 @@
             pltpu.SemaphoreType.DMA((groups,)),
             pltpu.SemaphoreType.DMA,
         ],
-        compiler_params=params(1, 40),
+        compiler_params=params(1, 30),
         cost_estimate=cost(60),
     )(parts, x, gain, slab)
 
@@ -818,16 +818,15 @@
         scratch_shapes=scatter_scratch(slots, width)
         + [VMEM((slots, width), jnp.bfloat16)]
         + gather_scratch(),
-        compiler_params=params(2, 48),
+        compiler_params=params(2, 30),
         cost_estimate=cost(60),
     )(parts, mid, gy, gain)
 
 
 def home_kernel(
-    parts, x, d_mid, ff_parts, mid, gain, give, take, chan_sums, side_sums, ff_gain_sums, kv_parts, ff_sums,
-    output, gradient, small_all, kv_sums, ff_land,
-    near, out2, far, s1, r1, s2, r2, total, first, second, buf, land, csend, crecv, here, osend, orecv,
-    d_gain, stages, stage_land, tsend, trecv, gsend, grecv, ghere, *more
+    parts, x, d_mid, ff_parts, mid, gain, take, chan_sums, side_sums, ff_gain_sums, kv_parts, ff_sums,
+    buf, small_all, kv_sums, ff_land,
+    near, out2, far, s1, r1, s2, r2, total, first, second, d_gain, stages, stage_land, tsend, trecv, gsend, grecv, ghere, *more
 ):
     r, c = place()
     slots, width = x.shape
@@ -864,8 +863,6 @@
 
     stage_copy(0).start()
     permute_out(take, buf, first, second, slots)
-    exchange_rows(buf, land, csend, crecv)
-    land[r] = buf[r]
     own = member(r, MIX)
     groups = kv_parts.shape[0]
     kv_sent = []
@@ -904,14 +901,6 @@
             )
         )
         kv_far_sent[-1].start()
-    finish_rows(buf, land, csend, crecv)
-    permute_in(give, land, first, second, slots)
-    copies = []
-    for i, (mine, out) in enumerate(((first, output), (second, gradient))):
-        copies.append(pltpu.make_async_copy(mine, out.at[c], here.at[i]))
-        copies.append(remote(mine, out.at[c], osend.at[i], orecv.at[i], r, 1 - c))
-    for copy in copies:
-        copy.start()
     gather_finish(started, passed, small_all, gsend, grecv, MIX)
     for copy in kv_far_sent:
         copy.wait()
@@ -919,7 +908,7 @@
     for k in range(1, groups):
         kv_total = kv_total + kv_far[k].astype(jnp.float32)
     kv_sums[...] = kv_total
-    for copy in copies + delivered:
+    for copy in delivered:
         copy.wait()
 
 
@@ -942,36 +931,63 @@
     return [dma((TP,)), dma((TP,)), dma]
 
 
-def last_kernel(at, sums, land, other, s1, r1, here, send, recv):
-    r, c = place()
-    barrier = pltpu.get_barrier_semaphore()
-    for m in (1, 2, 3):
-        pl.semaphore_signal(barrier, inc=1, device_id=(partner(r, m, MIX), c), device_id_type=MESH)
-    pl.semaphore_signal(barrier, inc=1, device_id=(r, 1 - c), device_id_type=MESH)
-    pl.semaphore_wait(barrier, 4)
-    for copy in deliver(sums, land, s1, r1, here, MIX):
+def last_kernel(
+    at, buf, give, sums, output, gradient, sums_land, other,
+    land, first, second, csend, crecv, here, osend, orecv, s1, r1, h1, send, recv,
+):
+    r, c = place()
+    greet_rows()
+    exchange_rows(buf, land, csend, crecv)
+    delivered = deliver(sums, sums_land, s1, r1, h1, MIX)
+    land[r] = buf[r]
+    for copy in delivered:
         copy.wait()
-    across = remote(land.at[:, :, at : at + 128], other, send, recv, r, 1 - c)
+    across = remote(sums_land.at[:, :, at : at + 128], other, send, recv, r, 1 - c)
     across.start()
-    across.wait()
-
-
-def last(sums, at):
-    hb = pl.BlockSpec(memory_space=ANY)
+    finish_rows(buf, land, csend, crecv)
+    permute_in(give, land, first, second, first.shape[0])
+    copies = [across]
+    for i, (mine, out) in enumerate(((first, output), (second, gradient))):
+        copies.append(pltpu.make_async_copy(mine, out.at[c], here.at[i]))
+        copies.append(remote(mine, out.at[c], osend.at[i], orecv.at[i], r, 1 - c))
+    for copy in copies[1:]:
+        copy.start()
+    for copy in copies:
+        copy.wait()
+
+
+def last(buf, give, sums, at):
+    n_row, chunk, width = buf.shape
+    slots = give.shape[1] // 2
+    vm, hb = pl.BlockSpec(memory_space=VMEM), pl.BlockSpec(memory_space=ANY)
     dma = pltpu.SemaphoreType.DMA
+    bf = jnp.bfloat16
     return pl.pallas_call(
         partial(last_kernel, at),
         name="last",
         out_shape=(
+            jax.ShapeDtypeStruct((2, slots, width), bf),
+            jax.ShapeDtypeStruct((2, slots, width), bf),
             jax.ShapeDtypeStruct(sums.shape, sums.dtype),
             jax.ShapeDtypeStruct(sums.shape[:2] + (128,), sums.dtype),
         ),
-        in_specs=[hb],
-        out_specs=(hb,) * 2,
-        scratch_shapes=deliver_scratch() + [dma, dma],
-        compiler_params=params(6, 4),
-        cost_estimate=cost(25),
-    )(sums)
+        in_specs=[vm, vm, hb],
+        out_specs=(hb,) * 4,
+        scratch_shapes=[
+            VMEM(buf.shape, bf),
+            VMEM((slots, width), bf),
+            VMEM((slots, width), bf),
+            dma((n_row,)),
+            dma((n_row,)),
+            dma((2,)),
+            dma((2,)),
+            dma((2,)),
+        ]
+        + deliver_scratch()
+        + [dma, dma],
+        compiler_params=params(6, 32),
+        cost_estimate=cost(35),
+    )(buf, give, sums)
 
 
 def products_kernel(parts, *refs):
@@ -999,7 +1015,7 @@
         out_shape=tuple(jax.ShapeDtypeStruct((width, total), jnp.bfloat16) for total in totals),
         in_specs=specs,
         out_specs=tuple(pl.BlockSpec((tile, total), lambda i: (i, 0)) for total in totals),
-        compiler_params=pltpu.CompilerParams(vmem_limit_bytes=40 << 20),
+        compiler_params=pltpu.CompilerParams(vmem_limit_bytes=30 << 20),
         cost_estimate=cost(10),
     )(*[array for pair in pairs for array in pair])
 
@@ -1145,7 +1161,7 @@
     )(ff, mixer, misc, small, kv, output, gradient)
 
 
-def send_home(parts, x, d_mid, ff_parts, mid, gain, give, take, small, kv_parts, ff_sums, n_row):
+def send_home(parts, x, d_mid, ff_parts, mid, gain, take, small, kv_parts, ff_sums, n_row):
     slots, width = x.shape
     bf = jnp.bfloat16
     size = sum(part.size for part in small) // 128 + width // 128
@@ -1154,29 +1170,23 @@
         home_kernel,
         name="home",
         out_shape=(
-            jax.ShapeDtypeStruct((2, slots, width), bf),
-            jax.ShapeDtypeStruct((2, slots, width), bf),
+            jax.ShapeDtypeStruct((n_row, CHUNK, width), bf),
             jax.ShapeDtypeStruct((GROUP, size, 128), jnp.float32),
             jax.ShapeDtypeStruct(kv_parts.shape[2:], jnp.float32),
             jax.ShapeDtypeStruct(ff_sums.shape, bf),
         ),
-        in_specs=[pl.BlockSpec(memory_space=VMEM)] * 12 + [pl.BlockSpec(memory_space=ANY)],
+        in_specs=[pl.BlockSpec(memory_space=VMEM)] * 11 + [pl.BlockSpec(memory_space=ANY)],
         out_specs=(
-            (pl.BlockSpec(memory_space=ANY),) * 3
-            + (pl.BlockSpec(memory_space=VMEM), pl.BlockSpec(memory_space=ANY))
+            pl.BlockSpec(memory_space=VMEM),
+            pl.BlockSpec(memory_space=ANY),
+            pl.BlockSpec(memory_space=VMEM),
+            pl.BlockSpec(memory_space=ANY),
         ),
         scratch_shapes=scatter_scratch(slots, width)
         + [
             VMEM((slots, width), jnp.float32),
             VMEM((slots, width), bf),
             VMEM((slots, width), bf),
-            VMEM((n_row, CHUNK, width), bf),
-            VMEM((n_row, CHUNK, width), bf),
-            pltpu.SemaphoreType.DMA((n_row,)),
-            pltpu.SemaphoreType.DMA((n_row,)),
-            pltpu.SemaphoreType.DMA((2,)),
-            pltpu.SemaphoreType.DMA((2,)),
-            pltpu.SemaphoreType.DMA((2,)),
             VMEM((1, width), jnp.float32),
             VMEM((phases + 1, size, 128), jnp.float32),
             VMEM((phases, size, 128), jnp.float32),
@@ -1196,9 +1206,9 @@
             VMEM((slots, width), jnp.float32),
         ]
         + scatter_scratch(slots, width),
-        compiler_params=params(3, 56),
+        compiler_params=params(3, 40),
         cost_estimate=cost(75),
-    )(parts, x, d_mid, ff_parts, mid, gain, give, take, *small, kv_parts, ff_sums)
+    )(parts, x, d_mid, ff_parts, mid, gain, take, *small, kv_parts, ff_sums)
 
 
 def blocks_start(low, land, s1, r1):
@@ -1782,12 +1792,12 @@
     mixer_sums, ff_sums = sum_groups(grad_mixer, MIX, ff_sums)
     normed_one_part = matmul_trans(grad_projected, w_in).astype(bf).reshape(GROUP, slots, width)
 
-    output, grad_tokens, small_all, delta_kv, ff_land = send_home(
-        normed_one_part, x_home, d_mid, ff_part, mid, mixer_norm_gain[None, :], give, take,
+    buf, small_all, delta_kv, ff_land = send_home(
+        normed_one_part, x_home, d_mid, ff_part, mid, mixer_norm_gain[None, :], take,
         (chan_sums, side_sums, delta_ff_gain),
         grad_kv.reshape(n_row // TP, TP, rows, 2 * kvh), ff_sums, n_row,
     )
-    mixer_land, other_land = last(mixer_sums, edges[3])
+    output, grad_tokens, mixer_land, other_land = last(buf, give, mixer_sums, edges[3])
     results = unpack(
         ff_land, mixer_land, other_land, small_all, delta_kv, output, grad_tokens, mh, qh, fh, sh, ph
     )

time: 584 us -> 570 us (0.976)
  Pallas kernels: 493 us -> 461 us
  waiting for transfers between devices: 7.44 us -> 22.6 us
    pallas_call x1, Pallas kernels: 127 us -> 92.7 us  [send_home(): pl.pallas_call(home_kernel, name='home', out_shape=(jax.ShapeDtypeStruct(...]
    pallas_call x1, Pallas kernels: 22.1 us -> 37.2 us  [last(): pl.pallas_call(partial(last_kernel, at), name='last', out_shape=(jax.Shap...]
    reduce_scatter x2, waiting for transfers between devices: 4.3 us -> 18.3 us  [sum_groups(): lax.psum_scatter(grad, 'row', scatter_dimension=0, axis_index_groups=alik...]
    pallas_call x1, Pallas kernels: 155 us -> 147 us  [deal(): pl.pallas_call(deal_kernel, name='deal', out_shape=(jax.ShapeDtypeStruct(...]
  transfers between devices with their start and end apart: 5 -> 5, of which waited for: 3 -> 3; matrix products, arithmetic and copies ran while one was open for 8% -> 7% of each run, Pallas kernels for 52% -> 47%
where the time goes in v6:
time: 570 us; the launch traced here: 566 us
  Pallas kernels  461 us (81%)
  matrix products  47.5 us (8%)
  waiting for transfers between devices  22.6 us (4%)
  local copies, waits for them, and re-layouts  17.6 us (3%)
  between operations  14.7 us (3%)
    pallas_call x1, Pallas kernels, deal(): pl.pallas_call(deal_kernel, name='deal', out_shape=(jax.ShapeDtypeStruct(...  147 us
    pallas_call x1, Pallas kernels, send_home(): pl.pallas_call(home_kernel, name='home', out_shape=(jax.ShapeDtypeStruct(...  92.7 us
    pallas_call x1, Pallas kernels, middle(): pl.pallas_call(middle_kernel, name='middle', out_shape=(jax.ShapeDtypeStr...  62.1 us
    pallas_call x1, Pallas kernels, turn(): pl.pallas_call(turn_kernel, name='turn', out_shape=(jax.ShapeDtypeStruct(...  45 us
    pallas_call x1, Pallas kernels, last(): pl.pallas_call(partial(last_kernel, at), name='last', out_shape=(jax.Shap...  37.2 us
    pallas_call x1, Pallas kernels, mixer_back(): pl.pallas_call(partial(mixer_back_kernel, sh, ph), name='mixer_back', out...  31.2 us
    dot_general x4, matrix products, matmul_trans(): lax.dot_general(first_op, second_op, (((1,), (1,)), ((), ())), preferred_...  26.5 us
    pallas_call x1, Pallas kernels, mixer(): pl.pallas_call(partial(mixer_kernel, sh, ph), name='mixer', out_shape=(ja...  22.3 us
  transfers between devices with their start and end apart: 5, of which 3 were waited for; matrix products, arithmetic and copies ran while one was open for 7% of the time, Pallas kernels for 47%

profile of v6, /device:TPU:9, one launch (start us, length us, event | category | flops | bytes accessed | tf_op | source)
XLA Modules:
  0.0 566.1 jit_solution(2496445511986702403)
XLA Ops:
  7.3 1.4 copy.48.refs_6_
  8.7 147.2 %deal.1 = (s32[16,8,128]{2,1,0:T(8,128)}, bf16[256,256]{1,0:T(8,128)(2,1)}, bf16[256,256]{1,0:T(8,128)(2,1)}, bf16[128,2048]{1,0:T(8,128)(2,1)}, bf16[128,2048]{...) custom-call(s32[2,128]{1,0:T(2,128)} %order.1, ...), custom_call_target="tpu_custom_call" | custom-call | bytes 340000000 | tf_op jit(solution)/shard_map/deal/pallas_call | solution.py:654
  155.9 0.9 collective-permute-start.1
  156.8 0.1 pad.18.clone
  156.9 0.1 pad.28.clone
  157.0 0.8 dynamic-slice.12
  157.9 0.1 broadcast_in_dim.29
  158.0 0.3 fusion.15
  158.3 0.1 dynamic-slice_bitcast_fusion
  158.4 0.1 fusion.18
  158.5 0.1 select_maximum_fusion
  158.5 8.9 %fusion.2.projected = f32[1024,1280]{1,0:T(8,128)S(1)} fusion(bf16[1024,2048]{1,0:T(8,128)(2,1)} %bitcast.41, bf16[2048,1792]{1,0:T(8,128)(2,1)} %bitcast.67), kind=kOutput, calls=%fused_computation.2 | convolution fusion | flops 5368709120 | bytes 14680064 | tf_op jit(solution)/shard_map/dot_general | solution.py:24
  167.5 0.1 pad_maximum_fusion.1.table
  167.6 0.7 constant_dynamic-slice_fusion.4
  168.3 0.1 select_maximum_fusion.1
  168.6 22.3 %mixer.1 = (bf16[1024,512]{1,0:T(8,128)(2,1)S(1)}, f32[1024,384]{1,0:T(8,128)S(1)}, bf16[8,128,128]{2,1,0:T(8,128)(2,1)S(1)}) custom-call(s32[8,3]{1,0:T(8,128)S(1)} %bitcast.57, f32[1024,1280]{1,0:T(8,128)S(1)} %fusion.2.projected, f32[8,384]{1,0:T(8,128)S(1)} %maximum_maximum_fusion.chan, f32[8,128]{1,0:T(8,128)S(1)} %maximum_maximum_fusion.1.side, ...), custom_call_target="tpu_custom_call" | custom-call | bytes 102000000 | tf_op jit(solution)/shard_map/mixer/pallas_call | solution.py:1451
  190.9 1.1 copy-done.13
  192.0 4.4 convolution_convert_fusion.1
  196.5 4.3 collective-permute-done.refs_1_
  200.8 0.2 collective-permute-start.2
  201.0 62.1 %middle.1 = (f32[128,2048]{1,0:T(8,128)S(1)}, bf16[8,128,2048]{2,1,0:T(8,128)(2,1)S(1)}, bf16[4,4,128,512]{3,2,1,0:T(8,128)(2,1)S(1)}) custom-call(bf16[8,128,2048]{2,1,0:T(8,128)(2,1)S(1)} %bitcast.49, bf16[128,2048]{1,0:T(8,128)(2,1)S(1)} %copy-done.10, f32[1,2048]{1,0:T(1,128)S(1)} %bitcast.59, bf16[4,128,512]{2,1,0:T(8,128)(2,1)S(1)} %copy-done.27), custom_call_target="tpu_custom_call" | custom-call | bytes 204000000 | tf_op jit(solution)/shard_map/middle/pallas_call | solution.py:754
  263.1 0.6 place.1
  263.7 4.5 fusion.19
  268.3 3.3 fusion.9
  271.6 0.3 pad_maximum_fusion.refs_1_
  271.9 0.6 copy-done.18
  272.6 8.0 %products.2 = bf16[2048,1536]{1,0:T(8,128)(2,1)S(1)} custom-call(bf16[1024,2048]{1,0:T(8,128)(2,1)S(1)} %bitcast.46, bf16[1024,1024]{1,0:T(8,128)(2,1)S(1)} %pad_maximum_fusion.refs_1_, bf16[1024,2048]{1,0:T(8,128)(2,1)S(1)} %bitcast.44, bf16[1024,512]{1,0:T(8,128)(2,1)S(1)} %get-tuple-element.107.refs_3_), custom_call_target="tpu_custom_call" | custom-call | bytes 34000000 | tf_op jit(solution)/shard_map/products/pallas_call | solution.py:1011
  280.6 2.6 copy-done.2
  283.3 7.2 %convolution_convert_fusion.2 = bf16[1024,2048]{1,0:T(8,128)(2,1)S(1)} fusion(bf16[1024,1024]{1,0:T(8,128)(2,1)S(1)} %pad_maximum_fusion.refs_1_, bf16[2048,1024]{1,0:T(8,128)(2,1)} %bitcast.51), kind=kOutput, calls=%fused_computation.7 | convolution fusion | flops 4297064448 | bytes 10485760 | tf_op jit(solution)/shard_map/dot_general | solution.py:28
  290.5 45.0 %turn.1 = (f32[128,2048]{1,0:T(8,128)S(1)}, f32[1,2048]{1,0:T(1,128)S(1)}, bf16[8,128,2048]{2,1,0:T(8,128)(2,1)S(1)}) custom-call(bf16[8,128,2048]{2,1,0:T(8,128)(2,1)S(1)} %bitcast.53, f32[128,2048]{1,0:T(8,128)S(1)} %get-tuple-element.100.mid, bf16[128,2048]{1,0:T(8,128)(2,1)S(1)} %copy-done.28, f32[1,2048]{1,0:T(1,128)S(1)} %bitcast.60), custom_call_target="tpu_custom_call" | custom-call | bytes 204000000 | tf_op jit(solution)/shard_map/turn/pallas_call | solution.py:808
  335.6 4.3 fusion.11.grads
  340.0 31.2 %mixer_back.1 = (bf16[1024,1280]{1,0:T(8,128)(2,1)}, f32[8,384]{1,0:T(8,128)S(1)}, f32[8,128]{1,0:T(8,128)S(1)}) custom-call(s32[8,3]{1,0:T(8,128)S(1)} %bitcast.58, f32[1024,1280]{1,0:T(8,128)} %copy-done.3, f32[8,384]{1,0:T(8,128)S(1)} %maximum_maximum_fusion.chan, f32[8,128]{1,0:T(8,128)S(1)} %maximum_maximum_fusion.1.side, ...), custom_call_target="tpu_custom_call" | custom-call | bytes 170000000 | tf_op jit(solution)/shard_map/mixer_back/pallas_call | solution.py:1582
  371.2 1.7 copy-done.8
  372.9 10.2 %products.3 = (bf16[2048,1536]{1,0:T(8,128)(2,1)S(1)}, bf16[2048,256]{1,0:T(8,128)(2,1)S(1)}) custom-call(bf16[1024,2048]{1,0:T(8,128)(2,1)S(1)} %bitcast.42, bf16[1024,1280]{1,0:T(8,128)(2,1)S(1)} %copy-done.8, bf16[1024,2048]{1,0:T(8,128)(2,1)S(1)} %bitcast.48, bf16[1024,512]{1,0:T(8,128)(2,1)S(1)} %copy-done.17), custom_call_target="tpu_custom_call" | custom-call | bytes 34000000 | tf_op jit(solution)/shard_map/products/pallas_call | solution.py:1011
  383.2 2.7 copy-done.4
  385.8 1.0 copy-done.25
  386.8 6.3 %reduce-scatter.3.cloned.1.call-done = bf16[512,1536]{1,0:T(8,128)(2,1)} async-done(((bf16[2048,1536]{1,0:T(8,128)(2,1)}), bf16[512,1536]{1,0:T(8,128)(2,1)}) %reduce-scatter.3.cloned.1.call-update) | async-done | bytes 1572880 | tf_op jit(solution)/shard_map/reduce_scatter | solution.py:1686
  393.2 6.1 %convolution_convert_fusion = bf16[1024,2048]{1,0:T(8,128)(2,1)} fusion(bf16[1024,512]{1,0:T(8,128)(2,1)S(1)} %copy-done.19, bf16[2048,512]{1,0:T(8,128)(2,1)} %bitcast.64), kind=kOutput, calls=%fused_computation.5 | convolution fusion | flops 2149580800 | bytes 7340032 | tf_op jit(solution)/shard_map/dot_general | solution.py:28
  399.3 8.8 %fusion.4 = bf16[1024,2048]{1,0:T(8,128)(2,1)S(1)} fusion(bf16[1024,1280]{1,0:T(8,128)(2,1)S(1)} %copy-done.9, bf16[2048,1792]{1,0:T(8,128)(2,1)} %bitcast.70), kind=kOutput, calls=%fused_computation.4 | convolution fusion | flops 5370806272 | bytes 12058624 | tf_op jit(solution)/shard_map/dot_general | solution.py:28
  408.1 92.7 %home.1 = (bf16[16,16,2048]{2,1,0:T(8,128)(2,1)S(1)}, f32[8,64,128]{2,1,0:T(8,128)S(1)}, f32[128,256]{1,0:T(8,128)S(1)}, bf16[4,128,1536]{2,1,0:T(8,128)(2,1)S(1)}) custom-call(bf16[8,128,2048]{2,1,0:T(8,128)(2,1)S(1)} %bitcast.52, bf16[128,2048]{1,0:T(8,128)(2,1)S(1)} %copy-done.11, f32[128,2048]{1,0:T(8,128)S(1)} %copy-done.24, ...), custom_call_target="tpu_custom_call" | custom-call | bytes 255000000 | tf_op jit(solution)/shard_map/home/pallas_call | solution.py:1169
  500.9 1.0 copy-done.20
  501.8 12.0 %reduce-scatter.5.cloned.1.call-done = bf16[512,1536]{1,0:T(8,128)(2,1)} async-done(((bf16[2048,1536]{1,0:T(8,128)(2,1)}), bf16[512,1536]{1,0:T(8,128)(2,1)}) %reduce-scatter.5.cloned.1.call-update) | async-done | bytes 1572880 | tf_op jit(solution)/shard_map/reduce_scatter | solution.py:1686
  513.8 1.4 copy-done.12
  515.2 1.2 copy-done.21
  516.4 37.2 %last.1 = (bf16[2,128,2048]{2,1,0:T(8,128)(2,1)S(1)}, bf16[2,128,2048]{2,1,0:T(8,128)(2,1)S(1)}, bf16[4,128,1536]{2,1,0:T(8,128)(2,1)S(1)}, bf16[4,128,128]{2,1,0:T(8,128)(2,1)S(1)}) custom-call(bf16[16,16,2048]{2,1,0:T(8,128)(2,1)S(1)} %copy-done.21, bf16[256,256]{1,0:T(8,128)(2,1)S(1)} %copy-done.32, bf16[4,128,1536]{2,1,0:T(8,128)(2,1)S(1)} %bitcast.54), custom_call_target="tpu_custom_call" | custom-call | bytes 119000000 | tf_op jit(solution)/shard_map/last/pallas_call | solution.py:965
  553.7 4.3 unpack.1
  558.0 0.7 copy.53
  558.7 0.6 reduce
  (89 shorter events, 0.6 us)
Async XLA Ops:
  7.2 150.8 %copy-start = (f32[4,1536]{1,0:T(4,128)S(1)}, f32[4,1536]{1,0:T(4,128)}, u32[]{:S(2)}) copy-start(f32[4,1536]{1,0:T(4,128)} %param.34) | copy-start | bytes 73732
  7.2 150.5 %copy-start.40 = (f32[24]{0:T(128)S(1)}, f32[24]{0:T(128)}, u32[]{:S(2)}) copy-start(f32[24]{0:T(128)} %param.40) | copy-start | bytes 292
  7.2 151.1 %copy-start.38 = (f32[24]{0:T(128)S(1)}, f32[24]{0:T(128)}, u32[]{:S(2)}) copy-start(f32[24]{0:T(128)} %param.39) | copy-start | bytes 292
  7.2 151.1 %copy-start.39 = (f32[24]{0:T(128)S(1)}, f32[24]{0:T(128)}, u32[]{:S(2)}) copy-start(f32[24]{0:T(128)} %param.38) | copy-start | bytes 292
  7.2 151.1 %copy-start.37 = (f32[512]{0:T(512)S(1)}, f32[512]{0:T(512)}, u32[]{:S(2)}) copy-start(f32[512]{0:T(512)} %param.37) | copy-start | bytes 6148
  7.3 151.1 %copy-start.36 = (f32[4,512]{1,0:T(4,128)S(1)}, f32[4,512]{1,0:T(4,128)}, u32[]{:S(2)}) copy-start(f32[4,512]{1,0:T(4,128)} %param.36) | copy-start | bytes 24580
  7.3 385.9 %reduce-scatter.3.cloned.1.call-start = ((), (), s32[]{:S(2)}) async-start(), calls=%async_computation.2 | async-start | bytes 7864320 | tf_op jit(solution)/shard_map/reduce_scatter | solution.py:1686
  155.9 107.2 %collective-permute-start.1 = (bf16[4,128,1024]{2,1,0:T(8,128)(2,1)}, bf16[4,128,1024]{2,1,0:T(8,128)(2,1)S(1)}, u32[]{:S(2)}, u32[]{:S(2)}) collective-permute-start(bf16[4,128,1024]{2,1,0:T(8,128)(2,1)} %get-tuple-element.97.refs_0_), channel_id=1, source_target_pairs={{0,8},{2,10},{4,12},{6,14},{8,0},{10,2},{12,4},{14,6},{16,24},{18,... | collective-permute-start | bytes 3145736 | tf_op jit(solution)/shard_map/ppermute | solution.py:1663
  156.8 44.0 %collective-permute-start = (bf16[4,128,1024]{2,1,0:T(8,128)(2,1)}, bf16[4,128,1024]{2,1,0:T(8,128)(2,1)S(1)}, u32[]{:S(2)}, u32[]{:S(2)}) collective-permute-start(bf16[4,128,1024]{2,1,0:T(8,128)(2,1)} %get-tuple-element.97.refs_0_), channel_id=1, source_target_pairs={{0,16},{2,18},{4,20},{6,22},{8,24},{10,26},{12,28},{14,30},{16,0},... | collective-permute-start | bytes 3145736 | tf_op jit(solution)/shard_map/ppermute | solution.py:1663
  167.5 29.0 %copy-start.3 = (f32[1024,1280]{1,0:T(8,128)}, f32[1024,1280]{1,0:T(8,128)S(1)}, u32[]{:S(2)}) copy-start(f32[1024,1280]{1,0:T(8,128)S(1)} %fusion.2.projected) | copy-start | bytes 15728644
  190.9 1.1 copy-start.13
  192.0 4.5 copy-start.16
  192.0 4.5 copy-start.29
  192.0 9.0 %copy-start.10 = (bf16[128,2048]{1,0:T(8,128)(2,1)S(1)}, bf16[128,2048]{1,0:T(8,128)(2,1)}, u32[]{:S(2)}) copy-start(bf16[128,2048]{1,0:T(8,128)(2,1)} %get-tuple-element.93.x) | copy-start | bytes 1572868
  192.0 9.0 %copy-start.27 = (bf16[4,128,512]{2,1,0:T(8,128)(2,1)S(1)}, bf16[4,128,512]{2,1,0:T(8,128)(2,1)}, u32[]{:S(2)}) copy-start(bf16[4,128,512]{2,1,0:T(8,128)(2,1)} %get-tuple-element.94.slab) | copy-start | bytes 1572868
  192.0 9.0 %copy-start.33 = (f32[2048]{0:T(1024)S(1)}, f32[2048]{0:T(1024)}, u32[]{:S(2)}) copy-start(f32[2048]{0:T(1024)} %param.46) | copy-start | bytes 24580
  196.5 66.6 %copy-start.22 = (bf16[4,128,1024]{2,1,0:T(8,128)(2,1)S(1)}, bf16[4,128,1024]{2,1,0:T(8,128)(2,1)}, u32[]{:S(2)}) copy-start(bf16[4,128,1024]{2,1,0:T(8,128)(2,1)} %get-tuple-element.97.refs_0_) | copy-start | bytes 3145732
  200.8 62.3 %collective-permute-start.2 = (bf16[4,128,1024]{2,1,0:T(8,128)(2,1)S(1)}, bf16[4,128,1024]{2,1,0:T(8,128)(2,1)S(1)}, u32[]{:S(2)}, u32[]{:S(2)}) collective-permute-start(bf16[4,128,1024]{2,1,0:T(8,128)(2,1)S(1)} %collective-permute-done.refs_1_), channel_id=1, source_target_pairs={{0,8},{2,10},{4,12},{6,14},{8,0},{10,2},{12,4},{14,6},{16,24},{18,... | collective-permute-start | bytes 3145736 | tf_op jit(solution)/shard_map/ppermute | solution.py:1663
  263.1 5.2 copy-start.35
  263.7 4.6 copy-start.7
  263.7 4.6 copy-start.6
  271.6 1.0 copy-start.18
  280.6 2.6 copy-start.2
  283.2 230.6 %reduce-scatter.5.cloned.1.call-start = ((), (), s32[]{:S(2)}) async-start(), calls=%async_computation.3 | async-start | bytes 7864320 | tf_op jit(solution)/shard_map/reduce_scatter | solution.py:1686
  283.2 7.2 %copy-start.28 = (bf16[128,2048]{1,0:T(8,128)(2,1)S(1)}, bf16[128,2048]{1,0:T(8,128)(2,1)}, u32[]{:S(2)}) copy-start(bf16[128,2048]{1,0:T(8,128)(2,1)} %get-tuple-element.101.gy) | copy-start | bytes 1572868
  335.5 4.4 copy-start.23
  335.5 4.4 copy-start.14
  335.5 4.4 copy-start.30
  339.9 31.2 %copy-start.5 = (bf16[8,128,2048]{2,1,0:T(8,128)(2,1)S(1)}, bf16[8,128,2048]{2,1,0:T(8,128)(2,1)}, u32[]{:S(2)}) copy-start(bf16[8,128,2048]{2,1,0:T(8,128)(2,1)} %get-tuple-element.87) | copy-start | bytes 12582916
  339.9 31.2 %copy-start.17 = (bf16[1024,512]{1,0:T(8,128)(2,1)S(1)}, bf16[1024,512]{1,0:T(8,128)(2,1)}, u32[]{:S(2)}) copy-start(bf16[1024,512]{1,0:T(8,128)(2,1)} %copy-done.16) | copy-start | bytes 3145732
  371.2 1.7 copy-start.8
  383.1 2.7 copy-start.4
  385.8 1.0 copy-start.25
  386.8 6.4 %copy-start.19 = (bf16[1024,512]{1,0:T(8,128)(2,1)S(1)}, bf16[1024,512]{1,0:T(8,128)(2,1)}, u32[]{:S(2)}) copy-start(bf16[1024,512]{1,0:T(8,128)(2,1)} %copy-done.18) | copy-start | bytes 3145732
  393.2 6.1 %copy-start.9 = (bf16[1024,1280]{1,0:T(8,128)(2,1)S(1)}, bf16[1024,1280]{1,0:T(8,128)(2,1)}, u32[]{:S(2)}) copy-start(bf16[1024,1280]{1,0:T(8,128)(2,1)} %get-tuple-element.105.refs_1_) | copy-start | bytes 7864324
  399.3 8.8 %copy-start.11 = (bf16[128,2048]{1,0:T(8,128)(2,1)S(1)}, bf16[128,2048]{1,0:T(8,128)(2,1)}, u32[]{:S(2)}) copy-start(bf16[128,2048]{1,0:T(8,128)(2,1)} %get-tuple-element.93.x) | copy-start | bytes 1572868
  399.3 8.8 %copy-start.15 = (bf16[512,1536]{1,0:T(8,128)(2,1)S(1)}, bf16[512,1536]{1,0:T(8,128)(2,1)}, u32[]{:S(2)}) copy-start(bf16[512,1536]{1,0:T(8,128)(2,1)} %reduce-scatter.3.cloned.1.call-done) | copy-start | bytes 4718596
  399.3 8.8 %copy-start.24 = (f32[128,2048]{1,0:T(8,128)S(1)}, f32[128,2048]{1,0:T(8,128)}, u32[]{:S(2)}) copy-start(f32[128,2048]{1,0:T(8,128)} %copy-done.23) | copy-start | bytes 3145732
  399.3 8.8 %copy-start.26 = (bf16[2048,256]{1,0:T(8,128)(2,1)S(1)}, bf16[2048,256]{1,0:T(8,128)(2,1)}, u32[]{:S(2)}) copy-start(bf16[2048,256]{1,0:T(8,128)(2,1)} %copy-done.25) | copy-start | bytes 3145732
  399.3 8.8 %copy-start.31 = (bf16[256,256]{1,0:T(8,128)(2,1)S(1)}, bf16[256,256]{1,0:T(8,128)(2,1)}, u32[]{:S(2)}) copy-start(bf16[256,256]{1,0:T(8,128)(2,1)} %get-tuple-element.108.take) | copy-start | bytes 393220
  399.3 8.8 %copy-start.34 = (f32[2048]{0:T(1024)S(1)}, f32[2048]{0:T(1024)}, u32[]{:S(2)}) copy-start(f32[2048]{0:T(1024)} %param.29) | copy-start | bytes 24580
  408.1 105.7 %copy-start.32 = (bf16[256,256]{1,0:T(8,128)(2,1)S(1)}, bf16[256,256]{1,0:T(8,128)(2,1)}, u32[]{:S(2)}) copy-start(bf16[256,256]{1,0:T(8,128)(2,1)} %get-tuple-element.118.give) | copy-start | bytes 393220
  500.8 1.0 copy-start.20
  513.8 45.5 %copy-start.1 = (f32[4,1536]{1,0:T(4,128)S(1)}, f32[4,1536]{1,0:T(4,128)}, u32[]{:S(2)}) copy-start(f32[4,1536]{1,0:T(4,128)} %param.34) | copy-start | bytes 73732
  513.8 1.4 copy-start.12
  515.2 1.2 copy-start.21
Sparse Core Ops, SparseCore 0:
  283.3 109.7 reduce-scatter.2
  395.4 118.2 reduce-scatter.4

commit v7 on v6

--- a/solution.py
+++ b/solution.py
@@ -446,7 +446,7 @@
     lax.fori_loop(0, buf.shape[2] // COLS, column, 0)
 
 
-def permute_in(choice, land, first, second, slots):
+def permute_in(choice, land, first, second, slots, then=None):
     n_row = land.shape[0]
 
     def column(i, carry):
@@ -454,6 +454,8 @@
         got = land[:, :, cols].reshape(n_row * CHUNK, COLS)
         first[:, cols] = matmul_left(choice[:, :slots], got).astype(jnp.bfloat16)
         second[:, cols] = matmul_left(choice[:, slots:], got).astype(jnp.bfloat16)
+        if then is not None:
+            then(i, cols)
         return carry
 
     lax.fori_loop(0, land.shape[2] // COLS, column, 0)
@@ -945,15 +947,28 @@
     across = remote(sums_land.at[:, :, at : at + 128], other, send, recv, r, 1 - c)
     across.start()
     finish_rows(buf, land, csend, crecv)
-    permute_in(give, land, first, second, first.shape[0])
-    copies = [across]
-    for i, (mine, out) in enumerate(((first, output), (second, gradient))):
-        copies.append(pltpu.make_async_copy(mine, out.at[c], here.at[i]))
-        copies.append(remote(mine, out.at[c], osend.at[i], orecv.at[i], r, 1 - c))
-    for copy in copies[1:]:
-        copy.start()
-    for copy in copies:
-        copy.wait()
+
+    def home_copies(i, cols):
+        copies = []
+        for k, (mine, out) in enumerate(((first, output), (second, gradient))):
+            source, target = mine.at[:, cols], out.at[c, :, cols]
+            copies.append(pltpu.make_async_copy(source, target, here.at[k, i]))
+            copies.append(remote(source, target, osend.at[k, i], orecv.at[k, i], r, 1 - c))
+        return copies
+
+    def send_column(i, cols):
+        for copy in home_copies(i, cols):
+            copy.start()
+
+    permute_in(give, land, first, second, first.shape[0], send_column)
+
+    def finish(i, carry):
+        for copy in home_copies(i, pl.ds(pl.multiple_of(i * COLS, COLS), COLS)):
+            copy.wait()
+        return carry
+
+    lax.fori_loop(0, first.shape[1] // COLS, finish, 0)
+    across.wait()
 
 
 def last(buf, give, sums, at):
@@ -979,13 +994,11 @@
             VMEM((slots, width), bf),
             dma((n_row,)),
             dma((n_row,)),
-            dma((2,)),
-            dma((2,)),
-            dma((2,)),
         ]
+        + [dma((2, width // COLS))] * 3
         + deliver_scratch()
         + [dma, dma],
-        compiler_params=params(6, 32),
+        compiler_params=params(6, 48),
         cost_estimate=cost(35),
     )(buf, give, sums)
 
@@ -1015,7 +1028,7 @@
         out_shape=tuple(jax.ShapeDtypeStruct((width, total), jnp.bfloat16) for total in totals),
         in_specs=specs,
         out_specs=tuple(pl.BlockSpec((tile, total), lambda i: (i, 0)) for total in totals),
-        compiler_params=pltpu.CompilerParams(vmem_limit_bytes=30 << 20),
+        compiler_params=pltpu.CompilerParams(vmem_limit_bytes=40 << 20),
         cost_estimate=cost(10),
     )(*[array for pair in pairs for array in pair])
 
@@ -1206,7 +1219,7 @@
             VMEM((slots, width), jnp.float32),
         ]
         + scatter_scratch(slots, width),
-        compiler_params=params(3, 40),
+        compiler_params=params(3, 48),
         cost_estimate=cost(75),
     )(parts, x, d_mid, ff_parts, mid, gain, take, *small, kv_parts, ff_sums)
 
@@ -1789,7 +1802,7 @@
         (grad_projected, grad_mixer, ff_hidden)
     )
     ff_part = matmul_trans(ff_hidden, w_down).astype(bf).reshape(GROUP, slots, width)
-    mixer_sums, ff_sums = sum_groups(grad_mixer, MIX, ff_sums)
+    mixer_sums, unused_value = sum_groups(grad_mixer, MIX)
     normed_one_part = matmul_trans(grad_projected, w_in).astype(bf).reshape(GROUP, slots, width)
 
     buf, small_all, delta_kv, ff_land = send_home(

time: 570 us -> 566 us (level)
    unnamed x84 -> x74, local copies, waits for them, and re-layouts: 15.6 us -> 11 us
  transfers between devices with their start and end apart: 5 -> 5, of which waited for: 3 -> 2; matrix products, arithmetic and copies ran while one was open for 7% -> 8% of each run, Pallas kernels for 47% -> 47%
where the time goes in v7:
time: 566 us; the launch traced here: 563 us
  Pallas kernels  461 us (81%)
  matrix products  49.2 us (9%)
  waiting for transfers between devices  22.3 us (4%)
  between operations  14.6 us (3%)
  local copies, waits for them, and re-layouts  12.9 us (2%)
    pallas_call x1, Pallas kernels, deal(): pl.pallas_call(deal_kernel, name='deal', out_shape=(jax.ShapeDtypeStruct(...  147 us
    pallas_call x1, Pallas kernels, send_home(): pl.pallas_call(home_kernel, name='home', out_shape=(jax.ShapeDtypeStruct(...  91.1 us
    pallas_call x1, Pallas kernels, middle(): pl.pallas_call(middle_kernel, name='middle', out_shape=(jax.ShapeDtypeStr...  62.1 us
    pallas_call x1, Pallas kernels, turn(): pl.pallas_call(turn_kernel, name='turn', out_shape=(jax.ShapeDtypeStruct(...  45.1 us
    pallas_call x1, Pallas kernels, last(): pl.pallas_call(partial(last_kernel, at), name='last', out_shape=(jax.Shap...  36.7 us
    pallas_call x1, Pallas kernels, mixer_back(): pl.pallas_call(partial(mixer_back_kernel, sh, ph), name='mixer_back', out...  31.2 us
    dot_general x4, matrix products, matmul_trans(): lax.dot_general(first_op, second_op, (((1,), (1,)), ((), ())), preferred_...  28.1 us
    pallas_call x1, Pallas kernels, mixer(): pl.pallas_call(partial(mixer_kernel, sh, ph), name='mixer', out_shape=(ja...  22.4 us
  transfers between devices with their start and end apart: 5, of which 2 were waited for; matrix products, arithmetic and copies ran while one was open for 8% of the time, Pallas kernels for 47%

profile of v7, /device:TPU:9, one launch (start us, length us, event | category | flops | bytes accessed | tf_op | source)
XLA Modules:
  0.0 563.0 jit_solution(17455129759780223269)
XLA Ops:
  7.3 1.4 copy.48.refs_6_
  8.7 147.3 %deal.1 = (s32[16,8,128]{2,1,0:T(8,128)}, bf16[256,256]{1,0:T(8,128)(2,1)}, bf16[256,256]{1,0:T(8,128)(2,1)}, bf16[128,2048]{1,0:T(8,128)(2,1)}, bf16[128,2048]{...) custom-call(s32[2,128]{1,0:T(2,128)} %order.1, ...), custom_call_target="tpu_custom_call" | custom-call | bytes 340000000 | tf_op jit(solution)/shard_map/deal/pallas_call | solution.py:656
  156.0 0.3 collective-permute-start.1
  156.3 0.3 collective-permute-start
  156.7 0.1 pad.18.clone
  156.8 0.1 pad.28.clone
  156.8 0.8 dynamic-slice.12
  157.6 0.1 dynamic-slice.13
  157.8 0.1 broadcast_in_dim.29
  157.8 0.3 fusion.15
  158.2 0.1 dynamic-slice_bitcast_fusion
  158.2 0.1 fusion.18
  158.3 0.1 select_maximum_fusion
  158.4 8.9 %fusion.2.projected = f32[1024,1280]{1,0:T(8,128)S(1)} fusion(bf16[1024,2048]{1,0:T(8,128)(2,1)} %bitcast.41, bf16[2048,1792]{1,0:T(8,128)(2,1)} %bitcast.67), kind=kOutput, calls=%fused_computation.2 | convolution fusion | flops 5368709120 | bytes 14680064 | tf_op jit(solution)/shard_map/dot_general | solution.py:24
  167.3 0.1 pad_maximum_fusion.1.table
  167.4 0.7 constant_dynamic-slice_fusion.4
  168.2 0.1 select_maximum_fusion.1
  168.3 0.1 maximum_maximum_fusion.1.side
  168.4 22.4 %mixer.1 = (bf16[1024,512]{1,0:T(8,128)(2,1)S(1)}, f32[1024,384]{1,0:T(8,128)S(1)}, bf16[8,128,128]{2,1,0:T(8,128)(2,1)S(1)}) custom-call(s32[8,3]{1,0:T(8,128)S(1)} %bitcast.54, f32[1024,1280]{1,0:T(8,128)S(1)} %fusion.2.projected, f32[8,384]{1,0:T(8,128)S(1)} %maximum_maximum_fusion.chan, f32[8,128]{1,0:T(8,128)S(1)} %maximum_maximum_fusion.1.side, ...), custom_call_target="tpu_custom_call" | custom-call | bytes 102000000 | tf_op jit(solution)/shard_map/mixer/pallas_call | solution.py:1464
  190.9 5.0 convolution_convert_fusion.1
  196.0 4.9 collective-permute-done.refs_1_
  200.9 0.2 collective-permute-start.2
  201.1 62.1 %middle.1 = (f32[128,2048]{1,0:T(8,128)S(1)}, bf16[8,128,2048]{2,1,0:T(8,128)(2,1)S(1)}, bf16[4,4,128,512]{3,2,1,0:T(8,128)(2,1)S(1)}) custom-call(bf16[8,128,2048]{2,1,0:T(8,128)(2,1)S(1)} %bitcast.49, bf16[128,2048]{1,0:T(8,128)(2,1)S(1)} %copy-done.8, f32[1,2048]{1,0:T(1,128)S(1)} %bitcast.56, bf16[4,128,512]{2,1,0:T(8,128)(2,1)S(1)} %copy-done.22), custom_call_target="tpu_custom_call" | custom-call | bytes 204000000 | tf_op jit(solution)/shard_map/middle/pallas_call | solution.py:756
  263.2 0.6 place.1
  263.8 4.5 fusion.19
  268.4 3.3 fusion.9
  271.7 0.3 pad_maximum_fusion.refs_1_
  272.0 0.6 copy-done.15
  272.7 9.2 %products.2 = bf16[2048,1536]{1,0:T(8,128)(2,1)} custom-call(bf16[1024,2048]{1,0:T(8,128)(2,1)S(1)} %bitcast.46, bf16[1024,1024]{1,0:T(8,128)(2,1)S(1)} %pad_maximum_fusion.refs_1_, bf16[1024,2048]{1,0:T(8,128)(2,1)S(1)} %bitcast.44, bf16[1024,512]{1,0:T(8,128)(2,1)S(1)} %get-tuple-element.105.refs_3_), custom_call_target="tpu_custom_call" | custom-call | bytes 34000000 | tf_op jit(solution)/shard_map/products/pallas_call | solution.py:1024
  281.9 7.2 %convolution_convert_fusion.2 = bf16[1024,2048]{1,0:T(8,128)(2,1)S(1)} fusion(bf16[1024,1024]{1,0:T(8,128)(2,1)S(1)} %pad_maximum_fusion.refs_1_, bf16[2048,1024]{1,0:T(8,128)(2,1)} %bitcast.51), kind=kOutput, calls=%fused_computation.7 | convolution fusion | flops 4297064448 | bytes 10485760 | tf_op jit(solution)/shard_map/dot_general | solution.py:28
  289.2 45.1 %turn.1 = (f32[128,2048]{1,0:T(8,128)S(1)}, f32[1,2048]{1,0:T(1,128)S(1)}, bf16[8,128,2048]{2,1,0:T(8,128)(2,1)S(1)}) custom-call(bf16[8,128,2048]{2,1,0:T(8,128)(2,1)S(1)} %bitcast.52, f32[128,2048]{1,0:T(8,128)S(1)} %get-tuple-element.98.mid, bf16[128,2048]{1,0:T(8,128)(2,1)S(1)} %copy-done.23, f32[1,2048]{1,0:T(1,128)S(1)} %bitcast.57), custom_call_target="tpu_custom_call" | custom-call | bytes 204000000 | tf_op jit(solution)/shard_map/turn/pallas_call | solution.py:810
  334.3 4.3 fusion.11.grads
  338.6 31.2 %mixer_back.1 = (bf16[1024,1280]{1,0:T(8,128)(2,1)}, f32[8,384]{1,0:T(8,128)S(1)}, f32[8,128]{1,0:T(8,128)S(1)}) custom-call(s32[8,3]{1,0:T(8,128)S(1)} %bitcast.55, f32[1024,1280]{1,0:T(8,128)} %copy-done.2, f32[8,384]{1,0:T(8,128)S(1)} %maximum_maximum_fusion.chan, f32[8,128]{1,0:T(8,128)S(1)} %maximum_maximum_fusion.1.side, ...), custom_call_target="tpu_custom_call" | custom-call | bytes 170000000 | tf_op jit(solution)/shard_map/mixer_back/pallas_call | solution.py:1595
  369.9 1.7 copy-done.6
  371.6 11.4 %products.3 = (bf16[2048,1536]{1,0:T(8,128)(2,1)}, bf16[2048,256]{1,0:T(8,128)(2,1)S(1)}) custom-call(bf16[1024,2048]{1,0:T(8,128)(2,1)S(1)} %bitcast.42, bf16[1024,1280]{1,0:T(8,128)(2,1)S(1)} %copy-done.6, bf16[1024,2048]{1,0:T(8,128)(2,1)S(1)} %bitcast.48, bf16[1024,512]{1,0:T(8,128)(2,1)S(1)} %copy-done.14), custom_call_target="tpu_custom_call" | custom-call | bytes 34000000 | tf_op jit(solution)/shard_map/products/pallas_call | solution.py:1024
  383.0 1.0 copy-done.20
  384.0 1.2 copy-done.16
  385.2 6.1 %convolution_convert_fusion = bf16[1024,2048]{1,0:T(8,128)(2,1)} fusion(bf16[1024,512]{1,0:T(8,128)(2,1)S(1)} %copy-done.16, bf16[2048,512]{1,0:T(8,128)(2,1)} %bitcast.61), kind=kOutput, calls=%fused_computation.5 | convolution fusion | flops 2149580800 | bytes 7340032 | tf_op jit(solution)/shard_map/dot_general | solution.py:28
  391.3 9.9 %fusion.4 = bf16[1024,2048]{1,0:T(8,128)(2,1)} fusion(bf16[1024,1280]{1,0:T(8,128)(2,1)S(1)} %copy-done.7, bf16[2048,1792]{1,0:T(8,128)(2,1)} %bitcast.70), kind=kOutput, calls=%fused_computation.4 | convolution fusion | flops 5370806272 | bytes 12058624 | tf_op jit(solution)/shard_map/dot_general | solution.py:28
  401.2 1.5 copy-done.19
  402.7 1.2 copy-done.21
  404.0 91.1 %home.1 = (bf16[16,16,2048]{2,1,0:T(8,128)(2,1)S(1)}, f32[8,64,128]{2,1,0:T(8,128)S(1)}, f32[128,256]{1,0:T(8,128)S(1)}, bf16[4,128,1536]{2,1,0:T(8,128)(2,1)}) custom-call(bf16[8,128,2048]{2,1,0:T(8,128)(2,1)} %bitcast.63, bf16[128,2048]{1,0:T(8,128)(2,1)S(1)} %copy-done.9, f32[128,2048]{1,0:T(8,128)S(1)} %copy-done.19, bf16[8,128,2048]{2,1,0:T(8,128)(2,1)} %bitcast.62, ...), custom_call_target="tpu_custom_call" | custom-call | bytes 255000000 | tf_op jit(solution)/shard_map/home/pallas_call | solution.py:1182
  495.1 17.3 %reduce-scatter.5.cloned.1.call-done = bf16[512,1536]{1,0:T(8,128)(2,1)} async-done(((bf16[2048,1536]{1,0:T(8,128)(2,1)}), bf16[512,1536]{1,0:T(8,128)(2,1)}) %reduce-scatter.5.cloned.1.call-update) | async-done | bytes 1572880 | tf_op jit(solution)/shard_map/reduce_scatter | solution.py:1699
  512.4 36.7 %last.1 = (bf16[2,128,2048]{2,1,0:T(8,128)(2,1)S(1)}, bf16[2,128,2048]{2,1,0:T(8,128)(2,1)S(1)}, bf16[4,128,1536]{2,1,0:T(8,128)(2,1)S(1)}, bf16[4,128,128]{2,1,0:T(8,128)(2,1)S(1)}) custom-call(bf16[16,16,2048]{2,1,0:T(8,128)(2,1)S(1)} %get-tuple-element.113.buf, bf16[256,256]{1,0:T(8,128)(2,1)S(1)} %copy-done.27, bf16[4,128,1536]{2,1,0:T(8,128)(2,1)} %bitcast.64), custom_call_target="tpu_custom_call" | custom-call | bytes 119000000 | tf_op jit(solution)/shard_map/last/pallas_call | solution.py:980
  549.1 1.4 copy-done.10
  550.5 4.3 unpack.1
  554.8 0.7 copy.53
  555.5 0.6 reduce
  (79 shorter events, 0.4 us)
Async XLA Ops:
  7.2 150.6 %copy-start = (f32[4,1536]{1,0:T(4,128)S(1)}, f32[4,1536]{1,0:T(4,128)}, u32[]{:S(2)}) copy-start(f32[4,1536]{1,0:T(4,128)} %param.34) | copy-start | bytes 73732
  7.2 150.4 %copy-start.35 = (f32[24]{0:T(128)S(1)}, f32[24]{0:T(128)}, u32[]{:S(2)}) copy-start(f32[24]{0:T(128)} %param.40) | copy-start | bytes 292
  7.2 150.9 %copy-start.33 = (f32[24]{0:T(128)S(1)}, f32[24]{0:T(128)}, u32[]{:S(2)}) copy-start(f32[24]{0:T(128)} %param.39) | copy-start | bytes 292
  7.2 150.9 %copy-start.34 = (f32[24]{0:T(128)S(1)}, f32[24]{0:T(128)}, u32[]{:S(2)}) copy-start(f32[24]{0:T(128)} %param.38) | copy-start | bytes 292
  7.2 151.0 %copy-start.32 = (f32[512]{0:T(512)S(1)}, f32[512]{0:T(512)}, u32[]{:S(2)}) copy-start(f32[512]{0:T(512)} %param.37) | copy-start | bytes 6148
  7.3 151.0 %copy-start.31 = (f32[4,512]{1,0:T(4,128)S(1)}, f32[4,512]{1,0:T(4,128)}, u32[]{:S(2)}) copy-start(f32[4,512]{1,0:T(4,128)} %param.36) | copy-start | bytes 24580
  7.3 393.9 %reduce-scatter.3.cloned.1.call-start = ((), (), s32[]{:S(2)}) async-start(), calls=%async_computation.2 | async-start | bytes 7864320 | tf_op jit(solution)/shard_map/reduce_scatter | solution.py:1699
  156.0 107.2 %collective-permute-start.1 = (bf16[4,128,1024]{2,1,0:T(8,128)(2,1)}, bf16[4,128,1024]{2,1,0:T(8,128)(2,1)S(1)}, u32[]{:S(2)}, u32[]{:S(2)}) collective-permute-start(bf16[4,128,1024]{2,1,0:T(8,128)(2,1)} %get-tuple-element.95.refs_0_), channel_id=1, source_target_pairs={{0,8},{2,10},{4,12},{6,14},{8,0},{10,2},{12,4},{14,6},{16,24},{18,... | collective-permute-start | bytes 3145736 | tf_op jit(solution)/shard_map/ppermute | solution.py:1676
  156.3 44.6 %collective-permute-start = (bf16[4,128,1024]{2,1,0:T(8,128)(2,1)}, bf16[4,128,1024]{2,1,0:T(8,128)(2,1)S(1)}, u32[]{:S(2)}, u32[]{:S(2)}) collective-permute-start(bf16[4,128,1024]{2,1,0:T(8,128)(2,1)} %get-tuple-element.95.refs_0_), channel_id=1, source_target_pairs={{0,16},{2,18},{4,20},{6,22},{8,24},{10,26},{12,28},{14,30},{16,0},... | collective-permute-start | bytes 3145736 | tf_op jit(solution)/shard_map/ppermute | solution.py:1676
  167.3 28.6 %copy-start.2 = (f32[1024,1280]{1,0:T(8,128)}, f32[1024,1280]{1,0:T(8,128)S(1)}, u32[]{:S(2)}) copy-start(f32[1024,1280]{1,0:T(8,128)S(1)} %fusion.2.projected) | copy-start | bytes 15728644
  190.8 5.1 copy-start.11
  190.9 5.1 copy-start.13
  190.9 5.1 copy-start.24
  190.9 10.2 %copy-start.8 = (bf16[128,2048]{1,0:T(8,128)(2,1)S(1)}, bf16[128,2048]{1,0:T(8,128)(2,1)}, u32[]{:S(2)}) copy-start(bf16[128,2048]{1,0:T(8,128)(2,1)} %get-tuple-element.91.x) | copy-start | bytes 1572868
  190.9 10.2 %copy-start.22 = (bf16[4,128,512]{2,1,0:T(8,128)(2,1)S(1)}, bf16[4,128,512]{2,1,0:T(8,128)(2,1)}, u32[]{:S(2)}) copy-start(bf16[4,128,512]{2,1,0:T(8,128)(2,1)} %get-tuple-element.92.slab) | copy-start | bytes 1572868
  190.9 10.2 %copy-start.28 = (f32[2048]{0:T(1024)S(1)}, f32[2048]{0:T(1024)}, u32[]{:S(2)}) copy-start(f32[2048]{0:T(1024)} %param.46) | copy-start | bytes 24580
  196.0 67.2 %copy-start.17 = (bf16[4,128,1024]{2,1,0:T(8,128)(2,1)S(1)}, bf16[4,128,1024]{2,1,0:T(8,128)(2,1)}, u32[]{:S(2)}) copy-start(bf16[4,128,1024]{2,1,0:T(8,128)(2,1)} %get-tuple-element.95.refs_0_) | copy-start | bytes 3145732
  200.9 62.3 %collective-permute-start.2 = (bf16[4,128,1024]{2,1,0:T(8,128)(2,1)S(1)}, bf16[4,128,1024]{2,1,0:T(8,128)(2,1)S(1)}, u32[]{:S(2)}, u32[]{:S(2)}) collective-permute-start(bf16[4,128,1024]{2,1,0:T(8,128)(2,1)S(1)} %collective-permute-done.refs_1_), channel_id=1, source_target_pairs={{0,8},{2,10},{4,12},{6,14},{8,0},{10,2},{12,4},{14,6},{16,24},{18,... | collective-permute-start | bytes 3145736 | tf_op jit(solution)/shard_map/ppermute | solution.py:1676
  263.2 5.2 copy-start.30
  263.8 4.6 copy-start.5
  263.8 4.6 copy-start.4
  271.7 1.0 copy-start.15
  281.9 230.6 %reduce-scatter.5.cloned.1.call-start = ((), (), s32[]{:S(2)}) async-start(), calls=%async_computation.3 | async-start | bytes 7864320 | tf_op jit(solution)/shard_map/reduce_scatter | solution.py:1699
  281.9 7.2 %copy-start.23 = (bf16[128,2048]{1,0:T(8,128)(2,1)S(1)}, bf16[128,2048]{1,0:T(8,128)(2,1)}, u32[]{:S(2)}) copy-start(bf16[128,2048]{1,0:T(8,128)(2,1)} %get-tuple-element.99.gy) | copy-start | bytes 1572868
  334.2 4.4 copy-start.18
  334.2 4.4 copy-start.12
  334.3 4.4 copy-start.25
  338.6 31.2 %copy-start.3 = (bf16[8,128,2048]{2,1,0:T(8,128)(2,1)S(1)}, bf16[8,128,2048]{2,1,0:T(8,128)(2,1)}, u32[]{:S(2)}) copy-start(bf16[8,128,2048]{2,1,0:T(8,128)(2,1)} %get-tuple-element.85) | copy-start | bytes 12582916
  338.6 31.2 %copy-start.14 = (bf16[1024,512]{1,0:T(8,128)(2,1)S(1)}, bf16[1024,512]{1,0:T(8,128)(2,1)}, u32[]{:S(2)}) copy-start(bf16[1024,512]{1,0:T(8,128)(2,1)} %copy-done.13) | copy-start | bytes 3145732
  369.8 1.7 copy-start.6
  383.0 1.0 copy-start.20
  384.0 1.2 copy-start.16
  385.2 6.1 %copy-start.7 = (bf16[1024,1280]{1,0:T(8,128)(2,1)S(1)}, bf16[1024,1280]{1,0:T(8,128)(2,1)}, u32[]{:S(2)}) copy-start(bf16[1024,1280]{1,0:T(8,128)(2,1)} %get-tuple-element.103.refs_1_) | copy-start | bytes 7864324
  391.3 9.9 %copy-start.9 = (bf16[128,2048]{1,0:T(8,128)(2,1)S(1)}, bf16[128,2048]{1,0:T(8,128)(2,1)}, u32[]{:S(2)}) copy-start(bf16[128,2048]{1,0:T(8,128)(2,1)} %get-tuple-element.91.x) | copy-start | bytes 1572868
  391.3 9.9 %copy-start.26 = (bf16[256,256]{1,0:T(8,128)(2,1)S(1)}, bf16[256,256]{1,0:T(8,128)(2,1)}, u32[]{:S(2)}) copy-start(bf16[256,256]{1,0:T(8,128)(2,1)} %get-tuple-element.106.take) | copy-start | bytes 393220
  391.3 9.9 %copy-start.29 = (f32[2048]{0:T(1024)S(1)}, f32[2048]{0:T(1024)}, u32[]{:S(2)}) copy-start(f32[2048]{0:T(1024)} %param.29) | copy-start | bytes 24580
  401.2 1.5 copy-start.19
  402.7 1.2 copy-start.21
  404.0 108.5 %copy-start.27 = (bf16[256,256]{1,0:T(8,128)(2,1)S(1)}, bf16[256,256]{1,0:T(8,128)(2,1)}, u32[]{:S(2)}) copy-start(bf16[256,256]{1,0:T(8,128)(2,1)} %get-tuple-element.114.give) | copy-start | bytes 393220
  512.4 43.7 %copy-start.1 = (f32[4,1536]{1,0:T(4,128)S(1)}, f32[4,1536]{1,0:T(4,128)}, u32[]{:S(2)}) copy-start(f32[4,1536]{1,0:T(4,128)} %param.34) | copy-start | bytes 73732
  549.1 1.4 copy-start.10
Sparse Core Ops, SparseCore 0:
  282.0 109.7 reduce-scatter.2
  394.1 118.2 reduce-scatter.4

commit v8 on v7

--- a/solution.py
+++ b/solution.py
@@ -1097,7 +1097,7 @@
     ]
     for i in range(4):
         conv_k[i : i + 1, :] = channels[i]
-    conv_b[...] = channels[4]
+    conv_b[...] = channels[4][0]
     per_head = mh // ph
     shape = (TP * mh, TP * ph)
     heads = lax.broadcasted_iota(jnp.int32, shape, 1) * per_head
@@ -1116,7 +1116,7 @@
         axis=1,
     )
     state_k[...] = states[:4, :]
-    state_b[...] = states[4:5, :]
+    state_b[...] = states[4]
     own_heads = jnp.concatenate(
         [jnp.where(c == 0, sides[0][m], sides[1][m])[:, 2 * sh : 2 * sh + ph] for m in range(TP)], axis=1
     )
@@ -1124,10 +1124,10 @@
     decay[...] = own_heads[6:7, :]
     start = start + 8
     for gain in (ff_gain, mixer_gain):
-        count = gain.shape[1] // 128
+        count = gain.shape[0] // 128
         total = sum(small[i, start : start + count, :] for i in range(GROUP))
         for k in range(count):
-            gain[:, k * 128 : (k + 1) * 128] = total[k : k + 1, :]
+            gain[k * 128 : (k + 1) * 128] = total[k]
         start = start + count
     for copy in copies:
         copy.wait()
@@ -1139,15 +1139,15 @@
     vm, hb = pl.BlockSpec(memory_space=VMEM), pl.BlockSpec(memory_space=ANY)
     f32 = jnp.float32
     shapes = [
-        (1, width),
+        (width,),
         (rows, TP * mh),
         (rows, TP * mh),
         (rows, 2 * GROUP * sh),
         (rows, TP * ph),
         (4, TP * mh),
-        (1, TP * mh),
+        (TP * mh,),
         (4, 2 * GROUP * sh),
-        (1, 2 * GROUP * sh),
+        (2 * GROUP * sh,),
         (1, TP * ph),
         (1, TP * ph),
         (1, TP * ph),
@@ -1156,7 +1156,7 @@
         (rows, kvh),
         (rows, kvh),
         (TP * qh, rows),
-        (1, width),
+        (width,),
         (rows, TP * fh),
         (rows, TP * fh),
         (TP * fh, rows),
@@ -1814,7 +1814,7 @@
     results = unpack(
         ff_land, mixer_land, other_land, small_all, delta_kv, output, grad_tokens, mh, qh, fh, sh, ph
     )
-    flat = (2, 8, 10, 11, 12, 13, 19)
+    flat = (11, 12, 13)
     return tuple(
         array.reshape(array.shape[1]) if i in flat else array for i, array in enumerate(results)
     )

time: 566 us -> 566 us (level)
  no operation moved by 1% of the time
where the time goes in v8:
time: 566 us; the launch traced here: 562 us
  Pallas kernels  461 us (81%)
  matrix products  49.2 us (9%)
  waiting for transfers between devices  22.4 us (4%)
  between operations  14.6 us (3%)
  local copies, waits for them, and re-layouts  12.9 us (2%)
    pallas_call x1, Pallas kernels, deal(): pl.pallas_call(deal_kernel, name='deal', out_shape=(jax.ShapeDtypeStruct(...  147 us
    pallas_call x1, Pallas kernels, send_home(): pl.pallas_call(home_kernel, name='home', out_shape=(jax.ShapeDtypeStruct(...  91 us
    pallas_call x1, Pallas kernels, middle(): pl.pallas_call(middle_kernel, name='middle', out_shape=(jax.ShapeDtypeStr...  62.1 us
    pallas_call x1, Pallas kernels, turn(): pl.pallas_call(turn_kernel, name='turn', out_shape=(jax.ShapeDtypeStruct(...  45.1 us
    pallas_call x1, Pallas kernels, last(): pl.pallas_call(partial(last_kernel, at), name='last', out_shape=(jax.Shap...  36.7 us
    pallas_call x1, Pallas kernels, mixer_back(): pl.pallas_call(partial(mixer_back_kernel, sh, ph), name='mixer_back', out...  31.2 us
    dot_general x4, matrix products, matmul_trans(): lax.dot_general(first_op, second_op, (((1,), (1,)), ((), ())), preferred_...  28.1 us
    pallas_call x1, Pallas kernels, mixer(): pl.pallas_call(partial(mixer_kernel, sh, ph), name='mixer', out_shape=(ja...  22.5 us
  transfers between devices with their start and end apart: 5, of which 2 were waited for; matrix products, arithmetic and copies ran while one was open for 8% of the time, Pallas kernels for 47%

profile of v8, /device:TPU:9, one launch (start us, length us, event | category | flops | bytes accessed | tf_op | source)
XLA Modules:
  0.0 562.4 jit_solution(3279467203934103722)
XLA Ops:
  7.3 1.4 copy.48.refs_6_
  8.7 147.3 %deal.1 = (s32[16,8,128]{2,1,0:T(8,128)}, bf16[256,256]{1,0:T(8,128)(2,1)}, bf16[256,256]{1,0:T(8,128)(2,1)}, bf16[128,2048]{1,0:T(8,128)(2,1)}, bf16[128,2048]{...) custom-call(s32[2,128]{1,0:T(2,128)} %order.1, ...), custom_call_target="tpu_custom_call" | custom-call | bytes 340000000 | tf_op jit(solution)/shard_map/deal/pallas_call | solution.py:656
  156.0 0.4 collective-permute-start.1
  156.4 0.2 collective-permute-start
  156.6 0.1 pad.18.clone
  156.7 0.1 pad.28.clone
  156.8 0.8 dynamic-slice.12
  157.6 0.1 dynamic-slice.13
  157.6 0.1 broadcast_in_dim.28
  157.7 0.1 broadcast_in_dim.29
  157.8 0.3 fusion.15
  158.1 0.1 dynamic-slice_bitcast_fusion
  158.2 0.1 fusion.18
  158.3 0.1 select_maximum_fusion
  158.3 8.9 %fusion.2.projected = f32[1024,1280]{1,0:T(8,128)S(1)} fusion(bf16[1024,2048]{1,0:T(8,128)(2,1)} %bitcast.38, bf16[2048,1792]{1,0:T(8,128)(2,1)} %bitcast.64), kind=kOutput, calls=%fused_computation.2 | convolution fusion | flops 5368709120 | bytes 14680064 | tf_op jit(solution)/shard_map/dot_general | solution.py:24
  167.3 0.1 pad_maximum_fusion.1.table
  167.4 0.7 constant_dynamic-slice_fusion.4
  168.1 0.1 select_maximum_fusion.1
  168.2 0.1 maximum_maximum_fusion.1.side
  168.4 22.5 %mixer.1 = (bf16[1024,512]{1,0:T(8,128)(2,1)S(1)}, f32[1024,384]{1,0:T(8,128)S(1)}, bf16[8,128,128]{2,1,0:T(8,128)(2,1)S(1)}) custom-call(s32[8,3]{1,0:T(8,128)S(1)} %bitcast.51, f32[1024,1280]{1,0:T(8,128)S(1)} %fusion.2.projected, f32[8,384]{1,0:T(8,128)S(1)} %maximum_maximum_fusion.chan, f32[8,128]{1,0:T(8,128)S(1)} %maximum_maximum_fusion.1.side, ...), custom_call_target="tpu_custom_call" | custom-call | bytes 102000000 | tf_op jit(solution)/shard_map/mixer/pallas_call | solution.py:1464
  190.9 5.0 convolution_convert_fusion.1
  196.0 4.8 collective-permute-done.refs_1_
  200.8 0.2 collective-permute-start.2
  201.1 62.1 %middle.1 = (f32[128,2048]{1,0:T(8,128)S(1)}, bf16[8,128,2048]{2,1,0:T(8,128)(2,1)S(1)}, bf16[4,4,128,512]{3,2,1,0:T(8,128)(2,1)S(1)}) custom-call(bf16[8,128,2048]{2,1,0:T(8,128)(2,1)S(1)} %bitcast.46, bf16[128,2048]{1,0:T(8,128)(2,1)S(1)} %copy-done.8, f32[1,2048]{1,0:T(1,128)S(1)} %bitcast.53, bf16[4,128,512]{2,1,0:T(8,128)(2,1)S(1)} %copy-done.22), custom_call_target="tpu_custom_call" | custom-call | bytes 204000000 | tf_op jit(solution)/shard_map/middle/pallas_call | solution.py:756
  263.2 0.6 place.1
  263.8 4.5 fusion.19
  268.4 3.3 fusion.9
  271.7 0.3 pad_maximum_fusion.refs_1_
  272.0 0.6 copy-done.15
  272.7 9.2 %products.2 = bf16[2048,1536]{1,0:T(8,128)(2,1)} custom-call(bf16[1024,2048]{1,0:T(8,128)(2,1)S(1)} %bitcast.43, bf16[1024,1024]{1,0:T(8,128)(2,1)S(1)} %pad_maximum_fusion.refs_1_, bf16[1024,2048]{1,0:T(8,128)(2,1)S(1)} %bitcast.41, bf16[1024,512]{1,0:T(8,128)(2,1)S(1)} %get-tuple-element.105.refs_3_), custom_call_target="tpu_custom_call" | custom-call | bytes 34000000 | tf_op jit(solution)/shard_map/products/pallas_call | solution.py:1024
  281.9 7.2 %convolution_convert_fusion.2 = bf16[1024,2048]{1,0:T(8,128)(2,1)S(1)} fusion(bf16[1024,1024]{1,0:T(8,128)(2,1)S(1)} %pad_maximum_fusion.refs_1_, bf16[2048,1024]{1,0:T(8,128)(2,1)} %bitcast.48), kind=kOutput, calls=%fused_computation.7 | convolution fusion | flops 4297064448 | bytes 10485760 | tf_op jit(solution)/shard_map/dot_general | solution.py:28
  289.1 45.1 %turn.1 = (f32[128,2048]{1,0:T(8,128)S(1)}, f32[1,2048]{1,0:T(1,128)S(1)}, bf16[8,128,2048]{2,1,0:T(8,128)(2,1)S(1)}) custom-call(bf16[8,128,2048]{2,1,0:T(8,128)(2,1)S(1)} %bitcast.49, f32[128,2048]{1,0:T(8,128)S(1)} %get-tuple-element.98.mid, bf16[128,2048]{1,0:T(8,128)(2,1)S(1)} %copy-done.23, f32[1,2048]{1,0:T(1,128)S(1)} %bitcast.54), custom_call_target="tpu_custom_call" | custom-call | bytes 204000000 | tf_op jit(solution)/shard_map/turn/pallas_call | solution.py:810
  334.2 4.3 fusion.11.grads
  338.6 31.2 %mixer_back.1 = (bf16[1024,1280]{1,0:T(8,128)(2,1)}, f32[8,384]{1,0:T(8,128)S(1)}, f32[8,128]{1,0:T(8,128)S(1)}) custom-call(s32[8,3]{1,0:T(8,128)S(1)} %bitcast.52, f32[1024,1280]{1,0:T(8,128)} %copy-done.2, f32[8,384]{1,0:T(8,128)S(1)} %maximum_maximum_fusion.chan, f32[8,128]{1,0:T(8,128)S(1)} %maximum_maximum_fusion.1.side, ...), custom_call_target="tpu_custom_call" | custom-call | bytes 170000000 | tf_op jit(solution)/shard_map/mixer_back/pallas_call | solution.py:1595
  369.8 1.7 copy-done.6
  371.6 11.4 %products.3 = (bf16[2048,1536]{1,0:T(8,128)(2,1)}, bf16[2048,256]{1,0:T(8,128)(2,1)S(1)}) custom-call(bf16[1024,2048]{1,0:T(8,128)(2,1)S(1)} %bitcast.39, bf16[1024,1280]{1,0:T(8,128)(2,1)S(1)} %copy-done.6, bf16[1024,2048]{1,0:T(8,128)(2,1)S(1)} %bitcast.45, bf16[1024,512]{1,0:T(8,128)(2,1)S(1)} %copy-done.14), custom_call_target="tpu_custom_call" | custom-call | bytes 34000000 | tf_op jit(solution)/shard_map/products/pallas_call | solution.py:1024
  383.0 1.0 copy-done.20
  384.0 1.2 copy-done.16
  385.2 6.1 %convolution_convert_fusion = bf16[1024,2048]{1,0:T(8,128)(2,1)} fusion(bf16[1024,512]{1,0:T(8,128)(2,1)S(1)} %copy-done.16, bf16[2048,512]{1,0:T(8,128)(2,1)} %bitcast.58), kind=kOutput, calls=%fused_computation.5 | convolution fusion | flops 2149580800 | bytes 7340032 | tf_op jit(solution)/shard_map/dot_general | solution.py:28
  391.2 9.9 %fusion.4 = bf16[1024,2048]{1,0:T(8,128)(2,1)} fusion(bf16[1024,1280]{1,0:T(8,128)(2,1)S(1)} %copy-done.7, bf16[2048,1792]{1,0:T(8,128)(2,1)} %bitcast.67), kind=kOutput, calls=%fused_computation.4 | convolution fusion | flops 5370806272 | bytes 12058624 | tf_op jit(solution)/shard_map/dot_general | solution.py:28
  401.2 1.5 copy-done.19
  402.7 1.2 copy-done.21
  403.9 91.0 %home.1 = (bf16[16,16,2048]{2,1,0:T(8,128)(2,1)S(1)}, f32[8,64,128]{2,1,0:T(8,128)S(1)}, f32[128,256]{1,0:T(8,128)S(1)}, bf16[4,128,1536]{2,1,0:T(8,128)(2,1)}) custom-call(bf16[8,128,2048]{2,1,0:T(8,128)(2,1)} %bitcast.60, bf16[128,2048]{1,0:T(8,128)(2,1)S(1)} %copy-done.9, f32[128,2048]{1,0:T(8,128)S(1)} %copy-done.19, bf16[8,128,2048]{2,1,0:T(8,128)(2,1)} %bitcast.59, ...), custom_call_target="tpu_custom_call" | custom-call | bytes 255000000 | tf_op jit(solution)/shard_map/home/pallas_call | solution.py:1182
  494.9 17.5 %reduce-scatter.5.cloned.1.call-done = bf16[512,1536]{1,0:T(8,128)(2,1)} async-done(((bf16[2048,1536]{1,0:T(8,128)(2,1)}), bf16[512,1536]{1,0:T(8,128)(2,1)}) %reduce-scatter.5.cloned.1.call-update) | async-done | bytes 1572880 | tf_op jit(solution)/shard_map/reduce_scatter | solution.py:1699
  512.5 36.7 %last.1 = (bf16[2,128,2048]{2,1,0:T(8,128)(2,1)S(1)}, bf16[2,128,2048]{2,1,0:T(8,128)(2,1)S(1)}, bf16[4,128,1536]{2,1,0:T(8,128)(2,1)S(1)}, bf16[4,128,128]{2,1,0:T(8,128)(2,1)S(1)}) custom-call(bf16[16,16,2048]{2,1,0:T(8,128)(2,1)S(1)} %get-tuple-element.113.buf, bf16[256,256]{1,0:T(8,128)(2,1)S(1)} %copy-done.27, bf16[4,128,1536]{2,1,0:T(8,128)(2,1)} %bitcast.61), custom_call_target="tpu_custom_call" | custom-call | bytes 119000000 | tf_op jit(solution)/shard_map/last/pallas_call | solution.py:980
  549.2 1.4 copy-done.10
  550.6 4.3 unpack.1
  554.9 0.7 copy.53
  (78 shorter events, 0.4 us)
Async XLA Ops:
  7.2 150.6 %copy-start = (f32[4,1536]{1,0:T(4,128)S(1)}, f32[4,1536]{1,0:T(4,128)}, u32[]{:S(2)}) copy-start(f32[4,1536]{1,0:T(4,128)} %param.34) | copy-start | bytes 73732
  7.2 150.3 %copy-start.35 = (f32[24]{0:T(128)S(1)}, f32[24]{0:T(128)}, u32[]{:S(2)}) copy-start(f32[24]{0:T(128)} %param.40) | copy-start | bytes 292
  7.2 150.9 %copy-start.33 = (f32[24]{0:T(128)S(1)}, f32[24]{0:T(128)}, u32[]{:S(2)}) copy-start(f32[24]{0:T(128)} %param.39) | copy-start | bytes 292
  7.2 150.9 %copy-start.34 = (f32[24]{0:T(128)S(1)}, f32[24]{0:T(128)}, u32[]{:S(2)}) copy-start(f32[24]{0:T(128)} %param.38) | copy-start | bytes 292
  7.2 150.9 %copy-start.32 = (f32[512]{0:T(512)S(1)}, f32[512]{0:T(512)}, u32[]{:S(2)}) copy-start(f32[512]{0:T(512)} %param.37) | copy-start | bytes 6148
  7.3 150.9 %copy-start.31 = (f32[4,512]{1,0:T(4,128)S(1)}, f32[4,512]{1,0:T(4,128)}, u32[]{:S(2)}) copy-start(f32[4,512]{1,0:T(4,128)} %param.36) | copy-start | bytes 24580
  7.3 393.9 %reduce-scatter.3.cloned.1.call-start = ((), (), s32[]{:S(2)}) async-start(), calls=%async_computation.2 | async-start | bytes 7864320 | tf_op jit(solution)/shard_map/reduce_scatter | solution.py:1699
  156.0 107.2 %collective-permute-start.1 = (bf16[4,128,1024]{2,1,0:T(8,128)(2,1)}, bf16[4,128,1024]{2,1,0:T(8,128)(2,1)S(1)}, u32[]{:S(2)}, u32[]{:S(2)}) collective-permute-start(bf16[4,128,1024]{2,1,0:T(8,128)(2,1)} %get-tuple-element.95.refs_0_), channel_id=1, source_target_pairs={{0,8},{2,10},{4,12},{6,14},{8,0},{10,2},{12,4},{14,6},{16,24},{18,... | collective-permute-start | bytes 3145736 | tf_op jit(solution)/shard_map/ppermute | solution.py:1676
  156.4 44.5 %collective-permute-start = (bf16[4,128,1024]{2,1,0:T(8,128)(2,1)}, bf16[4,128,1024]{2,1,0:T(8,128)(2,1)S(1)}, u32[]{:S(2)}, u32[]{:S(2)}) collective-permute-start(bf16[4,128,1024]{2,1,0:T(8,128)(2,1)} %get-tuple-element.95.refs_0_), channel_id=1, source_target_pairs={{0,16},{2,18},{4,20},{6,22},{8,24},{10,26},{12,28},{14,30},{16,0},... | collective-permute-start | bytes 3145736 | tf_op jit(solution)/shard_map/ppermute | solution.py:1676
  167.2 28.7 %copy-start.2 = (f32[1024,1280]{1,0:T(8,128)}, f32[1024,1280]{1,0:T(8,128)S(1)}, u32[]{:S(2)}) copy-start(f32[1024,1280]{1,0:T(8,128)S(1)} %fusion.2.projected) | copy-start | bytes 15728644
  190.9 5.1 copy-start.11
  190.9 5.1 copy-start.13
  190.9 5.1 copy-start.24
  190.9 10.2 %copy-start.8 = (bf16[128,2048]{1,0:T(8,128)(2,1)S(1)}, bf16[128,2048]{1,0:T(8,128)(2,1)}, u32[]{:S(2)}) copy-start(bf16[128,2048]{1,0:T(8,128)(2,1)} %get-tuple-element.91.x) | copy-start | bytes 1572868
  190.9 10.2 %copy-start.22 = (bf16[4,128,512]{2,1,0:T(8,128)(2,1)S(1)}, bf16[4,128,512]{2,1,0:T(8,128)(2,1)}, u32[]{:S(2)}) copy-start(bf16[4,128,512]{2,1,0:T(8,128)(2,1)} %get-tuple-element.92.slab) | copy-start | bytes 1572868
  190.9 10.1 %copy-start.28 = (f32[2048]{0:T(1024)S(1)}, f32[2048]{0:T(1024)}, u32[]{:S(2)}) copy-start(f32[2048]{0:T(1024)} %param.46) | copy-start | bytes 24580
  196.0 67.2 %copy-start.17 = (bf16[4,128,1024]{2,1,0:T(8,128)(2,1)S(1)}, bf16[4,128,1024]{2,1,0:T(8,128)(2,1)}, u32[]{:S(2)}) copy-start(bf16[4,128,1024]{2,1,0:T(8,128)(2,1)} %get-tuple-element.95.refs_0_) | copy-start | bytes 3145732
  200.8 62.3 %collective-permute-start.2 = (bf16[4,128,1024]{2,1,0:T(8,128)(2,1)S(1)}, bf16[4,128,1024]{2,1,0:T(8,128)(2,1)S(1)}, u32[]{:S(2)}, u32[]{:S(2)}) collective-permute-start(bf16[4,128,1024]{2,1,0:T(8,128)(2,1)S(1)} %collective-permute-done.refs_1_), channel_id=1, source_target_pairs={{0,8},{2,10},{4,12},{6,14},{8,0},{10,2},{12,4},{14,6},{16,24},{18,... | collective-permute-start | bytes 3145736 | tf_op jit(solution)/shard_map/ppermute | solution.py:1676
  263.2 5.2 copy-start.30
  263.8 4.6 copy-start.5
  263.8 4.6 copy-start.4
  271.7 1.0 copy-start.15
  281.9 230.6 %reduce-scatter.5.cloned.1.call-start = ((), (), s32[]{:S(2)}) async-start(), calls=%async_computation.3 | async-start | bytes 7864320 | tf_op jit(solution)/shard_map/reduce_scatter | solution.py:1699
  281.9 7.2 %copy-start.23 = (bf16[128,2048]{1,0:T(8,128)(2,1)S(1)}, bf16[128,2048]{1,0:T(8,128)(2,1)}, u32[]{:S(2)}) copy-start(bf16[128,2048]{1,0:T(8,128)(2,1)} %get-tuple-element.99.gy) | copy-start | bytes 1572868
  334.2 4.4 copy-start.18
  334.2 4.4 copy-start.12
  334.2 4.4 copy-start.25
  338.6 31.2 %copy-start.3 = (bf16[8,128,2048]{2,1,0:T(8,128)(2,1)S(1)}, bf16[8,128,2048]{2,1,0:T(8,128)(2,1)}, u32[]{:S(2)}) copy-start(bf16[8,128,2048]{2,1,0:T(8,128)(2,1)} %get-tuple-element.85) | copy-start | bytes 12582916
  338.6 31.2 %copy-start.14 = (bf16[1024,512]{1,0:T(8,128)(2,1)S(1)}, bf16[1024,512]{1,0:T(8,128)(2,1)}, u32[]{:S(2)}) copy-start(bf16[1024,512]{1,0:T(8,128)(2,1)} %copy-done.13) | copy-start | bytes 3145732
  369.8 1.7 copy-start.6
  383.0 1.0 copy-start.20
  383.9 1.2 copy-start.16
  385.2 6.1 %copy-start.7 = (bf16[1024,1280]{1,0:T(8,128)(2,1)S(1)}, bf16[1024,1280]{1,0:T(8,128)(2,1)}, u32[]{:S(2)}) copy-start(bf16[1024,1280]{1,0:T(8,128)(2,1)} %get-tuple-element.103.refs_1_) | copy-start | bytes 7864324
  391.2 9.9 %copy-start.9 = (bf16[128,2048]{1,0:T(8,128)(2,1)S(1)}, bf16[128,2048]{1,0:T(8,128)(2,1)}, u32[]{:S(2)}) copy-start(bf16[128,2048]{1,0:T(8,128)(2,1)} %get-tuple-element.91.x) | copy-start | bytes 1572868
  391.2 9.9 %copy-start.26 = (bf16[256,256]{1,0:T(8,128)(2,1)S(1)}, bf16[256,256]{1,0:T(8,128)(2,1)}, u32[]{:S(2)}) copy-start(bf16[256,256]{1,0:T(8,128)(2,1)} %get-tuple-element.106.take) | copy-start | bytes 393220
  391.2 9.9 %copy-start.29 = (f32[2048]{0:T(1024)S(1)}, f32[2048]{0:T(1024)}, u32[]{:S(2)}) copy-start(f32[2048]{0:T(1024)} %param.29) | copy-start | bytes 24580
  401.2 1.5 copy-start.19
  402.7 1.3 copy-start.21
  403.9 108.5 %copy-start.27 = (bf16[256,256]{1,0:T(8,128)(2,1)S(1)}, bf16[256,256]{1,0:T(8,128)(2,1)}, u32[]{:S(2)}) copy-start(bf16[256,256]{1,0:T(8,128)(2,1)} %get-tuple-element.114.give) | copy-start | bytes 393220
  512.5 43.1 %copy-start.1 = (f32[4,1536]{1,0:T(4,128)S(1)}, f32[4,1536]{1,0:T(4,128)}, u32[]{:S(2)}) copy-start(f32[4,1536]{1,0:T(4,128)} %param.34) | copy-start | bytes 73732
  549.1 1.4 copy-start.10
Sparse Core Ops, SparseCore 0:
  282.0 109.8 reduce-scatter.2
  394.1 118.2 reduce-scatter.4
